TPU v7x, 256 devices: a whole 4x4x8 slice. The times are simulated.
256 devices in a mesh: line: 64 (over x, z, core), span: 4 (over y).
Axes of the slice: x: 4, y: 4, z: 8, core: 2. Of those that a mesh axis runs over, the one named last changes fastest.
Arguments:
- forcing: float32 [32, 2048, 256], P('span', 'line'), may hold values from -1 to 1
- blocks: float32 [2048, 256, 256], P(('line', 'span')), may hold values from -1 to 1
- upstream: float32 [2048, 256], P(('line', 'span')), may hold values from -2 to 0
Outputs:
- solution: float32 [32, 2048, 256], P('span', 'line')
All inputs are finite; a program needn't handle non-finite values.
Results may differ from a plain program's by a relative error of at most 0.0003.
Values sent between devices are 32-bit elements; how exact they have to be, the bound alone decides.
No kernel may reach another device: no remote copies, remote signals or barrier semaphores. Data moves between devices by JAX's collectives and lax.ppermute only.
A program may use at most 192 MiB of HBM per device.

v0:
```python
import jax
import jax.numpy as jnp
from jax import lax
from jax.sharding import PartitionSpec as P


def carried_in(value, axis, join, neutral):
    count, mine = (lax.axis_size(axis), lax.axis_index(axis))
    pieces = jax.tree.map(lambda part: lax.all_gather(part, axis), value)
    running = jax.tree.map(
        lambda part, zero: jnp.full_like(part, 0) + jnp.asarray(zero, part.dtype), value, neutral
    )

    def turn(position, running):
        longer = join(running, jax.tree.map(lambda part: part[position], pieces))
        return jax.tree.map(lambda new, old: jnp.where(position < mine, new, old), longer, running)

    return lax.fori_loop(0, count - 1, turn, running)


def sweep(initial, cell_forcing, cell_blocks, cell_upstream):
    carried = initial
    pieces = []
    for cell in range(cell_blocks.shape[0]):
        carried = jnp.dot(
            cell_forcing[:, cell, :] - cell_upstream[cell][None, :] * carried,
            cell_blocks[cell],
            precision=lax.Precision.HIGHEST,
            preferred_element_type=jnp.float32,
        )
        pieces.append(carried)
    return jnp.stack(pieces, axis=1)


def spike_product(cell_blocks, cell_upstream):
    transfer = -cell_upstream[:, :, None] * cell_blocks
    product = transfer[0]
    for cell in range(1, cell_blocks.shape[0]):
        product = jnp.dot(
            product,
            transfer[cell],
            precision=lax.Precision.HIGHEST,
            preferred_element_type=jnp.float32,
        )
    return product


def combine(earlier, later):
    early_map, early_state = earlier
    late_map, late_state = later
    joined_map = jnp.dot(
        early_map, late_map, precision=lax.Precision.HIGHEST, preferred_element_type=jnp.float32
    )
    joined_state = (
        jnp.dot(
            early_state,
            late_map,
            precision=lax.Precision.HIGHEST,
            preferred_element_type=jnp.float32,
        )
        + late_state
    )
    return (joined_map, joined_state)


def shards(forcing, blocks, upstream):
    levels = blocks.shape[-1]
    identity_block = jnp.eye(levels, dtype=jnp.float32)
    local_forcing = lax.all_to_all(forcing, "span", split_axis=1, concat_axis=0, tiled=True)
    cell_blocks, cell_upstream = (blocks, upstream)
    zero_state = jnp.zeros((local_forcing.shape[0], levels), jnp.float32)
    trial = sweep(zero_state, local_forcing, cell_blocks, cell_upstream)
    last_states = trial[:, -1, :]
    spike_map = spike_product(cell_blocks, cell_upstream)
    merged = carried_in(
        (spike_map, last_states), ("line", "span"), combine, (identity_block, zero_state)
    )
    incoming = merged[1]
    solved = sweep(incoming, local_forcing, cell_blocks, cell_upstream)
    return lax.all_to_all(solved, "span", split_axis=0, concat_axis=1, tiled=True)


def solution(mesh):
    placed = (P("span", "line", None), P(("line", "span"), None, None), P(("line", "span"), None))
    return jax.shard_map(
        shards, mesh=mesh, in_specs=placed, out_specs=P("span", "line", None), check_vma=False
    )
```

profile of v0, /device:TPU:6, one launch (start us, length us, event | category | flops | bytes accessed | tf_op | source)
XLA Modules:
  0.0 696.5 jit_solution(3042014740385967955)
XLA Ops:
  6.5 2.0 copy.6
  8.5 4.6 all-to-all-start
  14.1 5.7 all-to-all-done
  28.2 115.1 %all-gather.7.cloned.1.call-done = f32[8192,256]{1,0:T(8,128)} async-done(((f32[32,256]{1,0:T(8,128)}), f32[8192,256]{1,0:T(8,128)}) %all-gather.7.cloned.1.call-update) | async-done | bytes 8388624 | tf_op jit(solution)/shard_map/all_gather | solution.py:9
  143.3 213.1 %all-gather.5.cloned.1.call-done = f32[65536,256]{1,0:T(8,128)} async-done(((f32[256,256]{1,0:T(8,128)}), f32[65536,256]{1,0:T(8,128)}) %all-gather.5.cloned.1.call-update) | async-done | bytes 67108880 | tf_op jit(solution)/shard_map/all_gather | solution.py:9
  356.4 320.7 %while.14 = (s32[]{:T(128)}, f32[32,256]{1,0:T(8,128)S(1)}, s32[]{:T(128)}, f32[256,256,256]{2,1,0:T(8,128)}, f32[256,32,256]{2,1,0:T(8,128)}, /*index=5*/s32[]{:T(128)}, s32[]{:T(128)}) while((s32[]{:T(128)}, f32[32,256]{1,0:T(8,128)S(1)}, s32[]{:T(128)}, f32[256,256,256]{2,1,0:T(8,128)}, f32[256,32,256]{2,1,0:T(8,128)}, ...), condition=%wide.region_1.2_spmd.clone, body=%wide.region_0.1_spmd.clone.sunk | while | flops 25198596 | bytes 461415 | solution.py:18
  358.9 1.2 fusion.111
  360.2 1.2 fusion.111
  362.7 1.2 fusion.111
  363.9 1.2 fusion.111
  365.2 1.2 fusion.111
  369.0 1.2 fusion.111
  370.2 1.2 fusion.111
  372.7 1.2 fusion.111
  374.0 1.2 fusion.111
  377.8 1.2 fusion.111
  380.3 1.2 fusion.111
  381.5 1.2 fusion.111
  382.8 1.2 fusion.111
  384.1 1.2 fusion.111
  386.6 1.2 fusion.111
  390.3 1.2 fusion.111
  391.6 1.2 fusion.111
  679.2 9.8 %all_to_all.36 = f32[32,8,256]{2,1,0:T(8,128)S(1)} all-to-all(f32[32,8,256]{2,1,0:T(8,128)S(1)} %copy.8), channel_id=1, replica_groups=mesh['line'=64,'span'=4] {'span'}, dimensions={0} | all-to-all | bytes 524288 | tf_op jit(solution)/shard_map/all_to_all | solution.py:80
  (532 shorter events, 301.7 us)
Async XLA Ops:
  6.5 15.7 %copy-start = (f32[8,256,256]{2,1,0:T(8,128)S(1)}, f32[8,256,256]{2,1,0:T(8,128)}, u32[]{:S(2)}) copy-start(f32[8,256,256]{2,1,0:T(8,128)} %param.6) | copy-start | bytes 6291460
  8.5 15.8 %copy-start.1 = (f32[8,256]{1,0:T(8,128)S(1)}, f32[8,256]{1,0:T(8,128)}, u32[]{:S(2)}) copy-start(f32[8,256]{1,0:T(8,128)} %param.7) | copy-start | bytes 24580
  8.5 11.3 %all-to-all-start = ((f32[8,32,256]{2,0,1:T(8,128)}), f32[8,32,256]{2,0,1:T(8,128)S(1)}, u32[]{:S(2)}, u32[]{:S(2)}) async-start(f32[8,32,256]{2,0,1:T(8,128)} %copy.6), calls=%async_computation | async-start | bytes 524288 | tf_op jit(solution)/shard_map/all_to_all | solution.py:69
  13.1 130.2 %all-gather.7.cloned.1.call-start = ((), (), s32[]{:S(2)}) async-start(), calls=%async_computation.3 | async-start | bytes 8421376 | tf_op jit(solution)/shard_map/all_gather | solution.py:9
  24.3 332.1 %all-gather.5.cloned.1.call-start = ((), (), s32[]{:S(2)}) async-start(), calls=%async_computation.2 | async-start | bytes 67371008 | tf_op jit(solution)/shard_map/all_gather | solution.py:9
Sparse Core Ops, SparseCore 0:
  24.4 118.8 all-gather.6
  146.9 209.4 all-gather.4
where the time goes:
time: 703 us; the launch traced here: 697 us
  waiting for transfers between devices  334 us (48%)
  matrix products  319 us (45%)
  between operations  13.6 us (2%)
  loops' own time  10.3 us (1%)
  blocking collectives  9.76 us (1%)
    all_gather x2, waiting for transfers between devices, carried_in(): pieces = jax.tree.map(lambda part: lax.all_gather(part, axis), value)  328 us
    dot_general x255, matrix products, combine(): jnp.dot(early_state, late_map, precision=lax.Precision.HIGHEST, preferred...  309 us
  transfers between devices with their start and end apart: 3, of which 3 were waited for; matrix products, arithmetic and copies ran while one was open for 1% of the time, Pallas kernels for 0%

commit v1 on v0

v1 whole, which is shorter than its diff:
```python
import functools

import jax
import jax.numpy as jnp
from jax import lax
from jax.experimental import pallas as pl
from jax.experimental.pallas import tpu as pltpu
from jax.sharding import PartitionSpec as P

F32 = jnp.float32
BIG = 2.0**40
STEP = 2.0**48
VMEM_BYTES = 48 * 2**20


def dot(a, b):
    return jnp.dot(a, b, precision=lax.Precision.HIGHEST, preferred_element_type=F32)


def whole(shape):
    return pl.BlockSpec(shape, lambda *_: (0,) * len(shape))


def call(kernel, grid, in_specs, out_specs, out_shape, scratch=(), flops=0):
    return pl.pallas_call(
        kernel,
        grid=grid,
        in_specs=in_specs,
        out_specs=out_specs,
        out_shape=out_shape,
        scratch_shapes=list(scratch),
        compiler_params=pltpu.CompilerParams(vmem_limit_bytes=VMEM_BYTES),
        cost_estimate=pl.CostEstimate(flops=flops, bytes_accessed=2**21, transcendentals=0),
    )


def settle(hat, count):
    large = jnp.max(jnp.abs(hat), keepdims=True) > BIG
    return hat * jnp.where(large, 1.0 / STEP, 1.0), count + jnp.where(large, 1.0, 0.0)


def unscale(value, count):
    for done in (0.0, 2.0, 4.0):
        left = count - done
        value = value * jnp.where(left > 1.5, STEP * STEP, jnp.where(left > 0.5, STEP, 1.0))
    return value


def maps_kernel(upstream_ref, block_ref, prefix_ref, last):
    cell = pl.program_id(0)
    scale = -upstream_ref[pl.ds(cell, 1), :]

    @pl.when(cell == 0)
    def _():
        levels = block_ref.shape[-1]
        row = lax.broadcasted_iota(jnp.int32, (levels, levels), 0)
        column = lax.broadcasted_iota(jnp.int32, (levels, levels), 1)
        last[...] = jnp.where(row == column, 1.0, 0.0).astype(F32)

    product = dot(last[...] * scale, block_ref[0])
    last[...] = product
    prefix_ref[0] = product


def prefix_maps(blocks, upstream):
    cells, levels, _ = blocks.shape
    block = pl.BlockSpec((1, levels, levels), lambda i: (i, 0, 0))
    return call(
        maps_kernel,
        (cells,),
        [whole((cells, levels)), block],
        block,
        jax.ShapeDtypeStruct(blocks.shape, F32),
        [pltpu.VMEM((levels, levels), F32)],
        12 * cells * levels**3,
    )(upstream, blocks)


def states_kernel(upstream_ref, block_ref, forcing_ref, product_ref, trial_ref, message_ref, last):
    cell = pl.program_id(0)
    lines, levels = last.shape

    @pl.when(cell == 0)
    def _():
        last[...] = jnp.zeros_like(last)

    state = dot(forcing_ref[:, cell, :] - upstream_ref[pl.ds(cell, 1), :] * last[...], block_ref[0])
    last[...] = state
    trial_ref[0] = state

    @pl.when(cell == pl.num_programs(0) - 1)
    def _():
        hat, count = settle(product_ref[0], jnp.zeros((8, levels), F32))
        message_ref[:levels] = hat
        message_ref[levels : levels + lines] = state
        message_ref[levels + lines :] = count


def trial_states(blocks, upstream, forcing, prefix):
    cells, levels, _ = blocks.shape
    lines = forcing.shape[0]
    rows = levels + lines + 8
    return call(
        states_kernel,
        (cells,),
        [
            whole((cells, levels)),
            pl.BlockSpec((1, levels, levels), lambda i: (i, 0, 0)),
            whole(forcing.shape),
            pl.BlockSpec((1, levels, levels), lambda i: (cells - 1, 0, 0)),
        ],
        [pl.BlockSpec((1, lines, levels), lambda i: (i, 0, 0)), whole((rows, levels))],
        [
            jax.ShapeDtypeStruct((cells, lines, levels), F32),
            jax.ShapeDtypeStruct((rows, levels), F32),
        ],
        [pltpu.VMEM((lines, levels), F32)],
        12 * cells * lines * levels**2,
    )(upstream, blocks, forcing, prefix)


def merge_kernel(levels, upper_ref, mine_ref, theirs_ref, before_ref, total_ref, ahead_ref):
    states = mine_ref.shape[0] - 8

    def joined(left_ref, right_ref, out_ref):
        both = dot(left_ref[:states], right_ref[:levels])
        hat, count = settle(both[:levels], left_ref[states:] + right_ref[states:])
        out_ref[:levels] = hat
        out_ref[levels:states] = (
            unscale(both[levels:], right_ref[states : states + 1]) + right_ref[levels:states]
        )
        out_ref[states:] = count

    @pl.when(upper_ref[0] == 1)
    def _():
        joined(theirs_ref, mine_ref, total_ref)
        joined(theirs_ref, before_ref, ahead_ref)

    @pl.when(upper_ref[0] == 0)
    def _():
        joined(mine_ref, theirs_ref, total_ref)
        ahead_ref[...] = before_ref[...]


def merge(levels, upper, mine, theirs, before):
    spec = whole(mine.shape)
    shape = jax.ShapeDtypeStruct(mine.shape, F32)
    return call(
        functools.partial(merge_kernel, levels),
        (1,),
        [pl.BlockSpec(memory_space=pltpu.SMEM), spec, spec, spec],
        [spec, spec],
        [shape, shape],
        (),
        24 * mine.shape[0] * levels**2,
    )(upper, mine, theirs, before)


def finish_kernel(
    levels, upper_ref, theirs_ref, before_ref, prefix_ref, trial_ref, solved_ref, incoming
):
    cell = pl.program_id(0)
    states = before_ref.shape[0] - 8

    @pl.when(cell == 0)
    def _():
        incoming[...] = before_ref[levels:states]

        @pl.when(upper_ref[0] == 1)
        def _():
            incoming[...] += unscale(
                dot(theirs_ref[...], before_ref[:levels]), before_ref[states : states + 1]
            )

    solved_ref[:, cell, :] = trial_ref[0] + dot(incoming[...], prefix_ref[0])


def finish(levels, upper, theirs, before, prefix, trial):
    cells, lines, _ = trial.shape
    return call(
        functools.partial(finish_kernel, levels),
        (cells,),
        [
            pl.BlockSpec(memory_space=pltpu.SMEM),
            whole(theirs.shape),
            whole(before.shape),
            pl.BlockSpec((1, levels, levels), lambda i: (i, 0, 0)),
            pl.BlockSpec((1, lines, levels), lambda i: (i, 0, 0)),
        ],
        whole((lines, cells, levels)),
        jax.ShapeDtypeStruct((lines, cells, levels), F32),
        [pltpu.VMEM((lines, levels), F32)],
        12 * (cells + 1) * lines * levels**2,
    )(upper, theirs, before, prefix, trial)


def shards(sizes, forcing, blocks, upstream):
    line_count, span_count = sizes
    cells, levels, _ = blocks.shape
    share = forcing.shape[0]
    lines = share * span_count
    parts = forcing.reshape(share, span_count, cells, levels).swapaxes(0, 1)
    parts = lax.all_to_all(parts, "span", split_axis=0, concat_axis=0, tiled=True)
    local_forcing = parts.reshape(lines, cells, levels)
    prefix = prefix_maps(blocks, upstream)
    trial, total = trial_states(blocks, upstream, local_forcing, prefix)

    rounds = [("span", 1 << b) for b in range(span_count.bit_length() - 1)]
    rounds += [("line", 1 << b) for b in range(line_count.bit_length() - 1)]
    before = jnp.concatenate(
        [jnp.eye(levels, dtype=F32), jnp.zeros((lines + 8, levels), F32)], axis=0
    )

    def partner(value, axis, bit):
        count = lax.axis_size(axis)
        return lax.ppermute(value, axis, [(i, i ^ bit) for i in range(count)])

    def is_upper(axis, bit):
        return jnp.where((lax.axis_index(axis) & bit) != 0, 1, 0).astype(jnp.int32).reshape(1)

    for axis, bit in rounds[:-1]:
        theirs = partner(total, axis, bit)
        total, before = merge(levels, is_upper(axis, bit), total, theirs, before)
    axis, bit = rounds[-1]
    theirs = partner(total[levels : levels + lines], axis, bit)
    solved = finish(levels, is_upper(axis, bit), theirs, before, prefix, trial)
    parts = solved.reshape(span_count, share, cells, levels)
    parts = lax.all_to_all(parts, "span", split_axis=0, concat_axis=0, tiled=True)
    return parts.swapaxes(0, 1).reshape(share, span_count * cells, levels)


def solution(mesh):
    placed = (P("span", "line", None), P(("line", "span"), None, None), P(("line", "span"), None))
    sizes = (mesh.shape["line"], mesh.shape["span"])
    return jax.shard_map(
        functools.partial(shards, sizes),
        mesh=mesh,
        in_specs=placed,
        out_specs=P("span", "line", None),
        check_vma=False,
    )
```

time: 703 us -> 123 us (0.17)
  matrix products: 319 us -> 0 us
  waiting for transfers between devices: 334 us -> 59.3 us
  starting transfers between devices: 4.64 us -> 21.9 us
  between operations: 13.6 us -> 0.17 us
  Pallas kernels: 0 us -> 11.5 us
  local copies, waits for them, and re-layouts: 4.93 us -> 16.3 us
  loops' own time: 10.3 us -> 0 us
    all_gather x2 -> x0, waiting for transfers between devices: 328 us -> none  [carried_in(): pieces = jax.tree.map(lambda part: lax.all_gather(part, axis), value)]
    dot_general x278 -> x0, matrix products: 319 us -> none  [the longest x255 309 us: combine(): jnp.dot(early_state, late_map, precision=lax.Precision.HIGHEST, preferred...]
    ppermute x0 -> x8, waiting for transfers between devices: none -> 58.1 us  [partner(): return lax.ppermute(value, axis, [(i, i ^ bit) for i in range(count)])]
    ppermute x0 -> x8, starting transfers between devices: none -> 17.5 us  [partner(): return lax.ppermute(value, axis, [(i, i ^ bit) for i in range(count)])]
    unnamed x5 -> x34, local copies, waits for them, and re-layouts: 1.96 us -> 14.9 us
    pallas_call x0 -> x10, Pallas kernels: none -> 11.5 us  [the longest x7 4.03 us: merge(): call(functools.partial(merge_kernel, levels), (1,), [pl.BlockSpec(memory_...]
    another operation x1 -> x0, loops' own time: 10.3 us -> none  [carried_in(): return lax.fori_loop(0, count - 1, turn, running)]
  transfers between devices with their start and end apart: 3 -> 9, of which waited for: 3 -> 9; matrix products, arithmetic and copies ran while one was open for 1% -> 0% of each run, Pallas kernels for 0% -> 3%
where the time goes in v1:
time: 123 us; the launch traced here: 121 us
  waiting for transfers between devices  59.3 us (48%)
  starting transfers between devices  21.9 us (18%)
  local copies, waits for them, and re-layouts  16.3 us (13%)
  Pallas kernels  11.5 us (9%)
  blocking collectives  11.3 us (9%)
    ppermute x8, waiting for transfers between devices, partner(): return lax.ppermute(value, axis, [(i, i ^ bit) for i in range(count)])  58.1 us
    ppermute x8, starting transfers between devices, partner(): return lax.ppermute(value, axis, [(i, i ^ bit) for i in range(count)])  17.5 us
    unnamed x34, local copies, waits for them, and re-layouts  14.9 us
    all_to_all x1, blocking collectives, shards(): lax.all_to_all(parts, 'span', split_axis=0, concat_axis=0, tiled=True)  11.3 us
    all_to_all x1, starting transfers between devices, shards(): lax.all_to_all(parts, 'span', split_axis=0, concat_axis=0, tiled=True)  4.46 us
    pallas_call x7, Pallas kernels, merge(): call(functools.partial(merge_kernel, levels), (1,), [pl.BlockSpec(memory_...  4.03 us
    pallas_call x1, Pallas kernels, prefix_maps(): call(maps_kernel, (cells,), [whole((cells, levels)), block], block, jax.S...  3.19 us
  transfers between devices with their start and end apart: 9, of which 9 were waited for; matrix products, arithmetic and copies ran while one was open for 0% of the time, Pallas kernels for 3%

profile of v1, /device:TPU:6, one launch (start us, length us, event | category | flops | bytes accessed | tf_op | source)
XLA Modules:
  0.0 120.6 jit_solution(8119297070886156477)
XLA Ops:
  1.7 4.5 %all-to-all-start = ((f32[4,8,8,256]{3,2,1,0:T(8,128)}), f32[4,8,8,256]{3,2,1,0:T(8,128)S(1)}, u32[]{:S(2)}, u32[]{:S(2)}) async-start(f32[4,8,8,256]{3,2,1,0:T(8,128)} %copy_bitcast_fusion.1), calls=%async_computation | async-start | bytes 524288 | tf_op jit(solution)/shard_map/all_to_all | solution.py:203
  6.1 1.6 %copy-done.1 = f32[8,256,256]{2,1,0:T(8,128)S(1)} copy-done((f32[8,256,256]{2,1,0:T(8,128)S(1)}, f32[8,256,256]{2,1,0:T(8,128)}, u32[]{:S(2)}) %copy-start.1) | copy-done | bytes 2097176
  8.4 3.2 %shard_map.37.product_ref.prefix_ref = f32[8,256,256]{2,1,0:T(8,128)S(1)} custom-call(f32[8,256]{1,0:T(8,128)S(1)} %copy-done.3, f32[8,256,256]{2,1,0:T(8,128)S(1)} %copy-done.1), custom_call_target="tpu_custom_call" | custom-call | flops 1610612736 | bytes 2097152 | tf_op jit(solution)/shard_map/pallas_call | solution.py:68
  11.6 1.2 all-to-all-done
  12.8 1.6 %copy-done.2 = f32[8,256,256]{2,1,0:T(8,128)S(1)} copy-done((f32[8,256,256]{2,1,0:T(8,128)S(1)}, f32[8,256,256]{2,1,0:T(8,128)}, u32[]{:S(2)}) %copy-start.2) | copy-done | bytes 2097176
  14.4 2.1 %shard_map.38 = (f32[8,32,256]{2,1,0:T(8,128)S(1)}, f32[296,256]{1,0:T(8,128)S(1)}) custom-call(f32[8,256]{1,0:T(8,128)S(1)} %copy-done.4, f32[8,256,256]{2,1,0:T(8,128)S(1)} %copy-done.2, f32[32,8,256]{2,1,0:T(8,128)S(1)} %bitcast.20, f32[8,256,256]{2,1,0:T(8,128)S(1)} %shard_map.37.product_ref.prefix_ref), custom_call_target="tpu_custom_call" | custom-call | flops 201326592 | bytes 2097152 | tf_op jit(solution)/shard_map/pallas_call | solution.py:103
  17.5 6.6 %collective-permute-done.theirs_ref = f32[296,256]{1,0:T(8,128)S(1)} collective-permute-done((f32[296,256]{1,0:T(8,128)S(1)}, f32[296,256]{1,0:T(8,128)S(1)}, u32[]{:S(2)}, u32[]{:S(2)}) %collective-permute-start) | collective-permute-done | bytes 303136 | tf_op jit(solution)/shard_map/ppermute | solution.py:216
  25.4 3.2 %collective-permute-start.1 = (f32[296,256]{1,0:T(8,128)S(1)}, f32[296,256]{1,0:T(8,128)S(1)}, u32[]{:S(2)}, u32[]{:S(2)}) collective-permute-start(f32[296,256]{1,0:T(8,128)S(1)} %get-tuple-element.22.mine_ref), channel_id=1, source_target_pairs={{0,2},{1,3},{2,0},{3,1},{4,6},{5,7},{6,4},{7,5},{8,10},{9,11},{10,... | collective-permute-start | bytes 909320 | tf_op jit(solution)/shard_map/ppermute | solution.py:216
  28.6 5.7 %collective-permute-done.1.theirs_ref = f32[296,256]{1,0:T(8,128)S(1)} collective-permute-done((f32[296,256]{1,0:T(8,128)S(1)}, f32[296,256]{1,0:T(8,128)S(1)}, u32[]{:S(2)}, u32[]{:S(2)}) %collective-permute-start.1) | collective-permute-done | bytes 303136 | tf_op jit(solution)/shard_map/ppermute | solution.py:216
  34.3 1.0 copy-done.8
  36.5 1.6 %collective-permute-done.2.theirs_ref = f32[296,256]{1,0:T(8,128)S(1)} collective-permute-done((f32[296,256]{1,0:T(8,128)S(1)}, f32[296,256]{1,0:T(8,128)S(1)}, u32[]{:S(2)}, u32[]{:S(2)}) %collective-permute-start.2) | collective-permute-done | bytes 303136 | tf_op jit(solution)/shard_map/ppermute | solution.py:216
  40.3 1.9 %collective-permute-start.3 = (f32[296,256]{1,0:T(8,128)S(1)}, f32[296,256]{1,0:T(8,128)S(1)}, u32[]{:S(2)}, u32[]{:S(2)}) collective-permute-start(f32[296,256]{1,0:T(8,128)S(1)} %get-tuple-element.26.mine_ref), channel_id=1, source_target_pairs={{0,8},{4,12},{8,0},{12,4},{16,24},{20,28},{24,16},{28,20},{32,40},... | collective-permute-start | bytes 909320 | tf_op jit(solution)/shard_map/ppermute | solution.py:216
  42.2 7.8 %collective-permute-done.3.theirs_ref = f32[296,256]{1,0:T(8,128)S(1)} collective-permute-done((f32[296,256]{1,0:T(8,128)S(1)}, f32[296,256]{1,0:T(8,128)S(1)}, u32[]{:S(2)}, u32[]{:S(2)}) %collective-permute-start.3) | collective-permute-done | bytes 303136 | tf_op jit(solution)/shard_map/ppermute | solution.py:216
  50.0 1.0 copy-done.10
  52.2 3.3 %collective-permute-start.4 = (f32[296,256]{1,0:T(8,128)S(1)}, f32[296,256]{1,0:T(8,128)S(1)}, u32[]{:S(2)}, u32[]{:S(2)}) collective-permute-start(f32[296,256]{1,0:T(8,128)S(1)} %get-tuple-element.28.mine_ref), channel_id=1, source_target_pairs={{0,16},{4,20},{8,24},{12,28},{16,0},{20,4},{24,8},{28,12},{32,48},... | collective-permute-start | bytes 909320 | tf_op jit(solution)/shard_map/ppermute | solution.py:216
  55.5 13.7 %collective-permute-done.4.theirs_ref = f32[296,256]{1,0:T(8,128)S(1)} collective-permute-done((f32[296,256]{1,0:T(8,128)S(1)}, f32[296,256]{1,0:T(8,128)S(1)}, u32[]{:S(2)}, u32[]{:S(2)}) %collective-permute-start.4) | collective-permute-done | bytes 303136 | tf_op jit(solution)/shard_map/ppermute | solution.py:216
  69.2 1.0 copy-done.12
  71.4 6.2 %collective-permute-start.5 = (f32[296,256]{1,0:T(8,128)S(1)}, f32[296,256]{1,0:T(8,128)S(1)}, u32[]{:S(2)}, u32[]{:S(2)}) collective-permute-start(f32[296,256]{1,0:T(8,128)S(1)} %get-tuple-element.30.mine_ref), channel_id=1, source_target_pairs={{0,32},{4,36},{8,40},{12,44},{16,48},{20,52},{24,56},{28,60},{32,0... | collective-permute-start | bytes 909320 | tf_op jit(solution)/shard_map/ppermute | solution.py:216
  77.6 12.0 %collective-permute-done.5.theirs_ref = f32[296,256]{1,0:T(8,128)S(1)} collective-permute-done((f32[296,256]{1,0:T(8,128)S(1)}, f32[296,256]{1,0:T(8,128)S(1)}, u32[]{:S(2)}, u32[]{:S(2)}) %collective-permute-start.5) | collective-permute-done | bytes 303136 | tf_op jit(solution)/shard_map/ppermute | solution.py:216
  92.7 6.4 %collective-permute-done.6.theirs_ref = f32[296,256]{1,0:T(8,128)S(1)} collective-permute-done((f32[296,256]{1,0:T(8,128)S(1)}, f32[296,256]{1,0:T(8,128)S(1)}, u32[]{:S(2)}, u32[]{:S(2)}) %collective-permute-start.6) | collective-permute-done | bytes 303136 | tf_op jit(solution)/shard_map/ppermute | solution.py:216
  100.9 1.1 collective-permute-start.7
  102.0 4.4 %collective-permute-done.7.theirs_ref = f32[32,256]{1,0:T(8,128)S(1)} collective-permute-done((f32[32,256]{1,0:T(8,128)S(1)}, f32[32,256]{1,0:T(8,128)S(1)}, u32[]{:S(2)}, u32[]{:S(2)}) %collective-permute-start.7) | collective-permute-done | bytes 32800 | tf_op jit(solution)/shard_map/ppermute | solution.py:216
  106.4 2.2 %shard_map.46 = f32[32,8,256]{2,1,0:T(8,128)S(1)} custom-call(s32[1]{0:T(128)} %bitcast.upper_ref, f32[32,256]{1,0:T(8,128)S(1)} %collective-permute-done.7.theirs_ref, f32[296,256]{1,0:T(8,128)S(1)} %get-tuple-element.35.before_ref, f32[8,256,256]{2,1,0:T(8,128)S(1)} %shard_map.37.product_ref.prefix_ref, f32[8,32,256]{2,1,0:T(8,128)S(1)} %get-tuple-element.36.trial_ref), custom_call_target="tpu_custom_call" | custom-call | flops 226492416 | bytes 2097152 | tf_op jit(solution)/shard_map/pallas_call | solution.py:180
  108.6 11.3 %all_to_all.10 = f32[4,8,8,256]{3,2,1,0:T(8,128)S(1)} all-to-all(f32[4,8,8,256]{3,2,1,0:T(8,128)S(1)} %bitcast.21), channel_id=1, replica_groups=mesh['line'=64,'span'=4] {'span'}, dimensions={0} | all-to-all | bytes 524288 | tf_op jit(solution)/shard_map/all_to_all | solution.py:228
  (44 shorter events, 16.1 us)
Async XLA Ops:
  0.0 1.0 copy-start
  1.7 11.1 %all-to-all-start = ((f32[4,8,8,256]{3,2,1,0:T(8,128)}), f32[4,8,8,256]{3,2,1,0:T(8,128)S(1)}, u32[]{:S(2)}, u32[]{:S(2)}) async-start(f32[4,8,8,256]{3,2,1,0:T(8,128)} %copy_bitcast_fusion.1), calls=%async_computation | async-start | bytes 524288 | tf_op jit(solution)/shard_map/all_to_all | solution.py:203
  6.1 1.6 %copy-start.1 = (f32[8,256,256]{2,1,0:T(8,128)S(1)}, f32[8,256,256]{2,1,0:T(8,128)}, u32[]{:S(2)}) copy-start(f32[8,256,256]{2,1,0:T(8,128)} %block_ref.3) | copy-start | bytes 6291460
  8.4 4.4 %copy-start.4 = (f32[8,256]{1,0:T(8,128)S(1)}, f32[8,256]{1,0:T(8,128)}, u32[]{:S(2)}) copy-start(f32[8,256]{1,0:T(8,128)} %upstream_ref.3) | copy-start | bytes 24580
  12.8 1.6 %copy-start.2 = (f32[8,256,256]{2,1,0:T(8,128)S(1)}, f32[8,256,256]{2,1,0:T(8,128)}, u32[]{:S(2)}) copy-start(f32[8,256,256]{2,1,0:T(8,128)} %block_ref.3) | copy-start | bytes 6291460
  16.5 7.6 %collective-permute-start = (f32[296,256]{1,0:T(8,128)S(1)}, f32[296,256]{1,0:T(8,128)S(1)}, u32[]{:S(2)}, u32[]{:S(2)}) collective-permute-start(f32[296,256]{1,0:T(8,128)S(1)} %get-tuple-element.21.mine_ref), channel_id=1, source_target_pairs={{0,1},{1,0},{2,3},{3,2},{4,5},{5,4},{6,7},{7,6},{8,9},{9,8},{10,11... | collective-permute-start | bytes 909320 | tf_op jit(solution)/shard_map/ppermute | solution.py:216
  24.7 0.7 copy-start.7
  25.4 8.9 %collective-permute-start.1 = (f32[296,256]{1,0:T(8,128)S(1)}, f32[296,256]{1,0:T(8,128)S(1)}, u32[]{:S(2)}, u32[]{:S(2)}) collective-permute-start(f32[296,256]{1,0:T(8,128)S(1)} %get-tuple-element.22.mine_ref), channel_id=1, source_target_pairs={{0,2},{1,3},{2,0},{3,1},{4,6},{5,7},{6,4},{7,5},{8,10},{9,11},{10,... | collective-permute-start | bytes 909320 | tf_op jit(solution)/shard_map/ppermute | solution.py:216
  34.3 1.0 copy-start.8
  36.5 1.6 %collective-permute-start.2 = (f32[296,256]{1,0:T(8,128)S(1)}, f32[296,256]{1,0:T(8,128)S(1)}, u32[]{:S(2)}, u32[]{:S(2)}) collective-permute-start(f32[296,256]{1,0:T(8,128)S(1)} %get-tuple-element.24.mine_ref), channel_id=1, source_target_pairs={{0,4},{4,0},{8,12},{12,8},{16,20},{20,16},{24,28},{28,24},{32,36},... | collective-permute-start | bytes 909320 | tf_op jit(solution)/shard_map/ppermute | solution.py:216
  38.1 1.0 copy-start.6
  39.6 0.7 copy-start.9
  40.3 9.7 %collective-permute-start.3 = (f32[296,256]{1,0:T(8,128)S(1)}, f32[296,256]{1,0:T(8,128)S(1)}, u32[]{:S(2)}, u32[]{:S(2)}) collective-permute-start(f32[296,256]{1,0:T(8,128)S(1)} %get-tuple-element.26.mine_ref), channel_id=1, source_target_pairs={{0,8},{4,12},{8,0},{12,4},{16,24},{20,28},{24,16},{28,20},{32,40},... | collective-permute-start | bytes 909320 | tf_op jit(solution)/shard_map/ppermute | solution.py:216
  50.0 1.0 copy-start.10
  51.5 0.7 copy-start.11
  52.2 16.9 %collective-permute-start.4 = (f32[296,256]{1,0:T(8,128)S(1)}, f32[296,256]{1,0:T(8,128)S(1)}, u32[]{:S(2)}, u32[]{:S(2)}) collective-permute-start(f32[296,256]{1,0:T(8,128)S(1)} %get-tuple-element.28.mine_ref), channel_id=1, source_target_pairs={{0,16},{4,20},{8,24},{12,28},{16,0},{20,4},{24,8},{28,12},{32,48},... | collective-permute-start | bytes 909320 | tf_op jit(solution)/shard_map/ppermute | solution.py:216
  69.2 1.0 copy-start.12
  70.7 0.7 copy-start.13
  71.4 18.3 %collective-permute-start.5 = (f32[296,256]{1,0:T(8,128)S(1)}, f32[296,256]{1,0:T(8,128)S(1)}, u32[]{:S(2)}, u32[]{:S(2)}) collective-permute-start(f32[296,256]{1,0:T(8,128)S(1)} %get-tuple-element.30.mine_ref), channel_id=1, source_target_pairs={{0,32},{4,36},{8,40},{12,44},{16,48},{20,52},{24,56},{28,60},{32,0... | collective-permute-start | bytes 909320 | tf_op jit(solution)/shard_map/ppermute | solution.py:216
  89.7 1.0 copy-start.14
  91.2 0.7 copy-start.15
  91.9 7.2 %collective-permute-start.6 = (f32[296,256]{1,0:T(8,128)S(1)}, f32[296,256]{1,0:T(8,128)S(1)}, u32[]{:S(2)}, u32[]{:S(2)}) collective-permute-start(f32[296,256]{1,0:T(8,128)S(1)} %get-tuple-element.32.mine_ref), channel_id=1, source_target_pairs={{0,64},{4,68},{8,72},{12,76},{16,80},{20,84},{24,88},{28,92},{32,9... | collective-permute-start | bytes 909320 | tf_op jit(solution)/shard_map/ppermute | solution.py:216
  99.0 1.0 copy-start.16
  100.9 5.5 %collective-permute-start.7 = (f32[32,256]{1,0:T(8,128)S(1)}, f32[32,256]{1,0:T(8,128)S(1)}, u32[]{:S(2)}, u32[]{:S(2)}) collective-permute-start(f32[32,256]{1,0:T(8,128)S(1)} %slice.3), channel_id=1, source_target_pairs={{0,128},{4,132},{8,136},{12,140},{16,144},{20,148},{24,152},{28,15... | collective-permute-start | bytes 98312 | tf_op jit(solution)/shard_map/ppermute | solution.py:216
  (2 other events, 1.4 us)

commit v2 on v1

--- a/solution.py
+++ b/solution.py
@@ -10,7 +10,18 @@
 F32 = jnp.float32
 BIG = 2.0**40
 STEP = 2.0**48
-VMEM_BYTES = 48 * 2**20
+CORE = 1
+ROUNDS = (
+    ("span", 1, 1, False),
+    ("span", 3, 2, False),
+    ("line", 1, 1, False),
+    ("line", 2, 2, True),
+    ("line", 4, 4, True),
+    ("line", 14, 8, True),
+    ("line", 16, 16, False),
+    ("line", 48, 32, False),
+)
+VMEM_BYTES = 60 * 2**20
 
 
 def dot(a, b):
@@ -21,7 +32,7 @@
     return pl.BlockSpec(shape, lambda *_: (0,) * len(shape))
 
 
-def call(kernel, grid, in_specs, out_specs, out_shape, scratch=(), flops=0):
+def call(kernel, grid, in_specs, out_specs, out_shape, scratch=(), flops=0, vmem=VMEM_BYTES):
     return pl.pallas_call(
         kernel,
         grid=grid,
@@ -29,7 +40,7 @@
         out_specs=out_specs,
         out_shape=out_shape,
         scratch_shapes=list(scratch),
-        compiler_params=pltpu.CompilerParams(vmem_limit_bytes=VMEM_BYTES),
+        compiler_params=pltpu.CompilerParams(vmem_limit_bytes=vmem),
         cost_estimate=pl.CostEstimate(flops=flops, bytes_accessed=2**21, transcendentals=0),
     )
 
@@ -93,13 +104,14 @@
         hat, count = settle(product_ref[0], jnp.zeros((8, levels), F32))
         message_ref[:levels] = hat
         message_ref[levels : levels + lines] = state
-        message_ref[levels + lines :] = count
+        message_ref[levels + lines : levels + lines + 8] = count
+        message_ref[levels + lines + 8 :] = jnp.zeros_like(count)
 
 
 def trial_states(blocks, upstream, forcing, prefix):
     cells, levels, _ = blocks.shape
     lines = forcing.shape[0]
-    rows = levels + lines + 8
+    rows = levels + lines + 16
     return call(
         states_kernel,
         (cells,),
@@ -116,51 +128,120 @@
         ],
         [pltpu.VMEM((lines, levels), F32)],
         12 * cells * lines * levels**2,
+        8 * 2**20,
     )(upstream, blocks, forcing, prefix)
 
 
-def merge_kernel(levels, upper_ref, mine_ref, theirs_ref, before_ref, total_ref, ahead_ref):
-    states = mine_ref.shape[0] - 8
-
-    def joined(left_ref, right_ref, out_ref):
-        both = dot(left_ref[:states], right_ref[:levels])
-        hat, count = settle(both[:levels], left_ref[states:] + right_ref[states:])
-        out_ref[:levels] = hat
-        out_ref[levels:states] = (
-            unscale(both[levels:], right_ref[states : states + 1]) + right_ref[levels:states]
-        )
-        out_ref[states:] = count
-
-    @pl.when(upper_ref[0] == 1)
-    def _():
-        joined(theirs_ref, mine_ref, total_ref)
-        joined(theirs_ref, before_ref, ahead_ref)
-
-    @pl.when(upper_ref[0] == 0)
-    def _():
-        joined(mine_ref, theirs_ref, total_ref)
+def joined(levels, left_ref, right_ref, out_ref):
+    states = right_ref.shape[0] - 16
+    both = dot(left_ref[:states], right_ref[:levels])
+    hat, count = settle(
+        both[:levels], left_ref[states : states + 8] + right_ref[states : states + 8]
+    )
+    out_ref[:levels] = hat
+    out_ref[levels:states] = (
+        unscale(both[levels:], right_ref[states : states + 1]) + right_ref[levels:states]
+    )
+    out_ref[states : states + 8] = count
+    out_ref[states + 8 :] = jnp.zeros_like(count)
+
+
+def merge_kernel(levels, halved, flags_ref, *refs):
+    if halved:
+        mine_ref, here_ref, there_ref, total_ref, theirs_ref, half_ref = refs
+        half = here_ref.shape[0]
+
+        @pl.when(flags_ref[1] == 0)
+        def _():
+            theirs_ref[:half] = here_ref[...]
+            theirs_ref[half:] = there_ref[...]
+
+        @pl.when(flags_ref[1] == 1)
+        def _():
+            theirs_ref[:half] = there_ref[...]
+            theirs_ref[half:] = here_ref[...]
+    else:
+        mine_ref, theirs_ref, total_ref, half_ref = refs
+        half = half_ref.shape[0]
+
+    @pl.when(flags_ref[0] == 1)
+    def _():
+        joined(levels, theirs_ref, mine_ref, total_ref)
+
+    @pl.when(flags_ref[0] == 0)
+    def _():
+        joined(levels, mine_ref, theirs_ref, total_ref)
+
+    @pl.when(flags_ref[1] == 0)
+    def _():
+        half_ref[...] = total_ref[:half]
+
+    @pl.when(flags_ref[1] == 1)
+    def _():
+        half_ref[...] = total_ref[half:]
+
+
+def merge(levels, flags, mine, *arrived):
+    rows = mine.shape[0]
+    spec, shape = whole(mine.shape), jax.ShapeDtypeStruct(mine.shape, F32)
+    half_spec = whole((rows // 2, levels))
+    half_shape = jax.ShapeDtypeStruct((rows // 2, levels), F32)
+    halved = len(arrived) == 2
+    got = call(
+        functools.partial(merge_kernel, levels, halved),
+        (1,),
+        [pl.BlockSpec(memory_space=pltpu.SMEM), spec] + [whole(a.shape) for a in arrived],
+        [spec] * (1 + halved) + [half_spec],
+        [shape] * (1 + halved) + [half_shape],
+        (),
+        12 * rows * levels**2,
+        8 * 2**20,
+    )(flags, mine, *arrived)
+    total, theirs, half = got if halved else (got[0], arrived[0], got[1])
+    return total, theirs, half
+
+
+def extend_kernel(levels, flags_ref, theirs_ref, before_ref, ahead_ref):
+    @pl.when(flags_ref[0] == 1)
+    def _():
+        joined(levels, theirs_ref, before_ref, ahead_ref)
+
+    @pl.when(flags_ref[0] == 0)
+    def _():
         ahead_ref[...] = before_ref[...]
 
 
-def merge(levels, upper, mine, theirs, before):
-    spec = whole(mine.shape)
-    shape = jax.ShapeDtypeStruct(mine.shape, F32)
+def begin_kernel(levels, flags_ref, theirs_ref, ahead_ref):
+    @pl.when(flags_ref[0] == 1)
+    def _():
+        ahead_ref[...] = theirs_ref[...]
+
+    @pl.when(flags_ref[0] == 0)
+    def _():
+        row = lax.broadcasted_iota(jnp.int32, ahead_ref.shape, 0)
+        column = lax.broadcasted_iota(jnp.int32, ahead_ref.shape, 1)
+        ahead_ref[...] = jnp.where(row == column, 1.0, 0.0).astype(F32)
+
+
+def extend(levels, flags, theirs, *before):
+    spec = whole(theirs.shape)
     return call(
-        functools.partial(merge_kernel, levels),
+        functools.partial(extend_kernel if before else begin_kernel, levels),
         (1,),
-        [pl.BlockSpec(memory_space=pltpu.SMEM), spec, spec, spec],
-        [spec, spec],
-        [shape, shape],
+        [pl.BlockSpec(memory_space=pltpu.SMEM), spec] + [spec] * len(before),
+        spec,
+        jax.ShapeDtypeStruct(theirs.shape, F32),
         (),
-        24 * mine.shape[0] * levels**2,
-    )(upper, mine, theirs, before)
+        12 * theirs.shape[0] * levels**2,
+        8 * 2**20,
+    )(flags, theirs, *before)
 
 
 def finish_kernel(
     levels, upper_ref, theirs_ref, before_ref, prefix_ref, trial_ref, solved_ref, incoming
 ):
     cell = pl.program_id(0)
-    states = before_ref.shape[0] - 8
+    states = before_ref.shape[0] - 16
 
     @pl.when(cell == 0)
     def _():
@@ -191,11 +272,12 @@
         jax.ShapeDtypeStruct((lines, cells, levels), F32),
         [pltpu.VMEM((lines, levels), F32)],
         12 * (cells + 1) * lines * levels**2,
+        8 * 2**20,
     )(upper, theirs, before, prefix, trial)
 
 
 def shards(sizes, forcing, blocks, upstream):
-    line_count, span_count = sizes
+    span_count = sizes
     cells, levels, _ = blocks.shape
     share = forcing.shape[0]
     lines = share * span_count
@@ -205,25 +287,30 @@
     prefix = prefix_maps(blocks, upstream)
     trial, total = trial_states(blocks, upstream, local_forcing, prefix)
 
-    rounds = [("span", 1 << b) for b in range(span_count.bit_length() - 1)]
-    rounds += [("line", 1 << b) for b in range(line_count.bit_length() - 1)]
-    before = jnp.concatenate(
-        [jnp.eye(levels, dtype=F32), jnp.zeros((lines + 8, levels), F32)], axis=0
-    )
-
-    def partner(value, axis, bit):
+    def partner(value, axis, mask):
         count = lax.axis_size(axis)
-        return lax.ppermute(value, axis, [(i, i ^ bit) for i in range(count)])
-
-    def is_upper(axis, bit):
-        return jnp.where((lax.axis_index(axis) & bit) != 0, 1, 0).astype(jnp.int32).reshape(1)
-
-    for axis, bit in rounds[:-1]:
-        theirs = partner(total, axis, bit)
-        total, before = merge(levels, is_upper(axis, bit), total, theirs, before)
-    axis, bit = rounds[-1]
-    theirs = partner(total[levels : levels + lines], axis, bit)
-    solved = finish(levels, is_upper(axis, bit), theirs, before, prefix, trial)
+        return lax.ppermute(value, axis, [(i, i ^ mask) for i in range(count)])
+
+    def flags_of(axis, bit):
+        core = lax.axis_index("line") & CORE
+        upper = jnp.where((lax.axis_index(axis) & bit) != 0, 1, 0)
+        return jnp.stack([upper, core]).astype(jnp.int32)
+
+    half, before = None, ()
+    for axis, mask, bit, halved in ROUNDS[:-1]:
+        flags = flags_of(axis, bit)
+        if halved:
+            here = partner(half, axis, mask)
+            arrived = (here, partner(here, "line", CORE))
+        else:
+            arrived = (partner(total, axis, mask),)
+        total, theirs, half = merge(levels, flags, total, *arrived)
+        before = (extend(levels, flags, theirs, *before),)
+    axis, mask, bit, _ = ROUNDS[-1]
+    theirs = partner(total[levels : levels + lines], axis, mask)
+    before = before[0]
+    flags = flags_of(axis, bit)
+    solved = finish(levels, flags, theirs, before, prefix, trial)
     parts = solved.reshape(span_count, share, cells, levels)
     parts = lax.all_to_all(parts, "span", split_axis=0, concat_axis=0, tiled=True)
     return parts.swapaxes(0, 1).reshape(share, span_count * cells, levels)
@@ -231,7 +318,7 @@
 
 def solution(mesh):
     placed = (P("span", "line", None), P(("line", "span"), None, None), P(("line", "span"), None))
-    sizes = (mesh.shape["line"], mesh.shape["span"])
+    sizes = mesh.shape["span"]
     return jax.shard_map(
         functools.partial(shards, sizes),
         mesh=mesh,

time: 123 us -> 109 us (0.89); the launches traced: 121 us -> 109 us
  Pallas kernels: 11.5 us -> 27.3 us
  waiting for transfers between devices: 59.3 us -> 45.2 us
  local copies, waits for them, and re-layouts: 16.3 us -> 4 us
    ppermute x8 -> x11, waiting for transfers between devices: 58.1 us -> 45.2 us  [partner(): return lax.ppermute(value, axis, [(i, i ^ mask) for i in range(count)])]
    unnamed x34 -> x10, local copies, waits for them, and re-layouts: 14.9 us -> 2.55 us
    pallas_call x7 -> x14, Pallas kernels: 4.03 us -> 15.2 us  [the longest x7 10.5 us: merge(): call(functools.partial(merge_kernel, levels, halved), (1,), [pl.BlockSpec...]
    pallas_call x1, Pallas kernels: 3.19 us -> 7.19 us  [prefix_maps(): call(maps_kernel, (cells,), [whole((cells, levels)), block], block, jax.S...]
    ppermute x8 -> x11, starting transfers between devices: 17.5 us -> 16.9 us  [partner(): return lax.ppermute(value, axis, [(i, i ^ mask) for i in range(count)])]
  transfers between devices with their start and end apart: 9 -> 12, of which waited for: 9 -> 11; matrix products, arithmetic and copies ran while one was open for 0% -> 1% of each run, Pallas kernels for 3% -> 11%
where the time goes in v2:
time: 109 us
  waiting for transfers between devices  45.2 us (41%)
  Pallas kernels  27.3 us (25%)
  starting transfers between devices  21.4 us (20%)
  blocking collectives  10.4 us (10%)
  local copies, waits for them, and re-layouts  4 us (4%)
    ppermute x11, waiting for transfers between devices, partner(): return lax.ppermute(value, axis, [(i, i ^ mask) for i in range(count)])  45.2 us
    ppermute x11, starting transfers between devices, partner(): return lax.ppermute(value, axis, [(i, i ^ mask) for i in range(count)])  16.9 us
    pallas_call x7, Pallas kernels, merge(): call(functools.partial(merge_kernel, levels, halved), (1,), [pl.BlockSpec...  10.5 us
    all_to_all x1, blocking collectives, shards(): lax.all_to_all(parts, 'span', split_axis=0, concat_axis=0, tiled=True)  10.4 us
    pallas_call x1, Pallas kernels, prefix_maps(): call(maps_kernel, (cells,), [whole((cells, levels)), block], block, jax.S...  7.19 us
    pallas_call x7, Pallas kernels, extend(): call(functools.partial(extend_kernel if before else begin_kernel, levels)...  4.7 us
    all_to_all x1, starting transfers between devices, shards(): lax.all_to_all(parts, 'span', split_axis=0, concat_axis=0, tiled=True)  4.46 us
    pallas_call x1, Pallas kernels, finish(): call(functools.partial(finish_kernel, levels), (cells,), [pl.BlockSpec(me...  2.81 us
  transfers between devices with their start and end apart: 12, of which 11 were waited for; matrix products, arithmetic and copies ran while one was open for 1% of the time, Pallas kernels for 11%

profile of v2, /device:TPU:6, one launch (start us, length us, event | category | flops | bytes accessed | tf_op | source)
XLA Modules:
  0.0 109.0 jit_solution(4826122364837043872)
XLA Ops:
  1.7 4.5 %all-to-all-start = ((f32[4,8,8,256]{3,2,1,0:T(8,128)}), f32[4,8,8,256]{3,2,1,0:T(8,128)S(1)}, u32[]{:S(2)}, u32[]{:S(2)}) async-start(f32[4,8,8,256]{3,2,1,0:T(8,128)} %copy_bitcast_fusion.1), calls=%async_computation | async-start | bytes 524288 | tf_op jit(solution)/shard_map/all_to_all | solution.py:285
  6.1 7.2 %shard_map.37.product_ref.prefix_ref = f32[8,256,256]{2,1,0:T(8,128)} custom-call(f32[8,256]{1,0:T(8,128)} %upstream_ref.3, f32[8,256,256]{2,1,0:T(8,128)} %block_ref.3), custom_call_target="tpu_custom_call" | custom-call | flops 1610612736 | bytes 2097152 | tf_op jit(solution)/shard_map/pallas_call | solution.py:79
  13.4 1.6 %copy-done.1 = f32[8,256,256]{2,1,0:T(8,128)S(1)} copy-done((f32[8,256,256]{2,1,0:T(8,128)S(1)}, f32[8,256,256]{2,1,0:T(8,128)}, u32[]{:S(2)}) %copy-start.1) | copy-done | bytes 2097176
  14.9 2.1 %shard_map.38 = (f32[8,32,256]{2,1,0:T(8,128)S(1)}, f32[304,256]{1,0:T(8,128)S(1)}) custom-call(f32[8,256]{1,0:T(8,128)S(1)} %copy-done.4, f32[8,256,256]{2,1,0:T(8,128)S(1)} %copy-done.3, f32[32,8,256]{2,1,0:T(8,128)S(1)} %bitcast.21, f32[8,256,256]{2,1,0:T(8,128)S(1)} %copy-done.1), custom_call_target="tpu_custom_call" | custom-call | flops 201326592 | bytes 2097152 | tf_op jit(solution)/shard_map/pallas_call | solution.py:115
  17.1 2.1 %collective-permute-start = (f32[304,256]{1,0:T(8,128)S(1)}, f32[304,256]{1,0:T(8,128)S(1)}, u32[]{:S(2)}, u32[]{:S(2)}) collective-permute-start(f32[304,256]{1,0:T(8,128)S(1)} %get-tuple-element.20.refs_0_), channel_id=1, source_target_pairs={{0,1},{1,0},{2,3},{3,2},{4,5},{5,4},{6,7},{7,6},{8,9},{9,8},{10,11... | collective-permute-start | bytes 933896 | tf_op jit(solution)/shard_map/ppermute | solution.py:292
  19.2 6.7 %collective-permute-done.refs_1_.theirs_ref = f32[304,256]{1,0:T(8,128)S(1)} collective-permute-done((f32[304,256]{1,0:T(8,128)S(1)}, f32[304,256]{1,0:T(8,128)S(1)}, u32[]{:S(2)}, u32[]{:S(2)}) %collective-permute-start) | collective-permute-done | bytes 311328 | tf_op jit(solution)/shard_map/ppermute | solution.py:292
  26.0 1.8 %shard_map.39 = (f32[304,256]{1,0:T(8,128)S(1)}, f32[152,256]{1,0:T(8,128)}) custom-call(s32[2]{0:T(128)S(1)} %pad_add_fusion.7.flags_ref, f32[304,256]{1,0:T(8,128)S(1)} %get-tuple-element.20.refs_0_, f32[304,256]{1,0:T(8,128)S(1)} %collective-permute-done.refs_1_.theirs_ref), custom_call_target="tpu_custom_call" | custom-call | flops 239075328 | bytes 2097152 | tf_op jit(solution)/shard_map/pallas_call | solution.py:190
  27.7 3.0 %collective-permute-start.1 = (f32[304,256]{1,0:T(8,128)S(1)}, f32[304,256]{1,0:T(8,128)S(1)}, u32[]{:S(2)}, u32[]{:S(2)}) collective-permute-start(f32[304,256]{1,0:T(8,128)S(1)} %get-tuple-element.21.refs_0_), channel_id=1, source_target_pairs={{0,3},{1,2},{2,1},{3,0},{4,7},{5,6},{6,5},{7,4},{8,11},{9,10},{10,... | collective-permute-start | bytes 933896 | tf_op jit(solution)/shard_map/ppermute | solution.py:292
  30.8 6.1 %collective-permute-done.1.refs_1_.theirs_ref = f32[304,256]{1,0:T(8,128)S(1)} collective-permute-done((f32[304,256]{1,0:T(8,128)S(1)}, f32[304,256]{1,0:T(8,128)S(1)}, u32[]{:S(2)}, u32[]{:S(2)}) %collective-permute-start.1) | collective-permute-done | bytes 311328 | tf_op jit(solution)/shard_map/ppermute | solution.py:292
  36.9 1.8 %shard_map.40 = (f32[304,256]{1,0:T(8,128)S(1)}, f32[152,256]{1,0:T(8,128)}) custom-call(s32[2]{0:T(128)S(1)} %pad_add_fusion.6.flags_ref, f32[304,256]{1,0:T(8,128)S(1)} %get-tuple-element.21.refs_0_, f32[304,256]{1,0:T(8,128)S(1)} %collective-permute-done.1.refs_1_.theirs_ref), custom_call_target="tpu_custom_call" | custom-call | flops 239075328 | bytes 2097152 | tf_op jit(solution)/shard_map/pallas_call | solution.py:190
  38.7 1.5 %collective-permute-done.2.refs_1_.theirs_ref = f32[304,256]{1,0:T(8,128)S(1)} collective-permute-done((f32[304,256]{1,0:T(8,128)S(1)}, f32[304,256]{1,0:T(8,128)S(1)}, u32[]{:S(2)}, u32[]{:S(2)}) %collective-permute-start.2) | collective-permute-done | bytes 311328 | tf_op jit(solution)/shard_map/ppermute | solution.py:292
  41.4 2.0 %collective-permute-start.3 = (f32[152,256]{1,0:T(8,128)S(1)}, f32[152,256]{1,0:T(8,128)S(1)}, u32[]{:S(2)}, u32[]{:S(2)}) collective-permute-start(f32[152,256]{1,0:T(8,128)S(1)} %get-tuple-element.24), channel_id=1, source_target_pairs={{0,8},{4,12},{8,0},{12,4},{16,24},{20,28},{24,16},{28,20},{32,40},... | collective-permute-start | bytes 466952 | tf_op jit(solution)/shard_map/ppermute | solution.py:292
  43.4 4.3 %collective-permute-done.3.refs_1_ = f32[152,256]{1,0:T(8,128)S(1)} collective-permute-done((f32[152,256]{1,0:T(8,128)S(1)}, f32[152,256]{1,0:T(8,128)S(1)}, u32[]{:S(2)}, u32[]{:S(2)}) %collective-permute-start.3) | collective-permute-done | bytes 155680 | tf_op jit(solution)/shard_map/ppermute | solution.py:292
  47.8 1.3 %collective-permute-done.4.refs_2_ = f32[152,256]{1,0:T(8,128)S(1)} collective-permute-done((f32[152,256]{1,0:T(8,128)S(1)}, f32[152,256]{1,0:T(8,128)S(1)}, u32[]{:S(2)}, u32[]{:S(2)}) %collective-permute-start.4) | collective-permute-done | bytes 155680 | tf_op jit(solution)/shard_map/ppermute | solution.py:292
  50.2 3.4 %collective-permute-start.5 = (f32[152,256]{1,0:T(8,128)S(1)}, f32[152,256]{1,0:T(8,128)S(1)}, u32[]{:S(2)}, u32[]{:S(2)}) collective-permute-start(f32[152,256]{1,0:T(8,128)S(1)} %get-tuple-element.26), channel_id=1, source_target_pairs={{0,16},{4,20},{8,24},{12,28},{16,0},{20,4},{24,8},{28,12},{32,48},... | collective-permute-start | bytes 466952 | tf_op jit(solution)/shard_map/ppermute | solution.py:292
  53.6 7.7 %collective-permute-done.5.refs_1_ = f32[152,256]{1,0:T(8,128)S(1)} collective-permute-done((f32[152,256]{1,0:T(8,128)S(1)}, f32[152,256]{1,0:T(8,128)S(1)}, u32[]{:S(2)}, u32[]{:S(2)}) %collective-permute-start.5) | collective-permute-done | bytes 155680 | tf_op jit(solution)/shard_map/ppermute | solution.py:292
  63.8 5.1 %collective-permute-start.7 = (f32[152,256]{1,0:T(8,128)S(1)}, f32[152,256]{1,0:T(8,128)S(1)}, u32[]{:S(2)}, u32[]{:S(2)}) collective-permute-start(f32[152,256]{1,0:T(8,128)S(1)} %get-tuple-element.28), channel_id=1, source_target_pairs={{0,56},{4,60},{8,48},{12,52},{16,40},{20,44},{24,32},{28,36},{32,2... | collective-permute-start | bytes 466952 | tf_op jit(solution)/shard_map/ppermute | solution.py:292
  68.9 6.6 %collective-permute-done.7.refs_1_ = f32[152,256]{1,0:T(8,128)S(1)} collective-permute-done((f32[152,256]{1,0:T(8,128)S(1)}, f32[152,256]{1,0:T(8,128)S(1)}, u32[]{:S(2)}, u32[]{:S(2)}) %collective-permute-start.7) | collective-permute-done | bytes 155680 | tf_op jit(solution)/shard_map/ppermute | solution.py:292
  76.9 1.8 %shard_map.44 = (f32[304,256]{1,0:T(8,128)S(1)}, f32[304,256]{1,0:T(8,128)S(1)}, f32[152,256]{1,0:T(8,128)}) custom-call(s32[2]{0:T(128)S(1)} %pad_add_fusion.2.flags_ref, f32[304,256]{1,0:T(8,128)S(1)} %get-tuple-element.27.refs_0_, f32[152,256]{1,0:T(8,128)S(1)} %collective-permute-done.7.refs_1_, f32[152,256]{1,0:T(8,128)S(1)} %collective-permute-done.8.refs_2_), custom_call_target="tpu_custom_call" | custom-call | flops 239075328 | bytes 2097152 | tf_op jit(solution)/shard_map/pallas_call | solution.py:190
  82.8 5.4 %collective-permute-done.9.refs_1_.theirs_ref = f32[304,256]{1,0:T(8,128)S(1)} collective-permute-done((f32[304,256]{1,0:T(8,128)S(1)}, f32[304,256]{1,0:T(8,128)S(1)}, u32[]{:S(2)}, u32[]{:S(2)}) %collective-permute-start.9) | collective-permute-done | bytes 311328 | tf_op jit(solution)/shard_map/ppermute | solution.py:292
  88.1 1.8 %shard_map.45 = (f32[304,256]{1,0:T(8,128)S(1)}, f32[152,256]{1,0:T(8,128)}) custom-call(s32[2]{0:T(128)S(1)} %pad_add_fusion.1.flags_ref, f32[304,256]{1,0:T(8,128)S(1)} %get-tuple-element.29.refs_0_, f32[304,256]{1,0:T(8,128)S(1)} %collective-permute-done.9.refs_1_.theirs_ref), custom_call_target="tpu_custom_call" | custom-call | flops 239075328 | bytes 2097152 | tf_op jit(solution)/shard_map/pallas_call | solution.py:190
  92.1 3.0 %collective-permute-done.10.theirs_ref = f32[32,256]{1,0:T(8,128)S(1)} collective-permute-done((f32[32,256]{1,0:T(8,128)S(1)}, f32[32,256]{1,0:T(8,128)S(1)}, u32[]{:S(2)}, u32[]{:S(2)}) %collective-permute-start.10) | collective-permute-done | bytes 32800 | tf_op jit(solution)/shard_map/ppermute | solution.py:292
  95.1 2.8 %shard_map.53 = f32[32,8,256]{2,1,0:T(8,128)S(1)} custom-call(s32[2]{0:T(128)S(1)} %pad_add_fusion.upper_ref, f32[32,256]{1,0:T(8,128)S(1)} %collective-permute-done.10.theirs_ref, f32[304,256]{1,0:T(8,128)S(1)} %shard_map.52.before_ref, f32[8,256,256]{2,1,0:T(8,128)S(1)} %copy-done.2, f32[8,32,256]{2,1,0:T(8,128)S(1)} %get-tuple-element.34.trial_ref), custom_call_target="tpu_custom_call" | custom-call | flops 226492416 | bytes 2097152 | tf_op jit(solution)/shard_map/pallas_call | solution.py:261
  97.9 10.4 %all_to_all.10 = f32[4,8,8,256]{3,2,1,0:T(8,128)S(1)} all-to-all(f32[4,8,8,256]{3,2,1,0:T(8,128)S(1)} %bitcast.22), channel_id=1, replica_groups=mesh['line'=64,'span'=4] {'span'}, dimensions={0} | all-to-all | bytes 524288 | tf_op jit(solution)/shard_map/all_to_all | solution.py:315
  (39 shorter events, 15.0 us)
Async XLA Ops:
  0.0 1.0 copy-start
  1.7 11.7 %all-to-all-start = ((f32[4,8,8,256]{3,2,1,0:T(8,128)}), f32[4,8,8,256]{3,2,1,0:T(8,128)S(1)}, u32[]{:S(2)}, u32[]{:S(2)}) async-start(f32[4,8,8,256]{3,2,1,0:T(8,128)} %copy_bitcast_fusion.1), calls=%async_computation | async-start | bytes 524288 | tf_op jit(solution)/shard_map/all_to_all | solution.py:285
  6.1 7.2 %copy-start.3 = (f32[8,256,256]{2,1,0:T(8,128)S(1)}, f32[8,256,256]{2,1,0:T(8,128)}, u32[]{:S(2)}) copy-start(f32[8,256,256]{2,1,0:T(8,128)} %block_ref.3) | copy-start | bytes 6291460
  6.1 7.2 %copy-start.4 = (f32[8,256]{1,0:T(8,128)S(1)}, f32[8,256]{1,0:T(8,128)}, u32[]{:S(2)}) copy-start(f32[8,256]{1,0:T(8,128)} %upstream_ref.3) | copy-start | bytes 24580
  13.3 1.6 %copy-start.1 = (f32[8,256,256]{2,1,0:T(8,128)S(1)}, f32[8,256,256]{2,1,0:T(8,128)}, u32[]{:S(2)}) copy-start(f32[8,256,256]{2,1,0:T(8,128)} %shard_map.37.product_ref.prefix_ref) | copy-start | bytes 6291460
  17.1 8.9 %collective-permute-start = (f32[304,256]{1,0:T(8,128)S(1)}, f32[304,256]{1,0:T(8,128)S(1)}, u32[]{:S(2)}, u32[]{:S(2)}) collective-permute-start(f32[304,256]{1,0:T(8,128)S(1)} %get-tuple-element.20.refs_0_), channel_id=1, source_target_pairs={{0,1},{1,0},{2,3},{3,2},{4,5},{5,4},{6,7},{7,6},{8,9},{9,8},{10,11... | collective-permute-start | bytes 933896 | tf_op jit(solution)/shard_map/ppermute | solution.py:292
  27.7 9.1 %collective-permute-start.1 = (f32[304,256]{1,0:T(8,128)S(1)}, f32[304,256]{1,0:T(8,128)S(1)}, u32[]{:S(2)}, u32[]{:S(2)}) collective-permute-start(f32[304,256]{1,0:T(8,128)S(1)} %get-tuple-element.21.refs_0_), channel_id=1, source_target_pairs={{0,3},{1,2},{2,1},{3,0},{4,7},{5,6},{6,5},{7,4},{8,11},{9,10},{10,... | collective-permute-start | bytes 933896 | tf_op jit(solution)/shard_map/ppermute | solution.py:292
  38.6 1.6 %collective-permute-start.2 = (f32[304,256]{1,0:T(8,128)S(1)}, f32[304,256]{1,0:T(8,128)S(1)}, u32[]{:S(2)}, u32[]{:S(2)}) collective-permute-start(f32[304,256]{1,0:T(8,128)S(1)} %get-tuple-element.22.refs_0_), channel_id=1, source_target_pairs={{0,4},{4,0},{8,12},{12,8},{16,20},{20,16},{24,28},{28,24},{32,36},... | collective-permute-start | bytes 933896 | tf_op jit(solution)/shard_map/ppermute | solution.py:292
  41.4 6.3 %collective-permute-start.3 = (f32[152,256]{1,0:T(8,128)S(1)}, f32[152,256]{1,0:T(8,128)S(1)}, u32[]{:S(2)}, u32[]{:S(2)}) collective-permute-start(f32[152,256]{1,0:T(8,128)S(1)} %get-tuple-element.24), channel_id=1, source_target_pairs={{0,8},{4,12},{8,0},{12,4},{16,24},{20,28},{24,16},{28,20},{32,40},... | collective-permute-start | bytes 466952 | tf_op jit(solution)/shard_map/ppermute | solution.py:292
  47.7 1.4 %collective-permute-start.4 = (f32[152,256]{1,0:T(8,128)S(1)}, f32[152,256]{1,0:T(8,128)S(1)}, u32[]{:S(2)}, u32[]{:S(2)}) collective-permute-start(f32[152,256]{1,0:T(8,128)S(1)} %collective-permute-done.3.refs_1_), channel_id=1, source_target_pairs={{0,4},{4,0},{8,12},{12,8},{16,20},{20,16},{24,28},{28,24},{32,36},... | collective-permute-start | bytes 466952 | tf_op jit(solution)/shard_map/ppermute | solution.py:292
  50.2 11.0 %collective-permute-start.5 = (f32[152,256]{1,0:T(8,128)S(1)}, f32[152,256]{1,0:T(8,128)S(1)}, u32[]{:S(2)}, u32[]{:S(2)}) collective-permute-start(f32[152,256]{1,0:T(8,128)S(1)} %get-tuple-element.26), channel_id=1, source_target_pairs={{0,16},{4,20},{8,24},{12,28},{16,0},{20,4},{24,8},{28,12},{32,48},... | collective-permute-start | bytes 466952 | tf_op jit(solution)/shard_map/ppermute | solution.py:292
  61.2 1.4 %collective-permute-start.6 = (f32[152,256]{1,0:T(8,128)S(1)}, f32[152,256]{1,0:T(8,128)S(1)}, u32[]{:S(2)}, u32[]{:S(2)}) collective-permute-start(f32[152,256]{1,0:T(8,128)S(1)} %collective-permute-done.5.refs_1_), channel_id=1, source_target_pairs={{0,4},{4,0},{8,12},{12,8},{16,20},{20,16},{24,28},{28,24},{32,36},... | collective-permute-start | bytes 466952 | tf_op jit(solution)/shard_map/ppermute | solution.py:292
  63.8 11.8 %collective-permute-start.7 = (f32[152,256]{1,0:T(8,128)S(1)}, f32[152,256]{1,0:T(8,128)S(1)}, u32[]{:S(2)}, u32[]{:S(2)}) collective-permute-start(f32[152,256]{1,0:T(8,128)S(1)} %get-tuple-element.28), channel_id=1, source_target_pairs={{0,56},{4,60},{8,48},{12,52},{16,40},{20,44},{24,32},{28,36},{32,2... | collective-permute-start | bytes 466952 | tf_op jit(solution)/shard_map/ppermute | solution.py:292
  75.5 1.4 %collective-permute-start.8 = (f32[152,256]{1,0:T(8,128)S(1)}, f32[152,256]{1,0:T(8,128)S(1)}, u32[]{:S(2)}, u32[]{:S(2)}) collective-permute-start(f32[152,256]{1,0:T(8,128)S(1)} %collective-permute-done.7.refs_1_), channel_id=1, source_target_pairs={{0,4},{4,0},{8,12},{12,8},{16,20},{20,16},{24,28},{28,24},{32,36},... | collective-permute-start | bytes 466952 | tf_op jit(solution)/shard_map/ppermute | solution.py:292
  78.7 9.4 %collective-permute-start.9 = (f32[304,256]{1,0:T(8,128)S(1)}, f32[304,256]{1,0:T(8,128)S(1)}, u32[]{:S(2)}, u32[]{:S(2)}) collective-permute-start(f32[304,256]{1,0:T(8,128)S(1)} %get-tuple-element.29.refs_0_), channel_id=1, source_target_pairs={{0,64},{4,68},{8,72},{12,76},{16,80},{20,84},{24,88},{28,92},{32,9... | collective-permute-start | bytes 933896 | tf_op jit(solution)/shard_map/ppermute | solution.py:292
  82.2 12.8 %copy-start.2 = (f32[8,256,256]{2,1,0:T(8,128)S(1)}, f32[8,256,256]{2,1,0:T(8,128)}, u32[]{:S(2)}) copy-start(f32[8,256,256]{2,1,0:T(8,128)} %shard_map.37.product_ref.prefix_ref) | copy-start | bytes 6291460
  89.9 5.1 %collective-permute-start.10 = (f32[32,256]{1,0:T(8,128)S(1)}, f32[32,256]{1,0:T(8,128)S(1)}, u32[]{:S(2)}, u32[]{:S(2)}) collective-permute-start(f32[32,256]{1,0:T(8,128)S(1)} %slice.3), channel_id=1, source_target_pairs={{0,192},{4,196},{8,200},{12,204},{16,208},{20,212},{24,216},{28,22... | collective-permute-start | bytes 98312 | tf_op jit(solution)/shard_map/ppermute | solution.py:292

commit v3 on v0

v3 whole, which is shorter than its diff:
```python
import functools

import jax
import jax.numpy as jnp
from jax import lax
from jax.experimental import pallas as pl
from jax.experimental.pallas import tpu as pltpu
from jax.sharding import PartitionSpec as P

F32 = jnp.float32
BIG = 2.0**40
STEP = 2.0**48
PAD = 16
VMEM = pl.BlockSpec(memory_space=pltpu.VMEM)
HBM = pl.BlockSpec(memory_space=pltpu.HBM)
LARGE = 125 * 2**19
SMEM = pl.BlockSpec(memory_space=pltpu.SMEM)
CORE = 1
ROUNDS = (
    ("span", 1, 1, "apart"),
    ("span", 3, 2, "apart"),
    ("line", 1, 1, "together"),
    ("line", 2, 2, "halves"),
    ("line", 4, 4, "halves"),
    ("line", 14, 8, "halves"),
    ("line", 16, 16, "together"),
    ("line", 48, 32, "states"),
)


def dot(a, b):
    return jnp.dot(a, b, precision=lax.Precision.HIGHEST, preferred_element_type=F32)


def shape(*dims):
    return jax.ShapeDtypeStruct(dims, F32)


def call(kernel, in_specs, out_shape, flops, scratch=(), out_specs=None, vmem=8 * 2**20):
    return pl.pallas_call(
        kernel,
        in_specs=in_specs,
        out_specs=out_specs or jax.tree.map(lambda _: VMEM, out_shape),
        out_shape=out_shape,
        scratch_shapes=list(scratch),
        compiler_params=pltpu.CompilerParams(vmem_limit_bytes=vmem),
        cost_estimate=pl.CostEstimate(flops=flops, bytes_accessed=2**20, transcendentals=0),
    )


def settle(hat, count):
    large = jnp.max(jnp.abs(hat), keepdims=True) > BIG
    return hat * jnp.where(large, 1.0 / STEP, 1.0), count + jnp.where(large, 1.0, 0.0)


def unscale(value, count):
    for done in (0.0, 2.0, 4.0):
        left = count - done
        value = value * jnp.where(left > 1.5, STEP * STEP, jnp.where(left > 0.5, STEP, 1.0))
    return value


def put_map(hat, count, out_ref):
    levels = hat.shape[1]
    hat, count = settle(hat, count)
    out_ref[:levels] = hat
    out_ref[levels : levels + 8] = count
    out_ref[levels + 8 : levels + PAD] = jnp.zeros_like(count)


def join_maps(left_ref, right_ref, out_ref):
    levels = out_ref.shape[1]
    count = left_ref[levels : levels + 8] + right_ref[levels : levels + 8]
    put_map(dot(left_ref[:levels], right_ref[:levels]), count, out_ref)


def move_states(states, map_ref):
    levels = map_ref.shape[1]
    return unscale(dot(states, map_ref[:levels]), map_ref[levels : levels + 1])


def fetch(blocks_ref, held_ref, arrived):
    copies = [
        pltpu.make_async_copy(blocks_ref.at[cell], held_ref.at[cell], arrived.at[cell])
        for cell in range(held_ref.shape[0])
    ]
    for copy in copies:
        copy.start()
    return copies


def maps_kernel(upstream_ref, blocks_ref, prefix_ref, map_ref, held_ref, made_ref, arrived, left):
    cells, levels, _ = held_ref.shape
    copies = fetch(blocks_ref, held_ref, arrived)
    row = lax.broadcasted_iota(jnp.int32, (levels, levels), 0)
    column = lax.broadcasted_iota(jnp.int32, (levels, levels), 1)
    first = jnp.where(row == column, -upstream_ref[0:1, :], 0.0)
    first = jnp.sum(first, axis=1, keepdims=True)
    last = None
    sent = []
    for cell in range(cells):
        copies[cell].wait()
        if cell == 0:
            last = first * held_ref[0]
        else:
            last = dot(last * -upstream_ref[cell : cell + 1, :], held_ref[cell])
        made_ref[cell] = last
        sent.append(pltpu.make_async_copy(made_ref.at[cell], prefix_ref.at[cell], left.at[cell]))
        sent[-1].start()
    put_map(last, jnp.zeros((8, levels), F32), map_ref)
    for copy in sent:
        copy.wait()


def prefix_maps(blocks, upstream):
    cells, levels, _ = blocks.shape
    return call(
        maps_kernel,
        [VMEM, HBM],
        [shape(*blocks.shape), shape(levels + PAD, levels)],
        12 * cells * levels**3,
        [
            pltpu.VMEM(blocks.shape, F32),
            pltpu.VMEM(blocks.shape, F32),
            pltpu.SemaphoreType.DMA((cells,)),
            pltpu.SemaphoreType.DMA((cells,)),
        ],
        [HBM, VMEM],
        LARGE,
    )(upstream, blocks)


def states_kernel(
    upstream_ref, blocks_ref, forcing_ref, trial_ref, states_ref, held_ref, arrived
):
    copies = fetch(blocks_ref, held_ref, arrived)
    state = None
    for cell in range(held_ref.shape[0]):
        forced = forcing_ref[:, cell, :]
        if cell:
            forced = forced - upstream_ref[cell : cell + 1, :] * state
        copies[cell].wait()
        state = dot(forced, held_ref[cell])
        trial_ref[cell] = state
    states_ref[...] = state


def trial_states(blocks, upstream, forcing):
    cells, levels, _ = blocks.shape
    lines = forcing.shape[0]
    return call(
        states_kernel,
        [VMEM, HBM, VMEM],
        [shape(cells, lines, levels), shape(lines, levels)],
        12 * cells * lines * levels**2,
        [pltpu.VMEM(blocks.shape, F32), pltpu.SemaphoreType.DMA((cells,))],
        None,
        LARGE,
    )(upstream, blocks, forcing)


def later(code_ref, then, otherwise):
    upper = lax.rem(code_ref[0], 2)
    pl.when(upper == 1)(then)
    pl.when(upper == 0)(otherwise)


def merge_maps_kernel(code_ref, mine_ref, theirs_ref, total_ref):
    later(
        code_ref,
        lambda: join_maps(theirs_ref, mine_ref, total_ref),
        lambda: join_maps(mine_ref, theirs_ref, total_ref),
    )


def merge_maps(code, mine, theirs):
    levels = mine.shape[1]
    return call(merge_maps_kernel, [SMEM, VMEM, VMEM], shape(*mine.shape), 12 * levels**3)(
        code, mine, theirs
    )


def merge_states_kernel(code_ref, mine_ref, theirs_ref, my_map_ref, their_map_ref, out_ref):
    def then():
        out_ref[...] = move_states(theirs_ref[...], my_map_ref) + mine_ref[...]

    def otherwise():
        out_ref[...] = move_states(mine_ref[...], their_map_ref) + theirs_ref[...]

    later(code_ref, then, otherwise)


def merge_states(code, mine, theirs, my_map, their_map):
    lines, levels = mine.shape
    return call(
        merge_states_kernel, [SMEM] + [VMEM] * 4, shape(lines, levels), 12 * lines * levels**2
    )(code, mine, theirs, my_map, their_map)


def merge_kernel(levels, apart, halves, half, last, code_ref, *refs):
    refs = list(refs)
    mine_map = refs.pop(0)
    start = levels + PAD
    mine_states = refs.pop(0)[...] if apart else mine_map[start:]
    if apart:
        their_map, their_states = refs.pop(0), refs.pop(0)[...]
    elif halves:
        here_ref, there_ref = refs.pop(0), refs.pop(0)
    else:
        theirs = refs.pop(0)
        their_map, their_states = theirs, theirs[start:]
    total_ref = refs.pop(0)
    core = code_ref[0] // 2
    if halves:
        theirs = refs.pop(0)
        rows = here_ref.shape[0]

        @pl.when(core == 0)
        def _():
            theirs[:rows] = here_ref[...]
            theirs[rows:] = there_ref[...]

        @pl.when(core == 1)
        def _():
            theirs[:rows] = there_ref[...]
            theirs[rows:] = here_ref[...]

        their_map, their_states = theirs, theirs[start:]

    def then():
        states = move_states(their_states, mine_map) + mine_states
        if last:
            total_ref[...] = states
        else:
            join_maps(their_map, mine_map, total_ref)
            total_ref[start:] = states

    def otherwise():
        states = move_states(mine_states, their_map) + their_states
        if last:
            total_ref[...] = states
        else:
            join_maps(mine_map, their_map, total_ref)
            total_ref[start:] = states

    later(code_ref, then, otherwise)
    if half:
        half_ref = refs.pop(0)
        rows = half_ref.shape[0]

        @pl.when(core == 0)
        def _():
            half_ref[...] = total_ref[:rows]

        @pl.when(core == 1)
        def _():
            half_ref[...] = total_ref[rows:]


def merge(code, mine, theirs, apart, halves, half, last):
    levels = mine[0].shape[1]
    rows = levels + PAD + (mine[1].shape[0] if apart else mine[0].shape[0] - levels - PAD)
    out = [shape(rows - levels - PAD if last else rows, levels)]
    if halves:
        out.append(shape(rows, levels))
    if half:
        out.append(shape(rows // 2, levels))
    operands = (*mine, *theirs)
    return call(
        functools.partial(merge_kernel, levels, apart, halves, half, last),
        [SMEM] + [VMEM] * len(operands),
        out,
        12 * (rows - levels if last else rows) * levels**2,
    )(code, *operands)


def extend_kernel(first, apart, code_ref, *refs):
    refs = list(refs)
    their_map = refs.pop(0)
    levels = their_map.shape[1]
    start = levels + PAD
    their_states = refs.pop(0)[...] if apart else their_map[start:]
    if first:
        (ahead_ref,) = refs
    else:
        before_ref, ahead_ref = refs

    def then():
        if first:
            ahead_ref[:start] = their_map[:start]
            ahead_ref[start:] = their_states
        else:
            join_maps(their_map, before_ref, ahead_ref)
            ahead_ref[start:] = move_states(their_states, before_ref) + before_ref[start:]

    def otherwise():
        if first:
            row = lax.broadcasted_iota(jnp.int32, ahead_ref.shape, 0)
            column = lax.broadcasted_iota(jnp.int32, ahead_ref.shape, 1)
            ahead_ref[...] = jnp.where(row == column, 1.0, 0.0).astype(F32)
        else:
            ahead_ref[...] = before_ref[...]

    later(code_ref, then, otherwise)


def extend(code, theirs, before):
    levels = theirs[0].shape[1]
    apart = len(theirs) == 2
    rows = levels + PAD + (theirs[1].shape[0] if apart else theirs[0].shape[0] - levels - PAD)
    first = before is None
    operands = theirs if first else (*theirs, before)
    return call(
        functools.partial(extend_kernel, first, apart),
        [SMEM] + [VMEM] * len(operands),
        shape(rows, levels),
        12 * rows * levels**2,
    )(code, *operands)


def finish_kernel(
    code_ref, theirs_ref, before_ref, prefix_ref, trial_ref, solved_ref, held_ref, incoming, arrived
):
    copies = fetch(prefix_ref, held_ref, arrived)
    start = before_ref.shape[1] + PAD

    def then():
        incoming[...] = move_states(theirs_ref[...], before_ref) + before_ref[start:]

    def otherwise():
        incoming[...] = before_ref[start:]

    later(code_ref, then, otherwise)
    for cell, copy in enumerate(copies):
        copy.wait()
        solved_ref[:, cell, :] = trial_ref[cell] + dot(incoming[...], held_ref[cell])


def finish(code, theirs, before, prefix, trial):
    cells, lines, levels = trial.shape
    return call(
        finish_kernel,
        [SMEM, VMEM, VMEM, HBM, VMEM],
        shape(lines, cells, levels),
        12 * (cells + 1) * lines * levels**2,
        [
            pltpu.VMEM(prefix.shape, F32),
            pltpu.VMEM((lines, levels), F32),
            pltpu.SemaphoreType.DMA((cells,)),
        ],
        None,
        LARGE,
    )(code, theirs, before, prefix, trial)


def shards(span_count, forcing, blocks, upstream):
    cells, levels, _ = blocks.shape
    share = forcing.shape[0]
    lines = share * span_count
    parts = forcing.reshape(share, span_count, cells, levels).swapaxes(0, 1)
    parts = lax.all_to_all(parts, "span", split_axis=0, concat_axis=0, tiled=True)
    local_forcing = parts.reshape(lines, cells, levels)
    prefix, maps = prefix_maps(blocks, upstream)
    trial, states = trial_states(blocks, upstream, local_forcing)

    def partner(value, axis, mask):
        count = lax.axis_size(axis)
        return lax.ppermute(value, axis, [(i, i ^ mask) for i in range(count)])

    def code_of(axis, bit):
        upper = jnp.where((lax.axis_index(axis) & bit) != 0, 1, 0)
        core = jnp.where((lax.axis_index("line") & CORE) != 0, 2, 0)
        return (upper + core).astype(jnp.int32).reshape(1)

    total, half, before = None, None, None
    for turn, (axis, mask, bit, how) in enumerate(ROUNDS[:-1]):
        code = code_of(axis, bit)
        after = ROUNDS[turn + 1][3]
        apart, halves = how == "apart", how == "halves"
        if apart:
            theirs = (partner(maps, axis, mask), partner(states, axis, mask))
            mine = (maps, states)
        elif halves:
            here = partner(half, axis, mask)
            theirs = (here, partner(here, "line", CORE))
            mine = (total,)
        else:
            theirs = (partner(total, axis, mask),)
            mine = (total,)
        if before is not None:
            theirs, before = lax.optimization_barrier((theirs, before))
        if apart and after == "apart":
            states = merge_states(code, states, theirs[1], maps, theirs[0])
            maps = merge_maps(code, maps, theirs[0])
        else:
            got = merge(code, mine, theirs, apart, halves, after == "halves", after == "states")
            total = got[0]
            theirs = (got[1],) if halves else theirs
            half = got[-1]
        before = extend(code, theirs, before)
    axis, mask, bit, _ = ROUNDS[-1]
    theirs = partner(total, axis, mask)
    solved = finish(code_of(axis, bit), theirs, before, prefix, trial)
    parts = solved.reshape(span_count, share, cells, levels)
    parts = lax.all_to_all(parts, "span", split_axis=0, concat_axis=0, tiled=True)
    return parts.swapaxes(0, 1).reshape(share, span_count * cells, levels)


def solution(mesh):
    placed = (P("span", "line", None), P(("line", "span"), None, None), P(("line", "span"), None))
    return jax.shard_map(
        functools.partial(shards, mesh.shape["span"]),
        mesh=mesh,
        in_specs=placed,
        out_specs=P("span", "line", None),
        check_vma=False,
    )
```

time: 703 us -> 108 us (0.15)
  matrix products: 319 us -> 0 us
  waiting for transfers between devices: 334 us -> 47.3 us
  Pallas kernels: 0 us -> 23 us
  starting transfers between devices: 4.64 us -> 22.2 us
  between operations: 13.6 us -> 0.18 us
  loops' own time: 10.3 us -> 0 us
    all_gather x2 -> x0, waiting for transfers between devices: 328 us -> none  [carried_in(): pieces = jax.tree.map(lambda part: lax.all_gather(part, axis), value)]
    dot_general x278 -> x0, matrix products: 319 us -> none  [the longest x255 309 us: combine(): jnp.dot(early_state, late_map, precision=lax.Precision.HIGHEST, preferred...]
    ppermute x0 -> x13, waiting for transfers between devices: none -> 47.2 us  [partner(): return lax.ppermute(value, axis, [(i, i ^ mask) for i in range(count)])]
    pallas_call x0 -> x18, Pallas kernels: none -> 23 us  [the longest x1 7.08 us: prefix_maps(): call(maps_kernel, [VMEM, HBM], [shape(*blocks.shape), shape(levels + PAD,...]
    ppermute x0 -> x13, starting transfers between devices: none -> 18 us  [partner(): return lax.ppermute(value, axis, [(i, i ^ mask) for i in range(count)])]
    another operation x1 -> x0, loops' own time: 10.3 us -> none  [carried_in(): return lax.fori_loop(0, count - 1, turn, running)]
  transfers between devices with their start and end apart: 3 -> 14, of which waited for: 3 -> 13; matrix products, arithmetic and copies ran while one was open for 1% -> 1% of each run, Pallas kernels for 0% -> 6%
where the time goes in v3:
time: 108 us; the launch traced here: 107 us
  waiting for transfers between devices  47.3 us (44%)
  Pallas kernels  23 us (21%)
  starting transfers between devices  22.2 us (21%)
  blocking collectives  10.1 us (9%)
  local copies, waits for them, and re-layouts  4.47 us (4%)
    ppermute x13, waiting for transfers between devices, partner(): return lax.ppermute(value, axis, [(i, i ^ mask) for i in range(count)])  47.2 us
    ppermute x13, starting transfers between devices, partner(): return lax.ppermute(value, axis, [(i, i ^ mask) for i in range(count)])  18 us
    all_to_all x1, blocking collectives, shards(): lax.all_to_all(parts, 'span', split_axis=0, concat_axis=0, tiled=True)  10.1 us
    pallas_call x1, Pallas kernels, prefix_maps(): call(maps_kernel, [VMEM, HBM], [shape(*blocks.shape), shape(levels + PAD,...  7.08 us
    pallas_call x1, Pallas kernels, finish(): call(finish_kernel, [SMEM, VMEM, VMEM, HBM, VMEM], shape(lines, cells, le...  5.46 us
    pallas_call x1, Pallas kernels, trial_states(): call(states_kernel, [VMEM, HBM, VMEM], [shape(cells, lines, levels), shap...  5.31 us
    all_to_all x1, starting transfers between devices, shards(): lax.all_to_all(parts, 'span', split_axis=0, concat_axis=0, tiled=True)  4.17 us
    pallas_call x6, Pallas kernels, merge(): call(functools.partial(merge_kernel, levels, apart, halves, half, last),...  3.59 us
  transfers between devices with their start and end apart: 14, of which 13 were waited for; matrix products, arithmetic and copies ran while one was open for 1% of the time, Pallas kernels for 6%

profile of v3, /device:TPU:6, one launch (start us, length us, event | category | flops | bytes accessed | tf_op | source)
XLA Modules:
  0.0 107.2 jit_solution(11184864966401617068)
XLA Ops:
  0.0 7.1 %shard_map.37 = (f32[8,256,256]{2,1,0:T(8,128)}, f32[272,256]{1,0:T(8,128)}) custom-call(f32[8,256]{1,0:T(8,128)} %upstream_ref.3, f32[8,256,256]{2,1,0:T(8,128)} %blocks_ref.3), custom_call_target="tpu_custom_call" | custom-call | flops 1610612736 | bytes 1048576 | tf_op jit(solution)/shard_map/pallas_call | solution.py:117
  7.1 1.7 %collective-permute-start = (f32[272,256]{1,0:T(8,128)}, f32[272,256]{1,0:T(8,128)S(1)}, u32[]{:S(2)}, u32[]{:S(2)}) collective-permute-start(f32[272,256]{1,0:T(8,128)} %get-tuple-element.35.mine_ref.my_map_ref), channel_id=1, source_target_pairs={{0,1},{1,0},{2,3},{3,2},{4,5},{5,4},{6,7},{7,6},{8,9},{9,8},{10,11... | collective-permute-start | bytes 835592 | tf_op jit(solution)/shard_map/ppermute | solution.py:368
  9.5 4.2 %all-to-all-start = ((f32[4,8,8,256]{3,2,1,0:T(8,128)}), f32[4,8,8,256]{3,2,1,0:T(8,128)}, u32[]{:S(2)}, u32[]{:S(2)}) async-start(f32[4,8,8,256]{3,2,1,0:T(8,128)} %copy_bitcast_fusion.1), calls=%async_computation | async-start | bytes 524288 | tf_op jit(solution)/shard_map/all_to_all | solution.py:361
  13.7 2.5 %collective-permute-done.theirs_ref.their_map_ref.refs_0_ = f32[272,256]{1,0:T(8,128)S(1)} collective-permute-done((f32[272,256]{1,0:T(8,128)}, f32[272,256]{1,0:T(8,128)S(1)}, u32[]{:S(2)}, u32[]{:S(2)}) %collective-permute-start) | collective-permute-done | bytes 278560 | tf_op jit(solution)/shard_map/ppermute | solution.py:368
  16.1 1.0 copy-done.2
  17.6 3.6 %collective-permute-start.2 = (f32[272,256]{1,0:T(8,128)S(1)}, f32[272,256]{1,0:T(8,128)S(1)}, u32[]{:S(2)}, u32[]{:S(2)}) collective-permute-start(f32[272,256]{1,0:T(8,128)S(1)} %shard_map.38.refs_0_), channel_id=1, source_target_pairs={{0,3},{1,2},{2,1},{3,0},{4,7},{5,6},{6,5},{7,4},{8,11},{9,10},{10,... | collective-permute-start | bytes 835592 | tf_op jit(solution)/shard_map/ppermute | solution.py:368
  21.3 5.3 %shard_map.39 = (f32[8,32,256]{2,1,0:T(8,128)}, f32[32,256]{1,0:T(8,128)}) custom-call(f32[8,256]{1,0:T(8,128)} %upstream_ref.3, f32[8,256,256]{2,1,0:T(8,128)} %blocks_ref.3, f32[32,8,256]{2,1,0:T(8,128)} %bitcast.10.forcing_ref), custom_call_target="tpu_custom_call" | custom-call | flops 201326592 | bytes 1048576 | tf_op jit(solution)/shard_map/pallas_call | solution.py:151
  26.8 4.0 %collective-permute-done.1.theirs_ref.refs_1_ = f32[32,256]{1,0:T(8,128)S(1)} collective-permute-done((f32[32,256]{1,0:T(8,128)}, f32[32,256]{1,0:T(8,128)S(1)}, u32[]{:S(2)}, u32[]{:S(2)}) %collective-permute-start.1) | collective-permute-done | bytes 32800 | tf_op jit(solution)/shard_map/ppermute | solution.py:368
  32.3 4.7 %collective-permute-done.3.refs_3_.refs_1_ = f32[32,256]{1,0:T(8,128)S(1)} collective-permute-done((f32[32,256]{1,0:T(8,128)S(1)}, f32[32,256]{1,0:T(8,128)S(1)}, u32[]{:S(2)}, u32[]{:S(2)}) %collective-permute-start.3) | collective-permute-done | bytes 32800 | tf_op jit(solution)/shard_map/ppermute | solution.py:368
  37.8 1.5 %collective-permute-done.4.refs_1_.refs_0_ = f32[304,256]{1,0:T(8,128)S(1)} collective-permute-done((f32[304,256]{1,0:T(8,128)S(1)}, f32[304,256]{1,0:T(8,128)S(1)}, u32[]{:S(2)}, u32[]{:S(2)}) %collective-permute-start.4) | collective-permute-done | bytes 311328 | tf_op jit(solution)/shard_map/ppermute | solution.py:368
  40.0 2.0 %collective-permute-start.5 = (f32[152,256]{1,0:T(8,128)S(1)}, f32[152,256]{1,0:T(8,128)S(1)}, u32[]{:S(2)}, u32[]{:S(2)}) collective-permute-start(f32[152,256]{1,0:T(8,128)S(1)} %get-tuple-element.42), channel_id=1, source_target_pairs={{0,8},{4,12},{8,0},{12,4},{16,24},{20,28},{24,16},{28,20},{32,40},... | collective-permute-start | bytes 466952 | tf_op jit(solution)/shard_map/ppermute | solution.py:368
  42.0 4.3 %collective-permute-done.5.refs_1_ = f32[152,256]{1,0:T(8,128)S(1)} collective-permute-done((f32[152,256]{1,0:T(8,128)S(1)}, f32[152,256]{1,0:T(8,128)S(1)}, u32[]{:S(2)}, u32[]{:S(2)}) %collective-permute-start.5) | collective-permute-done | bytes 155680 | tf_op jit(solution)/shard_map/ppermute | solution.py:368
  46.4 1.4 %collective-permute-done.6.refs_2_ = f32[152,256]{1,0:T(8,128)S(1)} collective-permute-done((f32[152,256]{1,0:T(8,128)S(1)}, f32[152,256]{1,0:T(8,128)S(1)}, u32[]{:S(2)}, u32[]{:S(2)}) %collective-permute-start.6) | collective-permute-done | bytes 155680 | tf_op jit(solution)/shard_map/ppermute | solution.py:368
  48.4 3.4 %collective-permute-start.7 = (f32[152,256]{1,0:T(8,128)S(1)}, f32[152,256]{1,0:T(8,128)S(1)}, u32[]{:S(2)}, u32[]{:S(2)}) collective-permute-start(f32[152,256]{1,0:T(8,128)S(1)} %get-tuple-element.47), channel_id=1, source_target_pairs={{0,16},{4,20},{8,24},{12,28},{16,0},{20,4},{24,8},{28,12},{32,48},... | collective-permute-start | bytes 466952 | tf_op jit(solution)/shard_map/ppermute | solution.py:368
  51.8 7.7 %collective-permute-done.7.refs_1_ = f32[152,256]{1,0:T(8,128)S(1)} collective-permute-done((f32[152,256]{1,0:T(8,128)S(1)}, f32[152,256]{1,0:T(8,128)S(1)}, u32[]{:S(2)}, u32[]{:S(2)}) %collective-permute-start.7) | collective-permute-done | bytes 155680 | tf_op jit(solution)/shard_map/ppermute | solution.py:368
  59.5 1.4 %collective-permute-done.8.refs_2_ = f32[152,256]{1,0:T(8,128)S(1)} collective-permute-done((f32[152,256]{1,0:T(8,128)S(1)}, f32[152,256]{1,0:T(8,128)S(1)}, u32[]{:S(2)}, u32[]{:S(2)}) %collective-permute-start.8) | collective-permute-done | bytes 155680 | tf_op jit(solution)/shard_map/ppermute | solution.py:368
  61.5 5.1 %collective-permute-start.9 = (f32[152,256]{1,0:T(8,128)S(1)}, f32[152,256]{1,0:T(8,128)S(1)}, u32[]{:S(2)}, u32[]{:S(2)}) collective-permute-start(f32[152,256]{1,0:T(8,128)S(1)} %get-tuple-element.53), channel_id=1, source_target_pairs={{0,56},{4,60},{8,48},{12,52},{16,40},{20,44},{24,32},{28,36},{32,2... | collective-permute-start | bytes 466952 | tf_op jit(solution)/shard_map/ppermute | solution.py:368
  66.7 6.6 %collective-permute-done.9.refs_1_ = f32[152,256]{1,0:T(8,128)S(1)} collective-permute-done((f32[152,256]{1,0:T(8,128)S(1)}, f32[152,256]{1,0:T(8,128)S(1)}, u32[]{:S(2)}, u32[]{:S(2)}) %collective-permute-start.9) | collective-permute-done | bytes 155680 | tf_op jit(solution)/shard_map/ppermute | solution.py:368
  73.4 1.3 %collective-permute-done.10.refs_2_ = f32[152,256]{1,0:T(8,128)S(1)} collective-permute-done((f32[152,256]{1,0:T(8,128)S(1)}, f32[152,256]{1,0:T(8,128)S(1)}, u32[]{:S(2)}, u32[]{:S(2)}) %collective-permute-start.10) | collective-permute-done | bytes 155680 | tf_op jit(solution)/shard_map/ppermute | solution.py:368
  75.4 0.9 collective-permute-start.11
  76.3 8.5 %collective-permute-done.11.refs_1_.refs_0_ = f32[304,256]{1,0:T(8,128)S(1)} collective-permute-done((f32[304,256]{1,0:T(8,128)S(1)}, f32[304,256]{1,0:T(8,128)S(1)}, u32[]{:S(2)}, u32[]{:S(2)}) %collective-permute-start.11) | collective-permute-done | bytes 311328 | tf_op jit(solution)/shard_map/ppermute | solution.py:368
  87.0 3.3 %collective-permute-done.12.theirs_ref = f32[32,256]{1,0:T(8,128)S(1)} collective-permute-done((f32[32,256]{1,0:T(8,128)S(1)}, f32[32,256]{1,0:T(8,128)S(1)}, u32[]{:S(2)}, u32[]{:S(2)}) %collective-permute-start.12) | collective-permute-done | bytes 32800 | tf_op jit(solution)/shard_map/ppermute | solution.py:368
  90.9 5.5 %shard_map.54 = f32[32,8,256]{2,1,0:T(8,128)} custom-call(s32[1]{0:T(128)} %bitcast.code_ref, f32[32,256]{1,0:T(8,128)} %copy-done.5, f32[304,256]{1,0:T(8,128)} %copy-done.1, f32[8,256,256]{2,1,0:T(8,128)} %get-tuple-element.63.prefix_ref, f32[8,32,256]{2,1,0:T(8,128)} %get-tuple-element.64.trial_ref), custom_call_target="tpu_custom_call" | custom-call | flops 226492416 | bytes 1048576 | tf_op jit(solution)/shard_map/pallas_call | solution.py:341
  96.4 10.1 %all_to_all.10 = f32[4,8,8,256]{3,2,1,0:T(8,128)S(1)} all-to-all(f32[4,8,8,256]{3,2,1,0:T(8,128)} %bitcast.20), channel_id=1, replica_groups=mesh['line'=64,'span'=4] {'span'}, dimensions={0} | all-to-all | bytes 524288 | tf_op jit(solution)/shard_map/all_to_all | solution.py:405
  (37 shorter events, 10.1 us)
Async XLA Ops:
  0.0 8.8 %copy-start = (f32[8,32,256]{2,1,0:T(8,128)S(1)}, f32[8,32,256]{2,1,0:T(8,128)}, u32[]{:S(2)}) copy-start(f32[8,32,256]{2,1,0:T(8,128)} %param.3) | copy-start | bytes 786436
  7.1 23.7 %copy-start.3 = (f32[272,256]{1,0:T(8,128)S(1)}, f32[272,256]{1,0:T(8,128)}, u32[]{:S(2)}) copy-start(f32[272,256]{1,0:T(8,128)} %get-tuple-element.35.mine_ref.my_map_ref) | copy-start | bytes 835588
  7.1 9.0 %collective-permute-start = (f32[272,256]{1,0:T(8,128)}, f32[272,256]{1,0:T(8,128)S(1)}, u32[]{:S(2)}, u32[]{:S(2)}) collective-permute-start(f32[272,256]{1,0:T(8,128)} %get-tuple-element.35.mine_ref.my_map_ref), channel_id=1, source_target_pairs={{0,1},{1,0},{2,3},{3,2},{4,5},{5,4},{6,7},{7,6},{8,9},{9,8},{10,11... | collective-permute-start | bytes 835592 | tf_op jit(solution)/shard_map/ppermute | solution.py:368
  9.5 11.8 %all-to-all-start = ((f32[4,8,8,256]{3,2,1,0:T(8,128)}), f32[4,8,8,256]{3,2,1,0:T(8,128)}, u32[]{:S(2)}, u32[]{:S(2)}) async-start(f32[4,8,8,256]{3,2,1,0:T(8,128)} %copy_bitcast_fusion.1), calls=%async_computation | async-start | bytes 524288 | tf_op jit(solution)/shard_map/all_to_all | solution.py:361
  16.1 1.0 copy-start.2
  17.6 19.4 %collective-permute-start.2 = (f32[272,256]{1,0:T(8,128)S(1)}, f32[272,256]{1,0:T(8,128)S(1)}, u32[]{:S(2)}, u32[]{:S(2)}) collective-permute-start(f32[272,256]{1,0:T(8,128)S(1)} %shard_map.38.refs_0_), channel_id=1, source_target_pairs={{0,3},{1,2},{2,1},{3,0},{4,7},{5,6},{6,5},{7,4},{8,11},{9,10},{10,... | collective-permute-start | bytes 835592 | tf_op jit(solution)/shard_map/ppermute | solution.py:368
  26.6 4.2 %collective-permute-start.1 = (f32[32,256]{1,0:T(8,128)}, f32[32,256]{1,0:T(8,128)S(1)}, u32[]{:S(2)}, u32[]{:S(2)}) collective-permute-start(f32[32,256]{1,0:T(8,128)} %get-tuple-element.36.mine_ref), channel_id=1, source_target_pairs={{0,1},{1,0},{2,3},{3,2},{4,5},{5,4},{6,7},{7,6},{8,9},{9,8},{10,11... | collective-permute-start | bytes 98312 | tf_op jit(solution)/shard_map/ppermute | solution.py:368
  30.8 0.8 copy-start.4
  31.8 5.2 %collective-permute-start.3 = (f32[32,256]{1,0:T(8,128)S(1)}, f32[32,256]{1,0:T(8,128)S(1)}, u32[]{:S(2)}, u32[]{:S(2)}) collective-permute-start(f32[32,256]{1,0:T(8,128)S(1)} %shard_map.40.refs_1_), channel_id=1, source_target_pairs={{0,3},{1,2},{2,1},{3,0},{4,7},{5,6},{6,5},{7,4},{8,11},{9,10},{10,... | collective-permute-start | bytes 98312 | tf_op jit(solution)/shard_map/ppermute | solution.py:368
  37.7 1.7 %collective-permute-start.4 = (f32[304,256]{1,0:T(8,128)S(1)}, f32[304,256]{1,0:T(8,128)S(1)}, u32[]{:S(2)}, u32[]{:S(2)}) collective-permute-start(f32[304,256]{1,0:T(8,128)S(1)} %shard_map.42.refs_0_), channel_id=1, source_target_pairs={{0,4},{4,0},{8,12},{12,8},{16,20},{20,16},{24,28},{28,24},{32,36},... | collective-permute-start | bytes 933896 | tf_op jit(solution)/shard_map/ppermute | solution.py:368
  40.0 6.3 %collective-permute-start.5 = (f32[152,256]{1,0:T(8,128)S(1)}, f32[152,256]{1,0:T(8,128)S(1)}, u32[]{:S(2)}, u32[]{:S(2)}) collective-permute-start(f32[152,256]{1,0:T(8,128)S(1)} %get-tuple-element.42), channel_id=1, source_target_pairs={{0,8},{4,12},{8,0},{12,4},{16,24},{20,28},{24,16},{28,20},{32,40},... | collective-permute-start | bytes 466952 | tf_op jit(solution)/shard_map/ppermute | solution.py:368
  46.4 1.4 %collective-permute-start.6 = (f32[152,256]{1,0:T(8,128)S(1)}, f32[152,256]{1,0:T(8,128)S(1)}, u32[]{:S(2)}, u32[]{:S(2)}) collective-permute-start(f32[152,256]{1,0:T(8,128)S(1)} %collective-permute-done.5.refs_1_), channel_id=1, source_target_pairs={{0,4},{4,0},{8,12},{12,8},{16,20},{20,16},{24,28},{28,24},{32,36},... | collective-permute-start | bytes 466952 | tf_op jit(solution)/shard_map/ppermute | solution.py:368
  48.4 11.0 %collective-permute-start.7 = (f32[152,256]{1,0:T(8,128)S(1)}, f32[152,256]{1,0:T(8,128)S(1)}, u32[]{:S(2)}, u32[]{:S(2)}) collective-permute-start(f32[152,256]{1,0:T(8,128)S(1)} %get-tuple-element.47), channel_id=1, source_target_pairs={{0,16},{4,20},{8,24},{12,28},{16,0},{20,4},{24,8},{28,12},{32,48},... | collective-permute-start | bytes 466952 | tf_op jit(solution)/shard_map/ppermute | solution.py:368
  59.5 1.4 %collective-permute-start.8 = (f32[152,256]{1,0:T(8,128)S(1)}, f32[152,256]{1,0:T(8,128)S(1)}, u32[]{:S(2)}, u32[]{:S(2)}) collective-permute-start(f32[152,256]{1,0:T(8,128)S(1)} %collective-permute-done.7.refs_1_), channel_id=1, source_target_pairs={{0,4},{4,0},{8,12},{12,8},{16,20},{20,16},{24,28},{28,24},{32,36},... | collective-permute-start | bytes 466952 | tf_op jit(solution)/shard_map/ppermute | solution.py:368
  61.5 11.8 %collective-permute-start.9 = (f32[152,256]{1,0:T(8,128)S(1)}, f32[152,256]{1,0:T(8,128)S(1)}, u32[]{:S(2)}, u32[]{:S(2)}) collective-permute-start(f32[152,256]{1,0:T(8,128)S(1)} %get-tuple-element.53), channel_id=1, source_target_pairs={{0,56},{4,60},{8,48},{12,52},{16,40},{20,44},{24,32},{28,36},{32,2... | collective-permute-start | bytes 466952 | tf_op jit(solution)/shard_map/ppermute | solution.py:368
  73.3 1.4 %collective-permute-start.10 = (f32[152,256]{1,0:T(8,128)S(1)}, f32[152,256]{1,0:T(8,128)S(1)}, u32[]{:S(2)}, u32[]{:S(2)}) collective-permute-start(f32[152,256]{1,0:T(8,128)S(1)} %collective-permute-done.9.refs_1_), channel_id=1, source_target_pairs={{0,4},{4,0},{8,12},{12,8},{16,20},{20,16},{24,28},{28,24},{32,36},... | collective-permute-start | bytes 466952 | tf_op jit(solution)/shard_map/ppermute | solution.py:368
  75.4 9.5 %collective-permute-start.11 = (f32[304,256]{1,0:T(8,128)S(1)}, f32[304,256]{1,0:T(8,128)S(1)}, u32[]{:S(2)}, u32[]{:S(2)}) collective-permute-start(f32[304,256]{1,0:T(8,128)S(1)} %get-tuple-element.58.refs_0_), channel_id=1, source_target_pairs={{0,64},{4,68},{8,72},{12,76},{16,80},{20,84},{24,88},{28,92},{32,9... | collective-permute-start | bytes 933896 | tf_op jit(solution)/shard_map/ppermute | solution.py:368
  85.1 5.2 %collective-permute-start.12 = (f32[32,256]{1,0:T(8,128)S(1)}, f32[32,256]{1,0:T(8,128)S(1)}, u32[]{:S(2)}, u32[]{:S(2)}) collective-permute-start(f32[32,256]{1,0:T(8,128)S(1)} %shard_map.52), channel_id=1, source_target_pairs={{0,192},{4,196},{8,200},{12,204},{16,208},{20,212},{24,216},{28,22... | collective-permute-start | bytes 98312 | tf_op jit(solution)/shard_map/ppermute | solution.py:368
  86.3 0.7 copy-start.1
  90.3 0.6 copy-start.5

commit v4 on v3

--- a/solution.py
+++ b/solution.py
@@ -13,7 +13,9 @@
 PAD = 16
 VMEM = pl.BlockSpec(memory_space=pltpu.VMEM)
 HBM = pl.BlockSpec(memory_space=pltpu.HBM)
-LARGE = 125 * 2**19
+STATES_VMEM = 8 * 2**20
+FINISH_VMEM = 52 * 2**20
+LARGE = 52 * 2**20
 SMEM = pl.BlockSpec(memory_space=pltpu.SMEM)
 CORE = 1
 ROUNDS = (
@@ -79,37 +81,39 @@
     return unscale(dot(states, map_ref[:levels]), map_ref[levels : levels + 1])
 
 
+def block_copy(blocks_ref, held_ref, arrived, cell):
+    return pltpu.make_async_copy(blocks_ref.at[cell], held_ref.at[cell], arrived.at[cell])
+
+
 def fetch(blocks_ref, held_ref, arrived):
-    copies = [
-        pltpu.make_async_copy(blocks_ref.at[cell], held_ref.at[cell], arrived.at[cell])
-        for cell in range(held_ref.shape[0])
-    ]
-    for copy in copies:
-        copy.start()
-    return copies
-
-
-def maps_kernel(upstream_ref, blocks_ref, prefix_ref, map_ref, held_ref, made_ref, arrived, left):
+    @pl.loop(0, held_ref.shape[0])
+    def _(cell):
+        block_copy(blocks_ref, held_ref, arrived, cell).start()
+
+
+def maps_kernel(
+    upstream_ref, blocks_ref, prefix_ref, map_ref, held_ref, made_ref, last_ref, arrived, left
+):
     cells, levels, _ = held_ref.shape
-    copies = fetch(blocks_ref, held_ref, arrived)
+    fetch(blocks_ref, held_ref, arrived)
     row = lax.broadcasted_iota(jnp.int32, (levels, levels), 0)
     column = lax.broadcasted_iota(jnp.int32, (levels, levels), 1)
-    first = jnp.where(row == column, -upstream_ref[0:1, :], 0.0)
-    first = jnp.sum(first, axis=1, keepdims=True)
-    last = None
-    sent = []
-    for cell in range(cells):
-        copies[cell].wait()
-        if cell == 0:
-            last = first * held_ref[0]
-        else:
-            last = dot(last * -upstream_ref[cell : cell + 1, :], held_ref[cell])
-        made_ref[cell] = last
-        sent.append(pltpu.make_async_copy(made_ref.at[cell], prefix_ref.at[cell], left.at[cell]))
-        sent[-1].start()
-    put_map(last, jnp.zeros((8, levels), F32), map_ref)
-    for copy in sent:
-        copy.wait()
+    last_ref[...] = jnp.where(row == column, 1.0, 0.0).astype(F32)
+
+    @pl.loop(0, cells)
+    def _(cell):
+        scaled = last_ref[...] * -upstream_ref[pl.ds(cell, 1), :]
+        block_copy(blocks_ref, held_ref, arrived, cell).wait()
+        product = dot(scaled, held_ref[cell])
+        last_ref[...] = product
+        made_ref[cell] = product
+        block_copy(made_ref, prefix_ref, left, cell).start()
+
+    put_map(last_ref[...], jnp.zeros((8, levels), F32), map_ref)
+
+    @pl.loop(0, cells)
+    def _(cell):
+        block_copy(made_ref, prefix_ref, left, cell).wait()
 
 
 def prefix_maps(blocks, upstream):
@@ -122,6 +126,7 @@
         [
             pltpu.VMEM(blocks.shape, F32),
             pltpu.VMEM(blocks.shape, F32),
+            pltpu.VMEM((levels, levels), F32),
             pltpu.SemaphoreType.DMA((cells,)),
             pltpu.SemaphoreType.DMA((cells,)),
         ],
@@ -133,16 +138,16 @@
 def states_kernel(
     upstream_ref, blocks_ref, forcing_ref, trial_ref, states_ref, held_ref, arrived
 ):
-    copies = fetch(blocks_ref, held_ref, arrived)
-    state = None
-    for cell in range(held_ref.shape[0]):
-        forced = forcing_ref[:, cell, :]
-        if cell:
-            forced = forced - upstream_ref[cell : cell + 1, :] * state
-        copies[cell].wait()
+    fetch(blocks_ref, held_ref, arrived)
+    states_ref[...] = jnp.zeros_like(states_ref)
+
+    @pl.loop(0, held_ref.shape[0])
+    def _(cell):
+        forced = forcing_ref[:, cell, :] - upstream_ref[pl.ds(cell, 1), :] * states_ref[...]
+        block_copy(blocks_ref, held_ref, arrived, cell).wait()
         state = dot(forced, held_ref[cell])
+        states_ref[...] = state
         trial_ref[cell] = state
-    states_ref[...] = state
 
 
 def trial_states(blocks, upstream, forcing):
@@ -155,7 +160,7 @@
         12 * cells * lines * levels**2,
         [pltpu.VMEM(blocks.shape, F32), pltpu.SemaphoreType.DMA((cells,))],
         None,
-        LARGE,
+        STATES_VMEM,
     )(upstream, blocks, forcing)
 
 
@@ -321,7 +326,7 @@
 def finish_kernel(
     code_ref, theirs_ref, before_ref, prefix_ref, trial_ref, solved_ref, held_ref, incoming, arrived
 ):
-    copies = fetch(prefix_ref, held_ref, arrived)
+    fetch(prefix_ref, held_ref, arrived)
     start = before_ref.shape[1] + PAD
 
     def then():
@@ -331,8 +336,10 @@
         incoming[...] = before_ref[start:]
 
     later(code_ref, then, otherwise)
-    for cell, copy in enumerate(copies):
-        copy.wait()
+
+    @pl.loop(0, held_ref.shape[0])
+    def _(cell):
+        block_copy(prefix_ref, held_ref, arrived, cell).wait()
         solved_ref[:, cell, :] = trial_ref[cell] + dot(incoming[...], held_ref[cell])
 
 
@@ -349,7 +356,7 @@
             pltpu.SemaphoreType.DMA((cells,)),
         ],
         None,
-        LARGE,
+        FINISH_VMEM,
     )(code, theirs, before, prefix, trial)
 
 

time: 108 us -> 99.3 us (0.919)
  Pallas kernels: 23 us -> 16.6 us
  local copies, waits for them, and re-layouts: 4.47 us -> 2.21 us
  waiting for transfers between devices: 47.3 us -> 48.6 us
    pallas_call x1, Pallas kernels: 5.46 us -> 2.91 us  [finish(): call(finish_kernel, [SMEM, VMEM, VMEM, HBM, VMEM], shape(lines, cells, le...]
    unnamed x12, local copies, waits for them, and re-layouts: 3.03 us -> 0.76 us
    pallas_call x1, Pallas kernels: 5.31 us -> 3.22 us  [trial_states(): call(states_kernel, [VMEM, HBM, VMEM], [shape(cells, lines, levels), shap...]
    pallas_call x1, Pallas kernels: 7.08 us -> 5.15 us  [prefix_maps(): call(maps_kernel, [VMEM, HBM], [shape(*blocks.shape), shape(levels + PAD,...]
    all_to_all x1, waiting for transfers between devices: 0.07 us -> 1.54 us  [shards(): lax.all_to_all(parts, 'span', split_axis=0, concat_axis=0, tiled=True)]
  transfers between devices with their start and end apart: 14 -> 14, of which waited for: 13 -> 13; matrix products, arithmetic and copies ran while one was open for 1% -> 1% of each run, Pallas kernels for 6% -> 5%
where the time goes in v4:
time: 99.3 us; the launch traced here: 99.1 us
  waiting for transfers between devices  48.6 us (49%)
  starting transfers between devices  22.5 us (23%)
  Pallas kernels  16.6 us (17%)
  blocking collectives  9.07 us (9%)
  local copies, waits for them, and re-layouts  2.21 us (2%)
    ppermute x13, waiting for transfers between devices, partner(): return lax.ppermute(value, axis, [(i, i ^ mask) for i in range(count)])  47 us
    ppermute x13, starting transfers between devices, partner(): return lax.ppermute(value, axis, [(i, i ^ mask) for i in range(count)])  18.3 us
    all_to_all x1, blocking collectives, shards(): lax.all_to_all(parts, 'span', split_axis=0, concat_axis=0, tiled=True)  9.07 us
    pallas_call x1, Pallas kernels, prefix_maps(): call(maps_kernel, [VMEM, HBM], [shape(*blocks.shape), shape(levels + PAD,...  5.15 us
    all_to_all x1, starting transfers between devices, shards(): lax.all_to_all(parts, 'span', split_axis=0, concat_axis=0, tiled=True)  4.17 us
    pallas_call x6, Pallas kernels, merge(): call(functools.partial(merge_kernel, levels, apart, halves, half, last),...  3.77 us
    pallas_call x1, Pallas kernels, trial_states(): call(states_kernel, [VMEM, HBM, VMEM], [shape(cells, lines, levels), shap...  3.22 us
    pallas_call x1, Pallas kernels, finish(): call(finish_kernel, [SMEM, VMEM, VMEM, HBM, VMEM], shape(lines, cells, le...  2.91 us
  transfers between devices with their start and end apart: 14, of which 13 were waited for; matrix products, arithmetic and copies ran while one was open for 1% of the time, Pallas kernels for 5%

profile of v4, /device:TPU:6, one launch (start us, length us, event | category | flops | bytes accessed | tf_op | source)
XLA Modules:
  0.0 99.1 jit_solution(6658724350778481029)
XLA Ops:
  0.7 5.1 %shard_map.37 = (f32[8,256,256]{2,1,0:T(8,128)}, f32[272,256]{1,0:T(8,128)S(1)}) custom-call(f32[8,256]{1,0:T(8,128)S(1)} %copy-done.4, f32[8,256,256]{2,1,0:T(8,128)} %blocks_ref.3), custom_call_target="tpu_custom_call" | custom-call | flops 1610612736 | bytes 1048576 | tf_op jit(solution)/shard_map/pallas_call | solution.py:121
  5.9 1.7 %collective-permute-start = (f32[272,256]{1,0:T(8,128)S(1)}, f32[272,256]{1,0:T(8,128)S(1)}, u32[]{:S(2)}, u32[]{:S(2)}) collective-permute-start(f32[272,256]{1,0:T(8,128)S(1)} %get-tuple-element.35.mine_ref.my_map_ref), channel_id=1, source_target_pairs={{0,1},{1,0},{2,3},{3,2},{4,5},{5,4},{6,7},{7,6},{8,9},{9,8},{10,11... | collective-permute-start | bytes 835592 | tf_op jit(solution)/shard_map/ppermute | solution.py:375
  8.3 4.2 %all-to-all-start = ((f32[4,8,8,256]{3,2,1,0:T(8,128)}), f32[4,8,8,256]{3,2,1,0:T(8,128)}, u32[]{:S(2)}, u32[]{:S(2)}) async-start(f32[4,8,8,256]{3,2,1,0:T(8,128)} %copy_bitcast_fusion.1), calls=%async_computation | async-start | bytes 524288 | tf_op jit(solution)/shard_map/all_to_all | solution.py:368
  12.5 2.0 %collective-permute-done.theirs_ref.their_map_ref.refs_0_ = f32[272,256]{1,0:T(8,128)S(1)} collective-permute-done((f32[272,256]{1,0:T(8,128)S(1)}, f32[272,256]{1,0:T(8,128)S(1)}, u32[]{:S(2)}, u32[]{:S(2)}) %collective-permute-start) | collective-permute-done | bytes 278560 | tf_op jit(solution)/shard_map/ppermute | solution.py:375
  14.9 3.7 %collective-permute-start.2 = (f32[272,256]{1,0:T(8,128)S(1)}, f32[272,256]{1,0:T(8,128)S(1)}, u32[]{:S(2)}, u32[]{:S(2)}) collective-permute-start(f32[272,256]{1,0:T(8,128)S(1)} %shard_map.38.refs_0_), channel_id=1, source_target_pairs={{0,3},{1,2},{2,1},{3,0},{4,7},{5,6},{6,5},{7,4},{8,11},{9,10},{10,... | collective-permute-start | bytes 835592 | tf_op jit(solution)/shard_map/ppermute | solution.py:375
  18.6 1.5 %all-to-all-done = f32[4,8,8,256]{3,2,1,0:T(8,128)} async-done(((f32[4,8,8,256]{3,2,1,0:T(8,128)}), f32[4,8,8,256]{3,2,1,0:T(8,128)}, u32[]{:S(2)}, u32[]{:S(2)}) %all-to-all-start) | async-done | bytes 262176 | tf_op jit(solution)/shard_map/all_to_all | solution.py:368
  20.2 3.2 %shard_map.39 = (f32[8,32,256]{2,1,0:T(8,128)S(1)}, f32[32,256]{1,0:T(8,128)S(1)}) custom-call(f32[8,256]{1,0:T(8,128)S(1)} %copy-done.5, f32[8,256,256]{2,1,0:T(8,128)S(1)} %copy-done.1, f32[32,8,256]{2,1,0:T(8,128)} %bitcast.10.forcing_ref), custom_call_target="tpu_custom_call" | custom-call | flops 201326592 | bytes 1048576 | tf_op jit(solution)/shard_map/pallas_call | solution.py:156
  23.9 3.5 %collective-permute-done.1.theirs_ref.refs_1_ = f32[32,256]{1,0:T(8,128)S(1)} collective-permute-done((f32[32,256]{1,0:T(8,128)S(1)}, f32[32,256]{1,0:T(8,128)S(1)}, u32[]{:S(2)}, u32[]{:S(2)}) %collective-permute-start.1) | collective-permute-done | bytes 32800 | tf_op jit(solution)/shard_map/ppermute | solution.py:375
  28.0 4.8 %collective-permute-done.3.refs_3_.refs_1_ = f32[32,256]{1,0:T(8,128)S(1)} collective-permute-done((f32[32,256]{1,0:T(8,128)S(1)}, f32[32,256]{1,0:T(8,128)S(1)}, u32[]{:S(2)}, u32[]{:S(2)}) %collective-permute-start.3) | collective-permute-done | bytes 32800 | tf_op jit(solution)/shard_map/ppermute | solution.py:375
  33.7 1.5 %collective-permute-done.4.refs_1_.refs_0_ = f32[304,256]{1,0:T(8,128)S(1)} collective-permute-done((f32[304,256]{1,0:T(8,128)S(1)}, f32[304,256]{1,0:T(8,128)S(1)}, u32[]{:S(2)}, u32[]{:S(2)}) %collective-permute-start.4) | collective-permute-done | bytes 311328 | tf_op jit(solution)/shard_map/ppermute | solution.py:375
  35.9 2.0 %collective-permute-start.5 = (f32[152,256]{1,0:T(8,128)S(1)}, f32[152,256]{1,0:T(8,128)S(1)}, u32[]{:S(2)}, u32[]{:S(2)}) collective-permute-start(f32[152,256]{1,0:T(8,128)S(1)} %get-tuple-element.42), channel_id=1, source_target_pairs={{0,8},{4,12},{8,0},{12,4},{16,24},{20,28},{24,16},{28,20},{32,40},... | collective-permute-start | bytes 466952 | tf_op jit(solution)/shard_map/ppermute | solution.py:375
  37.9 4.3 %collective-permute-done.5.refs_1_ = f32[152,256]{1,0:T(8,128)S(1)} collective-permute-done((f32[152,256]{1,0:T(8,128)S(1)}, f32[152,256]{1,0:T(8,128)S(1)}, u32[]{:S(2)}, u32[]{:S(2)}) %collective-permute-start.5) | collective-permute-done | bytes 155680 | tf_op jit(solution)/shard_map/ppermute | solution.py:375
  42.2 1.4 %collective-permute-done.6.refs_2_ = f32[152,256]{1,0:T(8,128)S(1)} collective-permute-done((f32[152,256]{1,0:T(8,128)S(1)}, f32[152,256]{1,0:T(8,128)S(1)}, u32[]{:S(2)}, u32[]{:S(2)}) %collective-permute-start.6) | collective-permute-done | bytes 155680 | tf_op jit(solution)/shard_map/ppermute | solution.py:375
  44.3 3.4 %collective-permute-start.7 = (f32[152,256]{1,0:T(8,128)S(1)}, f32[152,256]{1,0:T(8,128)S(1)}, u32[]{:S(2)}, u32[]{:S(2)}) collective-permute-start(f32[152,256]{1,0:T(8,128)S(1)} %get-tuple-element.47), channel_id=1, source_target_pairs={{0,16},{4,20},{8,24},{12,28},{16,0},{20,4},{24,8},{28,12},{32,48},... | collective-permute-start | bytes 466952 | tf_op jit(solution)/shard_map/ppermute | solution.py:375
  47.7 7.7 %collective-permute-done.7.refs_1_ = f32[152,256]{1,0:T(8,128)S(1)} collective-permute-done((f32[152,256]{1,0:T(8,128)S(1)}, f32[152,256]{1,0:T(8,128)S(1)}, u32[]{:S(2)}, u32[]{:S(2)}) %collective-permute-start.7) | collective-permute-done | bytes 155680 | tf_op jit(solution)/shard_map/ppermute | solution.py:375
  55.3 1.4 %collective-permute-done.8.refs_2_ = f32[152,256]{1,0:T(8,128)S(1)} collective-permute-done((f32[152,256]{1,0:T(8,128)S(1)}, f32[152,256]{1,0:T(8,128)S(1)}, u32[]{:S(2)}, u32[]{:S(2)}) %collective-permute-start.8) | collective-permute-done | bytes 155680 | tf_op jit(solution)/shard_map/ppermute | solution.py:375
  57.6 5.1 %collective-permute-start.9 = (f32[152,256]{1,0:T(8,128)S(1)}, f32[152,256]{1,0:T(8,128)S(1)}, u32[]{:S(2)}, u32[]{:S(2)}) collective-permute-start(f32[152,256]{1,0:T(8,128)S(1)} %get-tuple-element.53), channel_id=1, source_target_pairs={{0,56},{4,60},{8,48},{12,52},{16,40},{20,44},{24,32},{28,36},{32,2... | collective-permute-start | bytes 466952 | tf_op jit(solution)/shard_map/ppermute | solution.py:375
  62.7 6.6 %collective-permute-done.9.refs_1_ = f32[152,256]{1,0:T(8,128)S(1)} collective-permute-done((f32[152,256]{1,0:T(8,128)S(1)}, f32[152,256]{1,0:T(8,128)S(1)}, u32[]{:S(2)}, u32[]{:S(2)}) %collective-permute-start.9) | collective-permute-done | bytes 155680 | tf_op jit(solution)/shard_map/ppermute | solution.py:375
  69.4 1.3 %collective-permute-done.10.refs_2_ = f32[152,256]{1,0:T(8,128)S(1)} collective-permute-done((f32[152,256]{1,0:T(8,128)S(1)}, f32[152,256]{1,0:T(8,128)S(1)}, u32[]{:S(2)}, u32[]{:S(2)}) %collective-permute-start.10) | collective-permute-done | bytes 155680 | tf_op jit(solution)/shard_map/ppermute | solution.py:375
  71.4 0.9 collective-permute-start.11
  72.3 8.6 %collective-permute-done.11.refs_1_.refs_0_ = f32[304,256]{1,0:T(8,128)S(1)} collective-permute-done((f32[304,256]{1,0:T(8,128)S(1)}, f32[304,256]{1,0:T(8,128)S(1)}, u32[]{:S(2)}, u32[]{:S(2)}) %collective-permute-start.11) | collective-permute-done | bytes 311328 | tf_op jit(solution)/shard_map/ppermute | solution.py:375
  82.4 4.0 %collective-permute-done.12.theirs_ref = f32[32,256]{1,0:T(8,128)S(1)} collective-permute-done((f32[32,256]{1,0:T(8,128)S(1)}, f32[32,256]{1,0:T(8,128)S(1)}, u32[]{:S(2)}, u32[]{:S(2)}) %collective-permute-start.12) | collective-permute-done | bytes 32800 | tf_op jit(solution)/shard_map/ppermute | solution.py:375
  86.4 2.9 %shard_map.54 = f32[32,8,256]{2,1,0:T(8,128)S(1)} custom-call(s32[1]{0:T(128)} %bitcast.code_ref, f32[32,256]{1,0:T(8,128)S(1)} %collective-permute-done.12.theirs_ref, f32[304,256]{1,0:T(8,128)S(1)} %shard_map.53.before_ref, f32[8,256,256]{2,1,0:T(8,128)} %get-tuple-element.63.prefix_ref, f32[8,32,256]{2,1,0:T(8,128)S(1)} %copy-done.3), custom_call_target="tpu_custom_call" | custom-call | flops 226492416 | bytes 1048576 | tf_op jit(solution)/shard_map/pallas_call | solution.py:348
  89.3 9.1 %all_to_all.10 = f32[4,8,8,256]{3,2,1,0:T(8,128)S(1)} all-to-all(f32[4,8,8,256]{3,2,1,0:T(8,128)S(1)} %bitcast.20), channel_id=1, replica_groups=mesh['line'=64,'span'=4] {'span'}, dimensions={0} | all-to-all | bytes 524288 | tf_op jit(solution)/shard_map/all_to_all | solution.py:412
  (37 shorter events, 9.1 us)
Async XLA Ops:
  0.0 7.6 %copy-start = (f32[8,32,256]{2,1,0:T(8,128)S(1)}, f32[8,32,256]{2,1,0:T(8,128)}, u32[]{:S(2)}) copy-start(f32[8,32,256]{2,1,0:T(8,128)} %param.3) | copy-start | bytes 786436
  0.0 0.7 copy-start.4
  0.7 19.4 %copy-start.1 = (f32[8,256,256]{2,1,0:T(8,128)S(1)}, f32[8,256,256]{2,1,0:T(8,128)}, u32[]{:S(2)}) copy-start(f32[8,256,256]{2,1,0:T(8,128)} %blocks_ref.3) | copy-start | bytes 6291460
  0.7 19.4 %copy-start.5 = (f32[8,256]{1,0:T(8,128)S(1)}, f32[8,256]{1,0:T(8,128)}, u32[]{:S(2)}) copy-start(f32[8,256]{1,0:T(8,128)} %upstream_ref.3) | copy-start | bytes 24580
  5.9 8.5 %collective-permute-start = (f32[272,256]{1,0:T(8,128)S(1)}, f32[272,256]{1,0:T(8,128)S(1)}, u32[]{:S(2)}, u32[]{:S(2)}) collective-permute-start(f32[272,256]{1,0:T(8,128)S(1)} %get-tuple-element.35.mine_ref.my_map_ref), channel_id=1, source_target_pairs={{0,1},{1,0},{2,3},{3,2},{4,5},{5,4},{6,7},{7,6},{8,9},{9,8},{10,11... | collective-permute-start | bytes 835592 | tf_op jit(solution)/shard_map/ppermute | solution.py:375
  8.3 11.9 %all-to-all-start = ((f32[4,8,8,256]{3,2,1,0:T(8,128)}), f32[4,8,8,256]{3,2,1,0:T(8,128)}, u32[]{:S(2)}, u32[]{:S(2)}) async-start(f32[4,8,8,256]{3,2,1,0:T(8,128)} %copy_bitcast_fusion.1), calls=%async_computation | async-start | bytes 524288 | tf_op jit(solution)/shard_map/all_to_all | solution.py:368
  14.9 17.9 %collective-permute-start.2 = (f32[272,256]{1,0:T(8,128)S(1)}, f32[272,256]{1,0:T(8,128)S(1)}, u32[]{:S(2)}, u32[]{:S(2)}) collective-permute-start(f32[272,256]{1,0:T(8,128)S(1)} %shard_map.38.refs_0_), channel_id=1, source_target_pairs={{0,3},{1,2},{2,1},{3,0},{4,7},{5,6},{6,5},{7,4},{8,11},{9,10},{10,... | collective-permute-start | bytes 835592 | tf_op jit(solution)/shard_map/ppermute | solution.py:375
  23.4 4.3 %copy-start.2 = (f32[8,32,256]{2,1,0:T(8,128)}, f32[8,32,256]{2,1,0:T(8,128)S(1)}, u32[]{:S(2)}) copy-start(f32[8,32,256]{2,1,0:T(8,128)S(1)} %get-tuple-element.64.trial_ref) | copy-start | bytes 786436
  23.4 4.0 %collective-permute-start.1 = (f32[32,256]{1,0:T(8,128)S(1)}, f32[32,256]{1,0:T(8,128)S(1)}, u32[]{:S(2)}, u32[]{:S(2)}) collective-permute-start(f32[32,256]{1,0:T(8,128)S(1)} %get-tuple-element.36.mine_ref), channel_id=1, source_target_pairs={{0,1},{1,0},{2,3},{3,2},{4,5},{5,4},{6,7},{7,6},{8,9},{9,8},{10,11... | collective-permute-start | bytes 98312 | tf_op jit(solution)/shard_map/ppermute | solution.py:375
  27.7 5.2 %collective-permute-start.3 = (f32[32,256]{1,0:T(8,128)S(1)}, f32[32,256]{1,0:T(8,128)S(1)}, u32[]{:S(2)}, u32[]{:S(2)}) collective-permute-start(f32[32,256]{1,0:T(8,128)S(1)} %shard_map.40.refs_1_), channel_id=1, source_target_pairs={{0,3},{1,2},{2,1},{3,0},{4,7},{5,6},{6,5},{7,4},{8,11},{9,10},{10,... | collective-permute-start | bytes 98312 | tf_op jit(solution)/shard_map/ppermute | solution.py:375
  33.5 1.7 %collective-permute-start.4 = (f32[304,256]{1,0:T(8,128)S(1)}, f32[304,256]{1,0:T(8,128)S(1)}, u32[]{:S(2)}, u32[]{:S(2)}) collective-permute-start(f32[304,256]{1,0:T(8,128)S(1)} %shard_map.42.refs_0_), channel_id=1, source_target_pairs={{0,4},{4,0},{8,12},{12,8},{16,20},{20,16},{24,28},{28,24},{32,36},... | collective-permute-start | bytes 933896 | tf_op jit(solution)/shard_map/ppermute | solution.py:375
  35.9 6.3 %collective-permute-start.5 = (f32[152,256]{1,0:T(8,128)S(1)}, f32[152,256]{1,0:T(8,128)S(1)}, u32[]{:S(2)}, u32[]{:S(2)}) collective-permute-start(f32[152,256]{1,0:T(8,128)S(1)} %get-tuple-element.42), channel_id=1, source_target_pairs={{0,8},{4,12},{8,0},{12,4},{16,24},{20,28},{24,16},{28,20},{32,40},... | collective-permute-start | bytes 466952 | tf_op jit(solution)/shard_map/ppermute | solution.py:375
  42.2 1.4 %collective-permute-start.6 = (f32[152,256]{1,0:T(8,128)S(1)}, f32[152,256]{1,0:T(8,128)S(1)}, u32[]{:S(2)}, u32[]{:S(2)}) collective-permute-start(f32[152,256]{1,0:T(8,128)S(1)} %collective-permute-done.5.refs_1_), channel_id=1, source_target_pairs={{0,4},{4,0},{8,12},{12,8},{16,20},{20,16},{24,28},{28,24},{32,36},... | collective-permute-start | bytes 466952 | tf_op jit(solution)/shard_map/ppermute | solution.py:375
  44.3 11.0 %collective-permute-start.7 = (f32[152,256]{1,0:T(8,128)S(1)}, f32[152,256]{1,0:T(8,128)S(1)}, u32[]{:S(2)}, u32[]{:S(2)}) collective-permute-start(f32[152,256]{1,0:T(8,128)S(1)} %get-tuple-element.47), channel_id=1, source_target_pairs={{0,16},{4,20},{8,24},{12,28},{16,0},{20,4},{24,8},{28,12},{32,48},... | collective-permute-start | bytes 466952 | tf_op jit(solution)/shard_map/ppermute | solution.py:375
  55.3 1.4 %collective-permute-start.8 = (f32[152,256]{1,0:T(8,128)S(1)}, f32[152,256]{1,0:T(8,128)S(1)}, u32[]{:S(2)}, u32[]{:S(2)}) collective-permute-start(f32[152,256]{1,0:T(8,128)S(1)} %collective-permute-done.7.refs_1_), channel_id=1, source_target_pairs={{0,4},{4,0},{8,12},{12,8},{16,20},{20,16},{24,28},{28,24},{32,36},... | collective-permute-start | bytes 466952 | tf_op jit(solution)/shard_map/ppermute | solution.py:375
  57.6 11.8 %collective-permute-start.9 = (f32[152,256]{1,0:T(8,128)S(1)}, f32[152,256]{1,0:T(8,128)S(1)}, u32[]{:S(2)}, u32[]{:S(2)}) collective-permute-start(f32[152,256]{1,0:T(8,128)S(1)} %get-tuple-element.53), channel_id=1, source_target_pairs={{0,56},{4,60},{8,48},{12,52},{16,40},{20,44},{24,32},{28,36},{32,2... | collective-permute-start | bytes 466952 | tf_op jit(solution)/shard_map/ppermute | solution.py:375
  69.3 1.4 %collective-permute-start.10 = (f32[152,256]{1,0:T(8,128)S(1)}, f32[152,256]{1,0:T(8,128)S(1)}, u32[]{:S(2)}, u32[]{:S(2)}) collective-permute-start(f32[152,256]{1,0:T(8,128)S(1)} %collective-permute-done.9.refs_1_), channel_id=1, source_target_pairs={{0,4},{4,0},{8,12},{12,8},{16,20},{20,16},{24,28},{28,24},{32,36},... | collective-permute-start | bytes 466952 | tf_op jit(solution)/shard_map/ppermute | solution.py:375
  69.4 16.9 %copy-start.3 = (f32[8,32,256]{2,1,0:T(8,128)S(1)}, f32[8,32,256]{2,1,0:T(8,128)}, u32[]{:S(2)}) copy-start(f32[8,32,256]{2,1,0:T(8,128)} %copy-done.2) | copy-start | bytes 786436
  71.4 9.5 %collective-permute-start.11 = (f32[304,256]{1,0:T(8,128)S(1)}, f32[304,256]{1,0:T(8,128)S(1)}, u32[]{:S(2)}, u32[]{:S(2)}) collective-permute-start(f32[304,256]{1,0:T(8,128)S(1)} %get-tuple-element.58.refs_0_), channel_id=1, source_target_pairs={{0,64},{4,68},{8,72},{12,76},{16,80},{20,84},{24,88},{28,92},{32,9... | collective-permute-start | bytes 933896 | tf_op jit(solution)/shard_map/ppermute | solution.py:375
  81.2 5.2 %collective-permute-start.12 = (f32[32,256]{1,0:T(8,128)S(1)}, f32[32,256]{1,0:T(8,128)S(1)}, u32[]{:S(2)}, u32[]{:S(2)}) collective-permute-start(f32[32,256]{1,0:T(8,128)S(1)} %shard_map.52), channel_id=1, source_target_pairs={{0,192},{4,196},{8,200},{12,204},{16,208},{20,212},{24,216},{28,22... | collective-permute-start | bytes 98312 | tf_op jit(solution)/shard_map/ppermute | solution.py:375

commit v5 on v4

--- a/solution.py
+++ b/solution.py
@@ -13,21 +13,18 @@
 PAD = 16
 VMEM = pl.BlockSpec(memory_space=pltpu.VMEM)
 HBM = pl.BlockSpec(memory_space=pltpu.HBM)
-STATES_VMEM = 8 * 2**20
-FINISH_VMEM = 52 * 2**20
 LARGE = 52 * 2**20
 SMEM = pl.BlockSpec(memory_space=pltpu.SMEM)
 CORE = 1
 ROUNDS = (
-    ("span", 1, 1, "apart"),
-    ("span", 3, 2, "apart"),
-    ("line", 1, 1, "together"),
-    ("line", 2, 2, "halves"),
-    ("line", 4, 4, "halves"),
-    ("line", 14, 8, "halves"),
-    ("line", 16, 16, "together"),
-    ("line", 48, 32, "states"),
+    ("span", 1, 1, False, True),
+    ("span", 3, 2, False, False),
+    ("line", 1, 1, False, False),
+    ("line", 2, 2, True, False),
+    ("line", 4, 4, True, False),
+    ("line", 14, 8, True, False),
 )
+PLANE = 16
 
 
 def dot(a, b):
@@ -135,17 +132,13 @@
     )(upstream, blocks)
 
 
-def states_kernel(
-    upstream_ref, blocks_ref, forcing_ref, trial_ref, states_ref, held_ref, arrived
-):
-    fetch(blocks_ref, held_ref, arrived)
+def states_kernel(upstream_ref, blocks_ref, forcing_ref, trial_ref, states_ref):
     states_ref[...] = jnp.zeros_like(states_ref)
 
-    @pl.loop(0, held_ref.shape[0])
+    @pl.loop(0, blocks_ref.shape[0])
     def _(cell):
         forced = forcing_ref[:, cell, :] - upstream_ref[pl.ds(cell, 1), :] * states_ref[...]
-        block_copy(blocks_ref, held_ref, arrived, cell).wait()
-        state = dot(forced, held_ref[cell])
+        state = dot(forced, blocks_ref[cell])
         states_ref[...] = state
         trial_ref[cell] = state
 
@@ -155,12 +148,9 @@
     lines = forcing.shape[0]
     return call(
         states_kernel,
-        [VMEM, HBM, VMEM],
+        [VMEM] * 3,
         [shape(cells, lines, levels), shape(lines, levels)],
         12 * cells * lines * levels**2,
-        [pltpu.VMEM(blocks.shape, F32), pltpu.SemaphoreType.DMA((cells,))],
-        None,
-        STATES_VMEM,
     )(upstream, blocks, forcing)
 
 
@@ -170,21 +160,6 @@
     pl.when(upper == 0)(otherwise)
 
 
-def merge_maps_kernel(code_ref, mine_ref, theirs_ref, total_ref):
-    later(
-        code_ref,
-        lambda: join_maps(theirs_ref, mine_ref, total_ref),
-        lambda: join_maps(mine_ref, theirs_ref, total_ref),
-    )
-
-
-def merge_maps(code, mine, theirs):
-    levels = mine.shape[1]
-    return call(merge_maps_kernel, [SMEM, VMEM, VMEM], shape(*mine.shape), 12 * levels**3)(
-        code, mine, theirs
-    )
-
-
 def merge_states_kernel(code_ref, mine_ref, theirs_ref, my_map_ref, their_map_ref, out_ref):
     def then():
         out_ref[...] = move_states(theirs_ref[...], my_map_ref) + mine_ref[...]
@@ -202,81 +177,82 @@
     )(code, mine, theirs, my_map, their_map)
 
 
-def merge_kernel(levels, apart, halves, half, last, code_ref, *refs):
+def merge_kernel(start, kind, apart, halves, half, code_ref, *refs):
     refs = list(refs)
     mine_map = refs.pop(0)
-    start = levels + PAD
-    mine_states = refs.pop(0)[...] if apart else mine_map[start:]
-    if apart:
-        their_map, their_states = refs.pop(0), refs.pop(0)[...]
-    elif halves:
-        here_ref, there_ref = refs.pop(0), refs.pop(0)
+    if apart and kind != "maps":
+        mine_states = refs.pop(0)
     else:
-        theirs = refs.pop(0)
-        their_map, their_states = theirs, theirs[start:]
-    total_ref = refs.pop(0)
+        mine_states = None if kind == "maps" else mine_map.at[start:]
+    here = refs.pop(0)
+    there = refs.pop(0) if halves else None
+    their_states = refs.pop(0) if apart and kind != "maps" else None
+    out = refs.pop(0)
     core = code_ref[0] // 2
+    their_map = here
     if halves:
-        theirs = refs.pop(0)
-        rows = here_ref.shape[0]
+        their_map = refs.pop(0)
+        rows = here.shape[0]
 
         @pl.when(core == 0)
         def _():
-            theirs[:rows] = here_ref[...]
-            theirs[rows:] = there_ref[...]
+            their_map[:rows] = here[...]
+            their_map[rows:] = there[...]
 
         @pl.when(core == 1)
         def _():
-            theirs[:rows] = there_ref[...]
-            theirs[rows:] = here_ref[...]
-
-        their_map, their_states = theirs, theirs[start:]
-
-    def then():
-        states = move_states(their_states, mine_map) + mine_states
-        if last:
-            total_ref[...] = states
+            their_map[:rows] = there[...]
+            their_map[rows:] = here[...]
+
+    if their_states is None and kind != "maps":
+        their_states = their_map.at[start:]
+
+    def joined(left_map, left_states, right_map, right_states):
+        if kind != "states":
+            join_maps(left_map, right_map, out)
+        if kind == "maps":
+            return
+        states = move_states(left_states[...], right_map) + right_states[...]
+        if kind == "both":
+            out[start:] = states
         else:
-            join_maps(their_map, mine_map, total_ref)
-            total_ref[start:] = states
-
-    def otherwise():
-        states = move_states(mine_states, their_map) + their_states
-        if last:
-            total_ref[...] = states
-        else:
-            join_maps(mine_map, their_map, total_ref)
-            total_ref[start:] = states
-
-    later(code_ref, then, otherwise)
+            out[...] = states
+
+    later(
+        code_ref,
+        lambda: joined(their_map, their_states, mine_map, mine_states),
+        lambda: joined(mine_map, mine_states, their_map, their_states),
+    )
     if half:
         half_ref = refs.pop(0)
         rows = half_ref.shape[0]
 
         @pl.when(core == 0)
         def _():
-            half_ref[...] = total_ref[:rows]
+            half_ref[...] = out[:rows]
 
         @pl.when(core == 1)
         def _():
-            half_ref[...] = total_ref[rows:]
-
-
-def merge(code, mine, theirs, apart, halves, half, last):
+            half_ref[...] = out[rows:]
+
+
+def merge(code, mine, theirs, kind, lines, apart, halves, half):
     levels = mine[0].shape[1]
-    rows = levels + PAD + (mine[1].shape[0] if apart else mine[0].shape[0] - levels - PAD)
-    out = [shape(rows - levels - PAD if last else rows, levels)]
+    start = levels + PAD
+    rows = {"maps": start, "both": start + lines, "states": lines}[kind]
+    out = [shape(rows, levels)]
     if halves:
-        out.append(shape(rows, levels))
+        out.append(shape(2 * theirs[0].shape[0], levels))
     if half:
         out.append(shape(rows // 2, levels))
     operands = (*mine, *theirs)
-    return call(
-        functools.partial(merge_kernel, levels, apart, halves, half, last),
+    got = call(
+        functools.partial(merge_kernel, start, kind, apart, halves, half),
         [SMEM] + [VMEM] * len(operands),
         out,
-        12 * (rows - levels if last else rows) * levels**2,
+        12 * rows * levels**2,
     )(code, *operands)
+    return got[0], got[1] if halves else theirs[0], got[-1]
 
 
 def extend_kernel(first, apart, code_ref, *refs):
@@ -323,41 +299,57 @@
     )(code, *operands)
 
 
-def finish_kernel(
-    code_ref, theirs_ref, before_ref, prefix_ref, trial_ref, solved_ref, held_ref, incoming, arrived
-):
-    fetch(prefix_ref, held_ref, arrived)
+def enter_kernel(from_ref, map_ref, own_ref, out_ref):
+    out_ref[...] = move_states(from_ref[...], map_ref) + own_ref[...]
+
+
+def enter(states, total, own):
+    lines, levels = own.shape
+    return call(enter_kernel, [VMEM] * 3, shape(lines, levels), 12 * lines * levels**2)(
+        states, total, own
+    )
+
+
+def settle_planes_kernel(code_ref, beside_ref, from_ref, before_ref, ahead_ref):
     start = before_ref.shape[1] + PAD
 
     def then():
-        incoming[...] = move_states(theirs_ref[...], before_ref) + before_ref[start:]
+        join_maps(beside_ref, before_ref, ahead_ref)
+        ahead_ref[start:] = move_states(beside_ref[start:], before_ref) + before_ref[start:]
 
     def otherwise():
-        incoming[...] = before_ref[start:]
+        ahead_ref[:start] = before_ref[:start]
+        ahead_ref[start:] = move_states(from_ref[...], before_ref) + before_ref[start:]
 
     later(code_ref, then, otherwise)
 
-    @pl.loop(0, held_ref.shape[0])
+
+def settle_planes(code, beside, from_first, before):
+    rows, levels = before.shape
+    return call(
+        settle_planes_kernel, [SMEM] + [VMEM] * 3, shape(rows, levels), 12 * rows * levels**2
+    )(code, beside, from_first, before)
+
+
+def finish_kernel(one_ref, two_ref, before_ref, prefix_ref, trial_ref, solved_ref, incoming):
+    start = before_ref.shape[1] + PAD
+    entering = one_ref[...] + two_ref[...]
+    incoming[...] = move_states(entering, before_ref) + before_ref[start:]
+
+    @pl.loop(0, prefix_ref.shape[0])
     def _(cell):
-        block_copy(prefix_ref, held_ref, arrived, cell).wait()
-        solved_ref[:, cell, :] = trial_ref[cell] + dot(incoming[...], held_ref[cell])
-
-
-def finish(code, theirs, before, prefix, trial):
+        solved_ref[:, cell, :] = trial_ref[cell] + dot(incoming[...], prefix_ref[cell])
+
+
+def finish(entering, before, prefix, trial):
     cells, lines, levels = trial.shape
     return call(
         finish_kernel,
-        [SMEM, VMEM, VMEM, HBM, VMEM],
+        [VMEM] * 5,
         shape(lines, cells, levels),
         12 * (cells + 1) * lines * levels**2,
-        [
-            pltpu.VMEM(prefix.shape, F32),
-            pltpu.VMEM((lines, levels), F32),
-            pltpu.SemaphoreType.DMA((cells,)),
-        ],
-        None,
-        FINISH_VMEM,
-    )(code, theirs, before, prefix, trial)
+        [pltpu.VMEM((lines, levels), F32)],
+    )(*entering, before, prefix, trial)
 
 
 def shards(span_count, forcing, blocks, upstream):
@@ -368,6 +360,7 @@
     parts = lax.all_to_all(parts, "span", split_axis=0, concat_axis=0, tiled=True)
     local_forcing = parts.reshape(lines, cells, levels)
     prefix, maps = prefix_maps(blocks, upstream)
+    local_forcing, maps = lax.optimization_barrier((local_forcing, maps))
     trial, states = trial_states(blocks, upstream, local_forcing)
 
     def partner(value, axis, mask):
@@ -380,34 +373,41 @@
         return (upper + core).astype(jnp.int32).reshape(1)
 
     total, half, before = None, None, None
-    for turn, (axis, mask, bit, how) in enumerate(ROUNDS[:-1]):
+    for turn, (axis, mask, bit, halves, apart) in enumerate(ROUNDS):
         code = code_of(axis, bit)
-        after = ROUNDS[turn + 1][3]
-        apart, halves = how == "apart", how == "halves"
-        if apart:
-            theirs = (partner(maps, axis, mask), partner(states, axis, mask))
-            mine = (maps, states)
-        elif halves:
+        last = turn == len(ROUNDS) - 1
+        next_halves = not last and ROUNDS[turn + 1][3]
+        if halves:
             here = partner(half, axis, mask)
             theirs = (here, partner(here, "line", CORE))
-            mine = (total,)
         else:
-            theirs = (partner(total, axis, mask),)
-            mine = (total,)
+            theirs = (partner(maps if apart else total, axis, mask),)
         if before is not None:
             theirs, before = lax.optimization_barrier((theirs, before))
-        if apart and after == "apart":
-            states = merge_states(code, states, theirs[1], maps, theirs[0])
-            maps = merge_maps(code, maps, theirs[0])
+        mine = (total,)
+        if apart:
+            their_states = partner(states, axis, mask)
+            mine, theirs = (maps, states), (*theirs, their_states)
+        if last:
+            plane, whole, _ = merge(code, mine, theirs, "states", lines, apart, halves, False)
+            total, _, _ = merge(code, mine, (whole,), "both", lines, False, False, False)
         else:
-            got = merge(code, mine, theirs, apart, halves, after == "halves", after == "states")
-            total = got[0]
-            theirs = (got[1],) if halves else theirs
-            half = got[-1]
-        before = extend(code, theirs, before)
-    axis, mask, bit, _ = ROUNDS[-1]
-    theirs = partner(total, axis, mask)
-    solved = finish(code_of(axis, bit), theirs, before, prefix, trial)
+            total, whole, half = merge(code, mine, theirs, "both", lines, apart, halves, next_halves)
+        before = extend(code, (whole, their_states) if apart else (whole,), before)
+
+    def across(value, source, target):
+        shift = (target - source) * PLANE
+        pairs = [(i, i + shift) for i in range(source * PLANE, (source + 1) * PLANE)]
+        return lax.ppermute(value, "line", pairs)
+
+    from_first = across(plane, 0, 1)
+    beside = across(total, 2, 3)
+    from_first, before = lax.optimization_barrier((from_first, before))
+    joined = enter(from_first, total, plane)
+    entering = (across(joined, 1, 2), across(joined, 1, 3))
+    in_last = jnp.where(lax.axis_index("line") >= 3 * PLANE, 1, 0).astype(jnp.int32).reshape(1)
+    before = settle_planes(in_last, beside, from_first, before)
+    solved = finish(entering, before, prefix, trial)
     parts = solved.reshape(span_count, share, cells, levels)
     parts = lax.all_to_all(parts, "span", split_axis=0, concat_axis=0, tiled=True)
     return parts.swapaxes(0, 1).reshape(share, span_count * cells, levels)

time: 99.3 us -> 98.3 us (0.990)
  waiting for transfers between devices: 48.6 us -> 42.1 us
  starting transfers between devices: 22.5 us -> 24.8 us
  local copies, waits for them, and re-layouts: 2.21 us -> 3.87 us
  blocking collectives: 9.07 us -> 10.7 us
    ppermute x13 -> x10, waiting for transfers between devices: 47 us -> 34 us  [partner(): return lax.ppermute(value, axis, [(i, i ^ mask) for i in range(count)])]
    ppermute x0 -> x4, waiting for transfers between devices: none -> 7.25 us  [across(): return lax.ppermute(value, 'line', pairs)]
    ppermute x0 -> x4, starting transfers between devices: none -> 4.5 us  [across(): return lax.ppermute(value, 'line', pairs)]
    ppermute x13 -> x10, starting transfers between devices: 18.3 us -> 15.8 us  [partner(): return lax.ppermute(value, axis, [(i, i ^ mask) for i in range(count)])]
    unnamed x12 -> x14, local copies, waits for them, and re-layouts: 0.76 us -> 2.42 us
    all_to_all x1, blocking collectives: 9.07 us -> 10.7 us  [shards(): lax.all_to_all(parts, 'span', split_axis=0, concat_axis=0, tiled=True)]
    pallas_call x10 -> x11, Pallas kernels: 10.6 us -> 10.9 us  [the longest x7 4.53 us: merge(): call(functools.partial(merge_kernel, start, kind, apart, halves, half), [...]
  transfers between devices with their start and end apart: 14 -> 15, of which waited for: 13 -> 12; matrix products, arithmetic and copies ran while one was open for 1% -> 0% of each run, Pallas kernels for 5% -> 9%
where the time goes in v5:
time: 98.3 us; the launch traced here: 97.8 us
  waiting for transfers between devices  42.1 us (43%)
  starting transfers between devices  24.8 us (25%)
  Pallas kernels  16.2 us (16%)
  blocking collectives  10.7 us (11%)
  local copies, waits for them, and re-layouts  3.87 us (4%)
    ppermute x10, waiting for transfers between devices, partner(): return lax.ppermute(value, axis, [(i, i ^ mask) for i in range(count)])  34 us
    ppermute x10, starting transfers between devices, partner(): return lax.ppermute(value, axis, [(i, i ^ mask) for i in range(count)])  15.8 us
    all_to_all x1, blocking collectives, shards(): lax.all_to_all(parts, 'span', split_axis=0, concat_axis=0, tiled=True)  10.7 us
    ppermute x4, waiting for transfers between devices, across(): return lax.ppermute(value, 'line', pairs)  7.25 us
    pallas_call x1, Pallas kernels, prefix_maps(): call(maps_kernel, [VMEM, HBM], [shape(*blocks.shape), shape(levels + PAD,...  5.14 us
    pallas_call x7, Pallas kernels, merge(): call(functools.partial(merge_kernel, start, kind, apart, halves, half), [...  4.53 us
    ppermute x4, starting transfers between devices, across(): return lax.ppermute(value, 'line', pairs)  4.5 us
    all_to_all x1, starting transfers between devices, shards(): lax.all_to_all(parts, 'span', split_axis=0, concat_axis=0, tiled=True)  4.46 us
  transfers between devices with their start and end apart: 15, of which 12 were waited for; matrix products, arithmetic and copies ran while one was open for 0% of the time, Pallas kernels for 9%

profile of v5, /device:TPU:6, one launch (start us, length us, event | category | flops | bytes accessed | tf_op | source)
XLA Modules:
  0.0 97.8 jit_solution(11084333977143339162)
XLA Ops:
  1.7 4.5 %all-to-all-start = ((f32[4,8,8,256]{3,2,1,0:T(8,128)}), f32[4,8,8,256]{3,2,1,0:T(8,128)S(1)}, u32[]{:S(2)}, u32[]{:S(2)}) async-start(f32[4,8,8,256]{3,2,1,0:T(8,128)} %copy_bitcast_fusion.1), calls=%async_computation | async-start | bytes 524288 | tf_op jit(solution)/shard_map/all_to_all | solution.py:360
  6.8 5.1 %shard_map.37 = (f32[8,256,256]{2,1,0:T(8,128)}, f32[272,256]{1,0:T(8,128)S(1)}) custom-call(f32[8,256]{1,0:T(8,128)S(1)} %copy-done.5, f32[8,256,256]{2,1,0:T(8,128)} %blocks_ref.3), custom_call_target="tpu_custom_call" | custom-call | flops 1610612736 | bytes 1048576 | tf_op jit(solution)/shard_map/pallas_call | solution.py:118
  12.8 1.3 %collective-permute-start = (f32[272,256]{1,0:T(8,128)S(1)}, f32[272,256]{1,0:T(8,128)S(1)}, u32[]{:S(2)}, u32[]{:S(2)}) collective-permute-start(f32[272,256]{1,0:T(8,128)S(1)} %get-tuple-element.37.refs_0_), channel_id=1, source_target_pairs={{0,1},{1,0},{2,3},{3,2},{4,5},{5,4},{6,7},{7,6},{8,9},{9,8},{10,11... | collective-permute-start | bytes 835592 | tf_op jit(solution)/shard_map/ppermute | solution.py:368
  14.1 1.9 %shard_map.38 = (f32[8,32,256]{2,1,0:T(8,128)S(1)}, f32[32,256]{1,0:T(8,128)S(1)}) custom-call(f32[8,256]{1,0:T(8,128)S(1)} %copy-done.6, f32[8,256,256]{2,1,0:T(8,128)S(1)} %copy-done.1, f32[32,8,256]{2,1,0:T(8,128)S(1)} %bitcast.19), custom_call_target="tpu_custom_call" | custom-call | flops 201326592 | bytes 1048576 | tf_op jit(solution)/shard_map/pallas_call | solution.py:149
  16.9 4.0 %collective-permute-done.1.refs_3_.refs_1_ = f32[32,256]{1,0:T(8,128)S(1)} collective-permute-done((f32[32,256]{1,0:T(8,128)S(1)}, f32[32,256]{1,0:T(8,128)S(1)}, u32[]{:S(2)}, u32[]{:S(2)}) %collective-permute-start.1) | collective-permute-done | bytes 32800 | tf_op jit(solution)/shard_map/ppermute | solution.py:368
  21.6 3.0 %collective-permute-start.2 = (f32[304,256]{1,0:T(8,128)S(1)}, f32[304,256]{1,0:T(8,128)S(1)}, u32[]{:S(2)}, u32[]{:S(2)}) collective-permute-start(f32[304,256]{1,0:T(8,128)S(1)} %shard_map.39.refs_0_), channel_id=1, source_target_pairs={{0,3},{1,2},{2,1},{3,0},{4,7},{5,6},{6,5},{7,4},{8,11},{9,10},{10,... | collective-permute-start | bytes 933896 | tf_op jit(solution)/shard_map/ppermute | solution.py:368
  24.6 5.8 %collective-permute-done.2.refs_1_.refs_0_ = f32[304,256]{1,0:T(8,128)S(1)} collective-permute-done((f32[304,256]{1,0:T(8,128)S(1)}, f32[304,256]{1,0:T(8,128)S(1)}, u32[]{:S(2)}, u32[]{:S(2)}) %collective-permute-start.2) | collective-permute-done | bytes 311328 | tf_op jit(solution)/shard_map/ppermute | solution.py:368
  31.3 1.5 %collective-permute-done.3.refs_1_.refs_0_ = f32[304,256]{1,0:T(8,128)S(1)} collective-permute-done((f32[304,256]{1,0:T(8,128)S(1)}, f32[304,256]{1,0:T(8,128)S(1)}, u32[]{:S(2)}, u32[]{:S(2)}) %collective-permute-start.3) | collective-permute-done | bytes 311328 | tf_op jit(solution)/shard_map/ppermute | solution.py:368
  33.5 2.0 %collective-permute-start.4 = (f32[152,256]{1,0:T(8,128)S(1)}, f32[152,256]{1,0:T(8,128)S(1)}, u32[]{:S(2)}, u32[]{:S(2)}) collective-permute-start(f32[152,256]{1,0:T(8,128)S(1)} %get-tuple-element.44), channel_id=1, source_target_pairs={{0,8},{4,12},{8,0},{12,4},{16,24},{20,28},{24,16},{28,20},{32,40},... | collective-permute-start | bytes 466952 | tf_op jit(solution)/shard_map/ppermute | solution.py:368
  35.5 4.3 %collective-permute-done.4.refs_1_ = f32[152,256]{1,0:T(8,128)S(1)} collective-permute-done((f32[152,256]{1,0:T(8,128)S(1)}, f32[152,256]{1,0:T(8,128)S(1)}, u32[]{:S(2)}, u32[]{:S(2)}) %collective-permute-start.4) | collective-permute-done | bytes 155680 | tf_op jit(solution)/shard_map/ppermute | solution.py:368
  39.9 1.4 %collective-permute-done.5.refs_2_ = f32[152,256]{1,0:T(8,128)S(1)} collective-permute-done((f32[152,256]{1,0:T(8,128)S(1)}, f32[152,256]{1,0:T(8,128)S(1)}, u32[]{:S(2)}, u32[]{:S(2)}) %collective-permute-start.5) | collective-permute-done | bytes 155680 | tf_op jit(solution)/shard_map/ppermute | solution.py:368
  42.0 3.4 %collective-permute-start.6 = (f32[152,256]{1,0:T(8,128)S(1)}, f32[152,256]{1,0:T(8,128)S(1)}, u32[]{:S(2)}, u32[]{:S(2)}) collective-permute-start(f32[152,256]{1,0:T(8,128)S(1)} %get-tuple-element.49), channel_id=1, source_target_pairs={{0,16},{4,20},{8,24},{12,28},{16,0},{20,4},{24,8},{28,12},{32,48},... | collective-permute-start | bytes 466952 | tf_op jit(solution)/shard_map/ppermute | solution.py:368
  45.3 7.7 %collective-permute-done.6.refs_1_ = f32[152,256]{1,0:T(8,128)S(1)} collective-permute-done((f32[152,256]{1,0:T(8,128)S(1)}, f32[152,256]{1,0:T(8,128)S(1)}, u32[]{:S(2)}, u32[]{:S(2)}) %collective-permute-start.6) | collective-permute-done | bytes 155680 | tf_op jit(solution)/shard_map/ppermute | solution.py:368
  53.0 1.4 %collective-permute-done.7.refs_2_ = f32[152,256]{1,0:T(8,128)S(1)} collective-permute-done((f32[152,256]{1,0:T(8,128)S(1)}, f32[152,256]{1,0:T(8,128)S(1)}, u32[]{:S(2)}, u32[]{:S(2)}) %collective-permute-start.7) | collective-permute-done | bytes 155680 | tf_op jit(solution)/shard_map/ppermute | solution.py:368
  55.3 5.1 %collective-permute-start.8 = (f32[152,256]{1,0:T(8,128)S(1)}, f32[152,256]{1,0:T(8,128)S(1)}, u32[]{:S(2)}, u32[]{:S(2)}) collective-permute-start(f32[152,256]{1,0:T(8,128)S(1)} %get-tuple-element.55), channel_id=1, source_target_pairs={{0,56},{4,60},{8,48},{12,52},{16,40},{20,44},{24,32},{28,36},{32,2... | collective-permute-start | bytes 466952 | tf_op jit(solution)/shard_map/ppermute | solution.py:368
  60.4 6.6 %collective-permute-done.8.refs_1_ = f32[152,256]{1,0:T(8,128)S(1)} collective-permute-done((f32[152,256]{1,0:T(8,128)S(1)}, f32[152,256]{1,0:T(8,128)S(1)}, u32[]{:S(2)}, u32[]{:S(2)}) %collective-permute-start.8) | collective-permute-done | bytes 155680 | tf_op jit(solution)/shard_map/ppermute | solution.py:368
  67.1 1.3 %collective-permute-done.9.refs_2_ = f32[152,256]{1,0:T(8,128)S(1)} collective-permute-done((f32[152,256]{1,0:T(8,128)S(1)}, f32[152,256]{1,0:T(8,128)S(1)}, u32[]{:S(2)}, u32[]{:S(2)}) %collective-permute-start.9) | collective-permute-done | bytes 155680 | tf_op jit(solution)/shard_map/ppermute | solution.py:368
  69.4 1.3 %collective-permute-start.13 = (f32[304,256]{1,0:T(8,128)S(1)}, f32[304,256]{1,0:T(8,128)S(1)}, u32[]{:S(2)}, u32[]{:S(2)}) collective-permute-start(f32[304,256]{1,0:T(8,128)S(1)} %shard_map.51.map_ref), channel_id=1, source_target_pairs={{128,192},{132,196},{136,200},{140,204},{144,208},{148,212},{152,2... | collective-permute-start | bytes 933896 | tf_op jit(solution)/shard_map/ppermute | solution.py:401
  72.2 1.3 %collective-permute-start.11 = (f32[32,256]{1,0:T(8,128)}, f32[32,256]{1,0:T(8,128)}, u32[]{:S(2)}, u32[]{:S(2)}) collective-permute-start(f32[32,256]{1,0:T(8,128)} %shard_map.52), channel_id=1, source_target_pairs={{64,128},{68,132},{72,136},{76,140},{80,144},{84,148},{88,152},{92... | collective-permute-start | bytes 98312 | tf_op jit(solution)/shard_map/ppermute | solution.py:401
  73.5 1.3 %collective-permute-start.12 = (f32[32,256]{1,0:T(8,128)}, f32[32,256]{1,0:T(8,128)}, u32[]{:S(2)}, u32[]{:S(2)}) collective-permute-start(f32[32,256]{1,0:T(8,128)} %shard_map.52), channel_id=1, source_target_pairs={{64,192},{68,196},{72,200},{76,204},{80,208},{84,212},{88,216},{92... | collective-permute-start | bytes 98312 | tf_op jit(solution)/shard_map/ppermute | solution.py:401
  74.8 5.9 %collective-permute-done.13.beside_ref = f32[304,256]{1,0:T(8,128)S(1)} collective-permute-done((f32[304,256]{1,0:T(8,128)S(1)}, f32[304,256]{1,0:T(8,128)S(1)}, u32[]{:S(2)}, u32[]{:S(2)}) %collective-permute-start.13) | collective-permute-done | bytes 311328 | tf_op jit(solution)/shard_map/ppermute | solution.py:401
  82.1 1.4 %collective-permute-done.12.two_ref = f32[32,256]{1,0:T(8,128)} collective-permute-done((f32[32,256]{1,0:T(8,128)}, f32[32,256]{1,0:T(8,128)}, u32[]{:S(2)}, u32[]{:S(2)}) %collective-permute-start.12) | collective-permute-done | bytes 32800 | tf_op jit(solution)/shard_map/ppermute | solution.py:401
  83.5 2.9 %shard_map.54 = f32[32,8,256]{2,1,0:T(8,128)S(1)} custom-call(f32[32,256]{1,0:T(8,128)} %collective-permute-done.11.one_ref, f32[32,256]{1,0:T(8,128)} %collective-permute-done.12.two_ref, f32[304,256]{1,0:T(8,128)S(1)} %shard_map.53.before_ref, f32[8,256,256]{2,1,0:T(8,128)S(1)} %copy-done.2, f32[8,32,256]{2,1,0:T(8,128)S(1)} %get-tuple-element.66.trial_ref), custom_call_target="tpu_custom_call" | custom-call | flops 226492416 | bytes 1048576 | tf_op jit(solution)/shard_map/pallas_call | solution.py:346
  86.4 10.7 %all_to_all.10 = f32[4,8,8,256]{3,2,1,0:T(8,128)S(1)} all-to-all(f32[4,8,8,256]{3,2,1,0:T(8,128)S(1)} %bitcast.20), channel_id=1, replica_groups=mesh['line'=64,'span'=4] {'span'}, dimensions={0} | all-to-all | bytes 524288 | tf_op jit(solution)/shard_map/all_to_all | solution.py:412
  (41 shorter events, 12.6 us)
Async XLA Ops:
  0.0 1.0 copy-start
  1.7 11.1 %all-to-all-start = ((f32[4,8,8,256]{3,2,1,0:T(8,128)}), f32[4,8,8,256]{3,2,1,0:T(8,128)S(1)}, u32[]{:S(2)}, u32[]{:S(2)}) async-start(f32[4,8,8,256]{3,2,1,0:T(8,128)} %copy_bitcast_fusion.1), calls=%async_computation | async-start | bytes 524288 | tf_op jit(solution)/shard_map/all_to_all | solution.py:360
  6.1 0.7 copy-start.5
  6.8 7.3 %copy-start.1 = (f32[8,256,256]{2,1,0:T(8,128)S(1)}, f32[8,256,256]{2,1,0:T(8,128)}, u32[]{:S(2)}) copy-start(f32[8,256,256]{2,1,0:T(8,128)} %blocks_ref.3) | copy-start | bytes 6291460
  6.8 7.3 %copy-start.6 = (f32[8,256]{1,0:T(8,128)S(1)}, f32[8,256]{1,0:T(8,128)}, u32[]{:S(2)}) copy-start(f32[8,256]{1,0:T(8,128)} %upstream_ref.3) | copy-start | bytes 24580
  12.8 8.1 %collective-permute-start = (f32[272,256]{1,0:T(8,128)S(1)}, f32[272,256]{1,0:T(8,128)S(1)}, u32[]{:S(2)}, u32[]{:S(2)}) collective-permute-start(f32[272,256]{1,0:T(8,128)S(1)} %get-tuple-element.37.refs_0_), channel_id=1, source_target_pairs={{0,1},{1,0},{2,3},{3,2},{4,5},{5,4},{6,7},{7,6},{8,9},{9,8},{10,11... | collective-permute-start | bytes 835592 | tf_op jit(solution)/shard_map/ppermute | solution.py:368
  16.1 4.8 %collective-permute-start.1 = (f32[32,256]{1,0:T(8,128)S(1)}, f32[32,256]{1,0:T(8,128)S(1)}, u32[]{:S(2)}, u32[]{:S(2)}) collective-permute-start(f32[32,256]{1,0:T(8,128)S(1)} %get-tuple-element.39.refs_1_), channel_id=1, source_target_pairs={{0,1},{1,0},{2,3},{3,2},{4,5},{5,4},{6,7},{7,6},{8,9},{9,8},{10,11... | collective-permute-start | bytes 98312 | tf_op jit(solution)/shard_map/ppermute | solution.py:368
  21.6 8.9 %collective-permute-start.2 = (f32[304,256]{1,0:T(8,128)S(1)}, f32[304,256]{1,0:T(8,128)S(1)}, u32[]{:S(2)}, u32[]{:S(2)}) collective-permute-start(f32[304,256]{1,0:T(8,128)S(1)} %shard_map.39.refs_0_), channel_id=1, source_target_pairs={{0,3},{1,2},{2,1},{3,0},{4,7},{5,6},{6,5},{7,4},{8,11},{9,10},{10,... | collective-permute-start | bytes 933896 | tf_op jit(solution)/shard_map/ppermute | solution.py:368
  31.2 1.7 %collective-permute-start.3 = (f32[304,256]{1,0:T(8,128)S(1)}, f32[304,256]{1,0:T(8,128)S(1)}, u32[]{:S(2)}, u32[]{:S(2)}) collective-permute-start(f32[304,256]{1,0:T(8,128)S(1)} %shard_map.41.refs_0_), channel_id=1, source_target_pairs={{0,4},{4,0},{8,12},{12,8},{16,20},{20,16},{24,28},{28,24},{32,36},... | collective-permute-start | bytes 933896 | tf_op jit(solution)/shard_map/ppermute | solution.py:368
  33.5 6.3 %collective-permute-start.4 = (f32[152,256]{1,0:T(8,128)S(1)}, f32[152,256]{1,0:T(8,128)S(1)}, u32[]{:S(2)}, u32[]{:S(2)}) collective-permute-start(f32[152,256]{1,0:T(8,128)S(1)} %get-tuple-element.44), channel_id=1, source_target_pairs={{0,8},{4,12},{8,0},{12,4},{16,24},{20,28},{24,16},{28,20},{32,40},... | collective-permute-start | bytes 466952 | tf_op jit(solution)/shard_map/ppermute | solution.py:368
  39.9 1.4 %collective-permute-start.5 = (f32[152,256]{1,0:T(8,128)S(1)}, f32[152,256]{1,0:T(8,128)S(1)}, u32[]{:S(2)}, u32[]{:S(2)}) collective-permute-start(f32[152,256]{1,0:T(8,128)S(1)} %collective-permute-done.4.refs_1_), channel_id=1, source_target_pairs={{0,4},{4,0},{8,12},{12,8},{16,20},{20,16},{24,28},{28,24},{32,36},... | collective-permute-start | bytes 466952 | tf_op jit(solution)/shard_map/ppermute | solution.py:368
  42.0 11.0 %collective-permute-start.6 = (f32[152,256]{1,0:T(8,128)S(1)}, f32[152,256]{1,0:T(8,128)S(1)}, u32[]{:S(2)}, u32[]{:S(2)}) collective-permute-start(f32[152,256]{1,0:T(8,128)S(1)} %get-tuple-element.49), channel_id=1, source_target_pairs={{0,16},{4,20},{8,24},{12,28},{16,0},{20,4},{24,8},{28,12},{32,48},... | collective-permute-start | bytes 466952 | tf_op jit(solution)/shard_map/ppermute | solution.py:368
  53.0 1.4 %collective-permute-start.7 = (f32[152,256]{1,0:T(8,128)S(1)}, f32[152,256]{1,0:T(8,128)S(1)}, u32[]{:S(2)}, u32[]{:S(2)}) collective-permute-start(f32[152,256]{1,0:T(8,128)S(1)} %collective-permute-done.6.refs_1_), channel_id=1, source_target_pairs={{0,4},{4,0},{8,12},{12,8},{16,20},{20,16},{24,28},{28,24},{32,36},... | collective-permute-start | bytes 466952 | tf_op jit(solution)/shard_map/ppermute | solution.py:368
  55.3 11.8 %collective-permute-start.8 = (f32[152,256]{1,0:T(8,128)S(1)}, f32[152,256]{1,0:T(8,128)S(1)}, u32[]{:S(2)}, u32[]{:S(2)}) collective-permute-start(f32[152,256]{1,0:T(8,128)S(1)} %get-tuple-element.55), channel_id=1, source_target_pairs={{0,56},{4,60},{8,48},{12,52},{16,40},{20,44},{24,32},{28,36},{32,2... | collective-permute-start | bytes 466952 | tf_op jit(solution)/shard_map/ppermute | solution.py:368
  67.0 1.4 %collective-permute-start.9 = (f32[152,256]{1,0:T(8,128)S(1)}, f32[152,256]{1,0:T(8,128)S(1)}, u32[]{:S(2)}, u32[]{:S(2)}) collective-permute-start(f32[152,256]{1,0:T(8,128)S(1)} %collective-permute-done.8.refs_1_), channel_id=1, source_target_pairs={{0,4},{4,0},{8,12},{12,8},{16,20},{20,16},{24,28},{28,24},{32,36},... | collective-permute-start | bytes 466952 | tf_op jit(solution)/shard_map/ppermute | solution.py:368
  67.1 16.4 %copy-start.2 = (f32[8,256,256]{2,1,0:T(8,128)S(1)}, f32[8,256,256]{2,1,0:T(8,128)}, u32[]{:S(2)}) copy-start(f32[8,256,256]{2,1,0:T(8,128)} %get-tuple-element.65.prefix_ref) | copy-start | bytes 6291460
  69.4 11.3 %collective-permute-start.13 = (f32[304,256]{1,0:T(8,128)S(1)}, f32[304,256]{1,0:T(8,128)S(1)}, u32[]{:S(2)}, u32[]{:S(2)}) collective-permute-start(f32[304,256]{1,0:T(8,128)S(1)} %shard_map.51.map_ref), channel_id=1, source_target_pairs={{128,192},{132,196},{136,200},{140,204},{144,208},{148,212},{152,2... | collective-permute-start | bytes 933896 | tf_op jit(solution)/shard_map/ppermute | solution.py:401
  70.7 0.7 collective-permute-start.10
  71.4 0.9 copy-start.3
  72.2 9.8 %collective-permute-start.11 = (f32[32,256]{1,0:T(8,128)}, f32[32,256]{1,0:T(8,128)}, u32[]{:S(2)}, u32[]{:S(2)}) collective-permute-start(f32[32,256]{1,0:T(8,128)} %shard_map.52), channel_id=1, source_target_pairs={{64,128},{68,132},{72,136},{76,140},{80,144},{84,148},{88,152},{92... | collective-permute-start | bytes 98312 | tf_op jit(solution)/shard_map/ppermute | solution.py:401
  73.5 10.0 %collective-permute-start.12 = (f32[32,256]{1,0:T(8,128)}, f32[32,256]{1,0:T(8,128)}, u32[]{:S(2)}, u32[]{:S(2)}) collective-permute-start(f32[32,256]{1,0:T(8,128)} %shard_map.52), channel_id=1, source_target_pairs={{64,192},{68,196},{72,200},{76,204},{80,208},{84,212},{88,216},{92... | collective-permute-start | bytes 98312 | tf_op jit(solution)/shard_map/ppermute | solution.py:401
  80.7 0.8 copy-start.4

commit v6 on v5

--- a/solution.py
+++ b/solution.py
@@ -20,15 +20,26 @@
     ("span", 1, 1, False, True),
     ("span", 3, 2, False, False),
     ("line", 1, 1, False, False),
-    ("line", 2, 2, True, False),
-    ("line", 4, 4, True, False),
     ("line", 14, 8, True, False),
 )
+FOUR = (2, 4)
+THIRD = 6
 PLANE = 16
 
 
 def dot(a, b):
     return jnp.dot(a, b, precision=lax.Precision.HIGHEST, preferred_element_type=F32)
+
+
+def split(a):
+    high = a.astype(jnp.bfloat16)
+    return high, (a - high.astype(F32)).astype(jnp.bfloat16)
+
+
+def dot3(a, b):
+    product = functools.partial(jnp.dot, preferred_element_type=F32)
+    (a_high, a_low), (b_high, b_low) = split(a), split(b)
+    return product(a_high, b_high) + (product(a_high, b_low) + product(a_low, b_high))
 
 
 def shape(*dims):
@@ -95,9 +106,15 @@
     fetch(blocks_ref, held_ref, arrived)
     row = lax.broadcasted_iota(jnp.int32, (levels, levels), 0)
     column = lax.broadcasted_iota(jnp.int32, (levels, levels), 1)
-    last_ref[...] = jnp.where(row == column, 1.0, 0.0).astype(F32)
-
-    @pl.loop(0, cells)
+    first = jnp.where(row == column, -upstream_ref[0:1, :], 0.0)
+    first = jnp.sum(first, axis=1, keepdims=True)
+    block_copy(blocks_ref, held_ref, arrived, 0).wait()
+    first = first * held_ref[0]
+    last_ref[...] = first
+    made_ref[0] = first
+    block_copy(made_ref, prefix_ref, left, 0).start()
+
+    @pl.loop(1, cells)
     def _(cell):
         scaled = last_ref[...] * -upstream_ref[pl.ds(cell, 1), :]
         block_copy(blocks_ref, held_ref, arrived, cell).wait()
@@ -255,6 +272,43 @@
     return got[0], got[1] if halves else theirs[0], got[-1]
 
 
+def join(left_ref, right_ref, out_ref):
+    start = out_ref.shape[1] + PAD
+    join_maps(left_ref, right_ref, out_ref)
+    out_ref[start:] = move_states(left_ref[start:], right_ref) + right_ref[start:]
+
+
+def four_kernel(
+    code_ref, mine_ref, here_ref, there_ref, this_ref, that_ref,
+    total_ref, beside_ref, front_ref, half_ref, four_ref, back_ref,
+):
+    core = lax.rem(code_ref[0], 2)
+    place = code_ref[0] // 2
+    rows = half_ref.shape[0]
+    four_ref[place] = mine_ref[...]
+    four_ref[place ^ (1 + core)] = here_ref[...]
+    four_ref[place ^ (2 - core)] = there_ref[...]
+    four_ref[place ^ 3, pl.ds(core * rows, rows)] = this_ref[...]
+    four_ref[place ^ 3, pl.ds((1 - core) * rows, rows)] = that_ref[...]
+    join(four_ref.at[0], four_ref.at[1], front_ref)
+    join(four_ref.at[2], four_ref.at[3], back_ref)
+    join(front_ref, back_ref, total_ref)
+    half_ref[...] = total_ref[pl.ds(core * rows, rows)]
+    beside_ref[...] = four_ref[place ^ 1]
+
+
+def join_four(code, mine, here, there, this, that):
+    rows, levels = mine.shape
+    whole = shape(rows, levels)
+    return call(
+        four_kernel,
+        [SMEM] + [VMEM] * 5,
+        [whole, whole, whole, shape(rows // 2, levels)],
+        36 * rows * levels**2,
+        [pltpu.VMEM((4, rows, levels), F32), pltpu.VMEM((rows, levels), F32)],
+    )(code, mine, here, there, this, that)
+
+
 def extend_kernel(first, apart, code_ref, *refs):
     refs = list(refs)
     their_map = refs.pop(0)
@@ -331,24 +385,34 @@
     )(code, beside, from_first, before)
 
 
-def finish_kernel(one_ref, two_ref, before_ref, prefix_ref, trial_ref, solved_ref, incoming):
+def finish_kernel(
+    one_ref, two_ref, before_ref, prefix_ref, trial_ref, solved_ref, held_ref, incoming, arrived
+):
+    fetch(prefix_ref, held_ref, arrived)
     start = before_ref.shape[1] + PAD
     entering = one_ref[...] + two_ref[...]
     incoming[...] = move_states(entering, before_ref) + before_ref[start:]
 
-    @pl.loop(0, prefix_ref.shape[0])
+    @pl.loop(0, held_ref.shape[0])
     def _(cell):
-        solved_ref[:, cell, :] = trial_ref[cell] + dot(incoming[...], prefix_ref[cell])
+        block_copy(prefix_ref, held_ref, arrived, cell).wait()
+        solved_ref[:, cell, :] = trial_ref[cell] + dot3(incoming[...], held_ref[cell])
 
 
 def finish(entering, before, prefix, trial):
     cells, lines, levels = trial.shape
     return call(
         finish_kernel,
-        [VMEM] * 5,
+        [VMEM, VMEM, VMEM, HBM, VMEM],
         shape(lines, cells, levels),
         12 * (cells + 1) * lines * levels**2,
-        [pltpu.VMEM((lines, levels), F32)],
+        [
+            pltpu.VMEM(prefix.shape, F32),
+            pltpu.VMEM((lines, levels), F32),
+            pltpu.SemaphoreType.DMA((cells,)),
+        ],
+        None,
+        LARGE,
     )(*entering, before, prefix, trial)
 
 
@@ -372,18 +436,30 @@
         core = jnp.where((lax.axis_index("line") & CORE) != 0, 2, 0)
         return (upper + core).astype(jnp.int32).reshape(1)
 
+    def along_four(total, half, before):
+        device = lax.axis_index("line")
+        pairs = [(i, i ^ FOUR[i & CORE]) for i in range(lax.axis_size("line"))]
+        here, this = lax.ppermute(total, "line", pairs), partner(half, "line", THIRD)
+        here, this, before = lax.optimization_barrier((here, this, before))
+        there, that = partner(here, "line", CORE), partner(this, "line", CORE)
+        code = (device & (CORE | THIRD)).astype(jnp.int32).reshape(1)
+        total, beside, front, half = join_four(code, total, here, there, this, that)
+        before = extend(code_of("line", FOUR[0]), (beside,), before)
+        before = extend(code_of("line", FOUR[1]), (front,), before)
+        return total, half, before
+
     total, half, before = None, None, None
     for turn, (axis, mask, bit, halves, apart) in enumerate(ROUNDS):
         code = code_of(axis, bit)
         last = turn == len(ROUNDS) - 1
-        next_halves = not last and ROUNDS[turn + 1][3]
         if halves:
             here = partner(half, axis, mask)
+            here, before = lax.optimization_barrier((here, before))
             theirs = (here, partner(here, "line", CORE))
         else:
             theirs = (partner(maps if apart else total, axis, mask),)
-        if before is not None:
-            theirs, before = lax.optimization_barrier((theirs, before))
+            if before is not None:
+                theirs, before = lax.optimization_barrier((theirs, before))
         mine = (total,)
         if apart:
             their_states = partner(states, axis, mask)
@@ -392,8 +468,11 @@
             plane, whole, _ = merge(code, mine, theirs, "states", lines, apart, halves, False)
             total, _, _ = merge(code, mine, (whole,), "both", lines, False, False, False)
         else:
-            total, whole, half = merge(code, mine, theirs, "both", lines, apart, halves, next_halves)
+            half_too = turn == len(ROUNDS) - 2
+            total, whole, half = merge(code, mine, theirs, "both", lines, apart, halves, half_too)
         before = extend(code, (whole, their_states) if apart else (whole,), before)
+        if turn == len(ROUNDS) - 2:
+            total, half, before = along_four(total, half, before)
 
     def across(value, source, target):
         shift = (target - source) * PLANE
@@ -404,7 +483,8 @@
     beside = across(total, 2, 3)
     from_first, before = lax.optimization_barrier((from_first, before))
     joined = enter(from_first, total, plane)
-    entering = (across(joined, 1, 2), across(joined, 1, 3))
+    two_on = across(joined, 1, 3)
+    entering = (two_on, across(joined, 1, 2))
     in_last = jnp.where(lax.axis_index("line") >= 3 * PLANE, 1, 0).astype(jnp.int32).reshape(1)
     before = settle_planes(in_last, beside, from_first, before)
     solved = finish(entering, before, prefix, trial)

time: 98.3 us -> 94.4 us (0.960)
  waiting for transfers between devices: 42.1 us -> 40.7 us
    ppermute x10 -> x9, starting transfers between devices: 15.8 us -> 13.6 us  [partner(): return lax.ppermute(value, axis, [(i, i ^ mask) for i in range(count)])]
    ppermute x0 -> x1, starting transfers between devices: none -> 2.01 us  [along_four(): lax.ppermute(total, 'line', pairs)]
    pallas_call x1 -> x2, Pallas kernels: 2.89 us -> 4.55 us  [the longest x1 2.7 us: finish(): call(finish_kernel, [VMEM, VMEM, VMEM, HBM, VMEM], shape(lines, cells, le...]
    pallas_call x7 -> x5, Pallas kernels: 4.53 us -> 2.93 us  [merge(): call(functools.partial(merge_kernel, start, kind, apart, halves, half), [...]
    ppermute x10 -> x9, waiting for transfers between devices: 34 us -> 32.5 us  [partner(): return lax.ppermute(value, axis, [(i, i ^ mask) for i in range(count)])]
    unnamed x14 -> x8, local copies, waits for them, and re-layouts: 2.42 us -> 1.65 us
  transfers between devices with their start and end apart: 15 -> 15, of which waited for: 12 -> 9; matrix products, arithmetic and copies ran while one was open for 0% -> 0% of each run, Pallas kernels for 9% -> 8%
where the time goes in v6:
time: 94.4 us; the launch traced here: 94.1 us
  waiting for transfers between devices  40.7 us (43%)
  starting transfers between devices  24 us (25%)
  Pallas kernels  15.3 us (16%)
  blocking collectives  10.7 us (11%)
  local copies, waits for them, and re-layouts  3.1 us (3%)
    ppermute x9, waiting for transfers between devices, partner(): return lax.ppermute(value, axis, [(i, i ^ mask) for i in range(count)])  32.5 us
    ppermute x9, starting transfers between devices, partner(): return lax.ppermute(value, axis, [(i, i ^ mask) for i in range(count)])  13.6 us
    all_to_all x1, blocking collectives, shards(): lax.all_to_all(parts, 'span', split_axis=0, concat_axis=0, tiled=True)  10.7 us
    ppermute x4, waiting for transfers between devices, across(): return lax.ppermute(value, 'line', pairs)  7.07 us
    pallas_call x1, Pallas kernels, prefix_maps(): call(maps_kernel, [VMEM, HBM], [shape(*blocks.shape), shape(levels + PAD,...  4.83 us
    all_to_all x1, starting transfers between devices, shards(): lax.all_to_all(parts, 'span', split_axis=0, concat_axis=0, tiled=True)  4.46 us
    ppermute x4, starting transfers between devices, across(): return lax.ppermute(value, 'line', pairs)  3.91 us
    pallas_call x5, Pallas kernels, merge(): call(functools.partial(merge_kernel, start, kind, apart, halves, half), [...  2.93 us
  transfers between devices with their start and end apart: 15, of which 9 were waited for; matrix products, arithmetic and copies ran while one was open for 0% of the time, Pallas kernels for 8%

profile of v6, /device:TPU:6, one launch (start us, length us, event | category | flops | bytes accessed | tf_op | source)
XLA Modules:
  0.0 94.1 jit_solution(244139801007648291)
XLA Ops:
  0.0 0.9 %copy-done = f32[8,32,256]{2,1,0:T(8,128)S(1)} copy-done((f32[8,32,256]{2,1,0:T(8,128)S(1)}, f32[8,32,256]{2,1,0:T(8,128)}, u32[]{:S(2)}) %copy-start) | copy-done | bytes 262168
  1.7 4.5 %all-to-all-start = ((f32[4,8,8,256]{3,2,1,0:T(8,128)}), f32[4,8,8,256]{3,2,1,0:T(8,128)S(1)}, u32[]{:S(2)}, u32[]{:S(2)}) async-start(f32[4,8,8,256]{3,2,1,0:T(8,128)} %copy_bitcast_fusion.1), calls=%async_computation | async-start | bytes 524288 | tf_op jit(solution)/shard_map/all_to_all | solution.py:424
  6.8 4.8 %shard_map.37 = (f32[8,256,256]{2,1,0:T(8,128)}, f32[272,256]{1,0:T(8,128)S(1)}) custom-call(f32[8,256]{1,0:T(8,128)S(1)} %copy-done.2, f32[8,256,256]{2,1,0:T(8,128)} %blocks_ref.3), custom_call_target="tpu_custom_call" | custom-call | flops 1610612736 | bytes 1048576 | tf_op jit(solution)/shard_map/pallas_call | solution.py:135
  11.7 1.1 %all-to-all-done = f32[4,8,8,256]{3,2,1,0:T(8,128)S(1)} async-done(((f32[4,8,8,256]{3,2,1,0:T(8,128)}), f32[4,8,8,256]{3,2,1,0:T(8,128)S(1)}, u32[]{:S(2)}, u32[]{:S(2)}) %all-to-all-start) | async-done | bytes 262176 | tf_op jit(solution)/shard_map/all_to_all | solution.py:424
  12.8 1.0 %collective-permute-start = (f32[272,256]{1,0:T(8,128)S(1)}, f32[272,256]{1,0:T(8,128)S(1)}, u32[]{:S(2)}, u32[]{:S(2)}) collective-permute-start(f32[272,256]{1,0:T(8,128)S(1)} %get-tuple-element.31.refs_0_), channel_id=1, source_target_pairs={{0,1},{1,0},{2,3},{3,2},{4,5},{5,4},{6,7},{7,6},{8,9},{9,8},{10,11... | collective-permute-start | bytes 835592 | tf_op jit(solution)/shard_map/ppermute | solution.py:432
  13.8 1.9 %shard_map.38 = (f32[8,32,256]{2,1,0:T(8,128)S(1)}, f32[32,256]{1,0:T(8,128)S(1)}) custom-call(f32[8,256]{1,0:T(8,128)S(1)} %copy-done.3, f32[8,256,256]{2,1,0:T(8,128)S(1)} %copy-done.1, f32[32,8,256]{2,1,0:T(8,128)S(1)} %bitcast.20), custom_call_target="tpu_custom_call" | custom-call | flops 201326592 | bytes 1048576 | tf_op jit(solution)/shard_map/pallas_call | solution.py:166
  15.8 1.1 %collective-permute-start.1 = (f32[32,256]{1,0:T(8,128)S(1)}, f32[32,256]{1,0:T(8,128)S(1)}, u32[]{:S(2)}, u32[]{:S(2)}) collective-permute-start(f32[32,256]{1,0:T(8,128)S(1)} %get-tuple-element.33.refs_1_), channel_id=1, source_target_pairs={{0,1},{1,0},{2,3},{3,2},{4,5},{5,4},{6,7},{7,6},{8,9},{9,8},{10,11... | collective-permute-start | bytes 98312 | tf_op jit(solution)/shard_map/ppermute | solution.py:432
  16.9 3.7 %collective-permute-done.1.refs_3_.refs_1_ = f32[32,256]{1,0:T(8,128)S(1)} collective-permute-done((f32[32,256]{1,0:T(8,128)S(1)}, f32[32,256]{1,0:T(8,128)S(1)}, u32[]{:S(2)}, u32[]{:S(2)}) %collective-permute-start.1) | collective-permute-done | bytes 32800 | tf_op jit(solution)/shard_map/ppermute | solution.py:432
  21.3 3.0 %collective-permute-start.2 = (f32[304,256]{1,0:T(8,128)S(1)}, f32[304,256]{1,0:T(8,128)S(1)}, u32[]{:S(2)}, u32[]{:S(2)}) collective-permute-start(f32[304,256]{1,0:T(8,128)S(1)} %shard_map.39.refs_0_), channel_id=1, source_target_pairs={{0,3},{1,2},{2,1},{3,0},{4,7},{5,6},{6,5},{7,4},{8,11},{9,10},{10,... | collective-permute-start | bytes 933896 | tf_op jit(solution)/shard_map/ppermute | solution.py:432
  24.3 5.8 %collective-permute-done.2.refs_1_.refs_0_ = f32[304,256]{1,0:T(8,128)S(1)} collective-permute-done((f32[304,256]{1,0:T(8,128)S(1)}, f32[304,256]{1,0:T(8,128)S(1)}, u32[]{:S(2)}, u32[]{:S(2)}) %collective-permute-start.2) | collective-permute-done | bytes 311328 | tf_op jit(solution)/shard_map/ppermute | solution.py:432
  31.0 1.5 %collective-permute-done.3.refs_1_.refs_0_ = f32[304,256]{1,0:T(8,128)S(1)} collective-permute-done((f32[304,256]{1,0:T(8,128)S(1)}, f32[304,256]{1,0:T(8,128)S(1)}, u32[]{:S(2)}, u32[]{:S(2)}) %collective-permute-start.3) | collective-permute-done | bytes 311328 | tf_op jit(solution)/shard_map/ppermute | solution.py:432
  33.2 2.0 %collective-permute-start.4 = (f32[304,256]{1,0:T(8,128)S(1)}, f32[304,256]{1,0:T(8,128)S(1)}, u32[]{:S(2)}, u32[]{:S(2)}) collective-permute-start(f32[304,256]{1,0:T(8,128)S(1)} %get-tuple-element.37.mine_ref), channel_id=1, source_target_pairs={{0,8},{4,20},{8,0},{12,28},{16,24},{20,4},{24,16},{28,12},{32,40},... | collective-permute-start | bytes 933896 | tf_op jit(solution)/shard_map/ppermute | solution.py:442
  35.2 2.8 %collective-permute-start.5 = (f32[152,256]{1,0:T(8,128)S(1)}, f32[152,256]{1,0:T(8,128)S(1)}, u32[]{:S(2)}, u32[]{:S(2)}) collective-permute-start(f32[152,256]{1,0:T(8,128)S(1)} %get-tuple-element.38), channel_id=1, source_target_pairs={{0,24},{4,28},{8,16},{12,20},{16,8},{20,12},{24,0},{28,4},{32,56},... | collective-permute-start | bytes 466952 | tf_op jit(solution)/shard_map/ppermute | solution.py:432
  38.1 10.9 %collective-permute-done.5.this_ref = f32[152,256]{1,0:T(8,128)S(1)} collective-permute-done((f32[152,256]{1,0:T(8,128)S(1)}, f32[152,256]{1,0:T(8,128)S(1)}, u32[]{:S(2)}, u32[]{:S(2)}) %collective-permute-start.5) | collective-permute-done | bytes 155680 | tf_op jit(solution)/shard_map/ppermute | solution.py:432
  49.5 1.3 %collective-permute-done.7.that_ref = f32[152,256]{1,0:T(8,128)S(1)} collective-permute-done((f32[152,256]{1,0:T(8,128)S(1)}, f32[152,256]{1,0:T(8,128)S(1)}, u32[]{:S(2)}, u32[]{:S(2)}) %collective-permute-start.7) | collective-permute-done | bytes 155680 | tf_op jit(solution)/shard_map/ppermute | solution.py:432
  50.8 1.9 %shard_map.45 = (f32[304,256]{1,0:T(8,128)S(1)}, f32[304,256]{1,0:T(8,128)S(1)}, f32[304,256]{1,0:T(8,128)S(1)}, f32[152,256]{1,0:T(8,128)S(1)}) custom-call(s32[1]{0:T(128)} %bitcast.1.code_ref, f32[304,256]{1,0:T(8,128)S(1)} %get-tuple-element.37.mine_ref, f32[304,256]{1,0:T(8,128)S(1)} %collective-permute-done.4.here_ref, ...), custom_call_target="tpu_custom_call" | custom-call | flops 717225984 | bytes 1048576 | tf_op jit(solution)/shard_map/pallas_call | solution.py:303
  52.7 5.1 %collective-permute-start.8 = (f32[152,256]{1,0:T(8,128)S(1)}, f32[152,256]{1,0:T(8,128)S(1)}, u32[]{:S(2)}, u32[]{:S(2)}) collective-permute-start(f32[152,256]{1,0:T(8,128)S(1)} %get-tuple-element.43), channel_id=1, source_target_pairs={{0,56},{4,60},{8,48},{12,52},{16,40},{20,44},{24,32},{28,36},{32,2... | collective-permute-start | bytes 466952 | tf_op jit(solution)/shard_map/ppermute | solution.py:432
  57.8 7.8 %collective-permute-done.8.refs_1_ = f32[152,256]{1,0:T(8,128)S(1)} collective-permute-done((f32[152,256]{1,0:T(8,128)S(1)}, f32[152,256]{1,0:T(8,128)S(1)}, u32[]{:S(2)}, u32[]{:S(2)}) %collective-permute-start.8) | collective-permute-done | bytes 155680 | tf_op jit(solution)/shard_map/ppermute | solution.py:432
  65.6 1.4 %collective-permute-done.9.refs_2_ = f32[152,256]{1,0:T(8,128)S(1)} collective-permute-done((f32[152,256]{1,0:T(8,128)S(1)}, f32[152,256]{1,0:T(8,128)S(1)}, u32[]{:S(2)}, u32[]{:S(2)}) %collective-permute-start.9) | collective-permute-done | bytes 155680 | tf_op jit(solution)/shard_map/ppermute | solution.py:432
  67.9 1.3 %collective-permute-start.13 = (f32[304,256]{1,0:T(8,128)S(1)}, f32[304,256]{1,0:T(8,128)S(1)}, u32[]{:S(2)}, u32[]{:S(2)}) collective-permute-start(f32[304,256]{1,0:T(8,128)S(1)} %shard_map.50.map_ref), channel_id=1, source_target_pairs={{128,192},{132,196},{136,200},{140,204},{144,208},{148,212},{152,2... | collective-permute-start | bytes 933896 | tf_op jit(solution)/shard_map/ppermute | solution.py:480
  70.2 1.3 %collective-permute-start.11 = (f32[32,256]{1,0:T(8,128)S(1)}, f32[32,256]{1,0:T(8,128)S(1)}, u32[]{:S(2)}, u32[]{:S(2)}) collective-permute-start(f32[32,256]{1,0:T(8,128)S(1)} %shard_map.51), channel_id=1, source_target_pairs={{64,192},{68,196},{72,200},{76,204},{80,208},{84,212},{88,216},{92... | collective-permute-start | bytes 98312 | tf_op jit(solution)/shard_map/ppermute | solution.py:480
  72.2 7.1 %collective-permute-done.13.beside_ref = f32[304,256]{1,0:T(8,128)S(1)} collective-permute-done((f32[304,256]{1,0:T(8,128)S(1)}, f32[304,256]{1,0:T(8,128)S(1)}, u32[]{:S(2)}, u32[]{:S(2)}) %collective-permute-start.13) | collective-permute-done | bytes 311328 | tf_op jit(solution)/shard_map/ppermute | solution.py:480
  79.9 2.7 %shard_map.53 = f32[32,8,256]{2,1,0:T(8,128)S(1)} custom-call(f32[32,256]{1,0:T(8,128)S(1)} %collective-permute-done.11.one_ref, f32[32,256]{1,0:T(8,128)S(1)} %collective-permute-done.12.two_ref, f32[304,256]{1,0:T(8,128)S(1)} %shard_map.52.before_ref, f32[8,256,256]{2,1,0:T(8,128)} %get-tuple-element.53.prefix_ref, ...), custom_call_target="tpu_custom_call" | custom-call | flops 226492416 | bytes 1048576 | tf_op jit(solution)/shard_map/pallas_call | solution.py:404
  82.6 10.7 %all_to_all.10 = f32[4,8,8,256]{3,2,1,0:T(8,128)S(1)} all-to-all(f32[4,8,8,256]{3,2,1,0:T(8,128)S(1)} %bitcast.21), channel_id=1, replica_groups=mesh['line'=64,'span'=4] {'span'}, dimensions={0} | all-to-all | bytes 524288 | tf_op jit(solution)/shard_map/all_to_all | solution.py:492
  (34 shorter events, 8.1 us)
Async XLA Ops:
  0.0 1.0 %copy-start = (f32[8,32,256]{2,1,0:T(8,128)S(1)}, f32[8,32,256]{2,1,0:T(8,128)}, u32[]{:S(2)}) copy-start(f32[8,32,256]{2,1,0:T(8,128)} %param.3) | copy-start | bytes 786436
  1.7 11.1 %all-to-all-start = ((f32[4,8,8,256]{3,2,1,0:T(8,128)}), f32[4,8,8,256]{3,2,1,0:T(8,128)S(1)}, u32[]{:S(2)}, u32[]{:S(2)}) async-start(f32[4,8,8,256]{3,2,1,0:T(8,128)} %copy_bitcast_fusion.1), calls=%async_computation | async-start | bytes 524288 | tf_op jit(solution)/shard_map/all_to_all | solution.py:424
  6.1 0.7 copy-start.2
  6.8 7.0 %copy-start.1 = (f32[8,256,256]{2,1,0:T(8,128)S(1)}, f32[8,256,256]{2,1,0:T(8,128)}, u32[]{:S(2)}) copy-start(f32[8,256,256]{2,1,0:T(8,128)} %blocks_ref.3) | copy-start | bytes 6291460
  6.8 7.0 %copy-start.3 = (f32[8,256]{1,0:T(8,128)S(1)}, f32[8,256]{1,0:T(8,128)}, u32[]{:S(2)}) copy-start(f32[8,256]{1,0:T(8,128)} %upstream_ref.3) | copy-start | bytes 24580
  12.8 7.8 %collective-permute-start = (f32[272,256]{1,0:T(8,128)S(1)}, f32[272,256]{1,0:T(8,128)S(1)}, u32[]{:S(2)}, u32[]{:S(2)}) collective-permute-start(f32[272,256]{1,0:T(8,128)S(1)} %get-tuple-element.31.refs_0_), channel_id=1, source_target_pairs={{0,1},{1,0},{2,3},{3,2},{4,5},{5,4},{6,7},{7,6},{8,9},{9,8},{10,11... | collective-permute-start | bytes 835592 | tf_op jit(solution)/shard_map/ppermute | solution.py:432
  15.8 4.8 %collective-permute-start.1 = (f32[32,256]{1,0:T(8,128)S(1)}, f32[32,256]{1,0:T(8,128)S(1)}, u32[]{:S(2)}, u32[]{:S(2)}) collective-permute-start(f32[32,256]{1,0:T(8,128)S(1)} %get-tuple-element.33.refs_1_), channel_id=1, source_target_pairs={{0,1},{1,0},{2,3},{3,2},{4,5},{5,4},{6,7},{7,6},{8,9},{9,8},{10,11... | collective-permute-start | bytes 98312 | tf_op jit(solution)/shard_map/ppermute | solution.py:432
  21.3 8.9 %collective-permute-start.2 = (f32[304,256]{1,0:T(8,128)S(1)}, f32[304,256]{1,0:T(8,128)S(1)}, u32[]{:S(2)}, u32[]{:S(2)}) collective-permute-start(f32[304,256]{1,0:T(8,128)S(1)} %shard_map.39.refs_0_), channel_id=1, source_target_pairs={{0,3},{1,2},{2,1},{3,0},{4,7},{5,6},{6,5},{7,4},{8,11},{9,10},{10,... | collective-permute-start | bytes 933896 | tf_op jit(solution)/shard_map/ppermute | solution.py:432
  30.9 1.7 %collective-permute-start.3 = (f32[304,256]{1,0:T(8,128)S(1)}, f32[304,256]{1,0:T(8,128)S(1)}, u32[]{:S(2)}, u32[]{:S(2)}) collective-permute-start(f32[304,256]{1,0:T(8,128)S(1)} %shard_map.41.refs_0_), channel_id=1, source_target_pairs={{0,4},{4,0},{8,12},{12,8},{16,20},{20,16},{24,28},{28,24},{32,36},... | collective-permute-start | bytes 933896 | tf_op jit(solution)/shard_map/ppermute | solution.py:432
  33.2 15.7 %collective-permute-start.4 = (f32[304,256]{1,0:T(8,128)S(1)}, f32[304,256]{1,0:T(8,128)S(1)}, u32[]{:S(2)}, u32[]{:S(2)}) collective-permute-start(f32[304,256]{1,0:T(8,128)S(1)} %get-tuple-element.37.mine_ref), channel_id=1, source_target_pairs={{0,8},{4,20},{8,0},{12,28},{16,24},{20,4},{24,16},{28,12},{32,40},... | collective-permute-start | bytes 933896 | tf_op jit(solution)/shard_map/ppermute | solution.py:442
  35.2 13.7 %collective-permute-start.5 = (f32[152,256]{1,0:T(8,128)S(1)}, f32[152,256]{1,0:T(8,128)S(1)}, u32[]{:S(2)}, u32[]{:S(2)}) collective-permute-start(f32[152,256]{1,0:T(8,128)S(1)} %get-tuple-element.38), channel_id=1, source_target_pairs={{0,24},{4,28},{8,16},{12,20},{16,8},{20,12},{24,0},{28,4},{32,56},... | collective-permute-start | bytes 466952 | tf_op jit(solution)/shard_map/ppermute | solution.py:432
  49.0 1.8 %collective-permute-start.6 = (f32[304,256]{1,0:T(8,128)S(1)}, f32[304,256]{1,0:T(8,128)S(1)}, u32[]{:S(2)}, u32[]{:S(2)}) collective-permute-start(f32[304,256]{1,0:T(8,128)S(1)} %collective-permute-done.4.here_ref), channel_id=1, source_target_pairs={{0,4},{4,0},{8,12},{12,8},{16,20},{20,16},{24,28},{28,24},{32,36},... | collective-permute-start | bytes 933896 | tf_op jit(solution)/shard_map/ppermute | solution.py:432
  49.1 1.7 %collective-permute-start.7 = (f32[152,256]{1,0:T(8,128)S(1)}, f32[152,256]{1,0:T(8,128)S(1)}, u32[]{:S(2)}, u32[]{:S(2)}) collective-permute-start(f32[152,256]{1,0:T(8,128)S(1)} %collective-permute-done.5.this_ref), channel_id=1, source_target_pairs={{0,4},{4,0},{8,12},{12,8},{16,20},{20,16},{24,28},{28,24},{32,36},... | collective-permute-start | bytes 466952 | tf_op jit(solution)/shard_map/ppermute | solution.py:432
  52.7 13.0 %collective-permute-start.8 = (f32[152,256]{1,0:T(8,128)S(1)}, f32[152,256]{1,0:T(8,128)S(1)}, u32[]{:S(2)}, u32[]{:S(2)}) collective-permute-start(f32[152,256]{1,0:T(8,128)S(1)} %get-tuple-element.43), channel_id=1, source_target_pairs={{0,56},{4,60},{8,48},{12,52},{16,40},{20,44},{24,32},{28,36},{32,2... | collective-permute-start | bytes 466952 | tf_op jit(solution)/shard_map/ppermute | solution.py:432
  65.6 1.4 %collective-permute-start.9 = (f32[152,256]{1,0:T(8,128)S(1)}, f32[152,256]{1,0:T(8,128)S(1)}, u32[]{:S(2)}, u32[]{:S(2)}) collective-permute-start(f32[152,256]{1,0:T(8,128)S(1)} %collective-permute-done.8.refs_1_), channel_id=1, source_target_pairs={{0,4},{4,0},{8,12},{12,8},{16,20},{20,16},{24,28},{28,24},{32,36},... | collective-permute-start | bytes 466952 | tf_op jit(solution)/shard_map/ppermute | solution.py:432
  67.9 11.3 %collective-permute-start.13 = (f32[304,256]{1,0:T(8,128)S(1)}, f32[304,256]{1,0:T(8,128)S(1)}, u32[]{:S(2)}, u32[]{:S(2)}) collective-permute-start(f32[304,256]{1,0:T(8,128)S(1)} %shard_map.50.map_ref), channel_id=1, source_target_pairs={{128,192},{132,196},{136,200},{140,204},{144,208},{148,212},{152,2... | collective-permute-start | bytes 933896 | tf_op jit(solution)/shard_map/ppermute | solution.py:480
  69.2 0.7 collective-permute-start.10
  70.2 9.7 %collective-permute-start.11 = (f32[32,256]{1,0:T(8,128)S(1)}, f32[32,256]{1,0:T(8,128)S(1)}, u32[]{:S(2)}, u32[]{:S(2)}) collective-permute-start(f32[32,256]{1,0:T(8,128)S(1)} %shard_map.51), channel_id=1, source_target_pairs={{64,192},{68,196},{72,200},{76,204},{80,208},{84,212},{88,216},{92... | collective-permute-start | bytes 98312 | tf_op jit(solution)/shard_map/ppermute | solution.py:480
  71.5 8.4 %collective-permute-start.12 = (f32[32,256]{1,0:T(8,128)S(1)}, f32[32,256]{1,0:T(8,128)S(1)}, u32[]{:S(2)}, u32[]{:S(2)}) collective-permute-start(f32[32,256]{1,0:T(8,128)S(1)} %shard_map.51), channel_id=1, source_target_pairs={{64,128},{68,132},{72,136},{76,140},{80,144},{84,148},{88,152},{92... | collective-permute-start | bytes 98312 | tf_op jit(solution)/shard_map/ppermute | solution.py:480

commit v7 on v6

--- a/solution.py
+++ b/solution.py
@@ -20,7 +20,7 @@
     ("span", 1, 1, False, True),
     ("span", 3, 2, False, False),
     ("line", 1, 1, False, False),
-    ("line", 14, 8, True, False),
+    ("line", 12, 8, True, False),
 )
 FOUR = (2, 4)
 THIRD = 6
@@ -353,23 +353,67 @@
     )(code, *operands)
 
 
-def enter_kernel(from_ref, map_ref, own_ref, out_ref):
-    out_ref[...] = move_states(from_ref[...], map_ref) + own_ref[...]
-
-
-def enter(states, total, own):
-    lines, levels = own.shape
-    return call(enter_kernel, [VMEM] * 3, shape(lines, levels), 12 * lines * levels**2)(
-        states, total, own
+def enter_kernel(code_ref, from_ref, mine_ref, theirs_ref, out_ref):
+    start = mine_ref.shape[1] + PAD
+
+    def through(first_ref, second_ref):
+        middle = move_states(from_ref[...], first_ref) + first_ref[start:]
+        out_ref[...] = move_states(middle, second_ref) + second_ref[start:]
+
+    later(
+        code_ref,
+        lambda: through(theirs_ref, mine_ref),
+        lambda: through(mine_ref, theirs_ref),
     )
 
 
-def settle_planes_kernel(code_ref, beside_ref, from_ref, before_ref, ahead_ref):
+def enter(code, states, mine, theirs):
+    lines, levels = states.shape
+    return call(
+        enter_kernel, [SMEM] + [VMEM] * 3, shape(lines, levels), 24 * lines * levels**2
+    )(code, states, mine, theirs)
+
+
+def plane_half_kernel(code_ref, mine_ref, theirs_ref, half_ref, total_ref):
+    rows = half_ref.shape[0]
+    core = lax.rem(code_ref[0] // 2, 2)
+
+    @pl.when(code_ref[0] < 4)
+    def _():
+        half_ref[...] = jnp.zeros_like(half_ref)
+
+    @pl.when(code_ref[0] >= 4)
+    def _():
+        later(
+            code_ref,
+            lambda: join(theirs_ref, mine_ref, total_ref),
+            lambda: join(mine_ref, theirs_ref, total_ref),
+        )
+        half_ref[...] = total_ref[pl.ds(core * rows, rows)]
+
+
+def plane_half(code, mine, theirs):
+    rows, levels = mine.shape
+    return call(
+        plane_half_kernel,
+        [SMEM, VMEM, VMEM],
+        shape(rows // 2, levels),
+        12 * rows * levels**2,
+        [pltpu.VMEM((rows, levels), F32)],
+    )(code, mine, theirs)
+
+
+def settle_planes_kernel(
+    code_ref, here_ref, there_ref, from_ref, before_ref, ahead_ref, beside_ref
+):
     start = before_ref.shape[1] + PAD
+    rows = here_ref.shape[0]
+    core = code_ref[0] // 2
 
     def then():
-        join_maps(beside_ref, before_ref, ahead_ref)
-        ahead_ref[start:] = move_states(beside_ref[start:], before_ref) + before_ref[start:]
+        beside_ref[pl.ds(core * rows, rows)] = here_ref[...]
+        beside_ref[pl.ds((1 - core) * rows, rows)] = there_ref[...]
+        join(beside_ref, before_ref, ahead_ref)
 
     def otherwise():
         ahead_ref[:start] = before_ref[:start]
@@ -378,11 +422,15 @@
     later(code_ref, then, otherwise)
 
 
-def settle_planes(code, beside, from_first, before):
+def settle_planes(code, here, there, from_first, before):
     rows, levels = before.shape
     return call(
-        settle_planes_kernel, [SMEM] + [VMEM] * 3, shape(rows, levels), 12 * rows * levels**2
-    )(code, beside, from_first, before)
+        settle_planes_kernel,
+        [SMEM] + [VMEM] * 4,
+        shape(rows, levels),
+        12 * rows * levels**2,
+        [pltpu.VMEM((rows, levels), F32)],
+    )(code, here, there, from_first, before)
 
 
 def finish_kernel(
@@ -466,7 +514,6 @@
             mine, theirs = (maps, states), (*theirs, their_states)
         if last:
             plane, whole, _ = merge(code, mine, theirs, "states", lines, apart, halves, False)
-            total, _, _ = merge(code, mine, (whole,), "both", lines, False, False, False)
         else:
             half_too = turn == len(ROUNDS) - 2
             total, whole, half = merge(code, mine, theirs, "both", lines, apart, halves, half_too)
@@ -480,13 +527,17 @@
         return lax.ppermute(value, "line", pairs)
 
     from_first = across(plane, 0, 1)
-    beside = across(total, 2, 3)
-    from_first, before = lax.optimization_barrier((from_first, before))
-    joined = enter(from_first, total, plane)
+    joined = enter(code, from_first, total, whole)
+    joined, total, whole = lax.optimization_barrier((joined, total, whole))
+    in_third = jnp.where(lax.axis_index("line") // PLANE == 2, 4, 0).astype(jnp.int32)
+    beside = across(plane_half(code + in_third, total, whole), 2, 3)
     two_on = across(joined, 1, 3)
     entering = (two_on, across(joined, 1, 2))
-    in_last = jnp.where(lax.axis_index("line") >= 3 * PLANE, 1, 0).astype(jnp.int32).reshape(1)
-    before = settle_planes(in_last, beside, from_first, before)
+    other = partner(beside, "line", CORE)
+    in_last = jnp.where(lax.axis_index("line") >= 3 * PLANE, 1, 0)
+    core = jnp.where((lax.axis_index("line") & CORE) != 0, 2, 0)
+    in_last = (in_last + core).astype(jnp.int32).reshape(1)
+    before = settle_planes(in_last, beside, other, from_first, before)
     solved = finish(entering, before, prefix, trial)
     parts = solved.reshape(span_count, share, cells, levels)
     parts = lax.all_to_all(parts, "span", split_axis=0, concat_axis=0, tiled=True)

time: 94.4 us -> 99 us (1.049)
  waiting for transfers between devices: 40.7 us -> 43.4 us
  starting transfers between devices: 24 us -> 25.7 us
    ppermute x4, waiting for transfers between devices: 7.07 us -> 11.3 us  [across(): return lax.ppermute(value, 'line', pairs)]
    ppermute x9 -> x10, starting transfers between devices: 13.6 us -> 15.4 us  [partner(): return lax.ppermute(value, axis, [(i, i ^ mask) for i in range(count)])]
    ppermute x9 -> x10, waiting for transfers between devices: 32.5 us -> 31 us  [partner(): return lax.ppermute(value, axis, [(i, i ^ mask) for i in range(count)])]
    pallas_call x5 -> x4, Pallas kernels: 2.93 us -> 2.26 us  [merge(): call(functools.partial(merge_kernel, start, kind, apart, halves, half), [...]
  transfers between devices with their start and end apart: 15 -> 16, of which waited for: 9 -> 10; matrix products, arithmetic and copies ran while one was open for 0% -> 0% of each run, Pallas kernels for 8% -> 8%
where the time goes in v7:
time: 99 us; the launch traced here: 98.2 us
  waiting for transfers between devices  43.4 us (44%)
  starting transfers between devices  25.7 us (26%)
  Pallas kernels  15.1 us (15%)
  blocking collectives  10.7 us (11%)
  local copies, waits for them, and re-layouts  3.1 us (3%)
    ppermute x10, waiting for transfers between devices, partner(): return lax.ppermute(value, axis, [(i, i ^ mask) for i in range(count)])  31 us
    ppermute x10, starting transfers between devices, partner(): return lax.ppermute(value, axis, [(i, i ^ mask) for i in range(count)])  15.4 us
    ppermute x4, waiting for transfers between devices, across(): return lax.ppermute(value, 'line', pairs)  11.3 us
    all_to_all x1, blocking collectives, shards(): lax.all_to_all(parts, 'span', split_axis=0, concat_axis=0, tiled=True)  10.7 us
    pallas_call x1, Pallas kernels, prefix_maps(): call(maps_kernel, [VMEM, HBM], [shape(*blocks.shape), shape(levels + PAD,...  4.82 us
    all_to_all x1, starting transfers between devices, shards(): lax.all_to_all(parts, 'span', split_axis=0, concat_axis=0, tiled=True)  4.46 us
    ppermute x4, starting transfers between devices, across(): return lax.ppermute(value, 'line', pairs)  3.9 us
    pallas_call x1, Pallas kernels, finish(): call(finish_kernel, [VMEM, VMEM, VMEM, HBM, VMEM], shape(lines, cells, le...  2.7 us
  transfers between devices with their start and end apart: 16, of which 10 were waited for; matrix products, arithmetic and copies ran while one was open for 0% of the time, Pallas kernels for 8%

profile of v7, /device:TPU:6, one launch (start us, length us, event | category | flops | bytes accessed | tf_op | source)
XLA Modules:
  0.0 98.2 jit_solution(9161473883872942201)
XLA Ops:
  1.7 4.5 %all-to-all-start = ((f32[4,8,8,256]{3,2,1,0:T(8,128)}), f32[4,8,8,256]{3,2,1,0:T(8,128)S(1)}, u32[]{:S(2)}, u32[]{:S(2)}) async-start(f32[4,8,8,256]{3,2,1,0:T(8,128)} %copy_bitcast_fusion.1), calls=%async_computation | async-start | bytes 524288 | tf_op jit(solution)/shard_map/all_to_all | solution.py:472
  6.8 4.8 %shard_map.37 = (f32[8,256,256]{2,1,0:T(8,128)}, f32[272,256]{1,0:T(8,128)S(1)}) custom-call(f32[8,256]{1,0:T(8,128)S(1)} %copy-done.2, f32[8,256,256]{2,1,0:T(8,128)} %blocks_ref.3), custom_call_target="tpu_custom_call" | custom-call | flops 1610612736 | bytes 1048576 | tf_op jit(solution)/shard_map/pallas_call | solution.py:135
  11.7 1.1 %all-to-all-done = f32[4,8,8,256]{3,2,1,0:T(8,128)S(1)} async-done(((f32[4,8,8,256]{3,2,1,0:T(8,128)}), f32[4,8,8,256]{3,2,1,0:T(8,128)S(1)}, u32[]{:S(2)}, u32[]{:S(2)}) %all-to-all-start) | async-done | bytes 262176 | tf_op jit(solution)/shard_map/all_to_all | solution.py:472
  12.8 1.0 collective-permute-start
  13.8 1.9 %shard_map.38 = (f32[8,32,256]{2,1,0:T(8,128)S(1)}, f32[32,256]{1,0:T(8,128)S(1)}) custom-call(f32[8,256]{1,0:T(8,128)S(1)} %copy-done.3, f32[8,256,256]{2,1,0:T(8,128)S(1)} %copy-done.1, f32[32,8,256]{2,1,0:T(8,128)S(1)} %bitcast.21), custom_call_target="tpu_custom_call" | custom-call | flops 201326592 | bytes 1048576 | tf_op jit(solution)/shard_map/pallas_call | solution.py:166
  15.7 1.1 %collective-permute-start.1 = (f32[32,256]{1,0:T(8,128)S(1)}, f32[32,256]{1,0:T(8,128)S(1)}, u32[]{:S(2)}, u32[]{:S(2)}) collective-permute-start(f32[32,256]{1,0:T(8,128)S(1)} %get-tuple-element.34.refs_1_), channel_id=1, source_target_pairs={{0,1},{1,0},{2,3},{3,2},{4,5},{5,4},{6,7},{7,6},{8,9},{9,8},{10,11... | collective-permute-start | bytes 98312 | tf_op jit(solution)/shard_map/ppermute | solution.py:480
  16.9 3.7 %collective-permute-done.1.refs_3_.refs_1_ = f32[32,256]{1,0:T(8,128)S(1)} collective-permute-done((f32[32,256]{1,0:T(8,128)S(1)}, f32[32,256]{1,0:T(8,128)S(1)}, u32[]{:S(2)}, u32[]{:S(2)}) %collective-permute-start.1) | collective-permute-done | bytes 32800 | tf_op jit(solution)/shard_map/ppermute | solution.py:480
  21.3 3.0 %collective-permute-start.2 = (f32[304,256]{1,0:T(8,128)S(1)}, f32[304,256]{1,0:T(8,128)S(1)}, u32[]{:S(2)}, u32[]{:S(2)}) collective-permute-start(f32[304,256]{1,0:T(8,128)S(1)} %shard_map.39.refs_0_), channel_id=1, source_target_pairs={{0,3},{1,2},{2,1},{3,0},{4,7},{5,6},{6,5},{7,4},{8,11},{9,10},{10,... | collective-permute-start | bytes 933896 | tf_op jit(solution)/shard_map/ppermute | solution.py:480
  24.3 5.8 %collective-permute-done.2.refs_1_.refs_0_ = f32[304,256]{1,0:T(8,128)S(1)} collective-permute-done((f32[304,256]{1,0:T(8,128)S(1)}, f32[304,256]{1,0:T(8,128)S(1)}, u32[]{:S(2)}, u32[]{:S(2)}) %collective-permute-start.2) | collective-permute-done | bytes 311328 | tf_op jit(solution)/shard_map/ppermute | solution.py:480
  31.0 1.5 %collective-permute-done.3.refs_1_.refs_0_ = f32[304,256]{1,0:T(8,128)S(1)} collective-permute-done((f32[304,256]{1,0:T(8,128)S(1)}, f32[304,256]{1,0:T(8,128)S(1)}, u32[]{:S(2)}, u32[]{:S(2)}) %collective-permute-start.3) | collective-permute-done | bytes 311328 | tf_op jit(solution)/shard_map/ppermute | solution.py:480
  33.2 2.0 %collective-permute-start.4 = (f32[304,256]{1,0:T(8,128)S(1)}, f32[304,256]{1,0:T(8,128)S(1)}, u32[]{:S(2)}, u32[]{:S(2)}) collective-permute-start(f32[304,256]{1,0:T(8,128)S(1)} %get-tuple-element.38.mine_ref), channel_id=1, source_target_pairs={{0,8},{4,20},{8,0},{12,28},{16,24},{20,4},{24,16},{28,12},{32,40},... | collective-permute-start | bytes 933896 | tf_op jit(solution)/shard_map/ppermute | solution.py:490
  35.2 2.8 %collective-permute-start.5 = (f32[152,256]{1,0:T(8,128)S(1)}, f32[152,256]{1,0:T(8,128)S(1)}, u32[]{:S(2)}, u32[]{:S(2)}) collective-permute-start(f32[152,256]{1,0:T(8,128)S(1)} %get-tuple-element.39), channel_id=1, source_target_pairs={{0,24},{4,28},{8,16},{12,20},{16,8},{20,12},{24,0},{28,4},{32,56},... | collective-permute-start | bytes 466952 | tf_op jit(solution)/shard_map/ppermute | solution.py:480
  38.1 10.9 %collective-permute-done.5.this_ref = f32[152,256]{1,0:T(8,128)S(1)} collective-permute-done((f32[152,256]{1,0:T(8,128)S(1)}, f32[152,256]{1,0:T(8,128)S(1)}, u32[]{:S(2)}, u32[]{:S(2)}) %collective-permute-start.5) | collective-permute-done | bytes 155680 | tf_op jit(solution)/shard_map/ppermute | solution.py:480
  49.5 1.3 %collective-permute-done.7.that_ref = f32[152,256]{1,0:T(8,128)S(1)} collective-permute-done((f32[152,256]{1,0:T(8,128)S(1)}, f32[152,256]{1,0:T(8,128)S(1)}, u32[]{:S(2)}, u32[]{:S(2)}) %collective-permute-start.7) | collective-permute-done | bytes 155680 | tf_op jit(solution)/shard_map/ppermute | solution.py:480
  50.8 1.9 %shard_map.45 = (f32[304,256]{1,0:T(8,128)S(1)}, f32[304,256]{1,0:T(8,128)S(1)}, f32[304,256]{1,0:T(8,128)S(1)}, f32[152,256]{1,0:T(8,128)S(1)}) custom-call(s32[1]{0:T(128)} %bitcast.1.code_ref, f32[304,256]{1,0:T(8,128)S(1)} %get-tuple-element.38.mine_ref, f32[304,256]{1,0:T(8,128)S(1)} %collective-permute-done.4.here_ref, ...), custom_call_target="tpu_custom_call" | custom-call | flops 717225984 | bytes 1048576 | tf_op jit(solution)/shard_map/pallas_call | solution.py:303
  52.6 6.7 %collective-permute-start.8 = (f32[152,256]{1,0:T(8,128)S(1)}, f32[152,256]{1,0:T(8,128)S(1)}, u32[]{:S(2)}, u32[]{:S(2)}) collective-permute-start(f32[152,256]{1,0:T(8,128)S(1)} %get-tuple-element.44), channel_id=1, source_target_pairs={{0,48},{4,52},{8,56},{12,60},{16,32},{20,36},{24,40},{28,44},{32,1... | collective-permute-start | bytes 466952 | tf_op jit(solution)/shard_map/ppermute | solution.py:480
  59.5 6.3 %collective-permute-done.8.refs_1_ = f32[152,256]{1,0:T(8,128)S(1)} collective-permute-done((f32[152,256]{1,0:T(8,128)S(1)}, f32[152,256]{1,0:T(8,128)S(1)}, u32[]{:S(2)}, u32[]{:S(2)}) %collective-permute-start.8) | collective-permute-done | bytes 155680 | tf_op jit(solution)/shard_map/ppermute | solution.py:480
  65.8 1.3 %collective-permute-done.9.refs_2_ = f32[152,256]{1,0:T(8,128)S(1)} collective-permute-done((f32[152,256]{1,0:T(8,128)S(1)}, f32[152,256]{1,0:T(8,128)S(1)}, u32[]{:S(2)}, u32[]{:S(2)}) %collective-permute-start.9) | collective-permute-done | bytes 155680 | tf_op jit(solution)/shard_map/ppermute | solution.py:480
  68.8 1.3 %collective-permute-start.13 = (f32[152,256]{1,0:T(8,128)S(1)}, f32[152,256]{1,0:T(8,128)S(1)}, u32[]{:S(2)}, u32[]{:S(2)}) collective-permute-start(f32[152,256]{1,0:T(8,128)S(1)} %shard_map.50), channel_id=1, source_target_pairs={{128,192},{132,196},{136,200},{140,204},{144,208},{148,212},{152,2... | collective-permute-start | bytes 466952 | tf_op jit(solution)/shard_map/ppermute | solution.py:527
  70.1 6.7 %collective-permute-done.13.here_ref = f32[152,256]{1,0:T(8,128)S(1)} collective-permute-done((f32[152,256]{1,0:T(8,128)S(1)}, f32[152,256]{1,0:T(8,128)S(1)}, u32[]{:S(2)}, u32[]{:S(2)}) %collective-permute-start.13) | collective-permute-done | bytes 155680 | tf_op jit(solution)/shard_map/ppermute | solution.py:527
  76.8 1.3 %collective-permute-start.11 = (f32[32,256]{1,0:T(8,128)S(1)}, f32[32,256]{1,0:T(8,128)S(1)}, u32[]{:S(2)}, u32[]{:S(2)}) collective-permute-start(f32[32,256]{1,0:T(8,128)S(1)} %shard_map.49), channel_id=1, source_target_pairs={{64,192},{68,196},{72,200},{76,204},{80,208},{84,212},{88,216},{92... | collective-permute-start | bytes 98312 | tf_op jit(solution)/shard_map/ppermute | solution.py:527
  79.5 4.6 %collective-permute-done.11.one_ref = f32[32,256]{1,0:T(8,128)S(1)} collective-permute-done((f32[32,256]{1,0:T(8,128)S(1)}, f32[32,256]{1,0:T(8,128)S(1)}, u32[]{:S(2)}, u32[]{:S(2)}) %collective-permute-start.11) | collective-permute-done | bytes 32800 | tf_op jit(solution)/shard_map/ppermute | solution.py:527
  84.1 2.7 %shard_map.53 = f32[32,8,256]{2,1,0:T(8,128)S(1)} custom-call(f32[32,256]{1,0:T(8,128)S(1)} %collective-permute-done.11.one_ref, f32[32,256]{1,0:T(8,128)S(1)} %collective-permute-done.12.two_ref, f32[304,256]{1,0:T(8,128)S(1)} %shard_map.52.before_ref, f32[8,256,256]{2,1,0:T(8,128)} %get-tuple-element.55.prefix_ref, ...), custom_call_target="tpu_custom_call" | custom-call | flops 226492416 | bytes 1048576 | tf_op jit(solution)/shard_map/pallas_call | solution.py:452
  86.8 10.7 %all_to_all.10 = f32[4,8,8,256]{3,2,1,0:T(8,128)S(1)} all-to-all(f32[4,8,8,256]{3,2,1,0:T(8,128)S(1)} %bitcast.22), channel_id=1, replica_groups=mesh['line'=64,'span'=4] {'span'}, dimensions={0} | all-to-all | bytes 524288 | tf_op jit(solution)/shard_map/all_to_all | solution.py:543
  (36 shorter events, 8.9 us)
Async XLA Ops:
  0.0 1.0 copy-start
  1.7 11.1 %all-to-all-start = ((f32[4,8,8,256]{3,2,1,0:T(8,128)}), f32[4,8,8,256]{3,2,1,0:T(8,128)S(1)}, u32[]{:S(2)}, u32[]{:S(2)}) async-start(f32[4,8,8,256]{3,2,1,0:T(8,128)} %copy_bitcast_fusion.1), calls=%async_computation | async-start | bytes 524288 | tf_op jit(solution)/shard_map/all_to_all | solution.py:472
  6.1 0.7 copy-start.2
  6.8 7.0 %copy-start.1 = (f32[8,256,256]{2,1,0:T(8,128)S(1)}, f32[8,256,256]{2,1,0:T(8,128)}, u32[]{:S(2)}) copy-start(f32[8,256,256]{2,1,0:T(8,128)} %blocks_ref.3) | copy-start | bytes 6291460
  6.8 7.0 %copy-start.3 = (f32[8,256]{1,0:T(8,128)S(1)}, f32[8,256]{1,0:T(8,128)}, u32[]{:S(2)}) copy-start(f32[8,256]{1,0:T(8,128)} %upstream_ref.3) | copy-start | bytes 24580
  12.8 7.8 %collective-permute-start = (f32[272,256]{1,0:T(8,128)S(1)}, f32[272,256]{1,0:T(8,128)S(1)}, u32[]{:S(2)}, u32[]{:S(2)}) collective-permute-start(f32[272,256]{1,0:T(8,128)S(1)} %get-tuple-element.32.refs_0_), channel_id=1, source_target_pairs={{0,1},{1,0},{2,3},{3,2},{4,5},{5,4},{6,7},{7,6},{8,9},{9,8},{10,11... | collective-permute-start | bytes 835592 | tf_op jit(solution)/shard_map/ppermute | solution.py:480
  15.7 4.8 %collective-permute-start.1 = (f32[32,256]{1,0:T(8,128)S(1)}, f32[32,256]{1,0:T(8,128)S(1)}, u32[]{:S(2)}, u32[]{:S(2)}) collective-permute-start(f32[32,256]{1,0:T(8,128)S(1)} %get-tuple-element.34.refs_1_), channel_id=1, source_target_pairs={{0,1},{1,0},{2,3},{3,2},{4,5},{5,4},{6,7},{7,6},{8,9},{9,8},{10,11... | collective-permute-start | bytes 98312 | tf_op jit(solution)/shard_map/ppermute | solution.py:480
  21.3 8.9 %collective-permute-start.2 = (f32[304,256]{1,0:T(8,128)S(1)}, f32[304,256]{1,0:T(8,128)S(1)}, u32[]{:S(2)}, u32[]{:S(2)}) collective-permute-start(f32[304,256]{1,0:T(8,128)S(1)} %shard_map.39.refs_0_), channel_id=1, source_target_pairs={{0,3},{1,2},{2,1},{3,0},{4,7},{5,6},{6,5},{7,4},{8,11},{9,10},{10,... | collective-permute-start | bytes 933896 | tf_op jit(solution)/shard_map/ppermute | solution.py:480
  30.8 1.7 %collective-permute-start.3 = (f32[304,256]{1,0:T(8,128)S(1)}, f32[304,256]{1,0:T(8,128)S(1)}, u32[]{:S(2)}, u32[]{:S(2)}) collective-permute-start(f32[304,256]{1,0:T(8,128)S(1)} %shard_map.41.refs_0_), channel_id=1, source_target_pairs={{0,4},{4,0},{8,12},{12,8},{16,20},{20,16},{24,28},{28,24},{32,36},... | collective-permute-start | bytes 933896 | tf_op jit(solution)/shard_map/ppermute | solution.py:480
  33.2 15.7 %collective-permute-start.4 = (f32[304,256]{1,0:T(8,128)S(1)}, f32[304,256]{1,0:T(8,128)S(1)}, u32[]{:S(2)}, u32[]{:S(2)}) collective-permute-start(f32[304,256]{1,0:T(8,128)S(1)} %get-tuple-element.38.mine_ref), channel_id=1, source_target_pairs={{0,8},{4,20},{8,0},{12,28},{16,24},{20,4},{24,16},{28,12},{32,40},... | collective-permute-start | bytes 933896 | tf_op jit(solution)/shard_map/ppermute | solution.py:490
  35.2 13.7 %collective-permute-start.5 = (f32[152,256]{1,0:T(8,128)S(1)}, f32[152,256]{1,0:T(8,128)S(1)}, u32[]{:S(2)}, u32[]{:S(2)}) collective-permute-start(f32[152,256]{1,0:T(8,128)S(1)} %get-tuple-element.39), channel_id=1, source_target_pairs={{0,24},{4,28},{8,16},{12,20},{16,8},{20,12},{24,0},{28,4},{32,56},... | collective-permute-start | bytes 466952 | tf_op jit(solution)/shard_map/ppermute | solution.py:480
  49.0 1.8 %collective-permute-start.6 = (f32[304,256]{1,0:T(8,128)S(1)}, f32[304,256]{1,0:T(8,128)S(1)}, u32[]{:S(2)}, u32[]{:S(2)}) collective-permute-start(f32[304,256]{1,0:T(8,128)S(1)} %collective-permute-done.4.here_ref), channel_id=1, source_target_pairs={{0,4},{4,0},{8,12},{12,8},{16,20},{20,16},{24,28},{28,24},{32,36},... | collective-permute-start | bytes 933896 | tf_op jit(solution)/shard_map/ppermute | solution.py:480
  49.1 1.7 %collective-permute-start.7 = (f32[152,256]{1,0:T(8,128)S(1)}, f32[152,256]{1,0:T(8,128)S(1)}, u32[]{:S(2)}, u32[]{:S(2)}) collective-permute-start(f32[152,256]{1,0:T(8,128)S(1)} %collective-permute-done.5.this_ref), channel_id=1, source_target_pairs={{0,4},{4,0},{8,12},{12,8},{16,20},{20,16},{24,28},{28,24},{32,36},... | collective-permute-start | bytes 466952 | tf_op jit(solution)/shard_map/ppermute | solution.py:480
  52.6 13.1 %collective-permute-start.8 = (f32[152,256]{1,0:T(8,128)S(1)}, f32[152,256]{1,0:T(8,128)S(1)}, u32[]{:S(2)}, u32[]{:S(2)}) collective-permute-start(f32[152,256]{1,0:T(8,128)S(1)} %get-tuple-element.44), channel_id=1, source_target_pairs={{0,48},{4,52},{8,56},{12,60},{16,32},{20,36},{24,40},{28,44},{32,1... | collective-permute-start | bytes 466952 | tf_op jit(solution)/shard_map/ppermute | solution.py:480
  65.8 1.4 %collective-permute-start.9 = (f32[152,256]{1,0:T(8,128)S(1)}, f32[152,256]{1,0:T(8,128)S(1)}, u32[]{:S(2)}, u32[]{:S(2)}) collective-permute-start(f32[152,256]{1,0:T(8,128)S(1)} %collective-permute-done.8.refs_1_), channel_id=1, source_target_pairs={{0,4},{4,0},{8,12},{12,8},{16,20},{20,16},{24,28},{28,24},{32,36},... | collective-permute-start | bytes 466952 | tf_op jit(solution)/shard_map/ppermute | solution.py:480
  67.4 0.7 collective-permute-start.10
  68.8 8.0 %collective-permute-start.13 = (f32[152,256]{1,0:T(8,128)S(1)}, f32[152,256]{1,0:T(8,128)S(1)}, u32[]{:S(2)}, u32[]{:S(2)}) collective-permute-start(f32[152,256]{1,0:T(8,128)S(1)} %shard_map.50), channel_id=1, source_target_pairs={{128,192},{132,196},{136,200},{140,204},{144,208},{148,212},{152,2... | collective-permute-start | bytes 466952 | tf_op jit(solution)/shard_map/ppermute | solution.py:527
  76.8 2.0 %collective-permute-start.14 = (f32[152,256]{1,0:T(8,128)S(1)}, f32[152,256]{1,0:T(8,128)S(1)}, u32[]{:S(2)}, u32[]{:S(2)}) collective-permute-start(f32[152,256]{1,0:T(8,128)S(1)} %collective-permute-done.13.here_ref), channel_id=1, source_target_pairs={{0,4},{4,0},{8,12},{12,8},{16,20},{20,16},{24,28},{28,24},{32,36},... | collective-permute-start | bytes 466952 | tf_op jit(solution)/shard_map/ppermute | solution.py:480
  76.8 7.3 %collective-permute-start.11 = (f32[32,256]{1,0:T(8,128)S(1)}, f32[32,256]{1,0:T(8,128)S(1)}, u32[]{:S(2)}, u32[]{:S(2)}) collective-permute-start(f32[32,256]{1,0:T(8,128)S(1)} %shard_map.49), channel_id=1, source_target_pairs={{64,192},{68,196},{72,200},{76,204},{80,208},{84,212},{88,216},{92... | collective-permute-start | bytes 98312 | tf_op jit(solution)/shard_map/ppermute | solution.py:527
  78.1 6.0 %collective-permute-start.12 = (f32[32,256]{1,0:T(8,128)S(1)}, f32[32,256]{1,0:T(8,128)S(1)}, u32[]{:S(2)}, u32[]{:S(2)}) collective-permute-start(f32[32,256]{1,0:T(8,128)S(1)} %shard_map.49), channel_id=1, source_target_pairs={{64,128},{68,132},{72,136},{76,140},{80,144},{84,148},{88,152},{92... | collective-permute-start | bytes 98312 | tf_op jit(solution)/shard_map/ppermute | solution.py:527

commit v8 on v6

--- a/solution.py
+++ b/solution.py
@@ -149,7 +149,40 @@
     )(upstream, blocks)
 
 
-def states_kernel(upstream_ref, blocks_ref, forcing_ref, trial_ref, states_ref):
+def cut_kernel(code_ref, forcing_ref, *part_refs):
+    cells = part_refs[0].shape[1]
+    for turn, part_ref in enumerate(part_refs):
+        first = pl.multiple_of((code_ref[0] ^ turn) * cells, cells)
+        part_ref[...] = forcing_ref[:, pl.ds(first, cells), :]
+
+
+def cut(here, forcing, parts):
+    share, length, levels = forcing.shape
+    return call(cut_kernel, [SMEM, VMEM], [shape(share, length // parts, levels)] * parts, 1)(
+        here, forcing
+    )
+
+
+def assemble_kernel(code_ref, *refs):
+    *part_refs, whole_ref = refs
+    cells = part_refs[0].shape[1]
+    for turn, part_ref in enumerate(part_refs):
+        first = pl.multiple_of((code_ref[0] ^ turn) * cells, cells)
+        whole_ref[:, pl.ds(first, cells), :] = part_ref[...]
+
+
+def assemble(here, parts):
+    share, cells, levels = parts[0].shape
+    return call(
+        assemble_kernel, [SMEM] + [VMEM] * len(parts), shape(share, len(parts) * cells, levels), 1
+    )(here, *parts)
+
+
+def states_kernel(code_ref, upstream_ref, blocks_ref, *refs):
+    *part_refs, trial_ref, states_ref, forcing_ref = refs
+    share = part_refs[0].shape[0]
+    for turn, part_ref in enumerate(part_refs):
+        forcing_ref[pl.ds((code_ref[0] ^ turn) * share, share)] = part_ref[...]
     states_ref[...] = jnp.zeros_like(states_ref)
 
     @pl.loop(0, blocks_ref.shape[0])
@@ -160,15 +193,16 @@
         trial_ref[cell] = state
 
 
-def trial_states(blocks, upstream, forcing):
+def trial_states(here, blocks, upstream, parts):
     cells, levels, _ = blocks.shape
-    lines = forcing.shape[0]
+    lines = len(parts) * parts[0].shape[0]
     return call(
         states_kernel,
-        [VMEM] * 3,
+        [SMEM] + [VMEM] * (2 + len(parts)),
         [shape(cells, lines, levels), shape(lines, levels)],
         12 * cells * lines * levels**2,
-    )(upstream, blocks, forcing)
+        [pltpu.VMEM((lines, cells, levels), F32)],
+    )(here, upstream, blocks, *parts)
 
 
 def later(code_ref, then, otherwise):
@@ -364,6 +398,27 @@
     )
 
 
+def plane_total_kernel(code_ref, mine_ref, theirs_ref, total_ref):
+    @pl.when(code_ref[0] < 4)
+    def _():
+        total_ref[...] = jnp.zeros_like(total_ref)
+
+    @pl.when(code_ref[0] >= 4)
+    def _():
+        later(
+            code_ref,
+            lambda: join(theirs_ref, mine_ref, total_ref),
+            lambda: join(mine_ref, theirs_ref, total_ref),
+        )
+
+
+def plane_total(code, mine, theirs):
+    rows, levels = mine.shape
+    return call(
+        plane_total_kernel, [SMEM, VMEM, VMEM], shape(rows, levels), 12 * rows * levels**2
+    )(code, mine, theirs)
+
+
 def settle_planes_kernel(code_ref, beside_ref, from_ref, before_ref, ahead_ref):
     start = before_ref.shape[1] + PAD
 
@@ -385,9 +440,8 @@
     )(code, beside, from_first, before)
 
 
-def finish_kernel(
-    one_ref, two_ref, before_ref, prefix_ref, trial_ref, solved_ref, held_ref, incoming, arrived
-):
+def finish_kernel(code_ref, one_ref, two_ref, before_ref, prefix_ref, trial_ref, *refs):
+    *part_refs, solved_ref, held_ref, incoming, arrived = refs
     fetch(prefix_ref, held_ref, arrived)
     start = before_ref.shape[1] + PAD
     entering = one_ref[...] + two_ref[...]
@@ -398,38 +452,47 @@
         block_copy(prefix_ref, held_ref, arrived, cell).wait()
         solved_ref[:, cell, :] = trial_ref[cell] + dot3(incoming[...], held_ref[cell])
 
-
-def finish(entering, before, prefix, trial):
+    share = part_refs[0].shape[0]
+    for turn, part_ref in enumerate(part_refs):
+        part_ref[...] = solved_ref[pl.ds((code_ref[0] ^ turn) * share, share)]
+
+
+def finish(here, entering, before, prefix, trial, parts):
     cells, lines, levels = trial.shape
     return call(
         finish_kernel,
-        [VMEM, VMEM, VMEM, HBM, VMEM],
-        shape(lines, cells, levels),
+        [SMEM, VMEM, VMEM, VMEM, HBM, VMEM],
+        [shape(lines // parts, cells, levels)] * parts,
         12 * (cells + 1) * lines * levels**2,
         [
+            pltpu.VMEM((lines, cells, levels), F32),
             pltpu.VMEM(prefix.shape, F32),
             pltpu.VMEM((lines, levels), F32),
             pltpu.SemaphoreType.DMA((cells,)),
         ],
         None,
         LARGE,
-    )(*entering, before, prefix, trial)
+    )(here, *entering, before, prefix, trial)
 
 
 def shards(span_count, forcing, blocks, upstream):
     cells, levels, _ = blocks.shape
     share = forcing.shape[0]
     lines = share * span_count
-    parts = forcing.reshape(share, span_count, cells, levels).swapaxes(0, 1)
-    parts = lax.all_to_all(parts, "span", split_axis=0, concat_axis=0, tiled=True)
-    local_forcing = parts.reshape(lines, cells, levels)
-    prefix, maps = prefix_maps(blocks, upstream)
-    local_forcing, maps = lax.optimization_barrier((local_forcing, maps))
-    trial, states = trial_states(blocks, upstream, local_forcing)
+    here = lax.axis_index("span").astype(jnp.int32).reshape(1)
+
+    def trade(parts):
+        kept, *sent = parts
+        return [kept] + [partner(part, "span", k + 1) for k, part in enumerate(sent)]
 
     def partner(value, axis, mask):
         count = lax.axis_size(axis)
         return lax.ppermute(value, axis, [(i, i ^ mask) for i in range(count)])
+
+    forcing_parts = trade(cut(here, forcing, span_count))
+    prefix, maps = prefix_maps(blocks, upstream)
+    forcing_parts, maps = lax.optimization_barrier((forcing_parts, maps))
+    trial, states = trial_states(here, blocks, upstream, forcing_parts)
 
     def code_of(axis, bit):
         upper = jnp.where((lax.axis_index(axis) & bit) != 0, 1, 0)
@@ -453,9 +516,9 @@
         code = code_of(axis, bit)
         last = turn == len(ROUNDS) - 1
         if halves:
-            here = partner(half, axis, mask)
-            here, before = lax.optimization_barrier((here, before))
-            theirs = (here, partner(here, "line", CORE))
+            mine_half = partner(half, axis, mask)
+            mine_half, before = lax.optimization_barrier((mine_half, before))
+            theirs = (mine_half, partner(mine_half, "line", CORE))
         else:
             theirs = (partner(maps if apart else total, axis, mask),)
             if before is not None:
@@ -466,7 +529,8 @@
             mine, theirs = (maps, states), (*theirs, their_states)
         if last:
             plane, whole, _ = merge(code, mine, theirs, "states", lines, apart, halves, False)
-            total, _, _ = merge(code, mine, (whole,), "both", lines, False, False, False)
+            inner = (lax.axis_index("line") // PLANE + 1) // 2 == 1
+            total = plane_total(code + jnp.where(inner, 4, 0).astype(jnp.int32), total, whole)
         else:
             half_too = turn == len(ROUNDS) - 2
             total, whole, half = merge(code, mine, theirs, "both", lines, apart, halves, half_too)
@@ -487,10 +551,7 @@
     entering = (two_on, across(joined, 1, 2))
     in_last = jnp.where(lax.axis_index("line") >= 3 * PLANE, 1, 0).astype(jnp.int32).reshape(1)
     before = settle_planes(in_last, beside, from_first, before)
-    solved = finish(entering, before, prefix, trial)
-    parts = solved.reshape(span_count, share, cells, levels)
-    parts = lax.all_to_all(parts, "span", split_axis=0, concat_axis=0, tiled=True)
-    return parts.swapaxes(0, 1).reshape(share, span_count * cells, levels)
+    return assemble(here, trade(finish(here, entering, before, prefix, trial, span_count)))
 
 
 def solution(mesh):

time: 94.4 us -> 92 us (0.975)
  blocking collectives: 10.7 us -> 0 us
  starting transfers between devices: 24 us -> 29.1 us
  waiting for transfers between devices: 40.7 us -> 45 us
  local copies, waits for them, and re-layouts: 3.1 us -> 1.77 us
    all_to_all x1 -> x0, blocking collectives: 10.7 us -> none  [shards(): lax.all_to_all(parts, 'span', split_axis=0, concat_axis=0, tiled=True)]
    ppermute x9 -> x15, starting transfers between devices: 13.6 us -> 23.2 us  [partner(): return lax.ppermute(value, axis, [(i, i ^ mask) for i in range(count)])]
    ppermute x9 -> x15, waiting for transfers between devices: 32.5 us -> 38 us  [partner(): return lax.ppermute(value, axis, [(i, i ^ mask) for i in range(count)])]
    all_to_all x1 -> x0, starting transfers between devices: 4.46 us -> none  [shards(): lax.all_to_all(parts, 'span', split_axis=0, concat_axis=0, tiled=True)]
    all_to_all x1 -> x0, waiting for transfers between devices: 1.14 us -> none  [shards(): lax.all_to_all(parts, 'span', split_axis=0, concat_axis=0, tiled=True)]
    pallas_call x2 -> x5, Pallas kernels: 4.64 us -> 5.45 us  [the longest x1 2.72 us: finish(): call(finish_kernel, [SMEM, VMEM, VMEM, VMEM, HBM, VMEM], [shape(lines //...]
    pallas_call x5 -> x4, Pallas kernels: 2.93 us -> 2.26 us  [merge(): call(functools.partial(merge_kernel, start, kind, apart, halves, half), [...]
  transfers between devices with their start and end apart: 15 -> 20, of which waited for: 9 -> 11; matrix products, arithmetic and copies ran while one was open for 0% -> 0% of each run, Pallas kernels for 8% -> 8%
where the time goes in v8:
time: 92 us; the launch traced here: 91.4 us
  waiting for transfers between devices  45 us (49%)
  starting transfers between devices  29.1 us (32%)
  Pallas kernels  15.3 us (17%)
  local copies, waits for them, and re-layouts  1.77 us (2%)
    ppermute x15, waiting for transfers between devices, partner(): return lax.ppermute(value, axis, [(i, i ^ mask) for i in range(count)])  38 us
    ppermute x15, starting transfers between devices, partner(): return lax.ppermute(value, axis, [(i, i ^ mask) for i in range(count)])  23.2 us
    ppermute x4, waiting for transfers between devices, across(): return lax.ppermute(value, 'line', pairs)  7.07 us
    pallas_call x1, Pallas kernels, prefix_maps(): call(maps_kernel, [VMEM, HBM], [shape(*blocks.shape), shape(levels + PAD,...  4.67 us
    ppermute x4, starting transfers between devices, across(): return lax.ppermute(value, 'line', pairs)  3.91 us
    pallas_call x1, Pallas kernels, finish(): call(finish_kernel, [SMEM, VMEM, VMEM, VMEM, HBM, VMEM], [shape(lines //...  2.72 us
    pallas_call x4, Pallas kernels, merge(): call(functools.partial(merge_kernel, start, kind, apart, halves, half), [...  2.26 us
    ppermute x1, starting transfers between devices, along_four(): lax.ppermute(total, 'line', pairs)  2 us
  transfers between devices with their start and end apart: 20, of which 11 were waited for; matrix products, arithmetic and copies ran while one was open for 0% of the time, Pallas kernels for 8%

profile of v8, /device:TPU:6, one launch (start us, length us, event | category | flops | bytes accessed | tf_op | source)
XLA Modules:
  0.0 91.4 jit_solution(8376896774719587488)
XLA Ops:
  1.0 1.7 %collective-permute-start = (f32[8,8,256]{2,1,0:T(8,128)S(1)}, f32[8,8,256]{2,1,0:T(8,128)S(1)}, u32[]{:S(2)}, u32[]{:S(2)}) collective-permute-start(f32[8,8,256]{2,1,0:T(8,128)S(1)} %get-tuple-element.42), channel_id=1, source_target_pairs={{0,1},{1,0},{2,3},{3,2},{4,5},{5,4},{6,7},{7,6},{8,9},{9,8},{10,11... | collective-permute-start | bytes 196616 | tf_op jit(solution)/shard_map/ppermute | solution.py:490
  2.6 2.9 %collective-permute-start.1 = (f32[8,8,256]{2,1,0:T(8,128)S(1)}, f32[8,8,256]{2,1,0:T(8,128)S(1)}, u32[]{:S(2)}, u32[]{:S(2)}) collective-permute-start(f32[8,8,256]{2,1,0:T(8,128)S(1)} %get-tuple-element.43), channel_id=1, source_target_pairs={{0,2},{1,3},{2,0},{3,1},{4,6},{5,7},{6,4},{7,5},{8,10},{9,11},{10,... | collective-permute-start | bytes 196616 | tf_op jit(solution)/shard_map/ppermute | solution.py:490
  6.6 4.7 %shard_map.38 = (f32[8,256,256]{2,1,0:T(8,128)}, f32[272,256]{1,0:T(8,128)S(1)}) custom-call(f32[8,256]{1,0:T(8,128)S(1)} %copy-done.2, f32[8,256,256]{2,1,0:T(8,128)} %blocks_ref.3), custom_call_target="tpu_custom_call" | custom-call | flops 1610612736 | bytes 1048576 | tf_op jit(solution)/shard_map/pallas_call | solution.py:135
  11.8 2.0 %shard_map.39 = (f32[8,32,256]{2,1,0:T(8,128)S(1)}, f32[32,256]{1,0:T(8,128)S(1)}) custom-call(s32[1]{0:T(128)} %bitcast.code_ref, f32[8,256]{1,0:T(8,128)S(1)} %copy-done.2, f32[8,256,256]{2,1,0:T(8,128)S(1)} %copy-done, f32[8,8,256]{2,1,0:T(8,128)S(1)} %get-tuple-element.47.refs_0_, f32[8,8,256]{2,1,0:T(8,128)S(1)} %collective-permute-done.refs_1_, ...), custom_call_target="tpu_custom_call" | custom-call | flops 201326592 | bytes 1048576 | tf_op jit(solution)/shard_map/pallas_call | solution.py:199
  13.8 1.7 %collective-permute-start.4 = (f32[32,256]{1,0:T(8,128)S(1)}, f32[32,256]{1,0:T(8,128)S(1)}, u32[]{:S(2)}, u32[]{:S(2)}) collective-permute-start(f32[32,256]{1,0:T(8,128)S(1)} %get-tuple-element.51.refs_1_), channel_id=1, source_target_pairs={{0,1},{1,0},{2,3},{3,2},{4,5},{5,4},{6,7},{7,6},{8,9},{9,8},{10,11... | collective-permute-start | bytes 98312 | tf_op jit(solution)/shard_map/ppermute | solution.py:490
  15.5 4.3 %collective-permute-done.4.refs_3_.refs_1_ = f32[32,256]{1,0:T(8,128)S(1)} collective-permute-done((f32[32,256]{1,0:T(8,128)S(1)}, f32[32,256]{1,0:T(8,128)S(1)}, u32[]{:S(2)}, u32[]{:S(2)}) %collective-permute-start.4) | collective-permute-done | bytes 32800 | tf_op jit(solution)/shard_map/ppermute | solution.py:490
  20.4 2.9 %collective-permute-start.5 = (f32[304,256]{1,0:T(8,128)S(1)}, f32[304,256]{1,0:T(8,128)S(1)}, u32[]{:S(2)}, u32[]{:S(2)}) collective-permute-start(f32[304,256]{1,0:T(8,128)S(1)} %shard_map.40.refs_0_), channel_id=1, source_target_pairs={{0,3},{1,2},{2,1},{3,0},{4,7},{5,6},{6,5},{7,4},{8,11},{9,10},{10,... | collective-permute-start | bytes 933896 | tf_op jit(solution)/shard_map/ppermute | solution.py:490
  23.3 5.8 %collective-permute-done.5.refs_1_.refs_0_ = f32[304,256]{1,0:T(8,128)S(1)} collective-permute-done((f32[304,256]{1,0:T(8,128)S(1)}, f32[304,256]{1,0:T(8,128)S(1)}, u32[]{:S(2)}, u32[]{:S(2)}) %collective-permute-start.5) | collective-permute-done | bytes 311328 | tf_op jit(solution)/shard_map/ppermute | solution.py:490
  29.9 1.5 %collective-permute-done.6.refs_1_.refs_0_ = f32[304,256]{1,0:T(8,128)S(1)} collective-permute-done((f32[304,256]{1,0:T(8,128)S(1)}, f32[304,256]{1,0:T(8,128)S(1)}, u32[]{:S(2)}, u32[]{:S(2)}) %collective-permute-start.6) | collective-permute-done | bytes 311328 | tf_op jit(solution)/shard_map/ppermute | solution.py:490
  32.2 2.0 %collective-permute-start.7 = (f32[304,256]{1,0:T(8,128)S(1)}, f32[304,256]{1,0:T(8,128)S(1)}, u32[]{:S(2)}, u32[]{:S(2)}) collective-permute-start(f32[304,256]{1,0:T(8,128)S(1)} %get-tuple-element.55.mine_ref), channel_id=1, source_target_pairs={{0,8},{4,20},{8,0},{12,28},{16,24},{20,4},{24,16},{28,12},{32,40},... | collective-permute-start | bytes 933896 | tf_op jit(solution)/shard_map/ppermute | solution.py:505
  34.2 2.8 %collective-permute-start.8 = (f32[152,256]{1,0:T(8,128)S(1)}, f32[152,256]{1,0:T(8,128)S(1)}, u32[]{:S(2)}, u32[]{:S(2)}) collective-permute-start(f32[152,256]{1,0:T(8,128)S(1)} %get-tuple-element.56), channel_id=1, source_target_pairs={{0,24},{4,28},{8,16},{12,20},{16,8},{20,12},{24,0},{28,4},{32,56},... | collective-permute-start | bytes 466952 | tf_op jit(solution)/shard_map/ppermute | solution.py:490
  37.0 10.9 %collective-permute-done.8.this_ref = f32[152,256]{1,0:T(8,128)S(1)} collective-permute-done((f32[152,256]{1,0:T(8,128)S(1)}, f32[152,256]{1,0:T(8,128)S(1)}, u32[]{:S(2)}, u32[]{:S(2)}) %collective-permute-start.8) | collective-permute-done | bytes 155680 | tf_op jit(solution)/shard_map/ppermute | solution.py:490
  48.4 1.3 %collective-permute-done.10.that_ref = f32[152,256]{1,0:T(8,128)S(1)} collective-permute-done((f32[152,256]{1,0:T(8,128)S(1)}, f32[152,256]{1,0:T(8,128)S(1)}, u32[]{:S(2)}, u32[]{:S(2)}) %collective-permute-start.10) | collective-permute-done | bytes 155680 | tf_op jit(solution)/shard_map/ppermute | solution.py:490
  49.7 1.9 %shard_map.46 = (f32[304,256]{1,0:T(8,128)S(1)}, f32[304,256]{1,0:T(8,128)S(1)}, f32[304,256]{1,0:T(8,128)S(1)}, f32[152,256]{1,0:T(8,128)S(1)}) custom-call(s32[1]{0:T(128)} %bitcast.2.code_ref, f32[304,256]{1,0:T(8,128)S(1)} %get-tuple-element.55.mine_ref, f32[304,256]{1,0:T(8,128)S(1)} %collective-permute-done.7.here_ref, ...), custom_call_target="tpu_custom_call" | custom-call | flops 717225984 | bytes 1048576 | tf_op jit(solution)/shard_map/pallas_call | solution.py:337
  51.6 5.1 %collective-permute-start.11 = (f32[152,256]{1,0:T(8,128)S(1)}, f32[152,256]{1,0:T(8,128)S(1)}, u32[]{:S(2)}, u32[]{:S(2)}) collective-permute-start(f32[152,256]{1,0:T(8,128)S(1)} %get-tuple-element.61), channel_id=1, source_target_pairs={{0,56},{4,60},{8,48},{12,52},{16,40},{20,44},{24,32},{28,36},{32,2... | collective-permute-start | bytes 466952 | tf_op jit(solution)/shard_map/ppermute | solution.py:490
  56.7 7.8 %collective-permute-done.11.refs_1_ = f32[152,256]{1,0:T(8,128)S(1)} collective-permute-done((f32[152,256]{1,0:T(8,128)S(1)}, f32[152,256]{1,0:T(8,128)S(1)}, u32[]{:S(2)}, u32[]{:S(2)}) %collective-permute-start.11) | collective-permute-done | bytes 155680 | tf_op jit(solution)/shard_map/ppermute | solution.py:490
  64.5 1.4 %collective-permute-done.12.refs_2_ = f32[152,256]{1,0:T(8,128)S(1)} collective-permute-done((f32[152,256]{1,0:T(8,128)S(1)}, f32[152,256]{1,0:T(8,128)S(1)}, u32[]{:S(2)}, u32[]{:S(2)}) %collective-permute-start.12) | collective-permute-done | bytes 155680 | tf_op jit(solution)/shard_map/ppermute | solution.py:490
  66.2 1.3 %collective-permute-start.16 = (f32[304,256]{1,0:T(8,128)S(1)}, f32[304,256]{1,0:T(8,128)S(1)}, u32[]{:S(2)}, u32[]{:S(2)}) collective-permute-start(f32[304,256]{1,0:T(8,128)S(1)} %shard_map.51.map_ref), channel_id=1, source_target_pairs={{128,192},{132,196},{136,200},{140,204},{144,208},{148,212},{152,2... | collective-permute-start | bytes 933896 | tf_op jit(solution)/shard_map/ppermute | solution.py:544
  68.5 1.3 %collective-permute-start.14 = (f32[32,256]{1,0:T(8,128)S(1)}, f32[32,256]{1,0:T(8,128)S(1)}, u32[]{:S(2)}, u32[]{:S(2)}) collective-permute-start(f32[32,256]{1,0:T(8,128)S(1)} %shard_map.52), channel_id=1, source_target_pairs={{64,192},{68,196},{72,200},{76,204},{80,208},{84,212},{88,216},{92... | collective-permute-start | bytes 98312 | tf_op jit(solution)/shard_map/ppermute | solution.py:544
  70.5 7.1 %collective-permute-done.16.beside_ref = f32[304,256]{1,0:T(8,128)S(1)} collective-permute-done((f32[304,256]{1,0:T(8,128)S(1)}, f32[304,256]{1,0:T(8,128)S(1)}, u32[]{:S(2)}, u32[]{:S(2)}) %collective-permute-start.16) | collective-permute-done | bytes 311328 | tf_op jit(solution)/shard_map/ppermute | solution.py:544
  78.2 2.7 %shard_map.54 = (f32[8,8,256]{2,1,0:T(8,128)S(1)}, f32[8,8,256]{2,1,0:T(8,128)S(1)}, f32[8,8,256]{2,1,0:T(8,128)S(1)}, f32[8,8,256]{2,1,0:T(8,128)S(1)}) custom-call(s32[1]{0:T(128)} %bitcast.code_ref, f32[32,256]{1,0:T(8,128)S(1)} %collective-permute-done.14.one_ref, f32[32,256]{1,0:T(8,128)S(1)} %collective-permute-done.15.two_ref, ...), custom_call_target="tpu_custom_call" | custom-call | flops 226492416 | bytes 1048576 | tf_op jit(solution)/shard_map/pallas_call | solution.py:462
  81.1 4.2 %collective-permute-start.18 = (f32[8,8,256]{2,1,0:T(8,128)S(1)}, f32[8,8,256]{2,1,0:T(8,128)S(1)}, u32[]{:S(2)}, u32[]{:S(2)}) collective-permute-start(f32[8,8,256]{2,1,0:T(8,128)S(1)} %get-tuple-element.75), channel_id=1, source_target_pairs={{0,2},{1,3},{2,0},{3,1},{4,6},{5,7},{6,4},{7,5},{8,10},{9,11},{10,... | collective-permute-start | bytes 196616 | tf_op jit(solution)/shard_map/ppermute | solution.py:490
  86.0 2.2 %collective-permute-done.18.refs_2_ = f32[8,8,256]{2,1,0:T(8,128)S(1)} collective-permute-done((f32[8,8,256]{2,1,0:T(8,128)S(1)}, f32[8,8,256]{2,1,0:T(8,128)S(1)}, u32[]{:S(2)}, u32[]{:S(2)}) %collective-permute-start.18) | collective-permute-done | bytes 65568 | tf_op jit(solution)/shard_map/ppermute | solution.py:490
  88.2 2.5 %collective-permute-done.19.refs_3_ = f32[8,8,256]{2,1,0:T(8,128)S(1)} collective-permute-done((f32[8,8,256]{2,1,0:T(8,128)S(1)}, f32[8,8,256]{2,1,0:T(8,128)S(1)}, u32[]{:S(2)}, u32[]{:S(2)}) %collective-permute-start.19) | collective-permute-done | bytes 65568 | tf_op jit(solution)/shard_map/ppermute | solution.py:490
  (41 shorter events, 9.4 us)
Async XLA Ops:
  0.0 0.9 %copy-start.1 = (f32[8,32,256]{2,1,0:T(8,128)S(1)}, f32[8,32,256]{2,1,0:T(8,128)}, u32[]{:S(2)}) copy-start(f32[8,32,256]{2,1,0:T(8,128)} %forcing_ref.1) | copy-start | bytes 786436
  1.0 10.3 %collective-permute-start = (f32[8,8,256]{2,1,0:T(8,128)S(1)}, f32[8,8,256]{2,1,0:T(8,128)S(1)}, u32[]{:S(2)}, u32[]{:S(2)}) collective-permute-start(f32[8,8,256]{2,1,0:T(8,128)S(1)} %get-tuple-element.42), channel_id=1, source_target_pairs={{0,1},{1,0},{2,3},{3,2},{4,5},{5,4},{6,7},{7,6},{8,9},{9,8},{10,11... | collective-permute-start | bytes 196616 | tf_op jit(solution)/shard_map/ppermute | solution.py:490
  2.6 8.6 %collective-permute-start.1 = (f32[8,8,256]{2,1,0:T(8,128)S(1)}, f32[8,8,256]{2,1,0:T(8,128)S(1)}, u32[]{:S(2)}, u32[]{:S(2)}) collective-permute-start(f32[8,8,256]{2,1,0:T(8,128)S(1)} %get-tuple-element.43), channel_id=1, source_target_pairs={{0,2},{1,3},{2,0},{3,1},{4,6},{5,7},{6,4},{7,5},{8,10},{9,11},{10,... | collective-permute-start | bytes 196616 | tf_op jit(solution)/shard_map/ppermute | solution.py:490
  5.5 6.3 %copy-start = (f32[8,256,256]{2,1,0:T(8,128)S(1)}, f32[8,256,256]{2,1,0:T(8,128)}, u32[]{:S(2)}) copy-start(f32[8,256,256]{2,1,0:T(8,128)} %blocks_ref.3) | copy-start | bytes 6291460
  5.5 5.7 %collective-permute-start.2 = (f32[8,8,256]{2,1,0:T(8,128)S(1)}, f32[8,8,256]{2,1,0:T(8,128)S(1)}, u32[]{:S(2)}, u32[]{:S(2)}) collective-permute-start(f32[8,8,256]{2,1,0:T(8,128)S(1)} %get-tuple-element.44), channel_id=1, source_target_pairs={{0,3},{1,2},{2,1},{3,0},{4,7},{5,6},{6,5},{7,4},{8,11},{9,10},{10,... | collective-permute-start | bytes 196616 | tf_op jit(solution)/shard_map/ppermute | solution.py:490
  5.8 0.8 copy-start.2
  11.3 8.4 %collective-permute-start.3 = (f32[272,256]{1,0:T(8,128)S(1)}, f32[272,256]{1,0:T(8,128)S(1)}, u32[]{:S(2)}, u32[]{:S(2)}) collective-permute-start(f32[272,256]{1,0:T(8,128)S(1)} %get-tuple-element.46.refs_0_), channel_id=1, source_target_pairs={{0,1},{1,0},{2,3},{3,2},{4,5},{5,4},{6,7},{7,6},{8,9},{9,8},{10,11... | collective-permute-start | bytes 835592 | tf_op jit(solution)/shard_map/ppermute | solution.py:490
  13.8 6.0 %collective-permute-start.4 = (f32[32,256]{1,0:T(8,128)S(1)}, f32[32,256]{1,0:T(8,128)S(1)}, u32[]{:S(2)}, u32[]{:S(2)}) collective-permute-start(f32[32,256]{1,0:T(8,128)S(1)} %get-tuple-element.51.refs_1_), channel_id=1, source_target_pairs={{0,1},{1,0},{2,3},{3,2},{4,5},{5,4},{6,7},{7,6},{8,9},{9,8},{10,11... | collective-permute-start | bytes 98312 | tf_op jit(solution)/shard_map/ppermute | solution.py:490
  20.4 8.7 %collective-permute-start.5 = (f32[304,256]{1,0:T(8,128)S(1)}, f32[304,256]{1,0:T(8,128)S(1)}, u32[]{:S(2)}, u32[]{:S(2)}) collective-permute-start(f32[304,256]{1,0:T(8,128)S(1)} %shard_map.40.refs_0_), channel_id=1, source_target_pairs={{0,3},{1,2},{2,1},{3,0},{4,7},{5,6},{6,5},{7,4},{8,11},{9,10},{10,... | collective-permute-start | bytes 933896 | tf_op jit(solution)/shard_map/ppermute | solution.py:490
  29.8 1.7 %collective-permute-start.6 = (f32[304,256]{1,0:T(8,128)S(1)}, f32[304,256]{1,0:T(8,128)S(1)}, u32[]{:S(2)}, u32[]{:S(2)}) collective-permute-start(f32[304,256]{1,0:T(8,128)S(1)} %shard_map.42.refs_0_), channel_id=1, source_target_pairs={{0,4},{4,0},{8,12},{12,8},{16,20},{20,16},{24,28},{28,24},{32,36},... | collective-permute-start | bytes 933896 | tf_op jit(solution)/shard_map/ppermute | solution.py:490
  32.2 15.7 %collective-permute-start.7 = (f32[304,256]{1,0:T(8,128)S(1)}, f32[304,256]{1,0:T(8,128)S(1)}, u32[]{:S(2)}, u32[]{:S(2)}) collective-permute-start(f32[304,256]{1,0:T(8,128)S(1)} %get-tuple-element.55.mine_ref), channel_id=1, source_target_pairs={{0,8},{4,20},{8,0},{12,28},{16,24},{20,4},{24,16},{28,12},{32,40},... | collective-permute-start | bytes 933896 | tf_op jit(solution)/shard_map/ppermute | solution.py:505
  34.2 13.7 %collective-permute-start.8 = (f32[152,256]{1,0:T(8,128)S(1)}, f32[152,256]{1,0:T(8,128)S(1)}, u32[]{:S(2)}, u32[]{:S(2)}) collective-permute-start(f32[152,256]{1,0:T(8,128)S(1)} %get-tuple-element.56), channel_id=1, source_target_pairs={{0,24},{4,28},{8,16},{12,20},{16,8},{20,12},{24,0},{28,4},{32,56},... | collective-permute-start | bytes 466952 | tf_op jit(solution)/shard_map/ppermute | solution.py:490
  47.9 1.8 %collective-permute-start.9 = (f32[304,256]{1,0:T(8,128)S(1)}, f32[304,256]{1,0:T(8,128)S(1)}, u32[]{:S(2)}, u32[]{:S(2)}) collective-permute-start(f32[304,256]{1,0:T(8,128)S(1)} %collective-permute-done.7.here_ref), channel_id=1, source_target_pairs={{0,4},{4,0},{8,12},{12,8},{16,20},{20,16},{24,28},{28,24},{32,36},... | collective-permute-start | bytes 933896 | tf_op jit(solution)/shard_map/ppermute | solution.py:490
  48.1 1.6 %collective-permute-start.10 = (f32[152,256]{1,0:T(8,128)S(1)}, f32[152,256]{1,0:T(8,128)S(1)}, u32[]{:S(2)}, u32[]{:S(2)}) collective-permute-start(f32[152,256]{1,0:T(8,128)S(1)} %collective-permute-done.8.this_ref), channel_id=1, source_target_pairs={{0,4},{4,0},{8,12},{12,8},{16,20},{20,16},{24,28},{28,24},{32,36},... | collective-permute-start | bytes 466952 | tf_op jit(solution)/shard_map/ppermute | solution.py:490
  51.6 13.0 %collective-permute-start.11 = (f32[152,256]{1,0:T(8,128)S(1)}, f32[152,256]{1,0:T(8,128)S(1)}, u32[]{:S(2)}, u32[]{:S(2)}) collective-permute-start(f32[152,256]{1,0:T(8,128)S(1)} %get-tuple-element.61), channel_id=1, source_target_pairs={{0,56},{4,60},{8,48},{12,52},{16,40},{20,44},{24,32},{28,36},{32,2... | collective-permute-start | bytes 466952 | tf_op jit(solution)/shard_map/ppermute | solution.py:490
  64.5 1.4 %collective-permute-start.12 = (f32[152,256]{1,0:T(8,128)S(1)}, f32[152,256]{1,0:T(8,128)S(1)}, u32[]{:S(2)}, u32[]{:S(2)}) collective-permute-start(f32[152,256]{1,0:T(8,128)S(1)} %collective-permute-done.11.refs_1_), channel_id=1, source_target_pairs={{0,4},{4,0},{8,12},{12,8},{16,20},{20,16},{24,28},{28,24},{32,36},... | collective-permute-start | bytes 466952 | tf_op jit(solution)/shard_map/ppermute | solution.py:490
  66.2 11.3 %collective-permute-start.16 = (f32[304,256]{1,0:T(8,128)S(1)}, f32[304,256]{1,0:T(8,128)S(1)}, u32[]{:S(2)}, u32[]{:S(2)}) collective-permute-start(f32[304,256]{1,0:T(8,128)S(1)} %shard_map.51.map_ref), channel_id=1, source_target_pairs={{128,192},{132,196},{136,200},{140,204},{144,208},{148,212},{152,2... | collective-permute-start | bytes 933896 | tf_op jit(solution)/shard_map/ppermute | solution.py:544
  67.5 0.7 collective-permute-start.13
  68.5 9.7 %collective-permute-start.14 = (f32[32,256]{1,0:T(8,128)S(1)}, f32[32,256]{1,0:T(8,128)S(1)}, u32[]{:S(2)}, u32[]{:S(2)}) collective-permute-start(f32[32,256]{1,0:T(8,128)S(1)} %shard_map.52), channel_id=1, source_target_pairs={{64,192},{68,196},{72,200},{76,204},{80,208},{84,212},{88,216},{92... | collective-permute-start | bytes 98312 | tf_op jit(solution)/shard_map/ppermute | solution.py:544
  69.8 8.4 %collective-permute-start.15 = (f32[32,256]{1,0:T(8,128)S(1)}, f32[32,256]{1,0:T(8,128)S(1)}, u32[]{:S(2)}, u32[]{:S(2)}) collective-permute-start(f32[32,256]{1,0:T(8,128)S(1)} %shard_map.52), channel_id=1, source_target_pairs={{64,128},{68,132},{72,136},{76,140},{80,144},{84,148},{88,152},{92... | collective-permute-start | bytes 98312 | tf_op jit(solution)/shard_map/ppermute | solution.py:544
  81.0 5.0 %collective-permute-start.17 = (f32[8,8,256]{2,1,0:T(8,128)S(1)}, f32[8,8,256]{2,1,0:T(8,128)S(1)}, u32[]{:S(2)}, u32[]{:S(2)}) collective-permute-start(f32[8,8,256]{2,1,0:T(8,128)S(1)} %get-tuple-element.74), channel_id=1, source_target_pairs={{0,1},{1,0},{2,3},{3,2},{4,5},{5,4},{6,7},{7,6},{8,9},{9,8},{10,11... | collective-permute-start | bytes 196616 | tf_op jit(solution)/shard_map/ppermute | solution.py:490
  81.1 7.2 %collective-permute-start.18 = (f32[8,8,256]{2,1,0:T(8,128)S(1)}, f32[8,8,256]{2,1,0:T(8,128)S(1)}, u32[]{:S(2)}, u32[]{:S(2)}) collective-permute-start(f32[8,8,256]{2,1,0:T(8,128)S(1)} %get-tuple-element.75), channel_id=1, source_target_pairs={{0,2},{1,3},{2,0},{3,1},{4,6},{5,7},{6,4},{7,5},{8,10},{9,11},{10,... | collective-permute-start | bytes 196616 | tf_op jit(solution)/shard_map/ppermute | solution.py:490
  85.2 5.5 %collective-permute-start.19 = (f32[8,8,256]{2,1,0:T(8,128)S(1)}, f32[8,8,256]{2,1,0:T(8,128)S(1)}, u32[]{:S(2)}, u32[]{:S(2)}) collective-permute-start(f32[8,8,256]{2,1,0:T(8,128)S(1)} %get-tuple-element.76), channel_id=1, source_target_pairs={{0,3},{1,2},{2,1},{3,0},{4,7},{5,6},{6,5},{7,4},{8,11},{9,10},{10,... | collective-permute-start | bytes 196616 | tf_op jit(solution)/shard_map/ppermute | solution.py:490

commit v9 on v8

--- a/solution.py
+++ b/solution.py
@@ -36,12 +36,6 @@
     return high, (a - high.astype(F32)).astype(jnp.bfloat16)
 
 
-def dot3(a, b):
-    product = functools.partial(jnp.dot, preferred_element_type=F32)
-    (a_high, a_low), (b_high, b_low) = split(a), split(b)
-    return product(a_high, b_high) + (product(a_high, b_low) + product(a_low, b_high))
-
-
 def shape(*dims):
     return jax.ShapeDtypeStruct(dims, F32)
 
@@ -114,14 +108,20 @@
     made_ref[0] = first
     block_copy(made_ref, prefix_ref, left, 0).start()
 
-    @pl.loop(1, cells)
-    def _(cell):
+    def extend_by(cell):
         scaled = last_ref[...] * -upstream_ref[pl.ds(cell, 1), :]
         block_copy(blocks_ref, held_ref, arrived, cell).wait()
         product = dot(scaled, held_ref[cell])
         last_ref[...] = product
         made_ref[cell] = product
         block_copy(made_ref, prefix_ref, left, cell).start()
+
+    extend_by(1)
+
+    @pl.loop(1, cells // 2)
+    def _(pair):
+        extend_by(2 * pair)
+        extend_by(2 * pair + 1)
 
     put_map(last_ref[...], jnp.zeros((8, levels), F32), map_ref)
 
@@ -185,12 +185,14 @@
         forcing_ref[pl.ds((code_ref[0] ^ turn) * share, share)] = part_ref[...]
     states_ref[...] = jnp.zeros_like(states_ref)
 
-    @pl.loop(0, blocks_ref.shape[0])
-    def _(cell):
-        forced = forcing_ref[:, cell, :] - upstream_ref[pl.ds(cell, 1), :] * states_ref[...]
-        state = dot(forced, blocks_ref[cell])
+    @pl.loop(0, blocks_ref.shape[0] // 2)
+    def _(pair):
+        state = states_ref[...]
+        for cell in (2 * pair, 2 * pair + 1):
+            forced = forcing_ref[:, cell, :] - upstream_ref[pl.ds(cell, 1), :] * state
+            state = dot(forced, blocks_ref[cell])
+            trial_ref[cell] = state
         states_ref[...] = state
-        trial_ref[cell] = state
 
 
 def trial_states(here, blocks, upstream, parts):
@@ -445,12 +447,21 @@
     fetch(prefix_ref, held_ref, arrived)
     start = before_ref.shape[1] + PAD
     entering = one_ref[...] + two_ref[...]
-    incoming[...] = move_states(entering, before_ref) + before_ref[start:]
-
-    @pl.loop(0, held_ref.shape[0])
-    def _(cell):
-        block_copy(prefix_ref, held_ref, arrived, cell).wait()
-        solved_ref[:, cell, :] = trial_ref[cell] + dot3(incoming[...], held_ref[cell])
+    high, low = split(move_states(entering, before_ref) + before_ref[start:])
+    lines = high.shape[0]
+    incoming[:lines] = high
+    incoming[lines:] = low
+    product = functools.partial(jnp.dot, preferred_element_type=F32)
+
+    @pl.loop(0, held_ref.shape[0] // 2)
+    def _(pair):
+        for turn in range(2):
+            cell = 2 * pair + turn
+            block_copy(prefix_ref, held_ref, arrived, cell).wait()
+            map_high, map_low = split(held_ref[cell])
+            both = product(incoming[...], map_high)
+            rest = both[lines:] + product(incoming[:lines], map_low)
+            solved_ref[:, cell, :] = trial_ref[cell] + (both[:lines] + rest)
 
     share = part_refs[0].shape[0]
     for turn, part_ref in enumerate(part_refs):
@@ -467,7 +478,7 @@
         [
             pltpu.VMEM((lines, cells, levels), F32),
             pltpu.VMEM(prefix.shape, F32),
-            pltpu.VMEM((lines, levels), F32),
+            pltpu.VMEM((2 * lines, levels), jnp.bfloat16),
             pltpu.SemaphoreType.DMA((cells,)),
         ],
         None,

time: 92 us -> 93 us (1.011)
  Pallas kernels: 15.3 us -> 16.8 us
    pallas_call x1, Pallas kernels: 4.67 us -> 5.69 us  [prefix_maps(): call(maps_kernel, [VMEM, HBM], [shape(*blocks.shape), shape(levels + PAD,...]
  transfers between devices with their start and end apart: 20 -> 20, of which waited for: 11 -> 11; matrix products, arithmetic and copies ran while one was open for 0% -> 0% of each run, Pallas kernels for 8% -> 10%
where the time goes in v9:
time: 93 us; the launch traced here: 92.4 us
  waiting for transfers between devices  44.6 us (48%)
  starting transfers between devices  29 us (31%)
  Pallas kernels  16.8 us (18%)
  local copies, waits for them, and re-layouts  1.77 us (2%)
    ppermute x15, waiting for transfers between devices, partner(): return lax.ppermute(value, axis, [(i, i ^ mask) for i in range(count)])  37.5 us
    ppermute x15, starting transfers between devices, partner(): return lax.ppermute(value, axis, [(i, i ^ mask) for i in range(count)])  23.1 us
    ppermute x4, waiting for transfers between devices, across(): return lax.ppermute(value, 'line', pairs)  7.07 us
    pallas_call x1, Pallas kernels, prefix_maps(): call(maps_kernel, [VMEM, HBM], [shape(*blocks.shape), shape(levels + PAD,...  5.69 us
    ppermute x4, starting transfers between devices, across(): return lax.ppermute(value, 'line', pairs)  3.91 us
    pallas_call x1, Pallas kernels, finish(): call(finish_kernel, [SMEM, VMEM, VMEM, VMEM, HBM, VMEM], [shape(lines //...  2.66 us
    pallas_call x1, Pallas kernels, trial_states(): call(states_kernel, [SMEM] + [VMEM] * (2 + len(parts)), [shape(cells, lin...  2.52 us
    pallas_call x4, Pallas kernels, merge(): call(functools.partial(merge_kernel, start, kind, apart, halves, half), [...  2.26 us
  transfers between devices with their start and end apart: 20, of which 11 were waited for; matrix products, arithmetic and copies ran while one was open for 0% of the time, Pallas kernels for 10%

profile of v9, /device:TPU:6, one launch (start us, length us, event | category | flops | bytes accessed | tf_op | source)
XLA Modules:
  0.0 92.4 jit_solution(16289014305482568554)
XLA Ops:
  1.0 1.7 %collective-permute-start = (f32[8,8,256]{2,1,0:T(8,128)S(1)}, f32[8,8,256]{2,1,0:T(8,128)S(1)}, u32[]{:S(2)}, u32[]{:S(2)}) collective-permute-start(f32[8,8,256]{2,1,0:T(8,128)S(1)} %get-tuple-element.42), channel_id=1, source_target_pairs={{0,1},{1,0},{2,3},{3,2},{4,5},{5,4},{6,7},{7,6},{8,9},{9,8},{10,11... | collective-permute-start | bytes 196616 | tf_op jit(solution)/shard_map/ppermute | solution.py:501
  2.6 2.9 %collective-permute-start.1 = (f32[8,8,256]{2,1,0:T(8,128)S(1)}, f32[8,8,256]{2,1,0:T(8,128)S(1)}, u32[]{:S(2)}, u32[]{:S(2)}) collective-permute-start(f32[8,8,256]{2,1,0:T(8,128)S(1)} %get-tuple-element.43), channel_id=1, source_target_pairs={{0,2},{1,3},{2,0},{3,1},{4,6},{5,7},{6,4},{7,5},{8,10},{9,11},{10,... | collective-permute-start | bytes 196616 | tf_op jit(solution)/shard_map/ppermute | solution.py:501
  6.6 5.7 %shard_map.38 = (f32[8,256,256]{2,1,0:T(8,128)}, f32[272,256]{1,0:T(8,128)S(1)}) custom-call(f32[8,256]{1,0:T(8,128)S(1)} %copy-done.2, f32[8,256,256]{2,1,0:T(8,128)} %blocks_ref.3), custom_call_target="tpu_custom_call" | custom-call | flops 1610612736 | bytes 1048576 | tf_op jit(solution)/shard_map/pallas_call | solution.py:135
  12.8 2.5 %shard_map.39 = (f32[8,32,256]{2,1,0:T(8,128)S(1)}, f32[32,256]{1,0:T(8,128)S(1)}) custom-call(s32[1]{0:T(128)} %bitcast.code_ref, f32[8,256]{1,0:T(8,128)S(1)} %copy-done.2, f32[8,256,256]{2,1,0:T(8,128)S(1)} %copy-done, f32[8,8,256]{2,1,0:T(8,128)S(1)} %get-tuple-element.47.refs_0_, f32[8,8,256]{2,1,0:T(8,128)S(1)} %collective-permute-done.refs_1_, ...), custom_call_target="tpu_custom_call" | custom-call | flops 201326592 | bytes 1048576 | tf_op jit(solution)/shard_map/pallas_call | solution.py:201
  15.3 1.6 %collective-permute-start.4 = (f32[32,256]{1,0:T(8,128)S(1)}, f32[32,256]{1,0:T(8,128)S(1)}, u32[]{:S(2)}, u32[]{:S(2)}) collective-permute-start(f32[32,256]{1,0:T(8,128)S(1)} %get-tuple-element.51.refs_1_), channel_id=1, source_target_pairs={{0,1},{1,0},{2,3},{3,2},{4,5},{5,4},{6,7},{7,6},{8,9},{9,8},{10,11... | collective-permute-start | bytes 98312 | tf_op jit(solution)/shard_map/ppermute | solution.py:501
  16.9 3.8 %collective-permute-done.4.refs_3_.refs_1_ = f32[32,256]{1,0:T(8,128)S(1)} collective-permute-done((f32[32,256]{1,0:T(8,128)S(1)}, f32[32,256]{1,0:T(8,128)S(1)}, u32[]{:S(2)}, u32[]{:S(2)}) %collective-permute-start.4) | collective-permute-done | bytes 32800 | tf_op jit(solution)/shard_map/ppermute | solution.py:501
  21.4 2.9 %collective-permute-start.5 = (f32[304,256]{1,0:T(8,128)S(1)}, f32[304,256]{1,0:T(8,128)S(1)}, u32[]{:S(2)}, u32[]{:S(2)}) collective-permute-start(f32[304,256]{1,0:T(8,128)S(1)} %shard_map.40.refs_0_), channel_id=1, source_target_pairs={{0,3},{1,2},{2,1},{3,0},{4,7},{5,6},{6,5},{7,4},{8,11},{9,10},{10,... | collective-permute-start | bytes 933896 | tf_op jit(solution)/shard_map/ppermute | solution.py:501
  24.3 5.8 %collective-permute-done.5.refs_1_.refs_0_ = f32[304,256]{1,0:T(8,128)S(1)} collective-permute-done((f32[304,256]{1,0:T(8,128)S(1)}, f32[304,256]{1,0:T(8,128)S(1)}, u32[]{:S(2)}, u32[]{:S(2)}) %collective-permute-start.5) | collective-permute-done | bytes 311328 | tf_op jit(solution)/shard_map/ppermute | solution.py:501
  31.0 1.5 %collective-permute-done.6.refs_1_.refs_0_ = f32[304,256]{1,0:T(8,128)S(1)} collective-permute-done((f32[304,256]{1,0:T(8,128)S(1)}, f32[304,256]{1,0:T(8,128)S(1)}, u32[]{:S(2)}, u32[]{:S(2)}) %collective-permute-start.6) | collective-permute-done | bytes 311328 | tf_op jit(solution)/shard_map/ppermute | solution.py:501
  33.2 2.0 %collective-permute-start.7 = (f32[304,256]{1,0:T(8,128)S(1)}, f32[304,256]{1,0:T(8,128)S(1)}, u32[]{:S(2)}, u32[]{:S(2)}) collective-permute-start(f32[304,256]{1,0:T(8,128)S(1)} %get-tuple-element.55.mine_ref), channel_id=1, source_target_pairs={{0,8},{4,20},{8,0},{12,28},{16,24},{20,4},{24,16},{28,12},{32,40},... | collective-permute-start | bytes 933896 | tf_op jit(solution)/shard_map/ppermute | solution.py:516
  35.2 2.8 %collective-permute-start.8 = (f32[152,256]{1,0:T(8,128)S(1)}, f32[152,256]{1,0:T(8,128)S(1)}, u32[]{:S(2)}, u32[]{:S(2)}) collective-permute-start(f32[152,256]{1,0:T(8,128)S(1)} %get-tuple-element.56), channel_id=1, source_target_pairs={{0,24},{4,28},{8,16},{12,20},{16,8},{20,12},{24,0},{28,4},{32,56},... | collective-permute-start | bytes 466952 | tf_op jit(solution)/shard_map/ppermute | solution.py:501
  38.0 10.9 %collective-permute-done.8.this_ref = f32[152,256]{1,0:T(8,128)S(1)} collective-permute-done((f32[152,256]{1,0:T(8,128)S(1)}, f32[152,256]{1,0:T(8,128)S(1)}, u32[]{:S(2)}, u32[]{:S(2)}) %collective-permute-start.8) | collective-permute-done | bytes 155680 | tf_op jit(solution)/shard_map/ppermute | solution.py:501
  49.4 1.3 %collective-permute-done.10.that_ref = f32[152,256]{1,0:T(8,128)S(1)} collective-permute-done((f32[152,256]{1,0:T(8,128)S(1)}, f32[152,256]{1,0:T(8,128)S(1)}, u32[]{:S(2)}, u32[]{:S(2)}) %collective-permute-start.10) | collective-permute-done | bytes 155680 | tf_op jit(solution)/shard_map/ppermute | solution.py:501
  50.7 1.9 %shard_map.46 = (f32[304,256]{1,0:T(8,128)S(1)}, f32[304,256]{1,0:T(8,128)S(1)}, f32[304,256]{1,0:T(8,128)S(1)}, f32[152,256]{1,0:T(8,128)S(1)}) custom-call(s32[1]{0:T(128)} %bitcast.2.code_ref, f32[304,256]{1,0:T(8,128)S(1)} %get-tuple-element.55.mine_ref, f32[304,256]{1,0:T(8,128)S(1)} %collective-permute-done.7.here_ref, ...), custom_call_target="tpu_custom_call" | custom-call | flops 717225984 | bytes 1048576 | tf_op jit(solution)/shard_map/pallas_call | solution.py:339
  52.6 5.1 %collective-permute-start.11 = (f32[152,256]{1,0:T(8,128)S(1)}, f32[152,256]{1,0:T(8,128)S(1)}, u32[]{:S(2)}, u32[]{:S(2)}) collective-permute-start(f32[152,256]{1,0:T(8,128)S(1)} %get-tuple-element.61), channel_id=1, source_target_pairs={{0,56},{4,60},{8,48},{12,52},{16,40},{20,44},{24,32},{28,36},{32,2... | collective-permute-start | bytes 466952 | tf_op jit(solution)/shard_map/ppermute | solution.py:501
  57.7 7.8 %collective-permute-done.11.refs_1_ = f32[152,256]{1,0:T(8,128)S(1)} collective-permute-done((f32[152,256]{1,0:T(8,128)S(1)}, f32[152,256]{1,0:T(8,128)S(1)}, u32[]{:S(2)}, u32[]{:S(2)}) %collective-permute-start.11) | collective-permute-done | bytes 155680 | tf_op jit(solution)/shard_map/ppermute | solution.py:501
  65.6 1.4 %collective-permute-done.12.refs_2_ = f32[152,256]{1,0:T(8,128)S(1)} collective-permute-done((f32[152,256]{1,0:T(8,128)S(1)}, f32[152,256]{1,0:T(8,128)S(1)}, u32[]{:S(2)}, u32[]{:S(2)}) %collective-permute-start.12) | collective-permute-done | bytes 155680 | tf_op jit(solution)/shard_map/ppermute | solution.py:501
  67.3 1.3 %collective-permute-start.16 = (f32[304,256]{1,0:T(8,128)S(1)}, f32[304,256]{1,0:T(8,128)S(1)}, u32[]{:S(2)}, u32[]{:S(2)}) collective-permute-start(f32[304,256]{1,0:T(8,128)S(1)} %shard_map.51.map_ref), channel_id=1, source_target_pairs={{128,192},{132,196},{136,200},{140,204},{144,208},{148,212},{152,2... | collective-permute-start | bytes 933896 | tf_op jit(solution)/shard_map/ppermute | solution.py:555
  69.5 1.3 %collective-permute-start.14 = (f32[32,256]{1,0:T(8,128)S(1)}, f32[32,256]{1,0:T(8,128)S(1)}, u32[]{:S(2)}, u32[]{:S(2)}) collective-permute-start(f32[32,256]{1,0:T(8,128)S(1)} %shard_map.52), channel_id=1, source_target_pairs={{64,192},{68,196},{72,200},{76,204},{80,208},{84,212},{88,216},{92... | collective-permute-start | bytes 98312 | tf_op jit(solution)/shard_map/ppermute | solution.py:555
  71.5 7.1 %collective-permute-done.16.beside_ref = f32[304,256]{1,0:T(8,128)S(1)} collective-permute-done((f32[304,256]{1,0:T(8,128)S(1)}, f32[304,256]{1,0:T(8,128)S(1)}, u32[]{:S(2)}, u32[]{:S(2)}) %collective-permute-start.16) | collective-permute-done | bytes 311328 | tf_op jit(solution)/shard_map/ppermute | solution.py:555
  79.2 2.7 %shard_map.54 = (f32[8,8,256]{2,1,0:T(8,128)S(1)}, f32[8,8,256]{2,1,0:T(8,128)S(1)}, f32[8,8,256]{2,1,0:T(8,128)S(1)}, f32[8,8,256]{2,1,0:T(8,128)S(1)}) custom-call(s32[1]{0:T(128)} %bitcast.code_ref, f32[32,256]{1,0:T(8,128)S(1)} %collective-permute-done.14.one_ref, f32[32,256]{1,0:T(8,128)S(1)} %collective-permute-done.15.two_ref, ...), custom_call_target="tpu_custom_call" | custom-call | flops 226492416 | bytes 1048576 | tf_op jit(solution)/shard_map/pallas_call | solution.py:473
  82.0 4.2 %collective-permute-start.18 = (f32[8,8,256]{2,1,0:T(8,128)S(1)}, f32[8,8,256]{2,1,0:T(8,128)S(1)}, u32[]{:S(2)}, u32[]{:S(2)}) collective-permute-start(f32[8,8,256]{2,1,0:T(8,128)S(1)} %get-tuple-element.75), channel_id=1, source_target_pairs={{0,2},{1,3},{2,0},{3,1},{4,6},{5,7},{6,4},{7,5},{8,10},{9,11},{10,... | collective-permute-start | bytes 196616 | tf_op jit(solution)/shard_map/ppermute | solution.py:501
  87.0 2.2 %collective-permute-done.18.refs_2_ = f32[8,8,256]{2,1,0:T(8,128)S(1)} collective-permute-done((f32[8,8,256]{2,1,0:T(8,128)S(1)}, f32[8,8,256]{2,1,0:T(8,128)S(1)}, u32[]{:S(2)}, u32[]{:S(2)}) %collective-permute-start.18) | collective-permute-done | bytes 65568 | tf_op jit(solution)/shard_map/ppermute | solution.py:501
  89.2 2.5 %collective-permute-done.19.refs_3_ = f32[8,8,256]{2,1,0:T(8,128)S(1)} collective-permute-done((f32[8,8,256]{2,1,0:T(8,128)S(1)}, f32[8,8,256]{2,1,0:T(8,128)S(1)}, u32[]{:S(2)}, u32[]{:S(2)}) %collective-permute-start.19) | collective-permute-done | bytes 65568 | tf_op jit(solution)/shard_map/ppermute | solution.py:501
  (41 shorter events, 9.4 us)
Async XLA Ops:
  0.0 0.9 %copy-start.1 = (f32[8,32,256]{2,1,0:T(8,128)S(1)}, f32[8,32,256]{2,1,0:T(8,128)}, u32[]{:S(2)}) copy-start(f32[8,32,256]{2,1,0:T(8,128)} %forcing_ref.1) | copy-start | bytes 786436
  1.0 11.3 %collective-permute-start = (f32[8,8,256]{2,1,0:T(8,128)S(1)}, f32[8,8,256]{2,1,0:T(8,128)S(1)}, u32[]{:S(2)}, u32[]{:S(2)}) collective-permute-start(f32[8,8,256]{2,1,0:T(8,128)S(1)} %get-tuple-element.42), channel_id=1, source_target_pairs={{0,1},{1,0},{2,3},{3,2},{4,5},{5,4},{6,7},{7,6},{8,9},{9,8},{10,11... | collective-permute-start | bytes 196616 | tf_op jit(solution)/shard_map/ppermute | solution.py:501
  2.6 9.6 %collective-permute-start.1 = (f32[8,8,256]{2,1,0:T(8,128)S(1)}, f32[8,8,256]{2,1,0:T(8,128)S(1)}, u32[]{:S(2)}, u32[]{:S(2)}) collective-permute-start(f32[8,8,256]{2,1,0:T(8,128)S(1)} %get-tuple-element.43), channel_id=1, source_target_pairs={{0,2},{1,3},{2,0},{3,1},{4,6},{5,7},{6,4},{7,5},{8,10},{9,11},{10,... | collective-permute-start | bytes 196616 | tf_op jit(solution)/shard_map/ppermute | solution.py:501
  5.5 7.3 %copy-start = (f32[8,256,256]{2,1,0:T(8,128)S(1)}, f32[8,256,256]{2,1,0:T(8,128)}, u32[]{:S(2)}) copy-start(f32[8,256,256]{2,1,0:T(8,128)} %blocks_ref.3) | copy-start | bytes 6291460
  5.5 6.8 %collective-permute-start.2 = (f32[8,8,256]{2,1,0:T(8,128)S(1)}, f32[8,8,256]{2,1,0:T(8,128)S(1)}, u32[]{:S(2)}, u32[]{:S(2)}) collective-permute-start(f32[8,8,256]{2,1,0:T(8,128)S(1)} %get-tuple-element.44), channel_id=1, source_target_pairs={{0,3},{1,2},{2,1},{3,0},{4,7},{5,6},{6,5},{7,4},{8,11},{9,10},{10,... | collective-permute-start | bytes 196616 | tf_op jit(solution)/shard_map/ppermute | solution.py:501
  5.8 0.8 copy-start.2
  12.3 8.4 %collective-permute-start.3 = (f32[272,256]{1,0:T(8,128)S(1)}, f32[272,256]{1,0:T(8,128)S(1)}, u32[]{:S(2)}, u32[]{:S(2)}) collective-permute-start(f32[272,256]{1,0:T(8,128)S(1)} %get-tuple-element.46.refs_0_), channel_id=1, source_target_pairs={{0,1},{1,0},{2,3},{3,2},{4,5},{5,4},{6,7},{7,6},{8,9},{9,8},{10,11... | collective-permute-start | bytes 835592 | tf_op jit(solution)/shard_map/ppermute | solution.py:501
  15.3 5.4 %collective-permute-start.4 = (f32[32,256]{1,0:T(8,128)S(1)}, f32[32,256]{1,0:T(8,128)S(1)}, u32[]{:S(2)}, u32[]{:S(2)}) collective-permute-start(f32[32,256]{1,0:T(8,128)S(1)} %get-tuple-element.51.refs_1_), channel_id=1, source_target_pairs={{0,1},{1,0},{2,3},{3,2},{4,5},{5,4},{6,7},{7,6},{8,9},{9,8},{10,11... | collective-permute-start | bytes 98312 | tf_op jit(solution)/shard_map/ppermute | solution.py:501
  21.4 8.7 %collective-permute-start.5 = (f32[304,256]{1,0:T(8,128)S(1)}, f32[304,256]{1,0:T(8,128)S(1)}, u32[]{:S(2)}, u32[]{:S(2)}) collective-permute-start(f32[304,256]{1,0:T(8,128)S(1)} %shard_map.40.refs_0_), channel_id=1, source_target_pairs={{0,3},{1,2},{2,1},{3,0},{4,7},{5,6},{6,5},{7,4},{8,11},{9,10},{10,... | collective-permute-start | bytes 933896 | tf_op jit(solution)/shard_map/ppermute | solution.py:501
  30.8 1.7 %collective-permute-start.6 = (f32[304,256]{1,0:T(8,128)S(1)}, f32[304,256]{1,0:T(8,128)S(1)}, u32[]{:S(2)}, u32[]{:S(2)}) collective-permute-start(f32[304,256]{1,0:T(8,128)S(1)} %shard_map.42.refs_0_), channel_id=1, source_target_pairs={{0,4},{4,0},{8,12},{12,8},{16,20},{20,16},{24,28},{28,24},{32,36},... | collective-permute-start | bytes 933896 | tf_op jit(solution)/shard_map/ppermute | solution.py:501
  33.2 15.7 %collective-permute-start.7 = (f32[304,256]{1,0:T(8,128)S(1)}, f32[304,256]{1,0:T(8,128)S(1)}, u32[]{:S(2)}, u32[]{:S(2)}) collective-permute-start(f32[304,256]{1,0:T(8,128)S(1)} %get-tuple-element.55.mine_ref), channel_id=1, source_target_pairs={{0,8},{4,20},{8,0},{12,28},{16,24},{20,4},{24,16},{28,12},{32,40},... | collective-permute-start | bytes 933896 | tf_op jit(solution)/shard_map/ppermute | solution.py:516
  35.2 13.7 %collective-permute-start.8 = (f32[152,256]{1,0:T(8,128)S(1)}, f32[152,256]{1,0:T(8,128)S(1)}, u32[]{:S(2)}, u32[]{:S(2)}) collective-permute-start(f32[152,256]{1,0:T(8,128)S(1)} %get-tuple-element.56), channel_id=1, source_target_pairs={{0,24},{4,28},{8,16},{12,20},{16,8},{20,12},{24,0},{28,4},{32,56},... | collective-permute-start | bytes 466952 | tf_op jit(solution)/shard_map/ppermute | solution.py:501
  48.9 1.8 %collective-permute-start.9 = (f32[304,256]{1,0:T(8,128)S(1)}, f32[304,256]{1,0:T(8,128)S(1)}, u32[]{:S(2)}, u32[]{:S(2)}) collective-permute-start(f32[304,256]{1,0:T(8,128)S(1)} %collective-permute-done.7.here_ref), channel_id=1, source_target_pairs={{0,4},{4,0},{8,12},{12,8},{16,20},{20,16},{24,28},{28,24},{32,36},... | collective-permute-start | bytes 933896 | tf_op jit(solution)/shard_map/ppermute | solution.py:501
  49.1 1.6 %collective-permute-start.10 = (f32[152,256]{1,0:T(8,128)S(1)}, f32[152,256]{1,0:T(8,128)S(1)}, u32[]{:S(2)}, u32[]{:S(2)}) collective-permute-start(f32[152,256]{1,0:T(8,128)S(1)} %collective-permute-done.8.this_ref), channel_id=1, source_target_pairs={{0,4},{4,0},{8,12},{12,8},{16,20},{20,16},{24,28},{28,24},{32,36},... | collective-permute-start | bytes 466952 | tf_op jit(solution)/shard_map/ppermute | solution.py:501
  52.6 13.0 %collective-permute-start.11 = (f32[152,256]{1,0:T(8,128)S(1)}, f32[152,256]{1,0:T(8,128)S(1)}, u32[]{:S(2)}, u32[]{:S(2)}) collective-permute-start(f32[152,256]{1,0:T(8,128)S(1)} %get-tuple-element.61), channel_id=1, source_target_pairs={{0,56},{4,60},{8,48},{12,52},{16,40},{20,44},{24,32},{28,36},{32,2... | collective-permute-start | bytes 466952 | tf_op jit(solution)/shard_map/ppermute | solution.py:501
  65.6 1.4 %collective-permute-start.12 = (f32[152,256]{1,0:T(8,128)S(1)}, f32[152,256]{1,0:T(8,128)S(1)}, u32[]{:S(2)}, u32[]{:S(2)}) collective-permute-start(f32[152,256]{1,0:T(8,128)S(1)} %collective-permute-done.11.refs_1_), channel_id=1, source_target_pairs={{0,4},{4,0},{8,12},{12,8},{16,20},{20,16},{24,28},{28,24},{32,36},... | collective-permute-start | bytes 466952 | tf_op jit(solution)/shard_map/ppermute | solution.py:501
  67.3 11.3 %collective-permute-start.16 = (f32[304,256]{1,0:T(8,128)S(1)}, f32[304,256]{1,0:T(8,128)S(1)}, u32[]{:S(2)}, u32[]{:S(2)}) collective-permute-start(f32[304,256]{1,0:T(8,128)S(1)} %shard_map.51.map_ref), channel_id=1, source_target_pairs={{128,192},{132,196},{136,200},{140,204},{144,208},{148,212},{152,2... | collective-permute-start | bytes 933896 | tf_op jit(solution)/shard_map/ppermute | solution.py:555
  68.6 0.7 collective-permute-start.13
  69.5 9.7 %collective-permute-start.14 = (f32[32,256]{1,0:T(8,128)S(1)}, f32[32,256]{1,0:T(8,128)S(1)}, u32[]{:S(2)}, u32[]{:S(2)}) collective-permute-start(f32[32,256]{1,0:T(8,128)S(1)} %shard_map.52), channel_id=1, source_target_pairs={{64,192},{68,196},{72,200},{76,204},{80,208},{84,212},{88,216},{92... | collective-permute-start | bytes 98312 | tf_op jit(solution)/shard_map/ppermute | solution.py:555
  70.8 8.4 %collective-permute-start.15 = (f32[32,256]{1,0:T(8,128)S(1)}, f32[32,256]{1,0:T(8,128)S(1)}, u32[]{:S(2)}, u32[]{:S(2)}) collective-permute-start(f32[32,256]{1,0:T(8,128)S(1)} %shard_map.52), channel_id=1, source_target_pairs={{64,128},{68,132},{72,136},{76,140},{80,144},{84,148},{88,152},{92... | collective-permute-start | bytes 98312 | tf_op jit(solution)/shard_map/ppermute | solution.py:555
  81.9 5.0 %collective-permute-start.17 = (f32[8,8,256]{2,1,0:T(8,128)S(1)}, f32[8,8,256]{2,1,0:T(8,128)S(1)}, u32[]{:S(2)}, u32[]{:S(2)}) collective-permute-start(f32[8,8,256]{2,1,0:T(8,128)S(1)} %get-tuple-element.74), channel_id=1, source_target_pairs={{0,1},{1,0},{2,3},{3,2},{4,5},{5,4},{6,7},{7,6},{8,9},{9,8},{10,11... | collective-permute-start | bytes 196616 | tf_op jit(solution)/shard_map/ppermute | solution.py:501
  82.0 7.2 %collective-permute-start.18 = (f32[8,8,256]{2,1,0:T(8,128)S(1)}, f32[8,8,256]{2,1,0:T(8,128)S(1)}, u32[]{:S(2)}, u32[]{:S(2)}) collective-permute-start(f32[8,8,256]{2,1,0:T(8,128)S(1)} %get-tuple-element.75), channel_id=1, source_target_pairs={{0,2},{1,3},{2,0},{3,1},{4,6},{5,7},{6,4},{7,5},{8,10},{9,11},{10,... | collective-permute-start | bytes 196616 | tf_op jit(solution)/shard_map/ppermute | solution.py:501
  86.2 5.5 %collective-permute-start.19 = (f32[8,8,256]{2,1,0:T(8,128)S(1)}, f32[8,8,256]{2,1,0:T(8,128)S(1)}, u32[]{:S(2)}, u32[]{:S(2)}) collective-permute-start(f32[8,8,256]{2,1,0:T(8,128)S(1)} %get-tuple-element.76), channel_id=1, source_target_pairs={{0,3},{1,2},{2,1},{3,0},{4,7},{5,6},{6,5},{7,4},{8,11},{9,10},{10,... | collective-permute-start | bytes 196616 | tf_op jit(solution)/shard_map/ppermute | solution.py:501

commit v10 on v8

--- a/solution.py
+++ b/solution.py
@@ -81,7 +81,7 @@
 def join_maps(left_ref, right_ref, out_ref):
     levels = out_ref.shape[1]
     count = left_ref[levels : levels + 8] + right_ref[levels : levels + 8]
-    put_map(dot(left_ref[:levels], right_ref[:levels]), count, out_ref)
+    put_map(dot3(left_ref[:levels], right_ref[:levels]), count, out_ref)
 
 
 def move_states(states, map_ref):
@@ -314,7 +314,7 @@
 
 def four_kernel(
     code_ref, mine_ref, here_ref, there_ref, this_ref, that_ref,
-    total_ref, beside_ref, front_ref, half_ref, four_ref, back_ref,
+    total_ref, beside_ref, front_ref, half_ref, four_ref,
 ):
     core = lax.rem(code_ref[0], 2)
     place = code_ref[0] // 2
@@ -324,10 +324,14 @@
     four_ref[place ^ (2 - core)] = there_ref[...]
     four_ref[place ^ 3, pl.ds(core * rows, rows)] = this_ref[...]
     four_ref[place ^ 3, pl.ds((1 - core) * rows, rows)] = that_ref[...]
-    join(four_ref.at[0], four_ref.at[1], front_ref)
-    join(four_ref.at[2], four_ref.at[3], back_ref)
-    join(front_ref, back_ref, total_ref)
-    half_ref[...] = total_ref[pl.ds(core * rows, rows)]
+
+    @pl.loop(0, 3)
+    def _(turn):
+        join(four_ref.at[2 * turn], four_ref.at[2 * turn + 1], four_ref.at[4 + turn])
+
+    front_ref[...] = four_ref[4]
+    total_ref[...] = four_ref[6]
+    half_ref[...] = four_ref[6, pl.ds(core * rows, rows)]
     beside_ref[...] = four_ref[place ^ 1]
 
 
@@ -339,7 +343,7 @@
         [SMEM] + [VMEM] * 5,
         [whole, whole, whole, shape(rows // 2, levels)],
         36 * rows * levels**2,
-        [pltpu.VMEM((4, rows, levels), F32), pltpu.VMEM((rows, levels), F32)],
+        [pltpu.VMEM((7, rows, levels), F32)],
     )(code, mine, here, there, this, that)
 
 
@@ -445,12 +449,19 @@
     fetch(prefix_ref, held_ref, arrived)
     start = before_ref.shape[1] + PAD
     entering = one_ref[...] + two_ref[...]
-    incoming[...] = move_states(entering, before_ref) + before_ref[start:]
+    high, low = split(move_states(entering, before_ref) + before_ref[start:])
+    lines = high.shape[0]
+    incoming[:lines] = high
+    incoming[lines:] = low
+    product = functools.partial(jnp.dot, preferred_element_type=F32)
 
     @pl.loop(0, held_ref.shape[0])
     def _(cell):
         block_copy(prefix_ref, held_ref, arrived, cell).wait()
-        solved_ref[:, cell, :] = trial_ref[cell] + dot3(incoming[...], held_ref[cell])
+        map_high, map_low = split(held_ref[cell])
+        both = product(incoming[...], map_high)
+        rest = both[lines:] + product(incoming[:lines], map_low)
+        solved_ref[:, cell, :] = trial_ref[cell] + (both[:lines] + rest)
 
     share = part_refs[0].shape[0]
     for turn, part_ref in enumerate(part_refs):
@@ -467,7 +478,7 @@
         [
             pltpu.VMEM((lines, cells, levels), F32),
             pltpu.VMEM(prefix.shape, F32),
-            pltpu.VMEM((lines, levels), F32),
+            pltpu.VMEM((2 * lines, levels), jnp.bfloat16),
             pltpu.SemaphoreType.DMA((cells,)),
         ],
         None,

time: 92 us -> 92.2 us (level)
  no operation moved by 1% of the time
where the time goes in v10:
time: 92.2 us; the launch traced here: 91.5 us
  waiting for transfers between devices  45 us (49%)
  starting transfers between devices  29.1 us (32%)
  Pallas kernels  15.4 us (17%)
  local copies, waits for them, and re-layouts  1.77 us (2%)
    ppermute x15, waiting for transfers between devices, partner(): return lax.ppermute(value, axis, [(i, i ^ mask) for i in range(count)])  38 us
    ppermute x15, starting transfers between devices, partner(): return lax.ppermute(value, axis, [(i, i ^ mask) for i in range(count)])  23.2 us
    ppermute x4, waiting for transfers between devices, across(): return lax.ppermute(value, 'line', pairs)  7.07 us
    pallas_call x1, Pallas kernels, prefix_maps(): call(maps_kernel, [VMEM, HBM], [shape(*blocks.shape), shape(levels + PAD,...  4.67 us
    ppermute x4, starting transfers between devices, across(): return lax.ppermute(value, 'line', pairs)  3.91 us
    pallas_call x1, Pallas kernels, join_four(): call(four_kernel, [SMEM] + [VMEM] * 5, [whole, whole, whole, shape(rows /...  2.64 us
    pallas_call x1, Pallas kernels, finish(): call(finish_kernel, [SMEM, VMEM, VMEM, VMEM, HBM, VMEM], [shape(lines //...  2.46 us
    ppermute x1, starting transfers between devices, along_four(): lax.ppermute(total, 'line', pairs)  2 us
  transfers between devices with their start and end apart: 20, of which 11 were waited for; matrix products, arithmetic and copies ran while one was open for 0% of the time, Pallas kernels for 8%

profile of v10, /device:TPU:6, one launch (start us, length us, event | category | flops | bytes accessed | tf_op | source)
XLA Modules:
  0.0 91.5 jit_solution(9047324309410979715)
XLA Ops:
  1.0 1.7 %collective-permute-start = (f32[8,8,256]{2,1,0:T(8,128)S(1)}, f32[8,8,256]{2,1,0:T(8,128)S(1)}, u32[]{:S(2)}, u32[]{:S(2)}) collective-permute-start(f32[8,8,256]{2,1,0:T(8,128)S(1)} %get-tuple-element.42), channel_id=1, source_target_pairs={{0,1},{1,0},{2,3},{3,2},{4,5},{5,4},{6,7},{7,6},{8,9},{9,8},{10,11... | collective-permute-start | bytes 196616 | tf_op jit(solution)/shard_map/ppermute | solution.py:501
  2.6 2.9 %collective-permute-start.1 = (f32[8,8,256]{2,1,0:T(8,128)S(1)}, f32[8,8,256]{2,1,0:T(8,128)S(1)}, u32[]{:S(2)}, u32[]{:S(2)}) collective-permute-start(f32[8,8,256]{2,1,0:T(8,128)S(1)} %get-tuple-element.43), channel_id=1, source_target_pairs={{0,2},{1,3},{2,0},{3,1},{4,6},{5,7},{6,4},{7,5},{8,10},{9,11},{10,... | collective-permute-start | bytes 196616 | tf_op jit(solution)/shard_map/ppermute | solution.py:501
  6.6 4.7 %shard_map.38 = (f32[8,256,256]{2,1,0:T(8,128)}, f32[272,256]{1,0:T(8,128)S(1)}) custom-call(f32[8,256]{1,0:T(8,128)S(1)} %copy-done.2, f32[8,256,256]{2,1,0:T(8,128)} %blocks_ref.3), custom_call_target="tpu_custom_call" | custom-call | flops 1610612736 | bytes 1048576 | tf_op jit(solution)/shard_map/pallas_call | solution.py:135
  11.8 2.0 %shard_map.39 = (f32[8,32,256]{2,1,0:T(8,128)S(1)}, f32[32,256]{1,0:T(8,128)S(1)}) custom-call(s32[1]{0:T(128)} %bitcast.code_ref, f32[8,256]{1,0:T(8,128)S(1)} %copy-done.2, f32[8,256,256]{2,1,0:T(8,128)S(1)} %copy-done, f32[8,8,256]{2,1,0:T(8,128)S(1)} %get-tuple-element.47.refs_0_, f32[8,8,256]{2,1,0:T(8,128)S(1)} %collective-permute-done.refs_1_, ...), custom_call_target="tpu_custom_call" | custom-call | flops 201326592 | bytes 1048576 | tf_op jit(solution)/shard_map/pallas_call | solution.py:199
  13.8 1.7 %collective-permute-start.4 = (f32[32,256]{1,0:T(8,128)S(1)}, f32[32,256]{1,0:T(8,128)S(1)}, u32[]{:S(2)}, u32[]{:S(2)}) collective-permute-start(f32[32,256]{1,0:T(8,128)S(1)} %get-tuple-element.51.refs_1_), channel_id=1, source_target_pairs={{0,1},{1,0},{2,3},{3,2},{4,5},{5,4},{6,7},{7,6},{8,9},{9,8},{10,11... | collective-permute-start | bytes 98312 | tf_op jit(solution)/shard_map/ppermute | solution.py:501
  15.5 4.3 %collective-permute-done.4.refs_3_.refs_1_ = f32[32,256]{1,0:T(8,128)S(1)} collective-permute-done((f32[32,256]{1,0:T(8,128)S(1)}, f32[32,256]{1,0:T(8,128)S(1)}, u32[]{:S(2)}, u32[]{:S(2)}) %collective-permute-start.4) | collective-permute-done | bytes 32800 | tf_op jit(solution)/shard_map/ppermute | solution.py:501
  20.3 2.9 %collective-permute-start.5 = (f32[304,256]{1,0:T(8,128)S(1)}, f32[304,256]{1,0:T(8,128)S(1)}, u32[]{:S(2)}, u32[]{:S(2)}) collective-permute-start(f32[304,256]{1,0:T(8,128)S(1)} %shard_map.40.refs_0_), channel_id=1, source_target_pairs={{0,3},{1,2},{2,1},{3,0},{4,7},{5,6},{6,5},{7,4},{8,11},{9,10},{10,... | collective-permute-start | bytes 933896 | tf_op jit(solution)/shard_map/ppermute | solution.py:501
  23.2 5.8 %collective-permute-done.5.refs_1_.refs_0_ = f32[304,256]{1,0:T(8,128)S(1)} collective-permute-done((f32[304,256]{1,0:T(8,128)S(1)}, f32[304,256]{1,0:T(8,128)S(1)}, u32[]{:S(2)}, u32[]{:S(2)}) %collective-permute-start.5) | collective-permute-done | bytes 311328 | tf_op jit(solution)/shard_map/ppermute | solution.py:501
  29.6 1.5 %collective-permute-done.6.refs_1_.refs_0_ = f32[304,256]{1,0:T(8,128)S(1)} collective-permute-done((f32[304,256]{1,0:T(8,128)S(1)}, f32[304,256]{1,0:T(8,128)S(1)}, u32[]{:S(2)}, u32[]{:S(2)}) %collective-permute-start.6) | collective-permute-done | bytes 311328 | tf_op jit(solution)/shard_map/ppermute | solution.py:501
  31.7 2.0 %collective-permute-start.7 = (f32[304,256]{1,0:T(8,128)S(1)}, f32[304,256]{1,0:T(8,128)S(1)}, u32[]{:S(2)}, u32[]{:S(2)}) collective-permute-start(f32[304,256]{1,0:T(8,128)S(1)} %get-tuple-element.55.mine_ref), channel_id=1, source_target_pairs={{0,8},{4,20},{8,0},{12,28},{16,24},{20,4},{24,16},{28,12},{32,40},... | collective-permute-start | bytes 933896 | tf_op jit(solution)/shard_map/ppermute | solution.py:516
  33.7 2.8 %collective-permute-start.8 = (f32[152,256]{1,0:T(8,128)S(1)}, f32[152,256]{1,0:T(8,128)S(1)}, u32[]{:S(2)}, u32[]{:S(2)}) collective-permute-start(f32[152,256]{1,0:T(8,128)S(1)} %get-tuple-element.56), channel_id=1, source_target_pairs={{0,24},{4,28},{8,16},{12,20},{16,8},{20,12},{24,0},{28,4},{32,56},... | collective-permute-start | bytes 466952 | tf_op jit(solution)/shard_map/ppermute | solution.py:501
  36.6 10.9 %collective-permute-done.8.this_ref = f32[152,256]{1,0:T(8,128)S(1)} collective-permute-done((f32[152,256]{1,0:T(8,128)S(1)}, f32[152,256]{1,0:T(8,128)S(1)}, u32[]{:S(2)}, u32[]{:S(2)}) %collective-permute-start.8) | collective-permute-done | bytes 155680 | tf_op jit(solution)/shard_map/ppermute | solution.py:501
  48.0 1.3 %collective-permute-done.10.that_ref = f32[152,256]{1,0:T(8,128)S(1)} collective-permute-done((f32[152,256]{1,0:T(8,128)S(1)}, f32[152,256]{1,0:T(8,128)S(1)}, u32[]{:S(2)}, u32[]{:S(2)}) %collective-permute-start.10) | collective-permute-done | bytes 155680 | tf_op jit(solution)/shard_map/ppermute | solution.py:501
  49.3 2.6 %shard_map.46 = (f32[304,256]{1,0:T(8,128)S(1)}, f32[304,256]{1,0:T(8,128)S(1)}, f32[304,256]{1,0:T(8,128)S(1)}, f32[152,256]{1,0:T(8,128)S(1)}) custom-call(s32[1]{0:T(128)} %bitcast.2.code_ref, f32[304,256]{1,0:T(8,128)S(1)} %get-tuple-element.55.mine_ref, f32[304,256]{1,0:T(8,128)S(1)} %collective-permute-done.7.here_ref, ...), custom_call_target="tpu_custom_call" | custom-call | flops 717225984 | bytes 1048576 | tf_op jit(solution)/shard_map/pallas_call | solution.py:341
  51.9 5.1 %collective-permute-start.11 = (f32[152,256]{1,0:T(8,128)S(1)}, f32[152,256]{1,0:T(8,128)S(1)}, u32[]{:S(2)}, u32[]{:S(2)}) collective-permute-start(f32[152,256]{1,0:T(8,128)S(1)} %get-tuple-element.61), channel_id=1, source_target_pairs={{0,56},{4,60},{8,48},{12,52},{16,40},{20,44},{24,32},{28,36},{32,2... | collective-permute-start | bytes 466952 | tf_op jit(solution)/shard_map/ppermute | solution.py:501
  57.1 7.8 %collective-permute-done.11.refs_1_ = f32[152,256]{1,0:T(8,128)S(1)} collective-permute-done((f32[152,256]{1,0:T(8,128)S(1)}, f32[152,256]{1,0:T(8,128)S(1)}, u32[]{:S(2)}, u32[]{:S(2)}) %collective-permute-start.11) | collective-permute-done | bytes 155680 | tf_op jit(solution)/shard_map/ppermute | solution.py:501
  64.9 1.4 %collective-permute-done.12.refs_2_ = f32[152,256]{1,0:T(8,128)S(1)} collective-permute-done((f32[152,256]{1,0:T(8,128)S(1)}, f32[152,256]{1,0:T(8,128)S(1)}, u32[]{:S(2)}, u32[]{:S(2)}) %collective-permute-start.12) | collective-permute-done | bytes 155680 | tf_op jit(solution)/shard_map/ppermute | solution.py:501
  66.8 1.3 %collective-permute-start.16 = (f32[304,256]{1,0:T(8,128)S(1)}, f32[304,256]{1,0:T(8,128)S(1)}, u32[]{:S(2)}, u32[]{:S(2)}) collective-permute-start(f32[304,256]{1,0:T(8,128)S(1)} %shard_map.51.map_ref), channel_id=1, source_target_pairs={{128,192},{132,196},{136,200},{140,204},{144,208},{148,212},{152,2... | collective-permute-start | bytes 933896 | tf_op jit(solution)/shard_map/ppermute | solution.py:555
  69.0 1.3 %collective-permute-start.14 = (f32[32,256]{1,0:T(8,128)S(1)}, f32[32,256]{1,0:T(8,128)S(1)}, u32[]{:S(2)}, u32[]{:S(2)}) collective-permute-start(f32[32,256]{1,0:T(8,128)S(1)} %shard_map.52), channel_id=1, source_target_pairs={{64,192},{68,196},{72,200},{76,204},{80,208},{84,212},{88,216},{92... | collective-permute-start | bytes 98312 | tf_op jit(solution)/shard_map/ppermute | solution.py:555
  71.0 7.1 %collective-permute-done.16.beside_ref = f32[304,256]{1,0:T(8,128)S(1)} collective-permute-done((f32[304,256]{1,0:T(8,128)S(1)}, f32[304,256]{1,0:T(8,128)S(1)}, u32[]{:S(2)}, u32[]{:S(2)}) %collective-permute-start.16) | collective-permute-done | bytes 311328 | tf_op jit(solution)/shard_map/ppermute | solution.py:555
  78.6 2.5 %shard_map.54 = (f32[8,8,256]{2,1,0:T(8,128)S(1)}, f32[8,8,256]{2,1,0:T(8,128)S(1)}, f32[8,8,256]{2,1,0:T(8,128)S(1)}, f32[8,8,256]{2,1,0:T(8,128)S(1)}) custom-call(s32[1]{0:T(128)} %bitcast.code_ref, f32[32,256]{1,0:T(8,128)S(1)} %collective-permute-done.14.one_ref, f32[32,256]{1,0:T(8,128)S(1)} %collective-permute-done.15.two_ref, ...), custom_call_target="tpu_custom_call" | custom-call | flops 226492416 | bytes 1048576 | tf_op jit(solution)/shard_map/pallas_call | solution.py:473
  81.2 4.2 %collective-permute-start.18 = (f32[8,8,256]{2,1,0:T(8,128)S(1)}, f32[8,8,256]{2,1,0:T(8,128)S(1)}, u32[]{:S(2)}, u32[]{:S(2)}) collective-permute-start(f32[8,8,256]{2,1,0:T(8,128)S(1)} %get-tuple-element.75), channel_id=1, source_target_pairs={{0,2},{1,3},{2,0},{3,1},{4,6},{5,7},{6,4},{7,5},{8,10},{9,11},{10,... | collective-permute-start | bytes 196616 | tf_op jit(solution)/shard_map/ppermute | solution.py:501
  86.1 2.2 %collective-permute-done.18.refs_2_ = f32[8,8,256]{2,1,0:T(8,128)S(1)} collective-permute-done((f32[8,8,256]{2,1,0:T(8,128)S(1)}, f32[8,8,256]{2,1,0:T(8,128)S(1)}, u32[]{:S(2)}, u32[]{:S(2)}) %collective-permute-start.18) | collective-permute-done | bytes 65568 | tf_op jit(solution)/shard_map/ppermute | solution.py:501
  88.3 2.5 %collective-permute-done.19.refs_3_ = f32[8,8,256]{2,1,0:T(8,128)S(1)} collective-permute-done((f32[8,8,256]{2,1,0:T(8,128)S(1)}, f32[8,8,256]{2,1,0:T(8,128)S(1)}, u32[]{:S(2)}, u32[]{:S(2)}) %collective-permute-start.19) | collective-permute-done | bytes 65568 | tf_op jit(solution)/shard_map/ppermute | solution.py:501
  (41 shorter events, 9.0 us)
Async XLA Ops:
  0.0 0.9 %copy-start.1 = (f32[8,32,256]{2,1,0:T(8,128)S(1)}, f32[8,32,256]{2,1,0:T(8,128)}, u32[]{:S(2)}) copy-start(f32[8,32,256]{2,1,0:T(8,128)} %forcing_ref.1) | copy-start | bytes 786436
  1.0 10.3 %collective-permute-start = (f32[8,8,256]{2,1,0:T(8,128)S(1)}, f32[8,8,256]{2,1,0:T(8,128)S(1)}, u32[]{:S(2)}, u32[]{:S(2)}) collective-permute-start(f32[8,8,256]{2,1,0:T(8,128)S(1)} %get-tuple-element.42), channel_id=1, source_target_pairs={{0,1},{1,0},{2,3},{3,2},{4,5},{5,4},{6,7},{7,6},{8,9},{9,8},{10,11... | collective-permute-start | bytes 196616 | tf_op jit(solution)/shard_map/ppermute | solution.py:501
  2.6 8.6 %collective-permute-start.1 = (f32[8,8,256]{2,1,0:T(8,128)S(1)}, f32[8,8,256]{2,1,0:T(8,128)S(1)}, u32[]{:S(2)}, u32[]{:S(2)}) collective-permute-start(f32[8,8,256]{2,1,0:T(8,128)S(1)} %get-tuple-element.43), channel_id=1, source_target_pairs={{0,2},{1,3},{2,0},{3,1},{4,6},{5,7},{6,4},{7,5},{8,10},{9,11},{10,... | collective-permute-start | bytes 196616 | tf_op jit(solution)/shard_map/ppermute | solution.py:501
  5.5 6.3 %copy-start = (f32[8,256,256]{2,1,0:T(8,128)S(1)}, f32[8,256,256]{2,1,0:T(8,128)}, u32[]{:S(2)}) copy-start(f32[8,256,256]{2,1,0:T(8,128)} %blocks_ref.3) | copy-start | bytes 6291460
  5.5 5.7 %collective-permute-start.2 = (f32[8,8,256]{2,1,0:T(8,128)S(1)}, f32[8,8,256]{2,1,0:T(8,128)S(1)}, u32[]{:S(2)}, u32[]{:S(2)}) collective-permute-start(f32[8,8,256]{2,1,0:T(8,128)S(1)} %get-tuple-element.44), channel_id=1, source_target_pairs={{0,3},{1,2},{2,1},{3,0},{4,7},{5,6},{6,5},{7,4},{8,11},{9,10},{10,... | collective-permute-start | bytes 196616 | tf_op jit(solution)/shard_map/ppermute | solution.py:501
  5.8 0.8 copy-start.2
  11.3 8.4 %collective-permute-start.3 = (f32[272,256]{1,0:T(8,128)S(1)}, f32[272,256]{1,0:T(8,128)S(1)}, u32[]{:S(2)}, u32[]{:S(2)}) collective-permute-start(f32[272,256]{1,0:T(8,128)S(1)} %get-tuple-element.46.refs_0_), channel_id=1, source_target_pairs={{0,1},{1,0},{2,3},{3,2},{4,5},{5,4},{6,7},{7,6},{8,9},{9,8},{10,11... | collective-permute-start | bytes 835592 | tf_op jit(solution)/shard_map/ppermute | solution.py:501
  13.8 6.0 %collective-permute-start.4 = (f32[32,256]{1,0:T(8,128)S(1)}, f32[32,256]{1,0:T(8,128)S(1)}, u32[]{:S(2)}, u32[]{:S(2)}) collective-permute-start(f32[32,256]{1,0:T(8,128)S(1)} %get-tuple-element.51.refs_1_), channel_id=1, source_target_pairs={{0,1},{1,0},{2,3},{3,2},{4,5},{5,4},{6,7},{7,6},{8,9},{9,8},{10,11... | collective-permute-start | bytes 98312 | tf_op jit(solution)/shard_map/ppermute | solution.py:501
  20.3 8.7 %collective-permute-start.5 = (f32[304,256]{1,0:T(8,128)S(1)}, f32[304,256]{1,0:T(8,128)S(1)}, u32[]{:S(2)}, u32[]{:S(2)}) collective-permute-start(f32[304,256]{1,0:T(8,128)S(1)} %shard_map.40.refs_0_), channel_id=1, source_target_pairs={{0,3},{1,2},{2,1},{3,0},{4,7},{5,6},{6,5},{7,4},{8,11},{9,10},{10,... | collective-permute-start | bytes 933896 | tf_op jit(solution)/shard_map/ppermute | solution.py:501
  29.5 1.7 %collective-permute-start.6 = (f32[304,256]{1,0:T(8,128)S(1)}, f32[304,256]{1,0:T(8,128)S(1)}, u32[]{:S(2)}, u32[]{:S(2)}) collective-permute-start(f32[304,256]{1,0:T(8,128)S(1)} %shard_map.42.refs_0_), channel_id=1, source_target_pairs={{0,4},{4,0},{8,12},{12,8},{16,20},{20,16},{24,28},{28,24},{32,36},... | collective-permute-start | bytes 933896 | tf_op jit(solution)/shard_map/ppermute | solution.py:501
  31.7 15.7 %collective-permute-start.7 = (f32[304,256]{1,0:T(8,128)S(1)}, f32[304,256]{1,0:T(8,128)S(1)}, u32[]{:S(2)}, u32[]{:S(2)}) collective-permute-start(f32[304,256]{1,0:T(8,128)S(1)} %get-tuple-element.55.mine_ref), channel_id=1, source_target_pairs={{0,8},{4,20},{8,0},{12,28},{16,24},{20,4},{24,16},{28,12},{32,40},... | collective-permute-start | bytes 933896 | tf_op jit(solution)/shard_map/ppermute | solution.py:516
  33.7 13.7 %collective-permute-start.8 = (f32[152,256]{1,0:T(8,128)S(1)}, f32[152,256]{1,0:T(8,128)S(1)}, u32[]{:S(2)}, u32[]{:S(2)}) collective-permute-start(f32[152,256]{1,0:T(8,128)S(1)} %get-tuple-element.56), channel_id=1, source_target_pairs={{0,24},{4,28},{8,16},{12,20},{16,8},{20,12},{24,0},{28,4},{32,56},... | collective-permute-start | bytes 466952 | tf_op jit(solution)/shard_map/ppermute | solution.py:501
  47.4 1.8 %collective-permute-start.9 = (f32[304,256]{1,0:T(8,128)S(1)}, f32[304,256]{1,0:T(8,128)S(1)}, u32[]{:S(2)}, u32[]{:S(2)}) collective-permute-start(f32[304,256]{1,0:T(8,128)S(1)} %collective-permute-done.7.here_ref), channel_id=1, source_target_pairs={{0,4},{4,0},{8,12},{12,8},{16,20},{20,16},{24,28},{28,24},{32,36},... | collective-permute-start | bytes 933896 | tf_op jit(solution)/shard_map/ppermute | solution.py:501
  47.6 1.7 %collective-permute-start.10 = (f32[152,256]{1,0:T(8,128)S(1)}, f32[152,256]{1,0:T(8,128)S(1)}, u32[]{:S(2)}, u32[]{:S(2)}) collective-permute-start(f32[152,256]{1,0:T(8,128)S(1)} %collective-permute-done.8.this_ref), channel_id=1, source_target_pairs={{0,4},{4,0},{8,12},{12,8},{16,20},{20,16},{24,28},{28,24},{32,36},... | collective-permute-start | bytes 466952 | tf_op jit(solution)/shard_map/ppermute | solution.py:501
  51.9 13.0 %collective-permute-start.11 = (f32[152,256]{1,0:T(8,128)S(1)}, f32[152,256]{1,0:T(8,128)S(1)}, u32[]{:S(2)}, u32[]{:S(2)}) collective-permute-start(f32[152,256]{1,0:T(8,128)S(1)} %get-tuple-element.61), channel_id=1, source_target_pairs={{0,56},{4,60},{8,48},{12,52},{16,40},{20,44},{24,32},{28,36},{32,2... | collective-permute-start | bytes 466952 | tf_op jit(solution)/shard_map/ppermute | solution.py:501
  64.9 1.4 %collective-permute-start.12 = (f32[152,256]{1,0:T(8,128)S(1)}, f32[152,256]{1,0:T(8,128)S(1)}, u32[]{:S(2)}, u32[]{:S(2)}) collective-permute-start(f32[152,256]{1,0:T(8,128)S(1)} %collective-permute-done.11.refs_1_), channel_id=1, source_target_pairs={{0,4},{4,0},{8,12},{12,8},{16,20},{20,16},{24,28},{28,24},{32,36},... | collective-permute-start | bytes 466952 | tf_op jit(solution)/shard_map/ppermute | solution.py:501
  66.8 11.3 %collective-permute-start.16 = (f32[304,256]{1,0:T(8,128)S(1)}, f32[304,256]{1,0:T(8,128)S(1)}, u32[]{:S(2)}, u32[]{:S(2)}) collective-permute-start(f32[304,256]{1,0:T(8,128)S(1)} %shard_map.51.map_ref), channel_id=1, source_target_pairs={{128,192},{132,196},{136,200},{140,204},{144,208},{148,212},{152,2... | collective-permute-start | bytes 933896 | tf_op jit(solution)/shard_map/ppermute | solution.py:555
  68.1 0.7 collective-permute-start.13
  69.0 9.6 %collective-permute-start.14 = (f32[32,256]{1,0:T(8,128)S(1)}, f32[32,256]{1,0:T(8,128)S(1)}, u32[]{:S(2)}, u32[]{:S(2)}) collective-permute-start(f32[32,256]{1,0:T(8,128)S(1)} %shard_map.52), channel_id=1, source_target_pairs={{64,192},{68,196},{72,200},{76,204},{80,208},{84,212},{88,216},{92... | collective-permute-start | bytes 98312 | tf_op jit(solution)/shard_map/ppermute | solution.py:555
  70.3 8.3 %collective-permute-start.15 = (f32[32,256]{1,0:T(8,128)S(1)}, f32[32,256]{1,0:T(8,128)S(1)}, u32[]{:S(2)}, u32[]{:S(2)}) collective-permute-start(f32[32,256]{1,0:T(8,128)S(1)} %shard_map.52), channel_id=1, source_target_pairs={{64,128},{68,132},{72,136},{76,140},{80,144},{84,148},{88,152},{92... | collective-permute-start | bytes 98312 | tf_op jit(solution)/shard_map/ppermute | solution.py:555
  81.1 5.0 %collective-permute-start.17 = (f32[8,8,256]{2,1,0:T(8,128)S(1)}, f32[8,8,256]{2,1,0:T(8,128)S(1)}, u32[]{:S(2)}, u32[]{:S(2)}) collective-permute-start(f32[8,8,256]{2,1,0:T(8,128)S(1)} %get-tuple-element.74), channel_id=1, source_target_pairs={{0,1},{1,0},{2,3},{3,2},{4,5},{5,4},{6,7},{7,6},{8,9},{9,8},{10,11... | collective-permute-start | bytes 196616 | tf_op jit(solution)/shard_map/ppermute | solution.py:501
  81.2 7.2 %collective-permute-start.18 = (f32[8,8,256]{2,1,0:T(8,128)S(1)}, f32[8,8,256]{2,1,0:T(8,128)S(1)}, u32[]{:S(2)}, u32[]{:S(2)}) collective-permute-start(f32[8,8,256]{2,1,0:T(8,128)S(1)} %get-tuple-element.75), channel_id=1, source_target_pairs={{0,2},{1,3},{2,0},{3,1},{4,6},{5,7},{6,4},{7,5},{8,10},{9,11},{10,... | collective-permute-start | bytes 196616 | tf_op jit(solution)/shard_map/ppermute | solution.py:501
  85.3 5.5 %collective-permute-start.19 = (f32[8,8,256]{2,1,0:T(8,128)S(1)}, f32[8,8,256]{2,1,0:T(8,128)S(1)}, u32[]{:S(2)}, u32[]{:S(2)}) collective-permute-start(f32[8,8,256]{2,1,0:T(8,128)S(1)} %get-tuple-element.76), channel_id=1, source_target_pairs={{0,3},{1,2},{2,1},{3,0},{4,7},{5,6},{6,5},{7,4},{8,11},{9,10},{10,... | collective-permute-start | bytes 196616 | tf_op jit(solution)/shard_map/ppermute | solution.py:501

commit v11 on v10

--- a/solution.py
+++ b/solution.py
@@ -314,7 +314,7 @@
 
 def four_kernel(
     code_ref, mine_ref, here_ref, there_ref, this_ref, that_ref,
-    total_ref, beside_ref, front_ref, half_ref, four_ref,
+    total_ref, beside_ref, front_ref, half_ref, four_ref, back_ref,
 ):
     core = lax.rem(code_ref[0], 2)
     place = code_ref[0] // 2
@@ -324,14 +324,10 @@
     four_ref[place ^ (2 - core)] = there_ref[...]
     four_ref[place ^ 3, pl.ds(core * rows, rows)] = this_ref[...]
     four_ref[place ^ 3, pl.ds((1 - core) * rows, rows)] = that_ref[...]
-
-    @pl.loop(0, 3)
-    def _(turn):
-        join(four_ref.at[2 * turn], four_ref.at[2 * turn + 1], four_ref.at[4 + turn])
-
-    front_ref[...] = four_ref[4]
-    total_ref[...] = four_ref[6]
-    half_ref[...] = four_ref[6, pl.ds(core * rows, rows)]
+    join(four_ref.at[0], four_ref.at[1], front_ref)
+    join(four_ref.at[2], four_ref.at[3], back_ref)
+    join(front_ref, back_ref, total_ref)
+    half_ref[...] = total_ref[pl.ds(core * rows, rows)]
     beside_ref[...] = four_ref[place ^ 1]
 
 
@@ -343,7 +339,7 @@
         [SMEM] + [VMEM] * 5,
         [whole, whole, whole, shape(rows // 2, levels)],
         36 * rows * levels**2,
-        [pltpu.VMEM((7, rows, levels), F32)],
+        [pltpu.VMEM((4, rows, levels), F32), pltpu.VMEM((rows, levels), F32)],
     )(code, mine, here, there, this, that)
 
 

time: 92.2 us -> 90.7 us (0.984)
  Pallas kernels: 15.4 us -> 13.9 us
    pallas_call x1, Pallas kernels: 2.64 us -> 1.33 us  [join_four(): call(four_kernel, [SMEM] + [VMEM] * 5, [whole, whole, whole, shape(rows /...]
where the time goes in v11:
time: 90.7 us; the launch traced here: 90.1 us
  waiting for transfers between devices  45 us (50%)
  starting transfers between devices  29.1 us (32%)
  Pallas kernels  13.9 us (15%)
  local copies, waits for them, and re-layouts  1.77 us (2%)
    ppermute x15, waiting for transfers between devices, partner(): return lax.ppermute(value, axis, [(i, i ^ mask) for i in range(count)])  38 us
    ppermute x15, starting transfers between devices, partner(): return lax.ppermute(value, axis, [(i, i ^ mask) for i in range(count)])  23.2 us
    ppermute x4, waiting for transfers between devices, across(): return lax.ppermute(value, 'line', pairs)  7.07 us
    pallas_call x1, Pallas kernels, prefix_maps(): call(maps_kernel, [VMEM, HBM], [shape(*blocks.shape), shape(levels + PAD,...  4.67 us
    ppermute x4, starting transfers between devices, across(): return lax.ppermute(value, 'line', pairs)  3.91 us
    pallas_call x1, Pallas kernels, finish(): call(finish_kernel, [SMEM, VMEM, VMEM, VMEM, HBM, VMEM], [shape(lines //...  2.47 us
    ppermute x1, starting transfers between devices, along_four(): lax.ppermute(total, 'line', pairs)  2 us
    pallas_call x1, Pallas kernels, trial_states(): call(states_kernel, [SMEM] + [VMEM] * (2 + len(parts)), [shape(cells, lin...  1.96 us
  transfers between devices with their start and end apart: 20, of which 11 were waited for; matrix products, arithmetic and copies ran while one was open for 0% of the time, Pallas kernels for 8%

profile of v11, /device:TPU:6, one launch (start us, length us, event | category | flops | bytes accessed | tf_op | source)
XLA Modules:
  0.0 90.1 jit_solution(12195684561697927909)
XLA Ops:
  1.0 1.7 %collective-permute-start = (f32[8,8,256]{2,1,0:T(8,128)S(1)}, f32[8,8,256]{2,1,0:T(8,128)S(1)}, u32[]{:S(2)}, u32[]{:S(2)}) collective-permute-start(f32[8,8,256]{2,1,0:T(8,128)S(1)} %get-tuple-element.42), channel_id=1, source_target_pairs={{0,1},{1,0},{2,3},{3,2},{4,5},{5,4},{6,7},{7,6},{8,9},{9,8},{10,11... | collective-permute-start | bytes 196616 | tf_op jit(solution)/shard_map/ppermute | solution.py:497
  2.6 2.9 %collective-permute-start.1 = (f32[8,8,256]{2,1,0:T(8,128)S(1)}, f32[8,8,256]{2,1,0:T(8,128)S(1)}, u32[]{:S(2)}, u32[]{:S(2)}) collective-permute-start(f32[8,8,256]{2,1,0:T(8,128)S(1)} %get-tuple-element.43), channel_id=1, source_target_pairs={{0,2},{1,3},{2,0},{3,1},{4,6},{5,7},{6,4},{7,5},{8,10},{9,11},{10,... | collective-permute-start | bytes 196616 | tf_op jit(solution)/shard_map/ppermute | solution.py:497
  6.6 4.7 %shard_map.38 = (f32[8,256,256]{2,1,0:T(8,128)}, f32[272,256]{1,0:T(8,128)S(1)}) custom-call(f32[8,256]{1,0:T(8,128)S(1)} %copy-done.2, f32[8,256,256]{2,1,0:T(8,128)} %blocks_ref.3), custom_call_target="tpu_custom_call" | custom-call | flops 1610612736 | bytes 1048576 | tf_op jit(solution)/shard_map/pallas_call | solution.py:135
  11.8 2.0 %shard_map.39 = (f32[8,32,256]{2,1,0:T(8,128)S(1)}, f32[32,256]{1,0:T(8,128)S(1)}) custom-call(s32[1]{0:T(128)} %bitcast.code_ref, f32[8,256]{1,0:T(8,128)S(1)} %copy-done.2, f32[8,256,256]{2,1,0:T(8,128)S(1)} %copy-done, f32[8,8,256]{2,1,0:T(8,128)S(1)} %get-tuple-element.47.refs_0_, f32[8,8,256]{2,1,0:T(8,128)S(1)} %collective-permute-done.refs_1_, ...), custom_call_target="tpu_custom_call" | custom-call | flops 201326592 | bytes 1048576 | tf_op jit(solution)/shard_map/pallas_call | solution.py:199
  13.8 1.7 %collective-permute-start.4 = (f32[32,256]{1,0:T(8,128)S(1)}, f32[32,256]{1,0:T(8,128)S(1)}, u32[]{:S(2)}, u32[]{:S(2)}) collective-permute-start(f32[32,256]{1,0:T(8,128)S(1)} %get-tuple-element.51.refs_1_), channel_id=1, source_target_pairs={{0,1},{1,0},{2,3},{3,2},{4,5},{5,4},{6,7},{7,6},{8,9},{9,8},{10,11... | collective-permute-start | bytes 98312 | tf_op jit(solution)/shard_map/ppermute | solution.py:497
  15.5 4.3 %collective-permute-done.4.refs_3_.refs_1_ = f32[32,256]{1,0:T(8,128)S(1)} collective-permute-done((f32[32,256]{1,0:T(8,128)S(1)}, f32[32,256]{1,0:T(8,128)S(1)}, u32[]{:S(2)}, u32[]{:S(2)}) %collective-permute-start.4) | collective-permute-done | bytes 32800 | tf_op jit(solution)/shard_map/ppermute | solution.py:497
  20.3 2.9 %collective-permute-start.5 = (f32[304,256]{1,0:T(8,128)S(1)}, f32[304,256]{1,0:T(8,128)S(1)}, u32[]{:S(2)}, u32[]{:S(2)}) collective-permute-start(f32[304,256]{1,0:T(8,128)S(1)} %shard_map.40.refs_0_), channel_id=1, source_target_pairs={{0,3},{1,2},{2,1},{3,0},{4,7},{5,6},{6,5},{7,4},{8,11},{9,10},{10,... | collective-permute-start | bytes 933896 | tf_op jit(solution)/shard_map/ppermute | solution.py:497
  23.2 5.8 %collective-permute-done.5.refs_1_.refs_0_ = f32[304,256]{1,0:T(8,128)S(1)} collective-permute-done((f32[304,256]{1,0:T(8,128)S(1)}, f32[304,256]{1,0:T(8,128)S(1)}, u32[]{:S(2)}, u32[]{:S(2)}) %collective-permute-start.5) | collective-permute-done | bytes 311328 | tf_op jit(solution)/shard_map/ppermute | solution.py:497
  29.6 1.5 %collective-permute-done.6.refs_1_.refs_0_ = f32[304,256]{1,0:T(8,128)S(1)} collective-permute-done((f32[304,256]{1,0:T(8,128)S(1)}, f32[304,256]{1,0:T(8,128)S(1)}, u32[]{:S(2)}, u32[]{:S(2)}) %collective-permute-start.6) | collective-permute-done | bytes 311328 | tf_op jit(solution)/shard_map/ppermute | solution.py:497
  31.7 2.0 %collective-permute-start.7 = (f32[304,256]{1,0:T(8,128)S(1)}, f32[304,256]{1,0:T(8,128)S(1)}, u32[]{:S(2)}, u32[]{:S(2)}) collective-permute-start(f32[304,256]{1,0:T(8,128)S(1)} %get-tuple-element.55.mine_ref), channel_id=1, source_target_pairs={{0,8},{4,20},{8,0},{12,28},{16,24},{20,4},{24,16},{28,12},{32,40},... | collective-permute-start | bytes 933896 | tf_op jit(solution)/shard_map/ppermute | solution.py:512
  33.7 2.8 %collective-permute-start.8 = (f32[152,256]{1,0:T(8,128)S(1)}, f32[152,256]{1,0:T(8,128)S(1)}, u32[]{:S(2)}, u32[]{:S(2)}) collective-permute-start(f32[152,256]{1,0:T(8,128)S(1)} %get-tuple-element.56), channel_id=1, source_target_pairs={{0,24},{4,28},{8,16},{12,20},{16,8},{20,12},{24,0},{28,4},{32,56},... | collective-permute-start | bytes 466952 | tf_op jit(solution)/shard_map/ppermute | solution.py:497
  36.6 10.9 %collective-permute-done.8.this_ref = f32[152,256]{1,0:T(8,128)S(1)} collective-permute-done((f32[152,256]{1,0:T(8,128)S(1)}, f32[152,256]{1,0:T(8,128)S(1)}, u32[]{:S(2)}, u32[]{:S(2)}) %collective-permute-start.8) | collective-permute-done | bytes 155680 | tf_op jit(solution)/shard_map/ppermute | solution.py:497
  48.0 1.3 %collective-permute-done.10.that_ref = f32[152,256]{1,0:T(8,128)S(1)} collective-permute-done((f32[152,256]{1,0:T(8,128)S(1)}, f32[152,256]{1,0:T(8,128)S(1)}, u32[]{:S(2)}, u32[]{:S(2)}) %collective-permute-start.10) | collective-permute-done | bytes 155680 | tf_op jit(solution)/shard_map/ppermute | solution.py:497
  49.3 1.3 %shard_map.46 = (f32[304,256]{1,0:T(8,128)S(1)}, f32[304,256]{1,0:T(8,128)S(1)}, f32[304,256]{1,0:T(8,128)S(1)}, f32[152,256]{1,0:T(8,128)S(1)}) custom-call(s32[1]{0:T(128)} %bitcast.2.code_ref, f32[304,256]{1,0:T(8,128)S(1)} %get-tuple-element.55.mine_ref, f32[304,256]{1,0:T(8,128)S(1)} %collective-permute-done.7.here_ref, ...), custom_call_target="tpu_custom_call" | custom-call | flops 717225984 | bytes 1048576 | tf_op jit(solution)/shard_map/pallas_call | solution.py:337
  50.6 5.1 %collective-permute-start.11 = (f32[152,256]{1,0:T(8,128)S(1)}, f32[152,256]{1,0:T(8,128)S(1)}, u32[]{:S(2)}, u32[]{:S(2)}) collective-permute-start(f32[152,256]{1,0:T(8,128)S(1)} %get-tuple-element.61), channel_id=1, source_target_pairs={{0,56},{4,60},{8,48},{12,52},{16,40},{20,44},{24,32},{28,36},{32,2... | collective-permute-start | bytes 466952 | tf_op jit(solution)/shard_map/ppermute | solution.py:497
  55.8 7.8 %collective-permute-done.11.refs_1_ = f32[152,256]{1,0:T(8,128)S(1)} collective-permute-done((f32[152,256]{1,0:T(8,128)S(1)}, f32[152,256]{1,0:T(8,128)S(1)}, u32[]{:S(2)}, u32[]{:S(2)}) %collective-permute-start.11) | collective-permute-done | bytes 155680 | tf_op jit(solution)/shard_map/ppermute | solution.py:497
  63.6 1.4 %collective-permute-done.12.refs_2_ = f32[152,256]{1,0:T(8,128)S(1)} collective-permute-done((f32[152,256]{1,0:T(8,128)S(1)}, f32[152,256]{1,0:T(8,128)S(1)}, u32[]{:S(2)}, u32[]{:S(2)}) %collective-permute-start.12) | collective-permute-done | bytes 155680 | tf_op jit(solution)/shard_map/ppermute | solution.py:497
  65.3 1.3 %collective-permute-start.16 = (f32[304,256]{1,0:T(8,128)S(1)}, f32[304,256]{1,0:T(8,128)S(1)}, u32[]{:S(2)}, u32[]{:S(2)}) collective-permute-start(f32[304,256]{1,0:T(8,128)S(1)} %shard_map.51.map_ref), channel_id=1, source_target_pairs={{128,192},{132,196},{136,200},{140,204},{144,208},{148,212},{152,2... | collective-permute-start | bytes 933896 | tf_op jit(solution)/shard_map/ppermute | solution.py:551
  67.5 1.3 %collective-permute-start.14 = (f32[32,256]{1,0:T(8,128)S(1)}, f32[32,256]{1,0:T(8,128)S(1)}, u32[]{:S(2)}, u32[]{:S(2)}) collective-permute-start(f32[32,256]{1,0:T(8,128)S(1)} %shard_map.52), channel_id=1, source_target_pairs={{64,192},{68,196},{72,200},{76,204},{80,208},{84,212},{88,216},{92... | collective-permute-start | bytes 98312 | tf_op jit(solution)/shard_map/ppermute | solution.py:551
  69.5 7.1 %collective-permute-done.16.beside_ref = f32[304,256]{1,0:T(8,128)S(1)} collective-permute-done((f32[304,256]{1,0:T(8,128)S(1)}, f32[304,256]{1,0:T(8,128)S(1)}, u32[]{:S(2)}, u32[]{:S(2)}) %collective-permute-start.16) | collective-permute-done | bytes 311328 | tf_op jit(solution)/shard_map/ppermute | solution.py:551
  77.1 2.5 %shard_map.54 = (f32[8,8,256]{2,1,0:T(8,128)S(1)}, f32[8,8,256]{2,1,0:T(8,128)S(1)}, f32[8,8,256]{2,1,0:T(8,128)S(1)}, f32[8,8,256]{2,1,0:T(8,128)S(1)}) custom-call(s32[1]{0:T(128)} %bitcast.code_ref, f32[32,256]{1,0:T(8,128)S(1)} %collective-permute-done.14.one_ref, f32[32,256]{1,0:T(8,128)S(1)} %collective-permute-done.15.two_ref, ...), custom_call_target="tpu_custom_call" | custom-call | flops 226492416 | bytes 1048576 | tf_op jit(solution)/shard_map/pallas_call | solution.py:469
  79.7 4.2 %collective-permute-start.18 = (f32[8,8,256]{2,1,0:T(8,128)S(1)}, f32[8,8,256]{2,1,0:T(8,128)S(1)}, u32[]{:S(2)}, u32[]{:S(2)}) collective-permute-start(f32[8,8,256]{2,1,0:T(8,128)S(1)} %get-tuple-element.75), channel_id=1, source_target_pairs={{0,2},{1,3},{2,0},{3,1},{4,6},{5,7},{6,4},{7,5},{8,10},{9,11},{10,... | collective-permute-start | bytes 196616 | tf_op jit(solution)/shard_map/ppermute | solution.py:497
  84.6 2.2 %collective-permute-done.18.refs_2_ = f32[8,8,256]{2,1,0:T(8,128)S(1)} collective-permute-done((f32[8,8,256]{2,1,0:T(8,128)S(1)}, f32[8,8,256]{2,1,0:T(8,128)S(1)}, u32[]{:S(2)}, u32[]{:S(2)}) %collective-permute-start.18) | collective-permute-done | bytes 65568 | tf_op jit(solution)/shard_map/ppermute | solution.py:497
  86.8 2.5 %collective-permute-done.19.refs_3_ = f32[8,8,256]{2,1,0:T(8,128)S(1)} collective-permute-done((f32[8,8,256]{2,1,0:T(8,128)S(1)}, f32[8,8,256]{2,1,0:T(8,128)S(1)}, u32[]{:S(2)}, u32[]{:S(2)}) %collective-permute-start.19) | collective-permute-done | bytes 65568 | tf_op jit(solution)/shard_map/ppermute | solution.py:497
  (41 shorter events, 8.8 us)
Async XLA Ops:
  0.0 0.9 %copy-start.1 = (f32[8,32,256]{2,1,0:T(8,128)S(1)}, f32[8,32,256]{2,1,0:T(8,128)}, u32[]{:S(2)}) copy-start(f32[8,32,256]{2,1,0:T(8,128)} %forcing_ref.1) | copy-start | bytes 786436
  1.0 10.3 %collective-permute-start = (f32[8,8,256]{2,1,0:T(8,128)S(1)}, f32[8,8,256]{2,1,0:T(8,128)S(1)}, u32[]{:S(2)}, u32[]{:S(2)}) collective-permute-start(f32[8,8,256]{2,1,0:T(8,128)S(1)} %get-tuple-element.42), channel_id=1, source_target_pairs={{0,1},{1,0},{2,3},{3,2},{4,5},{5,4},{6,7},{7,6},{8,9},{9,8},{10,11... | collective-permute-start | bytes 196616 | tf_op jit(solution)/shard_map/ppermute | solution.py:497
  2.6 8.6 %collective-permute-start.1 = (f32[8,8,256]{2,1,0:T(8,128)S(1)}, f32[8,8,256]{2,1,0:T(8,128)S(1)}, u32[]{:S(2)}, u32[]{:S(2)}) collective-permute-start(f32[8,8,256]{2,1,0:T(8,128)S(1)} %get-tuple-element.43), channel_id=1, source_target_pairs={{0,2},{1,3},{2,0},{3,1},{4,6},{5,7},{6,4},{7,5},{8,10},{9,11},{10,... | collective-permute-start | bytes 196616 | tf_op jit(solution)/shard_map/ppermute | solution.py:497
  5.5 6.3 %copy-start = (f32[8,256,256]{2,1,0:T(8,128)S(1)}, f32[8,256,256]{2,1,0:T(8,128)}, u32[]{:S(2)}) copy-start(f32[8,256,256]{2,1,0:T(8,128)} %blocks_ref.3) | copy-start | bytes 6291460
  5.5 5.7 %collective-permute-start.2 = (f32[8,8,256]{2,1,0:T(8,128)S(1)}, f32[8,8,256]{2,1,0:T(8,128)S(1)}, u32[]{:S(2)}, u32[]{:S(2)}) collective-permute-start(f32[8,8,256]{2,1,0:T(8,128)S(1)} %get-tuple-element.44), channel_id=1, source_target_pairs={{0,3},{1,2},{2,1},{3,0},{4,7},{5,6},{6,5},{7,4},{8,11},{9,10},{10,... | collective-permute-start | bytes 196616 | tf_op jit(solution)/shard_map/ppermute | solution.py:497
  5.8 0.8 copy-start.2
  11.3 8.4 %collective-permute-start.3 = (f32[272,256]{1,0:T(8,128)S(1)}, f32[272,256]{1,0:T(8,128)S(1)}, u32[]{:S(2)}, u32[]{:S(2)}) collective-permute-start(f32[272,256]{1,0:T(8,128)S(1)} %get-tuple-element.46.refs_0_), channel_id=1, source_target_pairs={{0,1},{1,0},{2,3},{3,2},{4,5},{5,4},{6,7},{7,6},{8,9},{9,8},{10,11... | collective-permute-start | bytes 835592 | tf_op jit(solution)/shard_map/ppermute | solution.py:497
  13.8 6.0 %collective-permute-start.4 = (f32[32,256]{1,0:T(8,128)S(1)}, f32[32,256]{1,0:T(8,128)S(1)}, u32[]{:S(2)}, u32[]{:S(2)}) collective-permute-start(f32[32,256]{1,0:T(8,128)S(1)} %get-tuple-element.51.refs_1_), channel_id=1, source_target_pairs={{0,1},{1,0},{2,3},{3,2},{4,5},{5,4},{6,7},{7,6},{8,9},{9,8},{10,11... | collective-permute-start | bytes 98312 | tf_op jit(solution)/shard_map/ppermute | solution.py:497
  20.3 8.7 %collective-permute-start.5 = (f32[304,256]{1,0:T(8,128)S(1)}, f32[304,256]{1,0:T(8,128)S(1)}, u32[]{:S(2)}, u32[]{:S(2)}) collective-permute-start(f32[304,256]{1,0:T(8,128)S(1)} %shard_map.40.refs_0_), channel_id=1, source_target_pairs={{0,3},{1,2},{2,1},{3,0},{4,7},{5,6},{6,5},{7,4},{8,11},{9,10},{10,... | collective-permute-start | bytes 933896 | tf_op jit(solution)/shard_map/ppermute | solution.py:497
  29.5 1.7 %collective-permute-start.6 = (f32[304,256]{1,0:T(8,128)S(1)}, f32[304,256]{1,0:T(8,128)S(1)}, u32[]{:S(2)}, u32[]{:S(2)}) collective-permute-start(f32[304,256]{1,0:T(8,128)S(1)} %shard_map.42.refs_0_), channel_id=1, source_target_pairs={{0,4},{4,0},{8,12},{12,8},{16,20},{20,16},{24,28},{28,24},{32,36},... | collective-permute-start | bytes 933896 | tf_op jit(solution)/shard_map/ppermute | solution.py:497
  31.7 15.7 %collective-permute-start.7 = (f32[304,256]{1,0:T(8,128)S(1)}, f32[304,256]{1,0:T(8,128)S(1)}, u32[]{:S(2)}, u32[]{:S(2)}) collective-permute-start(f32[304,256]{1,0:T(8,128)S(1)} %get-tuple-element.55.mine_ref), channel_id=1, source_target_pairs={{0,8},{4,20},{8,0},{12,28},{16,24},{20,4},{24,16},{28,12},{32,40},... | collective-permute-start | bytes 933896 | tf_op jit(solution)/shard_map/ppermute | solution.py:512
  33.7 13.7 %collective-permute-start.8 = (f32[152,256]{1,0:T(8,128)S(1)}, f32[152,256]{1,0:T(8,128)S(1)}, u32[]{:S(2)}, u32[]{:S(2)}) collective-permute-start(f32[152,256]{1,0:T(8,128)S(1)} %get-tuple-element.56), channel_id=1, source_target_pairs={{0,24},{4,28},{8,16},{12,20},{16,8},{20,12},{24,0},{28,4},{32,56},... | collective-permute-start | bytes 466952 | tf_op jit(solution)/shard_map/ppermute | solution.py:497
  47.4 1.8 %collective-permute-start.9 = (f32[304,256]{1,0:T(8,128)S(1)}, f32[304,256]{1,0:T(8,128)S(1)}, u32[]{:S(2)}, u32[]{:S(2)}) collective-permute-start(f32[304,256]{1,0:T(8,128)S(1)} %collective-permute-done.7.here_ref), channel_id=1, source_target_pairs={{0,4},{4,0},{8,12},{12,8},{16,20},{20,16},{24,28},{28,24},{32,36},... | collective-permute-start | bytes 933896 | tf_op jit(solution)/shard_map/ppermute | solution.py:497
  47.6 1.7 %collective-permute-start.10 = (f32[152,256]{1,0:T(8,128)S(1)}, f32[152,256]{1,0:T(8,128)S(1)}, u32[]{:S(2)}, u32[]{:S(2)}) collective-permute-start(f32[152,256]{1,0:T(8,128)S(1)} %collective-permute-done.8.this_ref), channel_id=1, source_target_pairs={{0,4},{4,0},{8,12},{12,8},{16,20},{20,16},{24,28},{28,24},{32,36},... | collective-permute-start | bytes 466952 | tf_op jit(solution)/shard_map/ppermute | solution.py:497
  50.6 13.0 %collective-permute-start.11 = (f32[152,256]{1,0:T(8,128)S(1)}, f32[152,256]{1,0:T(8,128)S(1)}, u32[]{:S(2)}, u32[]{:S(2)}) collective-permute-start(f32[152,256]{1,0:T(8,128)S(1)} %get-tuple-element.61), channel_id=1, source_target_pairs={{0,56},{4,60},{8,48},{12,52},{16,40},{20,44},{24,32},{28,36},{32,2... | collective-permute-start | bytes 466952 | tf_op jit(solution)/shard_map/ppermute | solution.py:497
  63.6 1.4 %collective-permute-start.12 = (f32[152,256]{1,0:T(8,128)S(1)}, f32[152,256]{1,0:T(8,128)S(1)}, u32[]{:S(2)}, u32[]{:S(2)}) collective-permute-start(f32[152,256]{1,0:T(8,128)S(1)} %collective-permute-done.11.refs_1_), channel_id=1, source_target_pairs={{0,4},{4,0},{8,12},{12,8},{16,20},{20,16},{24,28},{28,24},{32,36},... | collective-permute-start | bytes 466952 | tf_op jit(solution)/shard_map/ppermute | solution.py:497
  65.3 11.3 %collective-permute-start.16 = (f32[304,256]{1,0:T(8,128)S(1)}, f32[304,256]{1,0:T(8,128)S(1)}, u32[]{:S(2)}, u32[]{:S(2)}) collective-permute-start(f32[304,256]{1,0:T(8,128)S(1)} %shard_map.51.map_ref), channel_id=1, source_target_pairs={{128,192},{132,196},{136,200},{140,204},{144,208},{148,212},{152,2... | collective-permute-start | bytes 933896 | tf_op jit(solution)/shard_map/ppermute | solution.py:551
  66.6 0.7 collective-permute-start.13
  67.5 9.6 %collective-permute-start.14 = (f32[32,256]{1,0:T(8,128)S(1)}, f32[32,256]{1,0:T(8,128)S(1)}, u32[]{:S(2)}, u32[]{:S(2)}) collective-permute-start(f32[32,256]{1,0:T(8,128)S(1)} %shard_map.52), channel_id=1, source_target_pairs={{64,192},{68,196},{72,200},{76,204},{80,208},{84,212},{88,216},{92... | collective-permute-start | bytes 98312 | tf_op jit(solution)/shard_map/ppermute | solution.py:551
  68.8 8.3 %collective-permute-start.15 = (f32[32,256]{1,0:T(8,128)S(1)}, f32[32,256]{1,0:T(8,128)S(1)}, u32[]{:S(2)}, u32[]{:S(2)}) collective-permute-start(f32[32,256]{1,0:T(8,128)S(1)} %shard_map.52), channel_id=1, source_target_pairs={{64,128},{68,132},{72,136},{76,140},{80,144},{84,148},{88,152},{92... | collective-permute-start | bytes 98312 | tf_op jit(solution)/shard_map/ppermute | solution.py:551
  79.6 5.0 %collective-permute-start.17 = (f32[8,8,256]{2,1,0:T(8,128)S(1)}, f32[8,8,256]{2,1,0:T(8,128)S(1)}, u32[]{:S(2)}, u32[]{:S(2)}) collective-permute-start(f32[8,8,256]{2,1,0:T(8,128)S(1)} %get-tuple-element.74), channel_id=1, source_target_pairs={{0,1},{1,0},{2,3},{3,2},{4,5},{5,4},{6,7},{7,6},{8,9},{9,8},{10,11... | collective-permute-start | bytes 196616 | tf_op jit(solution)/shard_map/ppermute | solution.py:497
  79.7 7.2 %collective-permute-start.18 = (f32[8,8,256]{2,1,0:T(8,128)S(1)}, f32[8,8,256]{2,1,0:T(8,128)S(1)}, u32[]{:S(2)}, u32[]{:S(2)}) collective-permute-start(f32[8,8,256]{2,1,0:T(8,128)S(1)} %get-tuple-element.75), channel_id=1, source_target_pairs={{0,2},{1,3},{2,0},{3,1},{4,6},{5,7},{6,4},{7,5},{8,10},{9,11},{10,... | collective-permute-start | bytes 196616 | tf_op jit(solution)/shard_map/ppermute | solution.py:497
  83.9 5.5 %collective-permute-start.19 = (f32[8,8,256]{2,1,0:T(8,128)S(1)}, f32[8,8,256]{2,1,0:T(8,128)S(1)}, u32[]{:S(2)}, u32[]{:S(2)}) collective-permute-start(f32[8,8,256]{2,1,0:T(8,128)S(1)} %get-tuple-element.76), channel_id=1, source_target_pairs={{0,3},{1,2},{2,1},{3,0},{4,7},{5,6},{6,5},{7,4},{8,11},{9,10},{10,... | collective-permute-start | bytes 196616 | tf_op jit(solution)/shard_map/ppermute | solution.py:497

commit v12 on v11

--- a/solution.py
+++ b/solution.py
@@ -86,7 +86,16 @@
 
 def move_states(states, map_ref):
     levels = map_ref.shape[1]
-    return unscale(dot(states, map_ref[:levels]), map_ref[levels : levels + 1])
+    return unscale(dot3(states, map_ref[:levels]), map_ref[levels : levels + 1])
+
+
+def join(left_ref, right_ref, out_ref):
+    levels = out_ref.shape[1]
+    start = levels + PAD
+    both = dot3(left_ref[...], right_ref[:levels])
+    count = left_ref[levels : levels + 8] + right_ref[levels : levels + 8]
+    put_map(both[:levels], count, out_ref)
+    out_ref[start:] = unscale(both[start:], right_ref[levels : levels + 1]) + right_ref[start:]
 
 
 def block_copy(blocks_ref, held_ref, arrived, cell):
@@ -188,7 +197,7 @@
     @pl.loop(0, blocks_ref.shape[0])
     def _(cell):
         forced = forcing_ref[:, cell, :] - upstream_ref[pl.ds(cell, 1), :] * states_ref[...]
-        state = dot(forced, blocks_ref[cell])
+        state = dot3(forced, blocks_ref[cell])
         states_ref[...] = state
         trial_ref[cell] = state
 
@@ -259,6 +268,9 @@
         their_states = their_map.at[start:]
 
     def joined(left_map, left_states, right_map, right_states):
+        if kind == "both" and not apart:
+            join(left_map, right_map, out)
+            return
         if kind != "states":
             join_maps(left_map, right_map, out)
         if kind == "maps":
@@ -306,12 +318,6 @@
     return got[0], got[1] if halves else theirs[0], got[-1]
 
 
-def join(left_ref, right_ref, out_ref):
-    start = out_ref.shape[1] + PAD
-    join_maps(left_ref, right_ref, out_ref)
-    out_ref[start:] = move_states(left_ref[start:], right_ref) + right_ref[start:]
-
-
 def four_kernel(
     code_ref, mine_ref, here_ref, there_ref, this_ref, that_ref,
     total_ref, beside_ref, front_ref, half_ref, four_ref, back_ref,
@@ -359,8 +365,7 @@
             ahead_ref[:start] = their_map[:start]
             ahead_ref[start:] = their_states
         else:
-            join_maps(their_map, before_ref, ahead_ref)
-            ahead_ref[start:] = move_states(their_states, before_ref) + before_ref[start:]
+            join(their_map, before_ref, ahead_ref)
 
     def otherwise():
         if first:
@@ -423,8 +428,7 @@
     start = before_ref.shape[1] + PAD
 
     def then():
-        join_maps(beside_ref, before_ref, ahead_ref)
-        ahead_ref[start:] = move_states(beside_ref[start:], before_ref) + before_ref[start:]
+        join(beside_ref, before_ref, ahead_ref)
 
     def otherwise():
         ahead_ref[:start] = before_ref[:start]

time: 90.7 us -> 90.4 us (level)
  no operation moved by 1% of the time
where the time goes in v12:
time: 90.4 us; the launch traced here: 89.9 us
  waiting for transfers between devices  45.4 us (50%)
  starting transfers between devices  29.1 us (32%)
  Pallas kernels  13.3 us (15%)
  local copies, waits for them, and re-layouts  1.77 us (2%)
    ppermute x15, waiting for transfers between devices, partner(): return lax.ppermute(value, axis, [(i, i ^ mask) for i in range(count)])  38.3 us
    ppermute x15, starting transfers between devices, partner(): return lax.ppermute(value, axis, [(i, i ^ mask) for i in range(count)])  23.2 us
    ppermute x4, waiting for transfers between devices, across(): return lax.ppermute(value, 'line', pairs)  7.1 us
    pallas_call x1, Pallas kernels, prefix_maps(): call(maps_kernel, [VMEM, HBM], [shape(*blocks.shape), shape(levels + PAD,...  4.67 us
    ppermute x4, starting transfers between devices, across(): return lax.ppermute(value, 'line', pairs)  3.91 us
    pallas_call x1, Pallas kernels, finish(): call(finish_kernel, [SMEM, VMEM, VMEM, VMEM, HBM, VMEM], [shape(lines //...  2.46 us
    ppermute x1, starting transfers between devices, along_four(): lax.ppermute(total, 'line', pairs)  2 us
  transfers between devices with their start and end apart: 20, of which 11 were waited for; matrix products, arithmetic and copies ran while one was open for 0% of the time, Pallas kernels for 8%

profile of v12, /device:TPU:6, one launch (start us, length us, event | category | flops | bytes accessed | tf_op | source)
XLA Modules:
  0.0 89.9 jit_solution(12376488303219117198)
XLA Ops:
  1.0 1.7 %collective-permute-start = (f32[8,8,256]{2,1,0:T(8,128)S(1)}, f32[8,8,256]{2,1,0:T(8,128)S(1)}, u32[]{:S(2)}, u32[]{:S(2)}) collective-permute-start(f32[8,8,256]{2,1,0:T(8,128)S(1)} %get-tuple-element.42), channel_id=1, source_target_pairs={{0,1},{1,0},{2,3},{3,2},{4,5},{5,4},{6,7},{7,6},{8,9},{9,8},{10,11... | collective-permute-start | bytes 196616 | tf_op jit(solution)/shard_map/ppermute | solution.py:501
  2.6 2.9 %collective-permute-start.1 = (f32[8,8,256]{2,1,0:T(8,128)S(1)}, f32[8,8,256]{2,1,0:T(8,128)S(1)}, u32[]{:S(2)}, u32[]{:S(2)}) collective-permute-start(f32[8,8,256]{2,1,0:T(8,128)S(1)} %get-tuple-element.43), channel_id=1, source_target_pairs={{0,2},{1,3},{2,0},{3,1},{4,6},{5,7},{6,4},{7,5},{8,10},{9,11},{10,... | collective-permute-start | bytes 196616 | tf_op jit(solution)/shard_map/ppermute | solution.py:501
  6.6 4.7 %shard_map.38 = (f32[8,256,256]{2,1,0:T(8,128)}, f32[272,256]{1,0:T(8,128)S(1)}) custom-call(f32[8,256]{1,0:T(8,128)S(1)} %copy-done.2, f32[8,256,256]{2,1,0:T(8,128)} %blocks_ref.3), custom_call_target="tpu_custom_call" | custom-call | flops 1610612736 | bytes 1048576 | tf_op jit(solution)/shard_map/pallas_call | solution.py:144
  11.8 1.6 %shard_map.39 = (f32[8,32,256]{2,1,0:T(8,128)S(1)}, f32[32,256]{1,0:T(8,128)S(1)}) custom-call(s32[1]{0:T(128)} %bitcast.code_ref, f32[8,256]{1,0:T(8,128)S(1)} %copy-done.2, f32[8,256,256]{2,1,0:T(8,128)S(1)} %copy-done, f32[8,8,256]{2,1,0:T(8,128)S(1)} %get-tuple-element.47.refs_0_, f32[8,8,256]{2,1,0:T(8,128)S(1)} %collective-permute-done.refs_1_, ...), custom_call_target="tpu_custom_call" | custom-call | flops 201326592 | bytes 1048576 | tf_op jit(solution)/shard_map/pallas_call | solution.py:208
  13.4 1.7 %collective-permute-start.4 = (f32[32,256]{1,0:T(8,128)S(1)}, f32[32,256]{1,0:T(8,128)S(1)}, u32[]{:S(2)}, u32[]{:S(2)}) collective-permute-start(f32[32,256]{1,0:T(8,128)S(1)} %get-tuple-element.51.refs_1_), channel_id=1, source_target_pairs={{0,1},{1,0},{2,3},{3,2},{4,5},{5,4},{6,7},{7,6},{8,9},{9,8},{10,11... | collective-permute-start | bytes 98312 | tf_op jit(solution)/shard_map/ppermute | solution.py:501
  15.1 4.6 %collective-permute-done.4.refs_3_.refs_1_ = f32[32,256]{1,0:T(8,128)S(1)} collective-permute-done((f32[32,256]{1,0:T(8,128)S(1)}, f32[32,256]{1,0:T(8,128)S(1)}, u32[]{:S(2)}, u32[]{:S(2)}) %collective-permute-start.4) | collective-permute-done | bytes 32800 | tf_op jit(solution)/shard_map/ppermute | solution.py:501
  20.2 2.9 %collective-permute-start.5 = (f32[304,256]{1,0:T(8,128)S(1)}, f32[304,256]{1,0:T(8,128)S(1)}, u32[]{:S(2)}, u32[]{:S(2)}) collective-permute-start(f32[304,256]{1,0:T(8,128)S(1)} %shard_map.40.refs_0_), channel_id=1, source_target_pairs={{0,3},{1,2},{2,1},{3,0},{4,7},{5,6},{6,5},{7,4},{8,11},{9,10},{10,... | collective-permute-start | bytes 933896 | tf_op jit(solution)/shard_map/ppermute | solution.py:501
  23.1 5.8 %collective-permute-done.5.refs_1_.refs_0_ = f32[304,256]{1,0:T(8,128)S(1)} collective-permute-done((f32[304,256]{1,0:T(8,128)S(1)}, f32[304,256]{1,0:T(8,128)S(1)}, u32[]{:S(2)}, u32[]{:S(2)}) %collective-permute-start.5) | collective-permute-done | bytes 311328 | tf_op jit(solution)/shard_map/ppermute | solution.py:501
  29.5 1.5 %collective-permute-done.6.refs_1_.refs_0_ = f32[304,256]{1,0:T(8,128)S(1)} collective-permute-done((f32[304,256]{1,0:T(8,128)S(1)}, f32[304,256]{1,0:T(8,128)S(1)}, u32[]{:S(2)}, u32[]{:S(2)}) %collective-permute-start.6) | collective-permute-done | bytes 311328 | tf_op jit(solution)/shard_map/ppermute | solution.py:501
  31.5 2.0 %collective-permute-start.7 = (f32[304,256]{1,0:T(8,128)S(1)}, f32[304,256]{1,0:T(8,128)S(1)}, u32[]{:S(2)}, u32[]{:S(2)}) collective-permute-start(f32[304,256]{1,0:T(8,128)S(1)} %get-tuple-element.55.mine_ref), channel_id=1, source_target_pairs={{0,8},{4,20},{8,0},{12,28},{16,24},{20,4},{24,16},{28,12},{32,40},... | collective-permute-start | bytes 933896 | tf_op jit(solution)/shard_map/ppermute | solution.py:516
  33.5 2.8 %collective-permute-start.8 = (f32[152,256]{1,0:T(8,128)S(1)}, f32[152,256]{1,0:T(8,128)S(1)}, u32[]{:S(2)}, u32[]{:S(2)}) collective-permute-start(f32[152,256]{1,0:T(8,128)S(1)} %get-tuple-element.56), channel_id=1, source_target_pairs={{0,24},{4,28},{8,16},{12,20},{16,8},{20,12},{24,0},{28,4},{32,56},... | collective-permute-start | bytes 466952 | tf_op jit(solution)/shard_map/ppermute | solution.py:501
  36.3 10.9 %collective-permute-done.8.this_ref = f32[152,256]{1,0:T(8,128)S(1)} collective-permute-done((f32[152,256]{1,0:T(8,128)S(1)}, f32[152,256]{1,0:T(8,128)S(1)}, u32[]{:S(2)}, u32[]{:S(2)}) %collective-permute-start.8) | collective-permute-done | bytes 155680 | tf_op jit(solution)/shard_map/ppermute | solution.py:501
  47.7 1.3 %collective-permute-done.10.that_ref = f32[152,256]{1,0:T(8,128)S(1)} collective-permute-done((f32[152,256]{1,0:T(8,128)S(1)}, f32[152,256]{1,0:T(8,128)S(1)}, u32[]{:S(2)}, u32[]{:S(2)}) %collective-permute-start.10) | collective-permute-done | bytes 155680 | tf_op jit(solution)/shard_map/ppermute | solution.py:501
  49.0 1.3 %shard_map.46 = (f32[304,256]{1,0:T(8,128)S(1)}, f32[304,256]{1,0:T(8,128)S(1)}, f32[304,256]{1,0:T(8,128)S(1)}, f32[152,256]{1,0:T(8,128)S(1)}) custom-call(s32[1]{0:T(128)} %bitcast.2.code_ref, f32[304,256]{1,0:T(8,128)S(1)} %get-tuple-element.55.mine_ref, f32[304,256]{1,0:T(8,128)S(1)} %collective-permute-done.7.here_ref, ...), custom_call_target="tpu_custom_call" | custom-call | flops 717225984 | bytes 1048576 | tf_op jit(solution)/shard_map/pallas_call | solution.py:343
  50.3 5.1 %collective-permute-start.11 = (f32[152,256]{1,0:T(8,128)S(1)}, f32[152,256]{1,0:T(8,128)S(1)}, u32[]{:S(2)}, u32[]{:S(2)}) collective-permute-start(f32[152,256]{1,0:T(8,128)S(1)} %get-tuple-element.61), channel_id=1, source_target_pairs={{0,56},{4,60},{8,48},{12,52},{16,40},{20,44},{24,32},{28,36},{32,2... | collective-permute-start | bytes 466952 | tf_op jit(solution)/shard_map/ppermute | solution.py:501
  55.5 7.8 %collective-permute-done.11.refs_1_ = f32[152,256]{1,0:T(8,128)S(1)} collective-permute-done((f32[152,256]{1,0:T(8,128)S(1)}, f32[152,256]{1,0:T(8,128)S(1)}, u32[]{:S(2)}, u32[]{:S(2)}) %collective-permute-start.11) | collective-permute-done | bytes 155680 | tf_op jit(solution)/shard_map/ppermute | solution.py:501
  63.3 1.4 %collective-permute-done.12.refs_2_ = f32[152,256]{1,0:T(8,128)S(1)} collective-permute-done((f32[152,256]{1,0:T(8,128)S(1)}, f32[152,256]{1,0:T(8,128)S(1)}, u32[]{:S(2)}, u32[]{:S(2)}) %collective-permute-start.12) | collective-permute-done | bytes 155680 | tf_op jit(solution)/shard_map/ppermute | solution.py:501
  65.1 1.3 %collective-permute-start.16 = (f32[304,256]{1,0:T(8,128)S(1)}, f32[304,256]{1,0:T(8,128)S(1)}, u32[]{:S(2)}, u32[]{:S(2)}) collective-permute-start(f32[304,256]{1,0:T(8,128)S(1)} %shard_map.51.map_ref), channel_id=1, source_target_pairs={{128,192},{132,196},{136,200},{140,204},{144,208},{148,212},{152,2... | collective-permute-start | bytes 933896 | tf_op jit(solution)/shard_map/ppermute | solution.py:555
  67.4 1.3 %collective-permute-start.14 = (f32[32,256]{1,0:T(8,128)S(1)}, f32[32,256]{1,0:T(8,128)S(1)}, u32[]{:S(2)}, u32[]{:S(2)}) collective-permute-start(f32[32,256]{1,0:T(8,128)S(1)} %shard_map.52), channel_id=1, source_target_pairs={{64,192},{68,196},{72,200},{76,204},{80,208},{84,212},{88,216},{92... | collective-permute-start | bytes 98312 | tf_op jit(solution)/shard_map/ppermute | solution.py:555
  69.4 7.1 %collective-permute-done.16.beside_ref = f32[304,256]{1,0:T(8,128)S(1)} collective-permute-done((f32[304,256]{1,0:T(8,128)S(1)}, f32[304,256]{1,0:T(8,128)S(1)}, u32[]{:S(2)}, u32[]{:S(2)}) %collective-permute-start.16) | collective-permute-done | bytes 311328 | tf_op jit(solution)/shard_map/ppermute | solution.py:555
  76.9 2.5 %shard_map.54 = (f32[8,8,256]{2,1,0:T(8,128)S(1)}, f32[8,8,256]{2,1,0:T(8,128)S(1)}, f32[8,8,256]{2,1,0:T(8,128)S(1)}, f32[8,8,256]{2,1,0:T(8,128)S(1)}) custom-call(s32[1]{0:T(128)} %bitcast.code_ref, f32[32,256]{1,0:T(8,128)S(1)} %collective-permute-done.14.one_ref, f32[32,256]{1,0:T(8,128)S(1)} %collective-permute-done.15.two_ref, ...), custom_call_target="tpu_custom_call" | custom-call | flops 226492416 | bytes 1048576 | tf_op jit(solution)/shard_map/pallas_call | solution.py:473
  79.5 4.2 %collective-permute-start.18 = (f32[8,8,256]{2,1,0:T(8,128)S(1)}, f32[8,8,256]{2,1,0:T(8,128)S(1)}, u32[]{:S(2)}, u32[]{:S(2)}) collective-permute-start(f32[8,8,256]{2,1,0:T(8,128)S(1)} %get-tuple-element.75), channel_id=1, source_target_pairs={{0,2},{1,3},{2,0},{3,1},{4,6},{5,7},{6,4},{7,5},{8,10},{9,11},{10,... | collective-permute-start | bytes 196616 | tf_op jit(solution)/shard_map/ppermute | solution.py:501
  84.4 2.2 %collective-permute-done.18.refs_2_ = f32[8,8,256]{2,1,0:T(8,128)S(1)} collective-permute-done((f32[8,8,256]{2,1,0:T(8,128)S(1)}, f32[8,8,256]{2,1,0:T(8,128)S(1)}, u32[]{:S(2)}, u32[]{:S(2)}) %collective-permute-start.18) | collective-permute-done | bytes 65568 | tf_op jit(solution)/shard_map/ppermute | solution.py:501
  86.6 2.5 %collective-permute-done.19.refs_3_ = f32[8,8,256]{2,1,0:T(8,128)S(1)} collective-permute-done((f32[8,8,256]{2,1,0:T(8,128)S(1)}, f32[8,8,256]{2,1,0:T(8,128)S(1)}, u32[]{:S(2)}, u32[]{:S(2)}) %collective-permute-start.19) | collective-permute-done | bytes 65568 | tf_op jit(solution)/shard_map/ppermute | solution.py:501
  (41 shorter events, 8.6 us)
Async XLA Ops:
  0.0 0.9 %copy-start.1 = (f32[8,32,256]{2,1,0:T(8,128)S(1)}, f32[8,32,256]{2,1,0:T(8,128)}, u32[]{:S(2)}) copy-start(f32[8,32,256]{2,1,0:T(8,128)} %forcing_ref.1) | copy-start | bytes 786436
  1.0 10.3 %collective-permute-start = (f32[8,8,256]{2,1,0:T(8,128)S(1)}, f32[8,8,256]{2,1,0:T(8,128)S(1)}, u32[]{:S(2)}, u32[]{:S(2)}) collective-permute-start(f32[8,8,256]{2,1,0:T(8,128)S(1)} %get-tuple-element.42), channel_id=1, source_target_pairs={{0,1},{1,0},{2,3},{3,2},{4,5},{5,4},{6,7},{7,6},{8,9},{9,8},{10,11... | collective-permute-start | bytes 196616 | tf_op jit(solution)/shard_map/ppermute | solution.py:501
  2.6 8.6 %collective-permute-start.1 = (f32[8,8,256]{2,1,0:T(8,128)S(1)}, f32[8,8,256]{2,1,0:T(8,128)S(1)}, u32[]{:S(2)}, u32[]{:S(2)}) collective-permute-start(f32[8,8,256]{2,1,0:T(8,128)S(1)} %get-tuple-element.43), channel_id=1, source_target_pairs={{0,2},{1,3},{2,0},{3,1},{4,6},{5,7},{6,4},{7,5},{8,10},{9,11},{10,... | collective-permute-start | bytes 196616 | tf_op jit(solution)/shard_map/ppermute | solution.py:501
  5.5 6.3 %copy-start = (f32[8,256,256]{2,1,0:T(8,128)S(1)}, f32[8,256,256]{2,1,0:T(8,128)}, u32[]{:S(2)}) copy-start(f32[8,256,256]{2,1,0:T(8,128)} %blocks_ref.3) | copy-start | bytes 6291460
  5.5 5.7 %collective-permute-start.2 = (f32[8,8,256]{2,1,0:T(8,128)S(1)}, f32[8,8,256]{2,1,0:T(8,128)S(1)}, u32[]{:S(2)}, u32[]{:S(2)}) collective-permute-start(f32[8,8,256]{2,1,0:T(8,128)S(1)} %get-tuple-element.44), channel_id=1, source_target_pairs={{0,3},{1,2},{2,1},{3,0},{4,7},{5,6},{6,5},{7,4},{8,11},{9,10},{10,... | collective-permute-start | bytes 196616 | tf_op jit(solution)/shard_map/ppermute | solution.py:501
  5.8 0.8 copy-start.2
  11.3 8.4 %collective-permute-start.3 = (f32[272,256]{1,0:T(8,128)S(1)}, f32[272,256]{1,0:T(8,128)S(1)}, u32[]{:S(2)}, u32[]{:S(2)}) collective-permute-start(f32[272,256]{1,0:T(8,128)S(1)} %get-tuple-element.46.refs_0_), channel_id=1, source_target_pairs={{0,1},{1,0},{2,3},{3,2},{4,5},{5,4},{6,7},{7,6},{8,9},{9,8},{10,11... | collective-permute-start | bytes 835592 | tf_op jit(solution)/shard_map/ppermute | solution.py:501
  13.4 6.3 %collective-permute-start.4 = (f32[32,256]{1,0:T(8,128)S(1)}, f32[32,256]{1,0:T(8,128)S(1)}, u32[]{:S(2)}, u32[]{:S(2)}) collective-permute-start(f32[32,256]{1,0:T(8,128)S(1)} %get-tuple-element.51.refs_1_), channel_id=1, source_target_pairs={{0,1},{1,0},{2,3},{3,2},{4,5},{5,4},{6,7},{7,6},{8,9},{9,8},{10,11... | collective-permute-start | bytes 98312 | tf_op jit(solution)/shard_map/ppermute | solution.py:501
  20.2 8.7 %collective-permute-start.5 = (f32[304,256]{1,0:T(8,128)S(1)}, f32[304,256]{1,0:T(8,128)S(1)}, u32[]{:S(2)}, u32[]{:S(2)}) collective-permute-start(f32[304,256]{1,0:T(8,128)S(1)} %shard_map.40.refs_0_), channel_id=1, source_target_pairs={{0,3},{1,2},{2,1},{3,0},{4,7},{5,6},{6,5},{7,4},{8,11},{9,10},{10,... | collective-permute-start | bytes 933896 | tf_op jit(solution)/shard_map/ppermute | solution.py:501
  29.4 1.7 %collective-permute-start.6 = (f32[304,256]{1,0:T(8,128)S(1)}, f32[304,256]{1,0:T(8,128)S(1)}, u32[]{:S(2)}, u32[]{:S(2)}) collective-permute-start(f32[304,256]{1,0:T(8,128)S(1)} %shard_map.42.refs_0_), channel_id=1, source_target_pairs={{0,4},{4,0},{8,12},{12,8},{16,20},{20,16},{24,28},{28,24},{32,36},... | collective-permute-start | bytes 933896 | tf_op jit(solution)/shard_map/ppermute | solution.py:501
  31.5 15.7 %collective-permute-start.7 = (f32[304,256]{1,0:T(8,128)S(1)}, f32[304,256]{1,0:T(8,128)S(1)}, u32[]{:S(2)}, u32[]{:S(2)}) collective-permute-start(f32[304,256]{1,0:T(8,128)S(1)} %get-tuple-element.55.mine_ref), channel_id=1, source_target_pairs={{0,8},{4,20},{8,0},{12,28},{16,24},{20,4},{24,16},{28,12},{32,40},... | collective-permute-start | bytes 933896 | tf_op jit(solution)/shard_map/ppermute | solution.py:516
  33.5 13.7 %collective-permute-start.8 = (f32[152,256]{1,0:T(8,128)S(1)}, f32[152,256]{1,0:T(8,128)S(1)}, u32[]{:S(2)}, u32[]{:S(2)}) collective-permute-start(f32[152,256]{1,0:T(8,128)S(1)} %get-tuple-element.56), channel_id=1, source_target_pairs={{0,24},{4,28},{8,16},{12,20},{16,8},{20,12},{24,0},{28,4},{32,56},... | collective-permute-start | bytes 466952 | tf_op jit(solution)/shard_map/ppermute | solution.py:501
  47.2 1.8 %collective-permute-start.9 = (f32[304,256]{1,0:T(8,128)S(1)}, f32[304,256]{1,0:T(8,128)S(1)}, u32[]{:S(2)}, u32[]{:S(2)}) collective-permute-start(f32[304,256]{1,0:T(8,128)S(1)} %collective-permute-done.7.here_ref), channel_id=1, source_target_pairs={{0,4},{4,0},{8,12},{12,8},{16,20},{20,16},{24,28},{28,24},{32,36},... | collective-permute-start | bytes 933896 | tf_op jit(solution)/shard_map/ppermute | solution.py:501
  47.4 1.7 %collective-permute-start.10 = (f32[152,256]{1,0:T(8,128)S(1)}, f32[152,256]{1,0:T(8,128)S(1)}, u32[]{:S(2)}, u32[]{:S(2)}) collective-permute-start(f32[152,256]{1,0:T(8,128)S(1)} %collective-permute-done.8.this_ref), channel_id=1, source_target_pairs={{0,4},{4,0},{8,12},{12,8},{16,20},{20,16},{24,28},{28,24},{32,36},... | collective-permute-start | bytes 466952 | tf_op jit(solution)/shard_map/ppermute | solution.py:501
  50.3 13.0 %collective-permute-start.11 = (f32[152,256]{1,0:T(8,128)S(1)}, f32[152,256]{1,0:T(8,128)S(1)}, u32[]{:S(2)}, u32[]{:S(2)}) collective-permute-start(f32[152,256]{1,0:T(8,128)S(1)} %get-tuple-element.61), channel_id=1, source_target_pairs={{0,56},{4,60},{8,48},{12,52},{16,40},{20,44},{24,32},{28,36},{32,2... | collective-permute-start | bytes 466952 | tf_op jit(solution)/shard_map/ppermute | solution.py:501
  63.3 1.4 %collective-permute-start.12 = (f32[152,256]{1,0:T(8,128)S(1)}, f32[152,256]{1,0:T(8,128)S(1)}, u32[]{:S(2)}, u32[]{:S(2)}) collective-permute-start(f32[152,256]{1,0:T(8,128)S(1)} %collective-permute-done.11.refs_1_), channel_id=1, source_target_pairs={{0,4},{4,0},{8,12},{12,8},{16,20},{20,16},{24,28},{28,24},{32,36},... | collective-permute-start | bytes 466952 | tf_op jit(solution)/shard_map/ppermute | solution.py:501
  65.1 11.3 %collective-permute-start.16 = (f32[304,256]{1,0:T(8,128)S(1)}, f32[304,256]{1,0:T(8,128)S(1)}, u32[]{:S(2)}, u32[]{:S(2)}) collective-permute-start(f32[304,256]{1,0:T(8,128)S(1)} %shard_map.51.map_ref), channel_id=1, source_target_pairs={{128,192},{132,196},{136,200},{140,204},{144,208},{148,212},{152,2... | collective-permute-start | bytes 933896 | tf_op jit(solution)/shard_map/ppermute | solution.py:555
  66.4 0.7 collective-permute-start.13
  67.4 9.5 %collective-permute-start.14 = (f32[32,256]{1,0:T(8,128)S(1)}, f32[32,256]{1,0:T(8,128)S(1)}, u32[]{:S(2)}, u32[]{:S(2)}) collective-permute-start(f32[32,256]{1,0:T(8,128)S(1)} %shard_map.52), channel_id=1, source_target_pairs={{64,192},{68,196},{72,200},{76,204},{80,208},{84,212},{88,216},{92... | collective-permute-start | bytes 98312 | tf_op jit(solution)/shard_map/ppermute | solution.py:555
  68.7 8.2 %collective-permute-start.15 = (f32[32,256]{1,0:T(8,128)S(1)}, f32[32,256]{1,0:T(8,128)S(1)}, u32[]{:S(2)}, u32[]{:S(2)}) collective-permute-start(f32[32,256]{1,0:T(8,128)S(1)} %shard_map.52), channel_id=1, source_target_pairs={{64,128},{68,132},{72,136},{76,140},{80,144},{84,148},{88,152},{92... | collective-permute-start | bytes 98312 | tf_op jit(solution)/shard_map/ppermute | solution.py:555
  79.4 5.0 %collective-permute-start.17 = (f32[8,8,256]{2,1,0:T(8,128)S(1)}, f32[8,8,256]{2,1,0:T(8,128)S(1)}, u32[]{:S(2)}, u32[]{:S(2)}) collective-permute-start(f32[8,8,256]{2,1,0:T(8,128)S(1)} %get-tuple-element.74), channel_id=1, source_target_pairs={{0,1},{1,0},{2,3},{3,2},{4,5},{5,4},{6,7},{7,6},{8,9},{9,8},{10,11... | collective-permute-start | bytes 196616 | tf_op jit(solution)/shard_map/ppermute | solution.py:501
  79.5 7.2 %collective-permute-start.18 = (f32[8,8,256]{2,1,0:T(8,128)S(1)}, f32[8,8,256]{2,1,0:T(8,128)S(1)}, u32[]{:S(2)}, u32[]{:S(2)}) collective-permute-start(f32[8,8,256]{2,1,0:T(8,128)S(1)} %get-tuple-element.75), channel_id=1, source_target_pairs={{0,2},{1,3},{2,0},{3,1},{4,6},{5,7},{6,4},{7,5},{8,10},{9,11},{10,... | collective-permute-start | bytes 196616 | tf_op jit(solution)/shard_map/ppermute | solution.py:501
  83.7 5.5 %collective-permute-start.19 = (f32[8,8,256]{2,1,0:T(8,128)S(1)}, f32[8,8,256]{2,1,0:T(8,128)S(1)}, u32[]{:S(2)}, u32[]{:S(2)}) collective-permute-start(f32[8,8,256]{2,1,0:T(8,128)S(1)} %get-tuple-element.76), channel_id=1, source_target_pairs={{0,3},{1,2},{2,1},{3,0},{4,7},{5,6},{6,5},{7,4},{8,11},{9,10},{10,... | collective-permute-start | bytes 196616 | tf_op jit(solution)/shard_map/ppermute | solution.py:501

commit v13 on v12

--- a/solution.py
+++ b/solution.py
@@ -27,10 +27,6 @@
 PLANE = 16
 
 
-def dot(a, b):
-    return jnp.dot(a, b, precision=lax.Precision.HIGHEST, preferred_element_type=F32)
-
-
 def split(a):
     high = a.astype(jnp.bfloat16)
     return high, (a - high.astype(F32)).astype(jnp.bfloat16)
@@ -127,7 +123,7 @@
     def _(cell):
         scaled = last_ref[...] * -upstream_ref[pl.ds(cell, 1), :]
         block_copy(blocks_ref, held_ref, arrived, cell).wait()
-        product = dot(scaled, held_ref[cell])
+        product = dot3(scaled, held_ref[cell])
         last_ref[...] = product
         made_ref[cell] = product
         block_copy(made_ref, prefix_ref, left, cell).start()

time: 90.4 us -> 89.7 us (level)
  transfers between devices with their start and end apart: 20 -> 20, of which waited for: 11 -> 11; matrix products, arithmetic and copies ran while one was open for 0% -> 0% of each run, Pallas kernels for 8% -> 7%
where the time goes in v13:
time: 89.7 us; the launch traced here: 89.1 us
  waiting for transfers between devices  45.5 us (51%)
  starting transfers between devices  29 us (32%)
  Pallas kernels  12.6 us (14%)
  local copies, waits for them, and re-layouts  1.77 us (2%)
    ppermute x15, waiting for transfers between devices, partner(): return lax.ppermute(value, axis, [(i, i ^ mask) for i in range(count)])  38.4 us
    ppermute x15, starting transfers between devices, partner(): return lax.ppermute(value, axis, [(i, i ^ mask) for i in range(count)])  23.1 us
    ppermute x4, waiting for transfers between devices, across(): return lax.ppermute(value, 'line', pairs)  7.1 us
    pallas_call x1, Pallas kernels, prefix_maps(): call(maps_kernel, [VMEM, HBM], [shape(*blocks.shape), shape(levels + PAD,...  3.96 us
    ppermute x4, starting transfers between devices, across(): return lax.ppermute(value, 'line', pairs)  3.91 us
    pallas_call x1, Pallas kernels, finish(): call(finish_kernel, [SMEM, VMEM, VMEM, VMEM, HBM, VMEM], [shape(lines //...  2.46 us
    ppermute x1, starting transfers between devices, along_four(): lax.ppermute(total, 'line', pairs)  1.99 us
  transfers between devices with their start and end apart: 20, of which 11 were waited for; matrix products, arithmetic and copies ran while one was open for 0% of the time, Pallas kernels for 7%

profile of v13, /device:TPU:6, one launch (start us, length us, event | category | flops | bytes accessed | tf_op | source)
XLA Modules:
  0.0 89.1 jit_solution(8679947458782506041)
XLA Ops:
  1.0 1.7 %collective-permute-start = (f32[8,8,256]{2,1,0:T(8,128)S(1)}, f32[8,8,256]{2,1,0:T(8,128)S(1)}, u32[]{:S(2)}, u32[]{:S(2)}) collective-permute-start(f32[8,8,256]{2,1,0:T(8,128)S(1)} %get-tuple-element.42), channel_id=1, source_target_pairs={{0,1},{1,0},{2,3},{3,2},{4,5},{5,4},{6,7},{7,6},{8,9},{9,8},{10,11... | collective-permute-start | bytes 196616 | tf_op jit(solution)/shard_map/ppermute | solution.py:497
  2.6 2.9 %collective-permute-start.1 = (f32[8,8,256]{2,1,0:T(8,128)S(1)}, f32[8,8,256]{2,1,0:T(8,128)S(1)}, u32[]{:S(2)}, u32[]{:S(2)}) collective-permute-start(f32[8,8,256]{2,1,0:T(8,128)S(1)} %get-tuple-element.43), channel_id=1, source_target_pairs={{0,2},{1,3},{2,0},{3,1},{4,6},{5,7},{6,4},{7,5},{8,10},{9,11},{10,... | collective-permute-start | bytes 196616 | tf_op jit(solution)/shard_map/ppermute | solution.py:497
  6.6 4.0 %shard_map.38 = (f32[8,256,256]{2,1,0:T(8,128)}, f32[272,256]{1,0:T(8,128)S(1)}) custom-call(f32[8,256]{1,0:T(8,128)S(1)} %copy-done.2, f32[8,256,256]{2,1,0:T(8,128)} %blocks_ref.3), custom_call_target="tpu_custom_call" | custom-call | flops 1610612736 | bytes 1048576 | tf_op jit(solution)/shard_map/pallas_call | solution.py:140
  11.1 1.6 %shard_map.39 = (f32[8,32,256]{2,1,0:T(8,128)S(1)}, f32[32,256]{1,0:T(8,128)S(1)}) custom-call(s32[1]{0:T(128)} %bitcast.code_ref, f32[8,256]{1,0:T(8,128)S(1)} %copy-done.2, f32[8,256,256]{2,1,0:T(8,128)S(1)} %copy-done, f32[8,8,256]{2,1,0:T(8,128)S(1)} %get-tuple-element.47.refs_0_, f32[8,8,256]{2,1,0:T(8,128)S(1)} %collective-permute-done.refs_1_, ...), custom_call_target="tpu_custom_call" | custom-call | flops 201326592 | bytes 1048576 | tf_op jit(solution)/shard_map/pallas_call | solution.py:204
  12.7 2.0 %collective-permute-start.4 = (f32[32,256]{1,0:T(8,128)S(1)}, f32[32,256]{1,0:T(8,128)S(1)}, u32[]{:S(2)}, u32[]{:S(2)}) collective-permute-start(f32[32,256]{1,0:T(8,128)S(1)} %get-tuple-element.51.refs_1_), channel_id=1, source_target_pairs={{0,1},{1,0},{2,3},{3,2},{4,5},{5,4},{6,7},{7,6},{8,9},{9,8},{10,11... | collective-permute-start | bytes 98312 | tf_op jit(solution)/shard_map/ppermute | solution.py:497
  14.7 4.3 %collective-permute-done.4.refs_3_.refs_1_ = f32[32,256]{1,0:T(8,128)S(1)} collective-permute-done((f32[32,256]{1,0:T(8,128)S(1)}, f32[32,256]{1,0:T(8,128)S(1)}, u32[]{:S(2)}, u32[]{:S(2)}) %collective-permute-start.4) | collective-permute-done | bytes 32800 | tf_op jit(solution)/shard_map/ppermute | solution.py:497
  19.5 2.9 %collective-permute-start.5 = (f32[304,256]{1,0:T(8,128)S(1)}, f32[304,256]{1,0:T(8,128)S(1)}, u32[]{:S(2)}, u32[]{:S(2)}) collective-permute-start(f32[304,256]{1,0:T(8,128)S(1)} %shard_map.40.refs_0_), channel_id=1, source_target_pairs={{0,3},{1,2},{2,1},{3,0},{4,7},{5,6},{6,5},{7,4},{8,11},{9,10},{10,... | collective-permute-start | bytes 933896 | tf_op jit(solution)/shard_map/ppermute | solution.py:497
  22.4 5.6 %collective-permute-done.5.refs_1_.refs_0_ = f32[304,256]{1,0:T(8,128)S(1)} collective-permute-done((f32[304,256]{1,0:T(8,128)S(1)}, f32[304,256]{1,0:T(8,128)S(1)}, u32[]{:S(2)}, u32[]{:S(2)}) %collective-permute-start.5) | collective-permute-done | bytes 311328 | tf_op jit(solution)/shard_map/ppermute | solution.py:497
  28.6 1.5 %collective-permute-done.6.refs_1_.refs_0_ = f32[304,256]{1,0:T(8,128)S(1)} collective-permute-done((f32[304,256]{1,0:T(8,128)S(1)}, f32[304,256]{1,0:T(8,128)S(1)}, u32[]{:S(2)}, u32[]{:S(2)}) %collective-permute-start.6) | collective-permute-done | bytes 311328 | tf_op jit(solution)/shard_map/ppermute | solution.py:497
  30.5 2.0 %collective-permute-start.7 = (f32[304,256]{1,0:T(8,128)S(1)}, f32[304,256]{1,0:T(8,128)S(1)}, u32[]{:S(2)}, u32[]{:S(2)}) collective-permute-start(f32[304,256]{1,0:T(8,128)S(1)} %get-tuple-element.55.mine_ref), channel_id=1, source_target_pairs={{0,8},{4,20},{8,0},{12,28},{16,24},{20,4},{24,16},{28,12},{32,40},... | collective-permute-start | bytes 933896 | tf_op jit(solution)/shard_map/ppermute | solution.py:512
  32.5 2.8 %collective-permute-start.8 = (f32[152,256]{1,0:T(8,128)S(1)}, f32[152,256]{1,0:T(8,128)S(1)}, u32[]{:S(2)}, u32[]{:S(2)}) collective-permute-start(f32[152,256]{1,0:T(8,128)S(1)} %get-tuple-element.56), channel_id=1, source_target_pairs={{0,24},{4,28},{8,16},{12,20},{16,8},{20,12},{24,0},{28,4},{32,56},... | collective-permute-start | bytes 466952 | tf_op jit(solution)/shard_map/ppermute | solution.py:497
  35.4 10.9 %collective-permute-done.8.this_ref = f32[152,256]{1,0:T(8,128)S(1)} collective-permute-done((f32[152,256]{1,0:T(8,128)S(1)}, f32[152,256]{1,0:T(8,128)S(1)}, u32[]{:S(2)}, u32[]{:S(2)}) %collective-permute-start.8) | collective-permute-done | bytes 155680 | tf_op jit(solution)/shard_map/ppermute | solution.py:497
  46.8 1.3 %collective-permute-done.10.that_ref = f32[152,256]{1,0:T(8,128)S(1)} collective-permute-done((f32[152,256]{1,0:T(8,128)S(1)}, f32[152,256]{1,0:T(8,128)S(1)}, u32[]{:S(2)}, u32[]{:S(2)}) %collective-permute-start.10) | collective-permute-done | bytes 155680 | tf_op jit(solution)/shard_map/ppermute | solution.py:497
  48.1 1.3 %shard_map.46 = (f32[304,256]{1,0:T(8,128)S(1)}, f32[304,256]{1,0:T(8,128)S(1)}, f32[304,256]{1,0:T(8,128)S(1)}, f32[152,256]{1,0:T(8,128)S(1)}) custom-call(s32[1]{0:T(128)} %bitcast.2.code_ref, f32[304,256]{1,0:T(8,128)S(1)} %get-tuple-element.55.mine_ref, f32[304,256]{1,0:T(8,128)S(1)} %collective-permute-done.7.here_ref, ...), custom_call_target="tpu_custom_call" | custom-call | flops 717225984 | bytes 1048576 | tf_op jit(solution)/shard_map/pallas_call | solution.py:339
  49.4 5.1 %collective-permute-start.11 = (f32[152,256]{1,0:T(8,128)S(1)}, f32[152,256]{1,0:T(8,128)S(1)}, u32[]{:S(2)}, u32[]{:S(2)}) collective-permute-start(f32[152,256]{1,0:T(8,128)S(1)} %get-tuple-element.61), channel_id=1, source_target_pairs={{0,56},{4,60},{8,48},{12,52},{16,40},{20,44},{24,32},{28,36},{32,2... | collective-permute-start | bytes 466952 | tf_op jit(solution)/shard_map/ppermute | solution.py:497
  54.5 7.8 %collective-permute-done.11.refs_1_ = f32[152,256]{1,0:T(8,128)S(1)} collective-permute-done((f32[152,256]{1,0:T(8,128)S(1)}, f32[152,256]{1,0:T(8,128)S(1)}, u32[]{:S(2)}, u32[]{:S(2)}) %collective-permute-start.11) | collective-permute-done | bytes 155680 | tf_op jit(solution)/shard_map/ppermute | solution.py:497
  62.4 1.4 %collective-permute-done.12.refs_2_ = f32[152,256]{1,0:T(8,128)S(1)} collective-permute-done((f32[152,256]{1,0:T(8,128)S(1)}, f32[152,256]{1,0:T(8,128)S(1)}, u32[]{:S(2)}, u32[]{:S(2)}) %collective-permute-start.12) | collective-permute-done | bytes 155680 | tf_op jit(solution)/shard_map/ppermute | solution.py:497
  64.2 1.3 %collective-permute-start.16 = (f32[304,256]{1,0:T(8,128)S(1)}, f32[304,256]{1,0:T(8,128)S(1)}, u32[]{:S(2)}, u32[]{:S(2)}) collective-permute-start(f32[304,256]{1,0:T(8,128)S(1)} %shard_map.51.map_ref), channel_id=1, source_target_pairs={{128,192},{132,196},{136,200},{140,204},{144,208},{148,212},{152,2... | collective-permute-start | bytes 933896 | tf_op jit(solution)/shard_map/ppermute | solution.py:551
  66.4 1.3 %collective-permute-start.14 = (f32[32,256]{1,0:T(8,128)S(1)}, f32[32,256]{1,0:T(8,128)S(1)}, u32[]{:S(2)}, u32[]{:S(2)}) collective-permute-start(f32[32,256]{1,0:T(8,128)S(1)} %shard_map.52), channel_id=1, source_target_pairs={{64,192},{68,196},{72,200},{76,204},{80,208},{84,212},{88,216},{92... | collective-permute-start | bytes 98312 | tf_op jit(solution)/shard_map/ppermute | solution.py:551
  68.4 7.1 %collective-permute-done.16.beside_ref = f32[304,256]{1,0:T(8,128)S(1)} collective-permute-done((f32[304,256]{1,0:T(8,128)S(1)}, f32[304,256]{1,0:T(8,128)S(1)}, u32[]{:S(2)}, u32[]{:S(2)}) %collective-permute-start.16) | collective-permute-done | bytes 311328 | tf_op jit(solution)/shard_map/ppermute | solution.py:551
  76.0 2.5 %shard_map.54 = (f32[8,8,256]{2,1,0:T(8,128)S(1)}, f32[8,8,256]{2,1,0:T(8,128)S(1)}, f32[8,8,256]{2,1,0:T(8,128)S(1)}, f32[8,8,256]{2,1,0:T(8,128)S(1)}) custom-call(s32[1]{0:T(128)} %bitcast.code_ref, f32[32,256]{1,0:T(8,128)S(1)} %collective-permute-done.14.one_ref, f32[32,256]{1,0:T(8,128)S(1)} %collective-permute-done.15.two_ref, ...), custom_call_target="tpu_custom_call" | custom-call | flops 226492416 | bytes 1048576 | tf_op jit(solution)/shard_map/pallas_call | solution.py:469
  78.5 4.4 %collective-permute-start.18 = (f32[8,8,256]{2,1,0:T(8,128)S(1)}, f32[8,8,256]{2,1,0:T(8,128)S(1)}, u32[]{:S(2)}, u32[]{:S(2)}) collective-permute-start(f32[8,8,256]{2,1,0:T(8,128)S(1)} %get-tuple-element.75), channel_id=1, source_target_pairs={{0,2},{1,3},{2,0},{3,1},{4,6},{5,7},{6,4},{7,5},{8,10},{9,11},{10,... | collective-permute-start | bytes 196616 | tf_op jit(solution)/shard_map/ppermute | solution.py:497
  83.3 2.7 %collective-permute-done.18.refs_2_ = f32[8,8,256]{2,1,0:T(8,128)S(1)} collective-permute-done((f32[8,8,256]{2,1,0:T(8,128)S(1)}, f32[8,8,256]{2,1,0:T(8,128)S(1)}, u32[]{:S(2)}, u32[]{:S(2)}) %collective-permute-start.18) | collective-permute-done | bytes 65568 | tf_op jit(solution)/shard_map/ppermute | solution.py:497
  85.9 2.5 %collective-permute-done.19.refs_3_ = f32[8,8,256]{2,1,0:T(8,128)S(1)} collective-permute-done((f32[8,8,256]{2,1,0:T(8,128)S(1)}, f32[8,8,256]{2,1,0:T(8,128)S(1)}, u32[]{:S(2)}, u32[]{:S(2)}) %collective-permute-start.19) | collective-permute-done | bytes 65568 | tf_op jit(solution)/shard_map/ppermute | solution.py:497
  (41 shorter events, 8.2 us)
Async XLA Ops:
  0.0 0.9 %copy-start.1 = (f32[8,32,256]{2,1,0:T(8,128)S(1)}, f32[8,32,256]{2,1,0:T(8,128)}, u32[]{:S(2)}) copy-start(f32[8,32,256]{2,1,0:T(8,128)} %forcing_ref.1) | copy-start | bytes 786436
  1.0 9.6 %collective-permute-start = (f32[8,8,256]{2,1,0:T(8,128)S(1)}, f32[8,8,256]{2,1,0:T(8,128)S(1)}, u32[]{:S(2)}, u32[]{:S(2)}) collective-permute-start(f32[8,8,256]{2,1,0:T(8,128)S(1)} %get-tuple-element.42), channel_id=1, source_target_pairs={{0,1},{1,0},{2,3},{3,2},{4,5},{5,4},{6,7},{7,6},{8,9},{9,8},{10,11... | collective-permute-start | bytes 196616 | tf_op jit(solution)/shard_map/ppermute | solution.py:497
  2.6 7.9 %collective-permute-start.1 = (f32[8,8,256]{2,1,0:T(8,128)S(1)}, f32[8,8,256]{2,1,0:T(8,128)S(1)}, u32[]{:S(2)}, u32[]{:S(2)}) collective-permute-start(f32[8,8,256]{2,1,0:T(8,128)S(1)} %get-tuple-element.43), channel_id=1, source_target_pairs={{0,2},{1,3},{2,0},{3,1},{4,6},{5,7},{6,4},{7,5},{8,10},{9,11},{10,... | collective-permute-start | bytes 196616 | tf_op jit(solution)/shard_map/ppermute | solution.py:497
  5.5 5.6 %copy-start = (f32[8,256,256]{2,1,0:T(8,128)S(1)}, f32[8,256,256]{2,1,0:T(8,128)}, u32[]{:S(2)}) copy-start(f32[8,256,256]{2,1,0:T(8,128)} %blocks_ref.3) | copy-start | bytes 6291460
  5.5 5.5 %collective-permute-start.2 = (f32[8,8,256]{2,1,0:T(8,128)S(1)}, f32[8,8,256]{2,1,0:T(8,128)S(1)}, u32[]{:S(2)}, u32[]{:S(2)}) collective-permute-start(f32[8,8,256]{2,1,0:T(8,128)S(1)} %get-tuple-element.44), channel_id=1, source_target_pairs={{0,3},{1,2},{2,1},{3,0},{4,7},{5,6},{6,5},{7,4},{8,11},{9,10},{10,... | collective-permute-start | bytes 196616 | tf_op jit(solution)/shard_map/ppermute | solution.py:497
  5.8 0.8 copy-start.2
  11.0 8.0 %collective-permute-start.3 = (f32[272,256]{1,0:T(8,128)S(1)}, f32[272,256]{1,0:T(8,128)S(1)}, u32[]{:S(2)}, u32[]{:S(2)}) collective-permute-start(f32[272,256]{1,0:T(8,128)S(1)} %get-tuple-element.46.refs_0_), channel_id=1, source_target_pairs={{0,1},{1,0},{2,3},{3,2},{4,5},{5,4},{6,7},{7,6},{8,9},{9,8},{10,11... | collective-permute-start | bytes 835592 | tf_op jit(solution)/shard_map/ppermute | solution.py:497
  12.7 6.3 %collective-permute-start.4 = (f32[32,256]{1,0:T(8,128)S(1)}, f32[32,256]{1,0:T(8,128)S(1)}, u32[]{:S(2)}, u32[]{:S(2)}) collective-permute-start(f32[32,256]{1,0:T(8,128)S(1)} %get-tuple-element.51.refs_1_), channel_id=1, source_target_pairs={{0,1},{1,0},{2,3},{3,2},{4,5},{5,4},{6,7},{7,6},{8,9},{9,8},{10,11... | collective-permute-start | bytes 98312 | tf_op jit(solution)/shard_map/ppermute | solution.py:497
  19.5 8.5 %collective-permute-start.5 = (f32[304,256]{1,0:T(8,128)S(1)}, f32[304,256]{1,0:T(8,128)S(1)}, u32[]{:S(2)}, u32[]{:S(2)}) collective-permute-start(f32[304,256]{1,0:T(8,128)S(1)} %shard_map.40.refs_0_), channel_id=1, source_target_pairs={{0,3},{1,2},{2,1},{3,0},{4,7},{5,6},{6,5},{7,4},{8,11},{9,10},{10,... | collective-permute-start | bytes 933896 | tf_op jit(solution)/shard_map/ppermute | solution.py:497
  28.4 1.7 %collective-permute-start.6 = (f32[304,256]{1,0:T(8,128)S(1)}, f32[304,256]{1,0:T(8,128)S(1)}, u32[]{:S(2)}, u32[]{:S(2)}) collective-permute-start(f32[304,256]{1,0:T(8,128)S(1)} %shard_map.42.refs_0_), channel_id=1, source_target_pairs={{0,4},{4,0},{8,12},{12,8},{16,20},{20,16},{24,28},{28,24},{32,36},... | collective-permute-start | bytes 933896 | tf_op jit(solution)/shard_map/ppermute | solution.py:497
  30.5 15.7 %collective-permute-start.7 = (f32[304,256]{1,0:T(8,128)S(1)}, f32[304,256]{1,0:T(8,128)S(1)}, u32[]{:S(2)}, u32[]{:S(2)}) collective-permute-start(f32[304,256]{1,0:T(8,128)S(1)} %get-tuple-element.55.mine_ref), channel_id=1, source_target_pairs={{0,8},{4,20},{8,0},{12,28},{16,24},{20,4},{24,16},{28,12},{32,40},... | collective-permute-start | bytes 933896 | tf_op jit(solution)/shard_map/ppermute | solution.py:512
  32.5 13.7 %collective-permute-start.8 = (f32[152,256]{1,0:T(8,128)S(1)}, f32[152,256]{1,0:T(8,128)S(1)}, u32[]{:S(2)}, u32[]{:S(2)}) collective-permute-start(f32[152,256]{1,0:T(8,128)S(1)} %get-tuple-element.56), channel_id=1, source_target_pairs={{0,24},{4,28},{8,16},{12,20},{16,8},{20,12},{24,0},{28,4},{32,56},... | collective-permute-start | bytes 466952 | tf_op jit(solution)/shard_map/ppermute | solution.py:497
  46.3 1.8 %collective-permute-start.9 = (f32[304,256]{1,0:T(8,128)S(1)}, f32[304,256]{1,0:T(8,128)S(1)}, u32[]{:S(2)}, u32[]{:S(2)}) collective-permute-start(f32[304,256]{1,0:T(8,128)S(1)} %collective-permute-done.7.here_ref), channel_id=1, source_target_pairs={{0,4},{4,0},{8,12},{12,8},{16,20},{20,16},{24,28},{28,24},{32,36},... | collective-permute-start | bytes 933896 | tf_op jit(solution)/shard_map/ppermute | solution.py:497
  46.4 1.7 %collective-permute-start.10 = (f32[152,256]{1,0:T(8,128)S(1)}, f32[152,256]{1,0:T(8,128)S(1)}, u32[]{:S(2)}, u32[]{:S(2)}) collective-permute-start(f32[152,256]{1,0:T(8,128)S(1)} %collective-permute-done.8.this_ref), channel_id=1, source_target_pairs={{0,4},{4,0},{8,12},{12,8},{16,20},{20,16},{24,28},{28,24},{32,36},... | collective-permute-start | bytes 466952 | tf_op jit(solution)/shard_map/ppermute | solution.py:497
  49.4 13.0 %collective-permute-start.11 = (f32[152,256]{1,0:T(8,128)S(1)}, f32[152,256]{1,0:T(8,128)S(1)}, u32[]{:S(2)}, u32[]{:S(2)}) collective-permute-start(f32[152,256]{1,0:T(8,128)S(1)} %get-tuple-element.61), channel_id=1, source_target_pairs={{0,56},{4,60},{8,48},{12,52},{16,40},{20,44},{24,32},{28,36},{32,2... | collective-permute-start | bytes 466952 | tf_op jit(solution)/shard_map/ppermute | solution.py:497
  62.4 1.4 %collective-permute-start.12 = (f32[152,256]{1,0:T(8,128)S(1)}, f32[152,256]{1,0:T(8,128)S(1)}, u32[]{:S(2)}, u32[]{:S(2)}) collective-permute-start(f32[152,256]{1,0:T(8,128)S(1)} %collective-permute-done.11.refs_1_), channel_id=1, source_target_pairs={{0,4},{4,0},{8,12},{12,8},{16,20},{20,16},{24,28},{28,24},{32,36},... | collective-permute-start | bytes 466952 | tf_op jit(solution)/shard_map/ppermute | solution.py:497
  64.2 11.3 %collective-permute-start.16 = (f32[304,256]{1,0:T(8,128)S(1)}, f32[304,256]{1,0:T(8,128)S(1)}, u32[]{:S(2)}, u32[]{:S(2)}) collective-permute-start(f32[304,256]{1,0:T(8,128)S(1)} %shard_map.51.map_ref), channel_id=1, source_target_pairs={{128,192},{132,196},{136,200},{140,204},{144,208},{148,212},{152,2... | collective-permute-start | bytes 933896 | tf_op jit(solution)/shard_map/ppermute | solution.py:551
  65.5 0.7 collective-permute-start.13
  66.4 9.5 %collective-permute-start.14 = (f32[32,256]{1,0:T(8,128)S(1)}, f32[32,256]{1,0:T(8,128)S(1)}, u32[]{:S(2)}, u32[]{:S(2)}) collective-permute-start(f32[32,256]{1,0:T(8,128)S(1)} %shard_map.52), channel_id=1, source_target_pairs={{64,192},{68,196},{72,200},{76,204},{80,208},{84,212},{88,216},{92... | collective-permute-start | bytes 98312 | tf_op jit(solution)/shard_map/ppermute | solution.py:551
  67.7 8.2 %collective-permute-start.15 = (f32[32,256]{1,0:T(8,128)S(1)}, f32[32,256]{1,0:T(8,128)S(1)}, u32[]{:S(2)}, u32[]{:S(2)}) collective-permute-start(f32[32,256]{1,0:T(8,128)S(1)} %shard_map.52), channel_id=1, source_target_pairs={{64,128},{68,132},{72,136},{76,140},{80,144},{84,148},{88,152},{92... | collective-permute-start | bytes 98312 | tf_op jit(solution)/shard_map/ppermute | solution.py:551
  78.4 4.8 %collective-permute-start.17 = (f32[8,8,256]{2,1,0:T(8,128)S(1)}, f32[8,8,256]{2,1,0:T(8,128)S(1)}, u32[]{:S(2)}, u32[]{:S(2)}) collective-permute-start(f32[8,8,256]{2,1,0:T(8,128)S(1)} %get-tuple-element.74), channel_id=1, source_target_pairs={{0,1},{1,0},{2,3},{3,2},{4,5},{5,4},{6,7},{7,6},{8,9},{9,8},{10,11... | collective-permute-start | bytes 196616 | tf_op jit(solution)/shard_map/ppermute | solution.py:497
  78.5 7.4 %collective-permute-start.18 = (f32[8,8,256]{2,1,0:T(8,128)S(1)}, f32[8,8,256]{2,1,0:T(8,128)S(1)}, u32[]{:S(2)}, u32[]{:S(2)}) collective-permute-start(f32[8,8,256]{2,1,0:T(8,128)S(1)} %get-tuple-element.75), channel_id=1, source_target_pairs={{0,2},{1,3},{2,0},{3,1},{4,6},{5,7},{6,4},{7,5},{8,10},{9,11},{10,... | collective-permute-start | bytes 196616 | tf_op jit(solution)/shard_map/ppermute | solution.py:497
  82.9 5.5 %collective-permute-start.19 = (f32[8,8,256]{2,1,0:T(8,128)S(1)}, f32[8,8,256]{2,1,0:T(8,128)S(1)}, u32[]{:S(2)}, u32[]{:S(2)}) collective-permute-start(f32[8,8,256]{2,1,0:T(8,128)S(1)} %get-tuple-element.76), channel_id=1, source_target_pairs={{0,3},{1,2},{2,1},{3,0},{4,7},{5,6},{6,5},{7,4},{8,11},{9,10},{10,... | collective-permute-start | bytes 196616 | tf_op jit(solution)/shard_map/ppermute | solution.py:497

commit v14 on v13

--- a/solution.py
+++ b/solution.py
@@ -35,7 +35,9 @@
 def dot3(a, b):
     product = functools.partial(jnp.dot, preferred_element_type=F32)
     (a_high, a_low), (b_high, b_low) = split(a), split(b)
-    return product(a_high, b_high) + (product(a_high, b_low) + product(a_low, b_high))
+    rows = a.shape[0]
+    both = product(jnp.concatenate([a_high, a_low], axis=0), b_high)
+    return both[:rows] + (product(a_high, b_low) + both[rows:])
 
 
 def shape(*dims):

time: 89.7 us -> 89.7 us (level)
  no operation moved by 1% of the time
where the time goes in v14:
time: 89.7 us; the launch traced here: 89.1 us
  waiting for transfers between devices  45.8 us (51%)
  starting transfers between devices  29 us (32%)
  Pallas kernels  12.2 us (14%)
  local copies, waits for them, and re-layouts  1.77 us (2%)
    ppermute x15, waiting for transfers between devices, partner(): return lax.ppermute(value, axis, [(i, i ^ mask) for i in range(count)])  38.7 us
    ppermute x15, starting transfers between devices, partner(): return lax.ppermute(value, axis, [(i, i ^ mask) for i in range(count)])  23 us
    ppermute x4, waiting for transfers between devices, across(): return lax.ppermute(value, 'line', pairs)  7.13 us
    pallas_call x1, Pallas kernels, prefix_maps(): call(maps_kernel, [VMEM, HBM], [shape(*blocks.shape), shape(levels + PAD,...  3.93 us
    ppermute x4, starting transfers between devices, across(): return lax.ppermute(value, 'line', pairs)  3.91 us
    pallas_call x1, Pallas kernels, finish(): call(finish_kernel, [SMEM, VMEM, VMEM, VMEM, HBM, VMEM], [shape(lines //...  2.46 us
    ppermute x1, starting transfers between devices, along_four(): lax.ppermute(total, 'line', pairs)  2.07 us
  transfers between devices with their start and end apart: 20, of which 11 were waited for; matrix products, arithmetic and copies ran while one was open for 0% of the time, Pallas kernels for 7%

profile of v14, /device:TPU:6, one launch (start us, length us, event | category | flops | bytes accessed | tf_op | source)
XLA Modules:
  0.0 89.1 jit_solution(10599204464099633706)
XLA Ops:
  1.0 1.7 %collective-permute-start = (f32[8,8,256]{2,1,0:T(8,128)S(1)}, f32[8,8,256]{2,1,0:T(8,128)S(1)}, u32[]{:S(2)}, u32[]{:S(2)}) collective-permute-start(f32[8,8,256]{2,1,0:T(8,128)S(1)} %get-tuple-element.42), channel_id=1, source_target_pairs={{0,1},{1,0},{2,3},{3,2},{4,5},{5,4},{6,7},{7,6},{8,9},{9,8},{10,11... | collective-permute-start | bytes 196616 | tf_op jit(solution)/shard_map/ppermute | solution.py:499
  2.6 2.9 %collective-permute-start.1 = (f32[8,8,256]{2,1,0:T(8,128)S(1)}, f32[8,8,256]{2,1,0:T(8,128)S(1)}, u32[]{:S(2)}, u32[]{:S(2)}) collective-permute-start(f32[8,8,256]{2,1,0:T(8,128)S(1)} %get-tuple-element.43), channel_id=1, source_target_pairs={{0,2},{1,3},{2,0},{3,1},{4,6},{5,7},{6,4},{7,5},{8,10},{9,11},{10,... | collective-permute-start | bytes 196616 | tf_op jit(solution)/shard_map/ppermute | solution.py:499
  6.6 3.9 %shard_map.38 = (f32[8,256,256]{2,1,0:T(8,128)}, f32[272,256]{1,0:T(8,128)S(1)}) custom-call(f32[8,256]{1,0:T(8,128)S(1)} %copy-done.2, f32[8,256,256]{2,1,0:T(8,128)} %blocks_ref.3), custom_call_target="tpu_custom_call" | custom-call | flops 1610612736 | bytes 1048576 | tf_op jit(solution)/shard_map/pallas_call | solution.py:142
  11.1 1.3 %shard_map.39 = (f32[8,32,256]{2,1,0:T(8,128)S(1)}, f32[32,256]{1,0:T(8,128)S(1)}) custom-call(s32[1]{0:T(128)} %bitcast.code_ref, f32[8,256]{1,0:T(8,128)S(1)} %copy-done.2, f32[8,256,256]{2,1,0:T(8,128)S(1)} %copy-done, f32[8,8,256]{2,1,0:T(8,128)S(1)} %get-tuple-element.47.refs_0_, f32[8,8,256]{2,1,0:T(8,128)S(1)} %collective-permute-done.refs_1_, ...), custom_call_target="tpu_custom_call" | custom-call | flops 201326592 | bytes 1048576 | tf_op jit(solution)/shard_map/pallas_call | solution.py:206
  12.4 2.1 %collective-permute-start.4 = (f32[32,256]{1,0:T(8,128)S(1)}, f32[32,256]{1,0:T(8,128)S(1)}, u32[]{:S(2)}, u32[]{:S(2)}) collective-permute-start(f32[32,256]{1,0:T(8,128)S(1)} %get-tuple-element.51.refs_1_), channel_id=1, source_target_pairs={{0,1},{1,0},{2,3},{3,2},{4,5},{5,4},{6,7},{7,6},{8,9},{9,8},{10,11... | collective-permute-start | bytes 98312 | tf_op jit(solution)/shard_map/ppermute | solution.py:499
  14.5 4.5 %collective-permute-done.4.refs_3_.refs_1_ = f32[32,256]{1,0:T(8,128)S(1)} collective-permute-done((f32[32,256]{1,0:T(8,128)S(1)}, f32[32,256]{1,0:T(8,128)S(1)}, u32[]{:S(2)}, u32[]{:S(2)}) %collective-permute-start.4) | collective-permute-done | bytes 32800 | tf_op jit(solution)/shard_map/ppermute | solution.py:499
  19.4 2.9 %collective-permute-start.5 = (f32[304,256]{1,0:T(8,128)S(1)}, f32[304,256]{1,0:T(8,128)S(1)}, u32[]{:S(2)}, u32[]{:S(2)}) collective-permute-start(f32[304,256]{1,0:T(8,128)S(1)} %shard_map.40.refs_0_), channel_id=1, source_target_pairs={{0,3},{1,2},{2,1},{3,0},{4,7},{5,6},{6,5},{7,4},{8,11},{9,10},{10,... | collective-permute-start | bytes 933896 | tf_op jit(solution)/shard_map/ppermute | solution.py:499
  22.4 5.5 %collective-permute-done.5.refs_1_.refs_0_ = f32[304,256]{1,0:T(8,128)S(1)} collective-permute-done((f32[304,256]{1,0:T(8,128)S(1)}, f32[304,256]{1,0:T(8,128)S(1)}, u32[]{:S(2)}, u32[]{:S(2)}) %collective-permute-start.5) | collective-permute-done | bytes 311328 | tf_op jit(solution)/shard_map/ppermute | solution.py:499
  28.5 1.5 %collective-permute-done.6.refs_1_.refs_0_ = f32[304,256]{1,0:T(8,128)S(1)} collective-permute-done((f32[304,256]{1,0:T(8,128)S(1)}, f32[304,256]{1,0:T(8,128)S(1)}, u32[]{:S(2)}, u32[]{:S(2)}) %collective-permute-start.6) | collective-permute-done | bytes 311328 | tf_op jit(solution)/shard_map/ppermute | solution.py:499
  30.4 2.1 %collective-permute-start.7 = (f32[304,256]{1,0:T(8,128)S(1)}, f32[304,256]{1,0:T(8,128)S(1)}, u32[]{:S(2)}, u32[]{:S(2)}) collective-permute-start(f32[304,256]{1,0:T(8,128)S(1)} %get-tuple-element.55.mine_ref), channel_id=1, source_target_pairs={{0,8},{4,20},{8,0},{12,28},{16,24},{20,4},{24,16},{28,12},{32,40},... | collective-permute-start | bytes 933896 | tf_op jit(solution)/shard_map/ppermute | solution.py:514
  32.5 2.8 %collective-permute-start.8 = (f32[152,256]{1,0:T(8,128)S(1)}, f32[152,256]{1,0:T(8,128)S(1)}, u32[]{:S(2)}, u32[]{:S(2)}) collective-permute-start(f32[152,256]{1,0:T(8,128)S(1)} %get-tuple-element.56), channel_id=1, source_target_pairs={{0,24},{4,28},{8,16},{12,20},{16,8},{20,12},{24,0},{28,4},{32,56},... | collective-permute-start | bytes 466952 | tf_op jit(solution)/shard_map/ppermute | solution.py:499
  35.3 10.9 %collective-permute-done.8.this_ref = f32[152,256]{1,0:T(8,128)S(1)} collective-permute-done((f32[152,256]{1,0:T(8,128)S(1)}, f32[152,256]{1,0:T(8,128)S(1)}, u32[]{:S(2)}, u32[]{:S(2)}) %collective-permute-start.8) | collective-permute-done | bytes 155680 | tf_op jit(solution)/shard_map/ppermute | solution.py:499
  46.7 1.3 %collective-permute-done.10.that_ref = f32[152,256]{1,0:T(8,128)S(1)} collective-permute-done((f32[152,256]{1,0:T(8,128)S(1)}, f32[152,256]{1,0:T(8,128)S(1)}, u32[]{:S(2)}, u32[]{:S(2)}) %collective-permute-start.10) | collective-permute-done | bytes 155680 | tf_op jit(solution)/shard_map/ppermute | solution.py:499
  48.0 1.3 %shard_map.46 = (f32[304,256]{1,0:T(8,128)S(1)}, f32[304,256]{1,0:T(8,128)S(1)}, f32[304,256]{1,0:T(8,128)S(1)}, f32[152,256]{1,0:T(8,128)S(1)}) custom-call(s32[1]{0:T(128)} %bitcast.2.code_ref, f32[304,256]{1,0:T(8,128)S(1)} %get-tuple-element.55.mine_ref, f32[304,256]{1,0:T(8,128)S(1)} %collective-permute-done.7.here_ref, ...), custom_call_target="tpu_custom_call" | custom-call | flops 717225984 | bytes 1048576 | tf_op jit(solution)/shard_map/pallas_call | solution.py:341
  49.3 5.1 %collective-permute-start.11 = (f32[152,256]{1,0:T(8,128)S(1)}, f32[152,256]{1,0:T(8,128)S(1)}, u32[]{:S(2)}, u32[]{:S(2)}) collective-permute-start(f32[152,256]{1,0:T(8,128)S(1)} %get-tuple-element.61), channel_id=1, source_target_pairs={{0,56},{4,60},{8,48},{12,52},{16,40},{20,44},{24,32},{28,36},{32,2... | collective-permute-start | bytes 466952 | tf_op jit(solution)/shard_map/ppermute | solution.py:499
  54.5 7.8 %collective-permute-done.11.refs_1_ = f32[152,256]{1,0:T(8,128)S(1)} collective-permute-done((f32[152,256]{1,0:T(8,128)S(1)}, f32[152,256]{1,0:T(8,128)S(1)}, u32[]{:S(2)}, u32[]{:S(2)}) %collective-permute-start.11) | collective-permute-done | bytes 155680 | tf_op jit(solution)/shard_map/ppermute | solution.py:499
  62.3 1.4 %collective-permute-done.12.refs_2_ = f32[152,256]{1,0:T(8,128)S(1)} collective-permute-done((f32[152,256]{1,0:T(8,128)S(1)}, f32[152,256]{1,0:T(8,128)S(1)}, u32[]{:S(2)}, u32[]{:S(2)}) %collective-permute-start.12) | collective-permute-done | bytes 155680 | tf_op jit(solution)/shard_map/ppermute | solution.py:499
  64.1 1.3 %collective-permute-start.16 = (f32[304,256]{1,0:T(8,128)S(1)}, f32[304,256]{1,0:T(8,128)S(1)}, u32[]{:S(2)}, u32[]{:S(2)}) collective-permute-start(f32[304,256]{1,0:T(8,128)S(1)} %shard_map.51.map_ref), channel_id=1, source_target_pairs={{128,192},{132,196},{136,200},{140,204},{144,208},{148,212},{152,2... | collective-permute-start | bytes 933896 | tf_op jit(solution)/shard_map/ppermute | solution.py:553
  66.3 1.3 %collective-permute-start.14 = (f32[32,256]{1,0:T(8,128)S(1)}, f32[32,256]{1,0:T(8,128)S(1)}, u32[]{:S(2)}, u32[]{:S(2)}) collective-permute-start(f32[32,256]{1,0:T(8,128)S(1)} %shard_map.52), channel_id=1, source_target_pairs={{64,192},{68,196},{72,200},{76,204},{80,208},{84,212},{88,216},{92... | collective-permute-start | bytes 98312 | tf_op jit(solution)/shard_map/ppermute | solution.py:553
  68.3 7.1 %collective-permute-done.16.beside_ref = f32[304,256]{1,0:T(8,128)S(1)} collective-permute-done((f32[304,256]{1,0:T(8,128)S(1)}, f32[304,256]{1,0:T(8,128)S(1)}, u32[]{:S(2)}, u32[]{:S(2)}) %collective-permute-start.16) | collective-permute-done | bytes 311328 | tf_op jit(solution)/shard_map/ppermute | solution.py:553
  75.9 2.5 %shard_map.54 = (f32[8,8,256]{2,1,0:T(8,128)S(1)}, f32[8,8,256]{2,1,0:T(8,128)S(1)}, f32[8,8,256]{2,1,0:T(8,128)S(1)}, f32[8,8,256]{2,1,0:T(8,128)S(1)}) custom-call(s32[1]{0:T(128)} %bitcast.code_ref, f32[32,256]{1,0:T(8,128)S(1)} %collective-permute-done.14.one_ref, f32[32,256]{1,0:T(8,128)S(1)} %collective-permute-done.15.two_ref, ...), custom_call_target="tpu_custom_call" | custom-call | flops 226492416 | bytes 1048576 | tf_op jit(solution)/shard_map/pallas_call | solution.py:471
  78.4 4.4 %collective-permute-start.18 = (f32[8,8,256]{2,1,0:T(8,128)S(1)}, f32[8,8,256]{2,1,0:T(8,128)S(1)}, u32[]{:S(2)}, u32[]{:S(2)}) collective-permute-start(f32[8,8,256]{2,1,0:T(8,128)S(1)} %get-tuple-element.75), channel_id=1, source_target_pairs={{0,2},{1,3},{2,0},{3,1},{4,6},{5,7},{6,4},{7,5},{8,10},{9,11},{10,... | collective-permute-start | bytes 196616 | tf_op jit(solution)/shard_map/ppermute | solution.py:499
  83.2 2.7 %collective-permute-done.18.refs_2_ = f32[8,8,256]{2,1,0:T(8,128)S(1)} collective-permute-done((f32[8,8,256]{2,1,0:T(8,128)S(1)}, f32[8,8,256]{2,1,0:T(8,128)S(1)}, u32[]{:S(2)}, u32[]{:S(2)}) %collective-permute-start.18) | collective-permute-done | bytes 65568 | tf_op jit(solution)/shard_map/ppermute | solution.py:499
  85.8 2.5 %collective-permute-done.19.refs_3_ = f32[8,8,256]{2,1,0:T(8,128)S(1)} collective-permute-done((f32[8,8,256]{2,1,0:T(8,128)S(1)}, f32[8,8,256]{2,1,0:T(8,128)S(1)}, u32[]{:S(2)}, u32[]{:S(2)}) %collective-permute-start.19) | collective-permute-done | bytes 65568 | tf_op jit(solution)/shard_map/ppermute | solution.py:499
  (41 shorter events, 8.1 us)
Async XLA Ops:
  0.0 0.9 %copy-start.1 = (f32[8,32,256]{2,1,0:T(8,128)S(1)}, f32[8,32,256]{2,1,0:T(8,128)}, u32[]{:S(2)}) copy-start(f32[8,32,256]{2,1,0:T(8,128)} %forcing_ref.1) | copy-start | bytes 786436
  1.0 9.5 %collective-permute-start = (f32[8,8,256]{2,1,0:T(8,128)S(1)}, f32[8,8,256]{2,1,0:T(8,128)S(1)}, u32[]{:S(2)}, u32[]{:S(2)}) collective-permute-start(f32[8,8,256]{2,1,0:T(8,128)S(1)} %get-tuple-element.42), channel_id=1, source_target_pairs={{0,1},{1,0},{2,3},{3,2},{4,5},{5,4},{6,7},{7,6},{8,9},{9,8},{10,11... | collective-permute-start | bytes 196616 | tf_op jit(solution)/shard_map/ppermute | solution.py:499
  2.6 7.9 %collective-permute-start.1 = (f32[8,8,256]{2,1,0:T(8,128)S(1)}, f32[8,8,256]{2,1,0:T(8,128)S(1)}, u32[]{:S(2)}, u32[]{:S(2)}) collective-permute-start(f32[8,8,256]{2,1,0:T(8,128)S(1)} %get-tuple-element.43), channel_id=1, source_target_pairs={{0,2},{1,3},{2,0},{3,1},{4,6},{5,7},{6,4},{7,5},{8,10},{9,11},{10,... | collective-permute-start | bytes 196616 | tf_op jit(solution)/shard_map/ppermute | solution.py:499
  5.5 5.5 %copy-start = (f32[8,256,256]{2,1,0:T(8,128)S(1)}, f32[8,256,256]{2,1,0:T(8,128)}, u32[]{:S(2)}) copy-start(f32[8,256,256]{2,1,0:T(8,128)} %blocks_ref.3) | copy-start | bytes 6291460
  5.5 5.5 %collective-permute-start.2 = (f32[8,8,256]{2,1,0:T(8,128)S(1)}, f32[8,8,256]{2,1,0:T(8,128)S(1)}, u32[]{:S(2)}, u32[]{:S(2)}) collective-permute-start(f32[8,8,256]{2,1,0:T(8,128)S(1)} %get-tuple-element.44), channel_id=1, source_target_pairs={{0,3},{1,2},{2,1},{3,0},{4,7},{5,6},{6,5},{7,4},{8,11},{9,10},{10,... | collective-permute-start | bytes 196616 | tf_op jit(solution)/shard_map/ppermute | solution.py:499
  5.8 0.8 copy-start.2
  11.0 8.0 %collective-permute-start.3 = (f32[272,256]{1,0:T(8,128)S(1)}, f32[272,256]{1,0:T(8,128)S(1)}, u32[]{:S(2)}, u32[]{:S(2)}) collective-permute-start(f32[272,256]{1,0:T(8,128)S(1)} %get-tuple-element.46.refs_0_), channel_id=1, source_target_pairs={{0,1},{1,0},{2,3},{3,2},{4,5},{5,4},{6,7},{7,6},{8,9},{9,8},{10,11... | collective-permute-start | bytes 835592 | tf_op jit(solution)/shard_map/ppermute | solution.py:499
  12.4 6.6 %collective-permute-start.4 = (f32[32,256]{1,0:T(8,128)S(1)}, f32[32,256]{1,0:T(8,128)S(1)}, u32[]{:S(2)}, u32[]{:S(2)}) collective-permute-start(f32[32,256]{1,0:T(8,128)S(1)} %get-tuple-element.51.refs_1_), channel_id=1, source_target_pairs={{0,1},{1,0},{2,3},{3,2},{4,5},{5,4},{6,7},{7,6},{8,9},{9,8},{10,11... | collective-permute-start | bytes 98312 | tf_op jit(solution)/shard_map/ppermute | solution.py:499
  19.4 8.5 %collective-permute-start.5 = (f32[304,256]{1,0:T(8,128)S(1)}, f32[304,256]{1,0:T(8,128)S(1)}, u32[]{:S(2)}, u32[]{:S(2)}) collective-permute-start(f32[304,256]{1,0:T(8,128)S(1)} %shard_map.40.refs_0_), channel_id=1, source_target_pairs={{0,3},{1,2},{2,1},{3,0},{4,7},{5,6},{6,5},{7,4},{8,11},{9,10},{10,... | collective-permute-start | bytes 933896 | tf_op jit(solution)/shard_map/ppermute | solution.py:499
  28.3 1.7 %collective-permute-start.6 = (f32[304,256]{1,0:T(8,128)S(1)}, f32[304,256]{1,0:T(8,128)S(1)}, u32[]{:S(2)}, u32[]{:S(2)}) collective-permute-start(f32[304,256]{1,0:T(8,128)S(1)} %shard_map.42.refs_0_), channel_id=1, source_target_pairs={{0,4},{4,0},{8,12},{12,8},{16,20},{20,16},{24,28},{28,24},{32,36},... | collective-permute-start | bytes 933896 | tf_op jit(solution)/shard_map/ppermute | solution.py:499
  30.4 15.7 %collective-permute-start.7 = (f32[304,256]{1,0:T(8,128)S(1)}, f32[304,256]{1,0:T(8,128)S(1)}, u32[]{:S(2)}, u32[]{:S(2)}) collective-permute-start(f32[304,256]{1,0:T(8,128)S(1)} %get-tuple-element.55.mine_ref), channel_id=1, source_target_pairs={{0,8},{4,20},{8,0},{12,28},{16,24},{20,4},{24,16},{28,12},{32,40},... | collective-permute-start | bytes 933896 | tf_op jit(solution)/shard_map/ppermute | solution.py:514
  32.5 13.7 %collective-permute-start.8 = (f32[152,256]{1,0:T(8,128)S(1)}, f32[152,256]{1,0:T(8,128)S(1)}, u32[]{:S(2)}, u32[]{:S(2)}) collective-permute-start(f32[152,256]{1,0:T(8,128)S(1)} %get-tuple-element.56), channel_id=1, source_target_pairs={{0,24},{4,28},{8,16},{12,20},{16,8},{20,12},{24,0},{28,4},{32,56},... | collective-permute-start | bytes 466952 | tf_op jit(solution)/shard_map/ppermute | solution.py:499
  46.2 1.8 %collective-permute-start.9 = (f32[304,256]{1,0:T(8,128)S(1)}, f32[304,256]{1,0:T(8,128)S(1)}, u32[]{:S(2)}, u32[]{:S(2)}) collective-permute-start(f32[304,256]{1,0:T(8,128)S(1)} %collective-permute-done.7.here_ref), channel_id=1, source_target_pairs={{0,4},{4,0},{8,12},{12,8},{16,20},{20,16},{24,28},{28,24},{32,36},... | collective-permute-start | bytes 933896 | tf_op jit(solution)/shard_map/ppermute | solution.py:499
  46.3 1.7 %collective-permute-start.10 = (f32[152,256]{1,0:T(8,128)S(1)}, f32[152,256]{1,0:T(8,128)S(1)}, u32[]{:S(2)}, u32[]{:S(2)}) collective-permute-start(f32[152,256]{1,0:T(8,128)S(1)} %collective-permute-done.8.this_ref), channel_id=1, source_target_pairs={{0,4},{4,0},{8,12},{12,8},{16,20},{20,16},{24,28},{28,24},{32,36},... | collective-permute-start | bytes 466952 | tf_op jit(solution)/shard_map/ppermute | solution.py:499
  49.3 13.0 %collective-permute-start.11 = (f32[152,256]{1,0:T(8,128)S(1)}, f32[152,256]{1,0:T(8,128)S(1)}, u32[]{:S(2)}, u32[]{:S(2)}) collective-permute-start(f32[152,256]{1,0:T(8,128)S(1)} %get-tuple-element.61), channel_id=1, source_target_pairs={{0,56},{4,60},{8,48},{12,52},{16,40},{20,44},{24,32},{28,36},{32,2... | collective-permute-start | bytes 466952 | tf_op jit(solution)/shard_map/ppermute | solution.py:499
  62.3 1.4 %collective-permute-start.12 = (f32[152,256]{1,0:T(8,128)S(1)}, f32[152,256]{1,0:T(8,128)S(1)}, u32[]{:S(2)}, u32[]{:S(2)}) collective-permute-start(f32[152,256]{1,0:T(8,128)S(1)} %collective-permute-done.11.refs_1_), channel_id=1, source_target_pairs={{0,4},{4,0},{8,12},{12,8},{16,20},{20,16},{24,28},{28,24},{32,36},... | collective-permute-start | bytes 466952 | tf_op jit(solution)/shard_map/ppermute | solution.py:499
  64.1 11.3 %collective-permute-start.16 = (f32[304,256]{1,0:T(8,128)S(1)}, f32[304,256]{1,0:T(8,128)S(1)}, u32[]{:S(2)}, u32[]{:S(2)}) collective-permute-start(f32[304,256]{1,0:T(8,128)S(1)} %shard_map.51.map_ref), channel_id=1, source_target_pairs={{128,192},{132,196},{136,200},{140,204},{144,208},{148,212},{152,2... | collective-permute-start | bytes 933896 | tf_op jit(solution)/shard_map/ppermute | solution.py:553
  65.4 0.7 collective-permute-start.13
  66.3 9.5 %collective-permute-start.14 = (f32[32,256]{1,0:T(8,128)S(1)}, f32[32,256]{1,0:T(8,128)S(1)}, u32[]{:S(2)}, u32[]{:S(2)}) collective-permute-start(f32[32,256]{1,0:T(8,128)S(1)} %shard_map.52), channel_id=1, source_target_pairs={{64,192},{68,196},{72,200},{76,204},{80,208},{84,212},{88,216},{92... | collective-permute-start | bytes 98312 | tf_op jit(solution)/shard_map/ppermute | solution.py:553
  67.6 8.2 %collective-permute-start.15 = (f32[32,256]{1,0:T(8,128)S(1)}, f32[32,256]{1,0:T(8,128)S(1)}, u32[]{:S(2)}, u32[]{:S(2)}) collective-permute-start(f32[32,256]{1,0:T(8,128)S(1)} %shard_map.52), channel_id=1, source_target_pairs={{64,128},{68,132},{72,136},{76,140},{80,144},{84,148},{88,152},{92... | collective-permute-start | bytes 98312 | tf_op jit(solution)/shard_map/ppermute | solution.py:553
  78.3 4.8 %collective-permute-start.17 = (f32[8,8,256]{2,1,0:T(8,128)S(1)}, f32[8,8,256]{2,1,0:T(8,128)S(1)}, u32[]{:S(2)}, u32[]{:S(2)}) collective-permute-start(f32[8,8,256]{2,1,0:T(8,128)S(1)} %get-tuple-element.74), channel_id=1, source_target_pairs={{0,1},{1,0},{2,3},{3,2},{4,5},{5,4},{6,7},{7,6},{8,9},{9,8},{10,11... | collective-permute-start | bytes 196616 | tf_op jit(solution)/shard_map/ppermute | solution.py:499
  78.4 7.4 %collective-permute-start.18 = (f32[8,8,256]{2,1,0:T(8,128)S(1)}, f32[8,8,256]{2,1,0:T(8,128)S(1)}, u32[]{:S(2)}, u32[]{:S(2)}) collective-permute-start(f32[8,8,256]{2,1,0:T(8,128)S(1)} %get-tuple-element.75), channel_id=1, source_target_pairs={{0,2},{1,3},{2,0},{3,1},{4,6},{5,7},{6,4},{7,5},{8,10},{9,11},{10,... | collective-permute-start | bytes 196616 | tf_op jit(solution)/shard_map/ppermute | solution.py:499
  82.9 5.5 %collective-permute-start.19 = (f32[8,8,256]{2,1,0:T(8,128)S(1)}, f32[8,8,256]{2,1,0:T(8,128)S(1)}, u32[]{:S(2)}, u32[]{:S(2)}) collective-permute-start(f32[8,8,256]{2,1,0:T(8,128)S(1)} %get-tuple-element.76), channel_id=1, source_target_pairs={{0,3},{1,2},{2,1},{3,0},{4,7},{5,6},{6,5},{7,4},{8,11},{9,10},{10,... | collective-permute-start | bytes 196616 | tf_op jit(solution)/shard_map/ppermute | solution.py:499
